TPU v7x, 512 devices: a whole 4x4x16 slice. The times are simulated.
512 devices in a mesh: outer: 4 (over y_lo, core), dp: 128 (over z, x, y_hi).
Axes of the slice: x: 4, y: 4 (y_hi: 2, y_lo: 2; y = y_hi * 2 + y_lo), z: 16, core: 2. Of those that a mesh axis runs over, the one named last changes fastest.
Arguments:
- frame_encodings: bfloat16 [16384, 1280], P('dp'), may hold values from -6 to 6
- frame_projector_matrix: bfloat16 [1280, 1024], replicated, may hold values from -0.15625 to 0.15625
- sound_latents: bfloat16 [16384, 1024], P(('outer', 'dp')), may hold values from -0.1875 to 0.1875
- matched_targets: int32 [16384, 5], P('dp'), may hold values from -1 to 16383, as said below
- score_coldness: float32 [1], replicated, may hold values from 30 to 100
- score_offset: float32 [1], replicated, may hold values from -4 to -1
Outputs:
- weight_grad: float32 [1280, 1024], P('outer', 'dp')
Inputs may be any that keep to these rules, and one draw needn't show every extreme that they name: `matched_targets`: clips are cut 16 to a recording in time order and placed on rows by a random permutation; a video row's partners are the rows of the clips of its recording at most 2 places from it, itself included, each listed once, the other entries -1. The relation is symmetric. Some row has 5 partners.
All inputs are finite; a program needn't handle non-finite values.
Results may differ from a plain program's by a relative error of at most 0.0034.
Values may be sent and summed in bfloat16 or wider, within the bound.
No kernel may reach another device: no remote copies, remote signals or barrier semaphores. Data moves between devices by JAX's collectives and lax.ppermute only.
A program may use at most 64 MiB of HBM per device.

v0:
```python
import jax
import jax.numpy as jnp
from jax import lax
from jax.sharding import PartitionSpec as P


def local(
    frame_encodings,
    frame_projector_matrix,
    sound_latents,
    matched_targets,
    score_coldness,
    score_offset,
):
    sharpness_factor = score_coldness[0]
    offset_adjusted = score_offset[0]
    projected = jnp.dot(frame_encodings, frame_projector_matrix, preferred_element_type=jnp.float32)
    magnitude = jnp.sqrt(jnp.sum(projected * projected, axis=1, keepdims=True) + 1e-06)
    unit = projected / magnitude
    unit_b = unit.astype(jnp.bfloat16)
    local_rows = unit_b.shape[0]
    group_count = lax.axis_size("outer")
    group_index = lax.axis_index("outer")
    member_count = lax.axis_size("dp")
    per_group = sound_latents.shape[0] * member_count
    base_row = group_index * per_group
    quarter = local_rows // group_count
    portion = lax.all_gather(sound_latents, "dp", axis=0, tiled=True)
    similarity_scores = (
        sharpness_factor
        * lax.dot_general(
            unit_b, portion, (((1,), (1,)), ((), ())), preferred_element_type=jnp.float32
        )
        + offset_adjusted
    )
    column_ids = base_row + jnp.arange(portion.shape[0], dtype=jnp.int32)
    positive = jnp.any(matched_targets[:, :, None] == column_ids[None, None, :], axis=1).astype(
        jnp.float32
    )
    pair_weight = (jax.nn.sigmoid(similarity_scores) - positive).astype(jnp.bfloat16)
    running = jnp.dot(pair_weight, portion, preferred_element_type=jnp.float32)
    objective_value = lax.psum(running, "outer")
    latent_derivative = sharpness_factor * objective_value
    inner = jnp.sum(unit * latent_derivative, axis=1, keepdims=True)
    grad_full = ((latent_derivative - unit * inner) / magnitude).astype(jnp.bfloat16)
    row_start = group_index * quarter
    grad_part = lax.dynamic_slice_in_dim(grad_full, row_start, quarter, 0)
    col_grads = lax.all_to_all(grad_part, "dp", split_axis=1, concat_axis=0, tiled=True)
    feature_part = lax.dynamic_slice_in_dim(frame_encodings, row_start, quarter, 0)
    group_term = lax.dot_general(
        lax.all_gather(feature_part, "dp", axis=0, tiled=True),
        col_grads,
        (((0,), (0,)), ((), ())),
        preferred_element_type=jnp.float32,
    )
    return lax.psum_scatter(group_term, "outer", scatter_dimension=0, tiled=True)


def solution(mesh):
    return jax.shard_map(
        local,
        mesh=mesh,
        in_specs=(P("dp", None), P(), P(("outer", "dp"), None), P("dp", None), P(), P()),
        out_specs=P("outer", "dp"),
        check_vma=False,
    )
```

profile of v0, /device:TPU:1, one launch (start us, length us, event | category | flops | bytes accessed | tf_op | source)
XLA Modules:
  0.0 610.6 jit_solution(7603876901559826577)
XLA Ops:
  6.5 0.7 all-gather.5.cloned.1.call-update
  7.3 0.0 all-reduce.2.cloned.1.call-start
  8.7 1.6 multiply_reduce_fusion.1
  10.3 3.0 compare_reduce_fusion
  13.2 0.9 broadcast_divide_fusion
  14.2 236.4 %all-gather.5.cloned.1.call-done = bf16[4096,1024]{1,0:T(8,128)(2,1)} async-done(((bf16[32,1024]{1,0:T(8,128)(2,1)}), bf16[4096,1024]{1,0:T(8,128)(2,1)}) %all-gather.5.cloned.1.call-update) | async-done | bytes 8388624 | tf_op jit(solution)/shard_map/all_gather | solution.py:28
  250.5 10.9 %fusion.7 = f32[128,1024]{1,0:T(8,128)} fusion(bf16[4096,1024]{1,0:T(8,128)(2,1)} %all-gather.5.cloned.1.call-done, pred[128,4096]{1,0:T(8,128)(4,1)} %compare_reduce_fusion, f32[]{:T(128)} %bitcast.21, f32[]{:T(128)} %bitcast.20, f32[128,1024]{1,0:T(8,128)} %broadcast_divide_fusion), kind=kOutput, calls=%fused_computation.9 | convolution fusion | flops 2151809024 | bytes 9961480 | tf_op jit(solution)/shard_map/dot_general | solution.py:41
  261.4 0.0 all-gather.3.cloned.1.call-start
  261.5 1.5 constant_dynamic-slice_fusion
  263.0 0.0 reduce-scatter.4.cloned.1.call-start
  263.1 0.1 dynamic-slice.1
  263.2 55.0 %all-reduce.2.cloned.1.call-done = f32[128,1024]{1,0:T(8,128)} async-done(((f32[128,1024]{1,0:T(8,128)}), f32[128,1024]{1,0:T(8,128)}) %all-reduce.2.cloned.1.call-update) | async-done | bytes 524304 | tf_op jit(solution)/shard_map/psum | solution.py:42
  318.2 1.2 multiply_reduce_fusion
  319.5 0.1 dynamic-slice
  319.5 1.0 fusion.11
  320.5 0.2 copy.14
  320.7 0.2 reshape.17
  320.9 33.2 %all_to_all.19 = bf16[128,2,128]{2,1,0:T(2,128)(2,1)S(1)} all-to-all(bf16[128,2,128]{2,1,0:T(2,128)(2,1)S(1)} %reshape.17), channel_id=1, replica_groups=mesh['outer'=4,'dp'=128] {'dp'}, dimensions={0} | all-to-all | bytes 131072 | tf_op jit(solution)/shard_map/all_to_all | solution.py:48
  354.2 0.2 reshape.18
  354.4 0.3 all_to_all.17
  354.7 211.3 %all-gather.3.cloned.1.call-done = bf16[4096,1280]{1,0:T(8,128)(2,1)} async-done(((bf16[32,1280]{1,0:T(8,128)(2,1)}), bf16[4096,1280]{1,0:T(8,128)(2,1)}) %all-gather.3.cloned.1.call-update) | async-done | bytes 10485776 | tf_op jit(solution)/shard_map/all_gather | solution.py:51
  566.0 6.5 %fusion.13 = f32[1280,8]{1,0:T(8,128)} fusion(bf16[4096,1280]{1,0:T(8,128)(2,1)} %all-gather.3.cloned.1.call-done, bf16[4096,8]{0,1:T(8,128)(2,1)S(1)} %all_to_all.17), kind=kOutput, calls=%fused_computation.25 | convolution fusion | flops 83886080 | bytes 10592256
  572.5 29.9 %reduce-scatter.4.cloned.1.call-done = f32[320,8]{1,0:T(8,128)} async-done(((f32[1280,8]{1,0:T(8,128)}), f32[320,8]{1,0:T(8,128)}) %reduce-scatter.4.cloned.1.call-update) | async-done | bytes 10256
  602.4 1.6 copy.17
  (13 shorter events, 0.1 us)
Async XLA Ops:
  6.5 2.1 copy-start
  6.5 3.7 copy-start.1
  6.5 244.0 %all-gather.5.cloned.1.call-start = ((), (), s32[]{:S(2)}) async-start(), calls=%async_computation.3 | async-start | bytes 8454144 | tf_op jit(solution)/shard_map/all_gather | solution.py:28
  7.3 311.0 %all-reduce.2.cloned.1.call-start = ((), (), s32[]{:S(2)}) async-start(), calls=%async_computation.4 | async-start | bytes 1048576 | tf_op jit(solution)/shard_map/psum | solution.py:42
  261.4 304.6 %all-gather.3.cloned.1.call-start = ((), (), s32[]{:S(2)}) async-start(), calls=%async_computation.2 | async-start | bytes 10567680 | tf_op jit(solution)/shard_map/all_gather | solution.py:51
  263.0 339.4 %reduce-scatter.4.cloned.1.call-start = ((), (), s32[]{:S(2)}) async-start(), calls=%async_computation.5 | async-start | bytes 819200
Sparse Core Ops, SparseCore 0:
  11.7 238.7 all-gather.4
  261.6 56.6 all-reduce.1
  322.6 243.3 all-gather.2
  572.6 29.7 reduce-scatter.3
where the time goes:
time: 611 us
  waiting for transfers between devices  533 us (87%)
  blocking collectives  33.2 us (5%)
  matrix products  19 us (3%)
  between operations  14.5 us (2%)
  other arithmetic  6.16 us (1%)
    all_gather x1, waiting for transfers between devices, local(): portion = lax.all_gather(sound_latents, 'dp', axis=0, tiled=True)  236 us
    all_gather x1, waiting for transfers between devices, local(): lax.all_gather(feature_part, 'dp', axis=0, tiled=True)  211 us
    psum x1, waiting for transfers between devices, local(): objective_value = lax.psum(running, 'outer')  55 us
    all_to_all x1, blocking collectives, local(): lax.all_to_all(grad_part, 'dp', split_axis=1, concat_axis=0, tiled=True)  33.2 us
    unnamed x5, waiting for transfers between devices  30.7 us
  transfers between devices with their start and end apart: 4, of which 4 were waited for; matrix products, arithmetic and copies ran while one was open for 2% of the time, Pallas kernels for 0%

commit v1 on v0

v1 whole, which is shorter than its diff:
```python
import functools

import jax
import jax.numpy as jnp
from jax import lax
from jax.experimental import pallas as pl
from jax.experimental.pallas import tpu as pltpu
from jax.sharding import Mesh, PartitionSpec as P

BF = jnp.bfloat16
F32 = jnp.float32
AXES = ("ylo", "core", "z", "x", "yhi")
SIZES = (2, 2, 16, 4, 2)
DP = ("z", "x", "yhi")
PLANE = ("x", "yhi", "ylo")
LINE = ("z", "ylo", "core")
PAD = 128
CompilerParams = pltpu.CompilerParams


def project_kernel(x_ref, w_ref, unit_ref, unit_b_ref, mag_ref):
    e = w_ref.shape[0]
    projected = jnp.dot(x_ref[:, :e], w_ref[...], preferred_element_type=F32)
    mag = jnp.sqrt(jnp.sum(projected * projected, axis=1, keepdims=True) + 1e-06)
    unit = projected / mag
    unit_ref[...] = unit
    unit_b_ref[...] = unit.astype(BF)
    mag_ref[...] = jnp.broadcast_to(mag, mag_ref.shape)


def pair_kernel(place_ref, scale_ref, unit_ref, unit_b_ref, mag_ref, t_ref, own_ref, other_ref, out_ref):
    cold = scale_ref[0]
    offset = scale_ref[1]
    unit_b = unit_b_ref[...]
    targets = t_ref[...].astype(F32)
    total = None
    for side, audio_ref in enumerate((own_ref, other_ref)):
        audio = audio_ref[...]
        n = audio.shape[0]
        lane = lax.broadcasted_iota(jnp.int32, (1, n), 1)
        ids = (place_ref[side] + (lane // 32) * 256 + lane % 32).astype(F32)
        sims = lax.dot_general(unit_b, audio, (((1,), (1,)), ((), ())), preferred_element_type=F32)
        logits = cold * sims + offset
        hit = None
        for p in range(5):
            target = targets[:, 2 * p : 2 * p + 1] * 128.0 + targets[:, 2 * p + 1 : 2 * p + 2]
            same = target == ids
            hit = same if hit is None else hit | same
        weight = (jax.nn.sigmoid(logits) - jnp.where(hit, 1.0, 0.0)).astype(BF)
        term = jnp.dot(weight, audio, preferred_element_type=F32)
        total = term if total is None else total + term
    grad = cold * total
    unit = unit_ref[...]
    inner = jnp.sum(unit * grad, axis=1, keepdims=True)
    gp = ((grad - unit * inner) / mag_ref[:, :1]).astype(BF)
    for t in range(8):
        out_ref[t, 0] = gp[:, 128 * t : 128 * (t + 1)]


def weight_kernel(place_ref, g_ref, x_ref, out_ref):
    total = g_ref[0].astype(F32)
    for s in range(1, g_ref.shape[0]):
        total = total + g_ref[s].astype(F32)
    gp = total.astype(BF)
    rows = x_ref[pl.ds(pl.multiple_of(place_ref[2] * 256, 256), 256), :1280]
    part = lax.dot_general(gp, rows, (((0,), (0,)), ((), ())), preferred_element_type=F32)
    for o in range(4):
        out_ref[:, o] = part[:, 320 * o : 320 * (o + 1)].reshape(16, 8, 320)


def by_owner(a):
    n = a.shape[0]
    return a.reshape(n, 16, 8, 8).transpose(0, 2, 1, 3).reshape(n, 1024)


def local(frames, projector, sounds, matched, coldness, offset):
    ylo, core, z, x, yhi = (lax.axis_index(a) for a in AXES)
    mine = by_owner(sounds)
    own = lax.all_to_all(
        jnp.broadcast_to(mine[None], (16, 32, 1024)), "z", 0, 0, tiled=True
    ).reshape(512, 1024)
    other = lax.ppermute(own, "core", [(0, 1), (1, 0)])
    base = ylo * 8192 + (2 * x + yhi) * 32
    place = jnp.stack([base + core * 4096, base + (1 - core) * 4096, ylo]).astype(jnp.int32)

    halves = jnp.stack([matched >> 7, matched & 127], axis=2).reshape(128, 10).astype(BF)
    wide = jnp.concatenate([frames, jnp.pad(halves, ((0, 0), (0, PAD - 10)))], axis=1)
    wide = lax.dynamic_slice_in_dim(wide, core * 64, 64, 0)
    row = lax.all_gather(wide, "x", axis=0, tiled=True)
    far = lax.ppermute(row, "yhi", [(0, 1), (1, 0)])
    rows = jnp.concatenate([jnp.where(yhi == 0, row, far), jnp.where(yhi == 0, far, row)], axis=0)

    width = 1280 + PAD
    block = 128
    unit, unit_b, mag = pl.pallas_call(
        project_kernel,
        grid=(4,),
        in_specs=[
            pl.BlockSpec((block, width), lambda i: (i, 0)),
            pl.BlockSpec((1280, 1024), lambda i: (0, 0)),
        ],
        out_specs=[
            pl.BlockSpec((block, 1024), lambda i: (i, 0)),
            pl.BlockSpec((block, 1024), lambda i: (i, 0)),
            pl.BlockSpec((block, 128), lambda i: (i, 0)),
        ],
        out_shape=[
            jax.ShapeDtypeStruct((512, 1024), F32),
            jax.ShapeDtypeStruct((512, 1024), BF),
            jax.ShapeDtypeStruct((512, 128), F32),
        ],
        compiler_params=CompilerParams(vmem_limit_bytes=40 * 2**20),
        cost_estimate=pl.CostEstimate(flops=2 * 512 * 1280 * 1024, bytes_accessed=8 * 2**20, transcendentals=0),
    )(rows, by_owner(projector))

    scale = jnp.concatenate([coldness, offset])
    smem = pl.BlockSpec(memory_space=pltpu.SMEM)
    parts = pl.pallas_call(
        pair_kernel,
        grid=(4,),
        in_specs=[
            smem,
            smem,
            pl.BlockSpec((block, 1024), lambda i: (i, 0)),
            pl.BlockSpec((block, 1024), lambda i: (i, 0)),
            pl.BlockSpec((block, 128), lambda i: (i, 0)),
            pl.BlockSpec((block, PAD), lambda i: (i, 10)),
            pl.BlockSpec((512, 1024), lambda i: (0, 0)),
            pl.BlockSpec((512, 1024), lambda i: (0, 0)),
        ],
        out_specs=pl.BlockSpec((8, 1, block, 128), lambda i: (0, i // 2, i % 2, 0)),
        out_shape=jax.ShapeDtypeStruct((8, 2, 256, 128), BF),
        compiler_params=CompilerParams(vmem_limit_bytes=40 * 2**20),
        cost_estimate=pl.CostEstimate(flops=4 * 512 * 1024 * 1024, bytes_accessed=8 * 2**20, transcendentals=2**20),
    )(place, scale, unit, unit_b, mag, rows, own, other)

    terms = lax.all_to_all(parts.reshape(16, 256, 128), PLANE, 0, 0, tiled=True)
    vmem = pl.BlockSpec(memory_space=pltpu.VMEM)
    pieces = pl.pallas_call(
        weight_kernel,
        in_specs=[smem, vmem, vmem],
        out_specs=vmem,
        out_shape=jax.ShapeDtypeStruct((16, 4, 8, 320), F32),
        compiler_params=CompilerParams(vmem_limit_bytes=40 * 2**20),
    )(place, terms, rows)
    sums = lax.all_to_all(pieces.reshape(64, 8, 320), LINE, 0, 0, tiled=True)
    return jnp.sum(sums, axis=0).T


def solution(mesh):
    fine = Mesh(mesh.devices.reshape(SIZES), AXES)
    return jax.shard_map(
        local,
        mesh=fine,
        in_specs=(P(DP, None), P(), P(AXES, None), P(DP, None), P(), P()),
        out_specs=P(("ylo", "core"), DP),
        check_vma=False,
    )
```

time: 611 us -> 161 us (0.26)
  waiting for transfers between devices: 533 us -> 13.6 us
  blocking collectives: 33.2 us -> 88.3 us
  starting transfers between devices: 0.12 us -> 28.5 us
  matrix products: 19 us -> 0 us
  between operations: 14.5 us -> 1.44 us
  local copies, waits for them, and re-layouts: 4.15 us -> 16.3 us
  Pallas kernels: 0 us -> 10.3 us
    all_gather x2 -> x0, waiting for transfers between devices: 448 us -> none  [the longest x1 236 us: local(): portion = lax.all_gather(sound_latents, 'dp', axis=0, tiled=True)]
    psum x1 -> x0, waiting for transfers between devices: 55 us -> none  [local(): objective_value = lax.psum(running, 'outer')]
    all_to_all x1 -> x2, blocking collectives: 33.2 us -> 75.9 us  [the longest x1 53.6 us: local(): sums = lax.all_to_all(pieces.reshape(64, 8, 320), LINE, 0, 0, tiled=True)]
    unnamed x5 -> x0, waiting for transfers between devices: 30.7 us -> none
    all_to_all x0 -> x1, starting transfers between devices: none -> 15.7 us  [local(): lax.all_to_all(jnp.broadcast_to(mine[None], (16, 32, 1024)), 'z', 0, 0, t...]
    all_to_all x0 -> x1, waiting for transfers between devices: none -> 13.6 us  [local(): lax.all_to_all(jnp.broadcast_to(mine[None], (16, 32, 1024)), 'z', 0, 0, t...]
    ppermute x0 -> x2, starting transfers between devices: none -> 12.8 us  [the longest x1 7.98 us: local(): other = lax.ppermute(own, 'core', [(0, 1), (1, 0)])]
    dot_general x2 -> x0, matrix products: 12.5 us -> none  [the longest x1 10.9 us: local(): running = jnp.dot(pair_weight, portion, preferred_element_type=jnp.float32)]
  transfers between devices with their start and end apart: 4 -> 3, of which waited for: 4 -> 1; matrix products, arithmetic and copies ran while one was open for 2% -> 8% of each run, Pallas kernels for 0% -> 2%
where the time goes in v1:
time: 161 us; the launch traced here: 160 us
  blocking collectives  88.3 us (55%)
  starting transfers between devices  28.5 us (18%)
  local copies, waits for them, and re-layouts  16.3 us (10%)
  waiting for transfers between devices  13.6 us (8%)
  Pallas kernels  10.3 us (6%)
    all_to_all x1, blocking collectives, local(): sums = lax.all_to_all(pieces.reshape(64, 8, 320), LINE, 0, 0, tiled=True)  53.6 us
    all_to_all x1, blocking collectives, local(): terms = lax.all_to_all(parts.reshape(16, 256, 128), PLANE, 0, 0, tiled=True)  22.3 us
    all_to_all x1, starting transfers between devices, local(): lax.all_to_all(jnp.broadcast_to(mine[None], (16, 32, 1024)), 'z', 0, 0, t...  15.7 us
    all_to_all x1, waiting for transfers between devices, local(): lax.all_to_all(jnp.broadcast_to(mine[None], (16, 32, 1024)), 'z', 0, 0, t...  13.6 us
    all_gather x1, blocking collectives, local(): row = lax.all_gather(wide, 'x', axis=0, tiled=True)  12.4 us
    ppermute x1, starting transfers between devices, local(): other = lax.ppermute(own, 'core', [(0, 1), (1, 0)])  7.98 us
    unnamed x8, local copies, waits for them, and re-layouts  6.91 us
    pallas_call x1, Pallas kernels, local(): pl.pallas_call(pair_kernel, grid=(4,), in_specs=[smem, smem, pl.BlockSpec...  6.66 us
  transfers between devices with their start and end apart: 3, of which 1 were waited for; matrix products, arithmetic and copies ran while one was open for 8% of the time, Pallas kernels for 2%

profile of v1, /device:TPU:1, one launch (start us, length us, event | category | flops | bytes accessed | tf_op | source)
XLA Modules:
  0.0 159.7 jit_solution(9222206571412721807)
XLA Ops:
  0.0 1.1 copy.14
  1.1 0.1 copy.16
  1.2 1.1 broadcast_in_dim.8
  2.4 15.7 %all-to-all-start = ((bf16[16,32,1024]{2,1,0:T(8,128)(2,1)}), bf16[16,32,1024]{2,1,0:T(8,128)(2,1)S(1)}, u32[]{:S(2)}, u32[]{:S(2)}) async-start(bf16[16,32,1024]{2,1,0:T(8,128)(2,1)} %broadcast_in_dim.8), calls=%async_computation | async-start | bytes 2097152 | tf_op jit(solution)/shard_map/all_to_all | solution.py:79
  18.2 0.1 copy.10
  18.4 12.4 %all_gather.3 = bf16[256,1408]{1,0:T(8,128)(2,1)S(1)} all-gather(bf16[64,1408]{1,0:T(8,128)(2,1)S(1)} %fusion.1), channel_id=1, replica_groups=mesh['ylo'=2,'core'=2,'z'=16,'x'=4,'yhi'=2] {'x'}, dimensions={0}, use_global_device_ids=true | all-gather | bytes 901120 | tf_op jit(solution)/shard_map/all_gather | solution.py:89
  30.8 4.8 %collective-permute-start = (bf16[256,1408]{1,0:T(8,128)(2,1)S(1)}, bf16[256,1408]{1,0:T(8,128)(2,1)S(1)}, u32[]{:S(2)}, u32[]{:S(2)}) collective-permute-start(bf16[256,1408]{1,0:T(8,128)(2,1)S(1)} %all_gather.3), channel_id=1, source_target_pairs={{0,1},{1,0},{2,3},{3,2},{4,5},{5,4},{6,7},{7,6},{8,9},{9,8},{10,11... | collective-permute-start | bytes 2162696 | tf_op jit(solution)/shard_map/ppermute | solution.py:90
  35.6 4.4 %copy.11 = bf16[1280,1024]{0,1:T(8,128)(2,1)} copy(bf16[1280,1024]{1,0:T(8,128)(2,1)} %param.7) | data formatting | bytes 5242880 | tf_op args[1]
  40.0 3.4 %copy.12 = bf16[1280,8,16,8]{0,3,2,1:T(8,128)(2,1)} copy(bf16[1280,8,16,8]{0,3,1,2:T(8,128)(2,1)} %bitcast.26) | data formatting | bytes 5242880 | tf_op jit(solution)/shard_map/transpose | solution.py:73
  43.4 4.5 %copy.13.w_ref = bf16[1280,1024]{1,0:T(8,128)(2,1)} copy(bf16[1280,1024]{0,1:T(8,128)(2,1)} %bitcast.25) | data formatting | bytes 5242880 | tf_op jit(solution)/shard_map/reshape | solution.py:73
  49.3 0.1 pad_maximum_fusion.2.scale_ref
  49.4 13.6 %all-to-all-done = bf16[16,32,1024]{2,1,0:T(8,128)(2,1)S(1)} async-done(((bf16[16,32,1024]{2,1,0:T(8,128)(2,1)}), bf16[16,32,1024]{2,1,0:T(8,128)(2,1)S(1)}, u32[]{:S(2)}, u32[]{:S(2)}) %all-to-all-start) | async-done | bytes 1048608 | tf_op jit(solution)/shard_map/all_to_all | solution.py:79
  63.0 8.0 %collective-permute-start.1 = (bf16[512,1024]{1,0:T(8,128)(2,1)S(1)}, bf16[512,1024]{1,0:T(8,128)(2,1)S(1)}, u32[]{:S(2)}, u32[]{:S(2)}) collective-permute-start(bf16[512,1024]{1,0:T(8,128)(2,1)S(1)} %bitcast.21), channel_id=1, source_target_pairs={{0,128},{128,0},{1,129},{129,1},{2,130},{130,2},{3,131},{131,3},{4... | collective-permute-start | bytes 3145736 | tf_op jit(solution)/shard_map/ppermute | solution.py:82
  71.0 0.1 pad_add_fusion.place_ref
  71.1 0.1 broadcast_select_fusion.1
  71.2 0.1 pad_maximum_fusion.x_ref.t_ref
  71.3 1.5 copy-done
  72.8 2.6 %shard_map.64 = (f32[512,1024]{1,0:T(8,128)S(1)}, bf16[512,1024]{1,0:T(8,128)(2,1)S(1)}, f32[512,128]{1,0:T(8,128)S(1)}) custom-call(bf16[512,1408]{1,0:T(8,128)(2,1)S(1)} %pad_maximum_fusion.x_ref.t_ref, bf16[1280,1024]{1,0:T(8,128)(2,1)S(1)} %copy-done), custom_call_target="tpu_custom_call" | custom-call | flops 1342177280 | bytes 8388608 | tf_op jit(solution)/shard_map/pallas_call | solution.py:95
  75.4 0.0 collective-permute-done.1.other_ref
  75.4 6.7 %shard_map.65 = bf16[8,2,256,128]{3,2,1,0:T(8,128)(2,1)S(1)} custom-call(s32[3]{0:T(128)S(1)} %pad_add_fusion.place_ref, f32[2]{0:T(128)S(1)} %pad_maximum_fusion.2.scale_ref, f32[512,1024]{1,0:T(8,128)S(1)} %get-tuple-element.8.unit_ref, bf16[512,1024]{1,0:T(8,128)(2,1)S(1)} %get-tuple-element.9.unit_b_ref, f32[512,128]{1,0:T(8,128)S(1)} %get-tuple-element.10.mag_ref, ...), custom_call_target="tpu_custom_call" | custom-call | flops 2147483648 | bytes 8388608 | tf_op jit(solution)/shard_map/pallas_call | solution.py:118
  82.0 22.3 %all_to_all.15.g_ref = bf16[16,256,128]{2,1,0:T(8,128)(2,1)S(1)} all-to-all(bf16[16,256,128]{2,1,0:T(8,128)(2,1)S(1)} %bitcast.23), channel_id=1, replica_groups=mesh['ylo'=2,'core'=2,'z'=16,'x'=4,'yhi'=2] {'x','yhi','ylo'}, dimensions={0} | all-to-all | bytes 2097152 | tf_op jit(solution)/shard_map/all_to_all | solution.py:137
  104.4 1.0 shard_map.66
  105.4 53.6 %all_to_all.16 = f32[64,8,320]{2,1,0:T(8,128)S(1)} all-to-all(f32[64,8,320]{2,1,0:T(8,128)S(1)} %bitcast.24), channel_id=1, replica_groups=mesh['ylo'=2,'core'=2,'z'=16,'x'=4,'yhi'=2] {'z','ylo','core'}, dimensions={0} | all-to-all | bytes 1310720 | tf_op jit(solution)/shard_map/all_to_all | solution.py:146
  159.0 0.7 reduce_sum.9
  (12 shorter events, 0.1 us)
Async XLA Ops:
  0.0 18.1 %copy-start.2 = (s32[128,5]{0,1:T(8,128)S(1)}, s32[128,5]{0,1:T(8,128)}, u32[]{:S(2)}) copy-start(s32[128,5]{0,1:T(8,128)} %param.9) | copy-start | bytes 7684
  0.0 18.3 %copy-start.1 = (bf16[128,1280]{1,0:T(8,128)(2,1)S(1)}, bf16[128,1280]{1,0:T(8,128)(2,1)}, u32[]{:S(2)}) copy-start(bf16[128,1280]{1,0:T(8,128)(2,1)} %param.6) | copy-start | bytes 983044
  2.4 60.6 %all-to-all-start = ((bf16[16,32,1024]{2,1,0:T(8,128)(2,1)}), bf16[16,32,1024]{2,1,0:T(8,128)(2,1)S(1)}, u32[]{:S(2)}, u32[]{:S(2)}) async-start(bf16[16,32,1024]{2,1,0:T(8,128)(2,1)} %broadcast_in_dim.8), calls=%async_computation | async-start | bytes 2097152 | tf_op jit(solution)/shard_map/all_to_all | solution.py:79
  30.8 40.2 %collective-permute-start = (bf16[256,1408]{1,0:T(8,128)(2,1)S(1)}, bf16[256,1408]{1,0:T(8,128)(2,1)S(1)}, u32[]{:S(2)}, u32[]{:S(2)}) collective-permute-start(bf16[256,1408]{1,0:T(8,128)(2,1)S(1)} %all_gather.3), channel_id=1, source_target_pairs={{0,1},{1,0},{2,3},{3,2},{4,5},{5,4},{6,7},{7,6},{8,9},{9,8},{10,11... | collective-permute-start | bytes 2162696 | tf_op jit(solution)/shard_map/ppermute | solution.py:90
  63.0 12.4 %collective-permute-start.1 = (bf16[512,1024]{1,0:T(8,128)(2,1)S(1)}, bf16[512,1024]{1,0:T(8,128)(2,1)S(1)}, u32[]{:S(2)}, u32[]{:S(2)}) collective-permute-start(bf16[512,1024]{1,0:T(8,128)(2,1)S(1)} %bitcast.21), channel_id=1, source_target_pairs={{0,128},{128,0},{1,129},{129,1},{2,130},{130,2},{3,131},{131,3},{4... | collective-permute-start | bytes 3145736 | tf_op jit(solution)/shard_map/ppermute | solution.py:82
  71.1 1.7 %copy-start = (bf16[1280,1024]{1,0:T(8,128)(2,1)S(1)}, bf16[1280,1024]{1,0:T(8,128)(2,1)}, u32[]{:S(2)}) copy-start(bf16[1280,1024]{1,0:T(8,128)(2,1)} %copy.13.w_ref) | copy-start | bytes 7864324

commit v2 on v1

v2 whole, which is shorter than its diff:
```python
import jax
import jax.numpy as jnp
from jax import lax
from jax.experimental import pallas as pl
from jax.experimental.pallas import tpu as pltpu
from jax.sharding import Mesh, PartitionSpec as P

BF = jnp.bfloat16
F32 = jnp.float32
AXES = ("ylo", "core", "z", "x", "yhi")
SIZES = (2, 2, 16, 4, 2)
DP = ("z", "x", "yhi")
PLANE = ("x", "yhi", "ylo")
LINE = ("core", "z")
PAD = 128
CompilerParams = pltpu.CompilerParams


def project_kernel(x_ref, w_ref, unit_ref, unit_b_ref, mag_ref, order_ref):
    n = order_ref.shape[0]
    was = lax.broadcasted_iota(jnp.int32, (n, 1024), 0) + pl.program_id(0) * n
    goes = (was // 8 % 8) * 128 + (was // 64) * 8 + was % 8
    lane = lax.broadcasted_iota(jnp.int32, (n, 1024), 1)
    order_ref[...] = jnp.where(goes == lane, 1.0, 0.0).astype(BF)
    e = w_ref.shape[0]
    projected = jnp.dot(x_ref[:, :e], w_ref[...], preferred_element_type=F32)
    mag = jnp.sqrt(jnp.sum(projected * projected, axis=1, keepdims=True) + 1e-06)
    unit = projected / mag
    unit_ref[...] = unit
    unit_b_ref[...] = unit.astype(BF)
    mag_ref[...] = jnp.broadcast_to(mag, mag_ref.shape)


def pair_kernel(scale_ref, unit_ref, unit_b_ref, mag_ref, t_ref, ids_ref, order_ref, *refs):
    *audio_refs, out_ref = refs
    cold = scale_ref[0]
    offset = scale_ref[1]
    unit_b = unit_b_ref[...]
    targets = t_ref[...].astype(F32)
    total = None
    at = 0
    for audio_ref in audio_refs:
        audio = audio_ref[...]
        n = audio.shape[0]
        ids = ids_ref[:1, at : at + n]
        at += n
        sims = lax.dot_general(unit_b, audio, (((1,), (1,)), ((), ())), preferred_element_type=F32)
        logits = cold * sims + offset
        hit = None
        for p in range(5):
            target = targets[:, 2 * p : 2 * p + 1] * 128.0 + targets[:, 2 * p + 1 : 2 * p + 2]
            same = target == ids
            hit = same if hit is None else hit | same
        weight = (jax.nn.sigmoid(logits) - jnp.where(hit, 1.0, 0.0)).astype(BF)
        term = jnp.dot(weight, audio, preferred_element_type=F32)
        total = term if total is None else total + term
    grad = cold * total
    unit = unit_ref[...]
    inner = jnp.sum(unit * grad, axis=1, keepdims=True)
    gp = ((grad - unit * inner) / mag_ref[:, :1]).astype(BF)
    gp = jnp.dot(gp, order_ref[...], preferred_element_type=F32).astype(BF)
    for t in range(8):
        out_ref[t, 0] = gp[:, 128 * t : 128 * (t + 1)]


def sum_kernel(g_ref, out_ref):
    total = g_ref[0].astype(F32)
    for s in range(1, g_ref.shape[0]):
        total = total + g_ref[s].astype(F32)
    out_ref[...] = total.astype(BF)


def weight_kernel(place_ref, g_ref, far_ref, x_ref, out_ref):
    ylo = place_ref[0]
    lanes = pl.ds(pl.multiple_of(ylo * 640, 128), 640)
    part = None
    for ref, half in ((g_ref, ylo), (far_ref, 1 - ylo)):
        rows = x_ref[pl.ds(pl.multiple_of(half * 256, 256), 256), lanes]
        term = lax.dot_general(ref[...], rows, (((0,), (0,)), ((), ())), preferred_element_type=F32)
        part = term if part is None else part + term
    for c in range(2):
        out_ref[c] = part[:, 320 * c : 320 * (c + 1)].reshape(16, 8, 320).astype(out_ref.dtype)


def fetch(a, far):
    perm = []
    for z in range(16):
        perm.append(((z + far) % 16, z))
        perm.append((16 + (z - far) % 16, 16 + z))
    return lax.ppermute(a, ("core", "z"), perm)


def swap(a, axis):
    return lax.ppermute(a, axis, [(0, 1), (1, 0)])


def local(frames, projector, sounds, matched, coldness, offset):
    ylo, core, z, x, yhi = (lax.axis_index(a) for a in AXES)
    up6 = fetch(sounds, 6)
    down6 = fetch(sounds, -6)
    up2 = fetch(jnp.concatenate([sounds, up6, down6], axis=0), 2)
    down2 = fetch(jnp.concatenate([sounds, up6], axis=0), -2)
    fours = jnp.concatenate([sounds, up2[32:], down2[32:]], axis=0)
    twos = jnp.concatenate([up6, down6, up2[:32], down2[:32]], axis=0)
    up1 = fetch(fours, 1)
    down1 = fetch(fours, -1)
    even = jnp.concatenate([fours, twos], axis=0)
    odd = jnp.concatenate([up1, down1], axis=0)
    far_even = swap(even, "core")
    far_odd = swap(odd, "core")
    evens = jnp.array([0, 8, -4, 4, 6, -6, 2, -2], jnp.int32)
    odds = jnp.array([1, 9, -3, 5, -1, 7, -5, 3], jnp.int32)
    sign = 1 - 2 * core
    steps = jnp.concatenate([sign * evens, -sign * evens, sign * odds, -sign * odds])
    cores = jnp.concatenate([jnp.full(8, core), jnp.full(8, 1 - core)] * 2)
    blocks = ylo * 8192 + cores * 4096 + (z + steps) % 16 * 256 + (2 * x + yhi) * 32
    ids = (blocks[:, None] + jnp.arange(32)[None, :]).reshape(1, 1024).astype(F32)
    ids = jnp.broadcast_to(ids, (8, 1024))

    halves = jnp.stack([matched >> 7, matched & 127], axis=2).reshape(128, 10).astype(BF)
    wide = jnp.concatenate([frames, jnp.pad(halves, ((0, 0), (0, PAD - 10)))], axis=1)
    wide = lax.dynamic_slice_in_dim(wide, core * 64, 64, 0)
    row = lax.all_gather(wide, "x", axis=0, tiled=True)
    far = swap(row, "yhi")
    rows = jnp.concatenate([jnp.where(yhi == 0, row, far), jnp.where(yhi == 0, far, row)], axis=0)

    width = 1280 + PAD
    block = 128
    whole = lambda i: (0, 0)
    by_row = lambda i: (i, 0)
    unit, unit_b, mag, order = pl.pallas_call(
        project_kernel,
        grid=(4,),
        in_specs=[pl.BlockSpec((block, width), by_row), pl.BlockSpec((1280, 1024), whole)],
        out_specs=[
            pl.BlockSpec((block, 1024), by_row),
            pl.BlockSpec((block, 1024), by_row),
            pl.BlockSpec((block, 128), by_row),
            pl.BlockSpec((256, 1024), by_row),
        ],
        out_shape=[
            jax.ShapeDtypeStruct((512, 1024), F32),
            jax.ShapeDtypeStruct((512, 1024), BF),
            jax.ShapeDtypeStruct((512, 128), F32),
            jax.ShapeDtypeStruct((1024, 1024), BF),
        ],
        compiler_params=CompilerParams(vmem_limit_bytes=40 * 2**20),
        cost_estimate=pl.CostEstimate(flops=2 * 512 * 1280 * 1024, bytes_accessed=8 * 2**20, transcendentals=0),
    )(rows, projector)

    scale = jnp.concatenate([coldness, offset])
    smem = pl.BlockSpec(memory_space=pltpu.SMEM)
    vmem = pl.BlockSpec(memory_space=pltpu.VMEM)
    parts = pl.pallas_call(
        pair_kernel,
        grid=(4,),
        in_specs=[
            smem,
            pl.BlockSpec((block, 1024), by_row),
            pl.BlockSpec((block, 1024), by_row),
            pl.BlockSpec((block, 128), by_row),
            pl.BlockSpec((block, PAD), lambda i: (i, 10)),
            pl.BlockSpec((8, 1024), whole),
            pl.BlockSpec((1024, 1024), whole),
        ]
        + [pl.BlockSpec((256, 1024), whole)] * 4,
        out_specs=pl.BlockSpec((8, 1, block, 128), lambda i: (0, i // 2, i % 2, 0)),
        out_shape=jax.ShapeDtypeStruct((8, 2, 256, 128), BF),
        compiler_params=CompilerParams(vmem_limit_bytes=40 * 2**20),
        cost_estimate=pl.CostEstimate(flops=5 * 512 * 1024 * 1024, bytes_accessed=8 * 2**20, transcendentals=2**20),
    )(scale, unit, unit_b, mag, rows, ids, order, even, far_even, odd, far_odd)

    terms = lax.all_to_all(parts.reshape(16, 256, 128), PLANE, 0, 0, tiled=True)
    params = CompilerParams(vmem_limit_bytes=40 * 2**20)
    gp = pl.pallas_call(
        sum_kernel, in_specs=[vmem], out_specs=vmem, out_shape=jax.ShapeDtypeStruct((256, 128), BF), compiler_params=params
    )(terms)
    far_gp = swap(gp, "ylo")
    pieces = pl.pallas_call(
        weight_kernel,
        in_specs=[smem, vmem, vmem, vmem],
        out_specs=vmem,
        out_shape=jax.ShapeDtypeStruct((2, 16, 8, 320), BF),
        compiler_params=params,
    )(ylo.reshape(1).astype(jnp.int32), gp, far_gp, rows)
    sums = lax.all_to_all(pieces.reshape(32, 8, 320), LINE, 0, 0, tiled=True)
    return jnp.sum(sums.astype(F32), axis=0).T


def solution(mesh):
    fine = Mesh(mesh.devices.reshape(SIZES), AXES)
    return jax.shard_map(
        local,
        mesh=fine,
        in_specs=(P(DP, None), P(), P(AXES, None), P(DP, None), P(), P()),
        out_specs=P(("ylo", "core"), DP),
        check_vma=False,
    )
```

time: 161 us -> 147 us (0.913)
  blocking collectives: 88.3 us -> 62 us
  starting transfers between devices: 28.5 us -> 50.3 us
  local copies, waits for them, and re-layouts: 16.3 us -> 2.81 us
  Pallas kernels: 10.3 us -> 15 us
  waiting for transfers between devices: 13.6 us -> 10 us
  other arithmetic: 1.14 us -> 4.33 us
    ppermute x2 -> x10, starting transfers between devices: 12.8 us -> 50.3 us  [the longest x6 34.8 us: fetch(): return lax.ppermute(a, ('core', 'z'), perm)]
    all_to_all x1, blocking collectives: 53.6 us -> 29.7 us  [local(): sums = lax.all_to_all(pieces.reshape(32, 8, 320), LINE, 0, 0, tiled=True)]
    all_to_all x1 -> x0, starting transfers between devices: 15.7 us -> none  [local(): lax.all_to_all(jnp.broadcast_to(mine[None], (16, 32, 1024)), 'z', 0, 0, t...]
    all_to_all x1 -> x0, waiting for transfers between devices: 13.6 us -> none  [local(): lax.all_to_all(jnp.broadcast_to(mine[None], (16, 32, 1024)), 'z', 0, 0, t...]
    ppermute x2 -> x10, waiting for transfers between devices: 0.01 us -> 10 us  [the longest x6 7.4 us: fetch(): return lax.ppermute(a, ('core', 'z'), perm)]
    reshape x1 -> x0, local copies, waits for them, and re-layouts: 4.53 us -> none  [by_owner(): return a.reshape(n, 16, 8, 8).transpose(0, 2, 1, 3).reshape(n, 1024)]
    unnamed x8 -> x9, local copies, waits for them, and re-layouts: 6.91 us -> 2.51 us
    transpose x2 -> x0, local copies, waits for them, and re-layouts: 3.47 us -> none  [by_owner(): return a.reshape(n, 16, 8, 8).transpose(0, 2, 1, 3).reshape(n, 1024)]
  transfers between devices with their start and end apart: 3 -> 10, of which waited for: 1 -> 4; matrix products, arithmetic and copies ran while one was open for 8% -> 3% of each run, Pallas kernels for 2% -> 3%
where the time goes in v2:
time: 147 us; the launch traced here: 146 us
  blocking collectives  62 us (42%)
  starting transfers between devices  50.3 us (34%)
  Pallas kernels  15 us (10%)
  waiting for transfers between devices  10 us (7%)
  other arithmetic  4.33 us (3%)
  local copies, waits for them, and re-layouts  2.81 us (2%)
  between operations  1.57 us (1%)
    ppermute x6, starting transfers between devices, fetch(): return lax.ppermute(a, ('core', 'z'), perm)  34.8 us
    all_to_all x1, blocking collectives, local(): sums = lax.all_to_all(pieces.reshape(32, 8, 320), LINE, 0, 0, tiled=True)  29.7 us
    all_to_all x1, blocking collectives, local(): terms = lax.all_to_all(parts.reshape(16, 256, 128), PLANE, 0, 0, tiled=True)  20 us
    ppermute x4, starting transfers between devices, swap(): return lax.ppermute(a, axis, [(0, 1), (1, 0)])  15.5 us
    all_gather x1, blocking collectives, local(): row = lax.all_gather(wide, 'x', axis=0, tiled=True)  12.2 us
    pallas_call x1, Pallas kernels, local(): pl.pallas_call(pair_kernel, grid=(4,), in_specs=[smem, pl.BlockSpec((bloc...  10.1 us
    ppermute x6, waiting for transfers between devices, fetch(): return lax.ppermute(a, ('core', 'z'), perm)  7.4 us
    pallas_call x1, Pallas kernels, local(): pl.pallas_call(project_kernel, grid=(4,), in_specs=[pl.BlockSpec((block,...  4.41 us
  transfers between devices with their start and end apart: 10, of which 4 were waited for; matrix products, arithmetic and copies ran while one was open for 3% of the time, Pallas kernels for 3%

profile of v2, /device:TPU:1, one launch (start us, length us, event | category | flops | bytes accessed | tf_op | source)
XLA Modules:
  0.0 146.0 jit_solution(13739172492782603162)
XLA Ops:
  0.0 15.5 %collective-permute-start.2 = (bf16[32,1024]{1,0:T(8,128)(2,1)}, bf16[32,1024]{1,0:T(8,128)(2,1)S(1)}, u32[]{:S(2)}, u32[]{:S(2)}) collective-permute-start(bf16[32,1024]{1,0:T(8,128)(2,1)} %param.10), channel_id=1, source_target_pairs={{80,0},{176,128},{88,8},{184,136},{96,16},{192,144},{104,24},{200,... | collective-permute-start | bytes 196616 | tf_op jit(solution)/shard_map/ppermute | solution.py:90
  15.5 1.9 %collective-permute-start.1 = (bf16[32,1024]{1,0:T(8,128)(2,1)}, bf16[32,1024]{1,0:T(8,128)(2,1)S(1)}, u32[]{:S(2)}, u32[]{:S(2)}) collective-permute-start(bf16[32,1024]{1,0:T(8,128)(2,1)} %param.10), channel_id=1, source_target_pairs={{48,0},{208,128},{56,8},{216,136},{64,16},{224,144},{72,24},{232,1... | collective-permute-start | bytes 196616 | tf_op jit(solution)/shard_map/ppermute | solution.py:90
  17.5 0.7 fusion.2
  18.3 0.9 fusion.1
  19.3 12.2 %all_gather.3 = bf16[256,1408]{1,0:T(8,128)(2,1)S(1)} all-gather(bf16[64,1408]{1,0:T(8,128)(2,1)S(1)} %fusion.1), channel_id=1, replica_groups=mesh['ylo'=2,'core'=2,'z'=16,'x'=4,'yhi'=2] {'x'}, dimensions={0}, use_global_device_ids=true | all-gather | bytes 901120 | tf_op jit(solution)/shard_map/all_gather | solution.py:123
  31.5 4.8 %collective-permute-start = (bf16[256,1408]{1,0:T(8,128)(2,1)S(1)}, bf16[256,1408]{1,0:T(8,128)(2,1)S(1)}, u32[]{:S(2)}, u32[]{:S(2)}) collective-permute-start(bf16[256,1408]{1,0:T(8,128)(2,1)S(1)} %all_gather.3), channel_id=1, source_target_pairs={{0,1},{1,0},{2,3},{3,2},{4,5},{5,4},{6,7},{7,6},{8,9},{9,8},{10,11... | collective-permute-start | bytes 2162696 | tf_op jit(solution)/shard_map/ppermute | solution.py:94
  38.5 0.8 constant_dynamic-update-slice_fusion.4
  39.4 0.9 pad_maximum_fusion.2
  40.2 3.3 %collective-permute-start.3 = (bf16[96,1024]{1,0:T(8,128)(2,1)S(1)}, bf16[96,1024]{1,0:T(8,128)(2,1)S(1)}, u32[]{:S(2)}, u32[]{:S(2)}) collective-permute-start(bf16[96,1024]{1,0:T(8,128)(2,1)S(1)} %pad_maximum_fusion.2), channel_id=1, source_target_pairs={{16,0},{240,128},{24,8},{248,136},{32,16},{128,144},{40,24},{136,1... | collective-permute-start | bytes 589832 | tf_op jit(solution)/shard_map/ppermute | solution.py:90
  43.6 5.6 %collective-permute-start.4 = (bf16[64,1024]{1,0:T(8,128)(2,1)S(1)}, bf16[64,1024]{1,0:T(8,128)(2,1)S(1)}, u32[]{:S(2)}, u32[]{:S(2)}) collective-permute-start(bf16[64,1024]{1,0:T(8,128)(2,1)S(1)} %pad_maximum_fusion.3), channel_id=1, source_target_pairs={{112,0},{144,128},{120,8},{152,136},{0,16},{160,144},{8,24},{168,1... | collective-permute-start | bytes 393224 | tf_op jit(solution)/shard_map/ppermute | solution.py:90
  49.3 1.9 %collective-permute-done.3 = bf16[96,1024]{1,0:T(8,128)(2,1)S(1)} collective-permute-done((bf16[96,1024]{1,0:T(8,128)(2,1)S(1)}, bf16[96,1024]{1,0:T(8,128)(2,1)S(1)}, u32[]{:S(2)}, u32[]{:S(2)}) %collective-permute-start.3) | collective-permute-done | bytes 196640 | tf_op jit(solution)/shard_map/ppermute | solution.py:90
  51.2 2.9 %collective-permute-done.4 = bf16[64,1024]{1,0:T(8,128)(2,1)S(1)} collective-permute-done((bf16[64,1024]{1,0:T(8,128)(2,1)S(1)}, bf16[64,1024]{1,0:T(8,128)(2,1)S(1)}, u32[]{:S(2)}, u32[]{:S(2)}) %collective-permute-start.4) | collective-permute-done | bytes 131104 | tf_op jit(solution)/shard_map/ppermute | solution.py:90
  54.2 6.5 %collective-permute-start.7 = (bf16[128,1024]{1,0:T(8,128)(2,1)S(1)}, bf16[128,1024]{1,0:T(8,128)(2,1)S(1)}, u32[]{:S(2)}, u32[]{:S(2)}) collective-permute-start(bf16[128,1024]{1,0:T(8,128)(2,1)S(1)} %pad_maximum_fusion.1), channel_id=1, source_target_pairs={{120,0},{136,128},{0,8},{144,136},{8,16},{152,144},{16,24},{160,15... | collective-permute-start | bytes 786440 | tf_op jit(solution)/shard_map/ppermute | solution.py:90
  60.7 1.9 %collective-permute-start.6 = (bf16[128,1024]{1,0:T(8,128)(2,1)S(1)}, bf16[128,1024]{1,0:T(8,128)(2,1)S(1)}, u32[]{:S(2)}, u32[]{:S(2)}) collective-permute-start(bf16[128,1024]{1,0:T(8,128)(2,1)S(1)} %pad_maximum_fusion.1), channel_id=1, source_target_pairs={{8,0},{248,128},{16,8},{128,136},{24,16},{136,144},{32,24},{144,15... | collective-permute-start | bytes 786440 | tf_op jit(solution)/shard_map/ppermute | solution.py:90
  62.7 5.9 %collective-permute-start.5 = (bf16[256,1024]{1,0:T(8,128)(2,1)S(1)}, bf16[256,1024]{1,0:T(8,128)(2,1)S(1)}, u32[]{:S(2)}, u32[]{:S(2)}) collective-permute-start(bf16[256,1024]{1,0:T(8,128)(2,1)S(1)} %slice_dynamic-update-slice_fusion.refs_0_), channel_id=1, source_target_pairs={{0,128},{128,0},{1,129},{129,1},{2,130},{130,2},{3,131},{131,3},{4... | collective-permute-start | bytes 1572872 | tf_op jit(solution)/shard_map/ppermute | solution.py:94
  68.6 2.6 %collective-permute-done.6 = bf16[128,1024]{1,0:T(8,128)(2,1)S(1)} collective-permute-done((bf16[128,1024]{1,0:T(8,128)(2,1)S(1)}, bf16[128,1024]{1,0:T(8,128)(2,1)S(1)}, u32[]{:S(2)}, u32[]{:S(2)}) %collective-permute-start.6) | collective-permute-done | bytes 262176 | tf_op jit(solution)/shard_map/ppermute | solution.py:90
  71.2 2.4 %collective-permute-start.8 = (bf16[256,1024]{1,0:T(8,128)(2,1)S(1)}, bf16[256,1024]{1,0:T(8,128)(2,1)S(1)}, u32[]{:S(2)}, u32[]{:S(2)}) collective-permute-start(bf16[256,1024]{1,0:T(8,128)(2,1)S(1)} %constant_dynamic-update-slice_fusion.5.refs_2_), channel_id=1, source_target_pairs={{0,128},{128,0},{1,129},{129,1},{2,130},{130,2},{3,131},{131,3},{4... | collective-permute-start | bytes 1572872 | tf_op jit(solution)/shard_map/ppermute | solution.py:94
  73.9 1.6 %copy-done = bf16[1280,1024]{1,0:T(8,128)(2,1)S(1)} copy-done((bf16[1280,1024]{1,0:T(8,128)(2,1)S(1)}, bf16[1280,1024]{1,0:T(8,128)(2,1)}, u32[]{:S(2)}) %copy-start) | copy-done | bytes 2621464
  75.5 4.4 %shard_map.82 = (f32[512,1024]{1,0:T(8,128)S(1)}, bf16[512,1024]{1,0:T(8,128)(2,1)S(1)}, f32[512,128]{1,0:T(8,128)S(1)}, bf16[1024,1024]{1,0:T(8,128)(2,1)S(1)}) custom-call(bf16[512,1408]{1,0:T(8,128)(2,1)S(1)} %pad_maximum_fusion.x_ref.t_ref, bf16[1280,1024]{1,0:T(8,128)(2,1)S(1)} %copy-done), custom_call_target="tpu_custom_call" | custom-call | flops 1342177280 | bytes 8388608 | tf_op jit(solution)/shard_map/pallas_call | solution.py:131
  80.0 10.1 %shard_map.83 = bf16[8,2,256,128]{3,2,1,0:T(8,128)(2,1)S(1)} custom-call(f32[2]{0:T(128)S(1)} %pad_maximum_fusion.5.scale_ref, f32[512,1024]{1,0:T(8,128)S(1)} %get-tuple-element.9.unit_ref, bf16[512,1024]{1,0:T(8,128)(2,1)S(1)} %get-tuple-element.10.unit_b_ref, f32[512,128]{1,0:T(8,128)S(1)} %get-tuple-element.11.mag_ref, ...), custom_call_target="tpu_custom_call" | custom-call | flops 2684354560 | bytes 8388608 | tf_op jit(solution)/shard_map/pallas_call | solution.py:154
  90.0 20.0 %all_to_all.10.g_ref = bf16[16,256,128]{2,1,0:T(8,128)(2,1)S(1)} all-to-all(bf16[16,256,128]{2,1,0:T(8,128)(2,1)S(1)} %bitcast.10), channel_id=1, replica_groups=mesh['ylo'=2,'core'=2,'z'=16,'x'=4,'yhi'=2] {'x','yhi','ylo'}, dimensions={0} | all-to-all | bytes 2097152 | tf_op jit(solution)/shard_map/all_to_all | solution.py:173
  110.2 2.4 %collective-permute-start.9 = (bf16[256,128]{1,0:T(8,128)(2,1)S(1)}, bf16[256,128]{1,0:T(8,128)(2,1)S(1)}, u32[]{:S(2)}, u32[]{:S(2)}) collective-permute-start(bf16[256,128]{1,0:T(8,128)(2,1)S(1)} %shard_map.84.g_ref), channel_id=1, source_target_pairs={{0,256},{256,0},{1,257},{257,1},{2,258},{258,2},{3,259},{259,3},{4... | collective-permute-start | bytes 196616 | tf_op jit(solution)/shard_map/ppermute | solution.py:94
  112.7 2.6 %collective-permute-done.9.far_ref = bf16[256,128]{1,0:T(8,128)(2,1)S(1)} collective-permute-done((bf16[256,128]{1,0:T(8,128)(2,1)S(1)}, bf16[256,128]{1,0:T(8,128)(2,1)S(1)}, u32[]{:S(2)}, u32[]{:S(2)}) %collective-permute-start.9) | collective-permute-done | bytes 65568 | tf_op jit(solution)/shard_map/ppermute | solution.py:94
  115.6 29.7 %all_to_all.11 = bf16[32,8,320]{2,1,0:T(8,128)(2,1)S(1)} all-to-all(bf16[32,8,320]{2,1,0:T(8,128)(2,1)S(1)} %bitcast.11), channel_id=1, replica_groups=mesh['ylo'=2,'core'=2,'z'=16,'x'=4,'yhi'=2] {'core','z'}, dimensions={0} | all-to-all | bytes 327680 | tf_op jit(solution)/shard_map/all_to_all | solution.py:186
  (36 shorter events, 2.7 us)
Async XLA Ops:
  0.0 43.6 %copy-start.1 = (bf16[32,1024]{1,0:T(8,128)(2,1)S(1)}, bf16[32,1024]{1,0:T(8,128)(2,1)}, u32[]{:S(2)}) copy-start(bf16[32,1024]{1,0:T(8,128)(2,1)} %param.10) | copy-start | bytes 196612
  0.0 39.4 %collective-permute-start.2 = (bf16[32,1024]{1,0:T(8,128)(2,1)}, bf16[32,1024]{1,0:T(8,128)(2,1)S(1)}, u32[]{:S(2)}, u32[]{:S(2)}) collective-permute-start(bf16[32,1024]{1,0:T(8,128)(2,1)} %param.10), channel_id=1, source_target_pairs={{80,0},{176,128},{88,8},{184,136},{96,16},{192,144},{104,24},{200,... | collective-permute-start | bytes 196616 | tf_op jit(solution)/shard_map/ppermute | solution.py:90
  15.5 23.9 %collective-permute-start.1 = (bf16[32,1024]{1,0:T(8,128)(2,1)}, bf16[32,1024]{1,0:T(8,128)(2,1)S(1)}, u32[]{:S(2)}, u32[]{:S(2)}) collective-permute-start(bf16[32,1024]{1,0:T(8,128)(2,1)} %param.10), channel_id=1, source_target_pairs={{48,0},{208,128},{56,8},{216,136},{64,16},{224,144},{72,24},{232,1... | collective-permute-start | bytes 196616 | tf_op jit(solution)/shard_map/ppermute | solution.py:90
  31.5 42.1 %collective-permute-start = (bf16[256,1408]{1,0:T(8,128)(2,1)S(1)}, bf16[256,1408]{1,0:T(8,128)(2,1)S(1)}, u32[]{:S(2)}, u32[]{:S(2)}) collective-permute-start(bf16[256,1408]{1,0:T(8,128)(2,1)S(1)} %all_gather.3), channel_id=1, source_target_pairs={{0,1},{1,0},{2,3},{3,2},{4,5},{5,4},{6,7},{7,6},{8,9},{9,8},{10,11... | collective-permute-start | bytes 2162696 | tf_op jit(solution)/shard_map/ppermute | solution.py:94
  40.2 10.9 %collective-permute-start.3 = (bf16[96,1024]{1,0:T(8,128)(2,1)S(1)}, bf16[96,1024]{1,0:T(8,128)(2,1)S(1)}, u32[]{:S(2)}, u32[]{:S(2)}) collective-permute-start(bf16[96,1024]{1,0:T(8,128)(2,1)S(1)} %pad_maximum_fusion.2), channel_id=1, source_target_pairs={{16,0},{240,128},{24,8},{248,136},{32,16},{128,144},{40,24},{136,1... | collective-permute-start | bytes 589832 | tf_op jit(solution)/shard_map/ppermute | solution.py:90
  43.6 10.5 %collective-permute-start.4 = (bf16[64,1024]{1,0:T(8,128)(2,1)S(1)}, bf16[64,1024]{1,0:T(8,128)(2,1)S(1)}, u32[]{:S(2)}, u32[]{:S(2)}) collective-permute-start(bf16[64,1024]{1,0:T(8,128)(2,1)S(1)} %pad_maximum_fusion.3), channel_id=1, source_target_pairs={{112,0},{144,128},{120,8},{152,136},{0,16},{160,144},{8,24},{168,1... | collective-permute-start | bytes 393224 | tf_op jit(solution)/shard_map/ppermute | solution.py:90
  54.2 17.0 %collective-permute-start.7 = (bf16[128,1024]{1,0:T(8,128)(2,1)S(1)}, bf16[128,1024]{1,0:T(8,128)(2,1)S(1)}, u32[]{:S(2)}, u32[]{:S(2)}) collective-permute-start(bf16[128,1024]{1,0:T(8,128)(2,1)S(1)} %pad_maximum_fusion.1), channel_id=1, source_target_pairs={{120,0},{136,128},{0,8},{144,136},{8,16},{152,144},{16,24},{160,15... | collective-permute-start | bytes 786440 | tf_op jit(solution)/shard_map/ppermute | solution.py:90
  60.7 10.5 %collective-permute-start.6 = (bf16[128,1024]{1,0:T(8,128)(2,1)S(1)}, bf16[128,1024]{1,0:T(8,128)(2,1)S(1)}, u32[]{:S(2)}, u32[]{:S(2)}) collective-permute-start(bf16[128,1024]{1,0:T(8,128)(2,1)S(1)} %pad_maximum_fusion.1), channel_id=1, source_target_pairs={{8,0},{248,128},{16,8},{128,136},{24,16},{136,144},{32,24},{144,15... | collective-permute-start | bytes 786440 | tf_op jit(solution)/shard_map/ppermute | solution.py:90
  62.7 17.2 %collective-permute-start.5 = (bf16[256,1024]{1,0:T(8,128)(2,1)S(1)}, bf16[256,1024]{1,0:T(8,128)(2,1)S(1)}, u32[]{:S(2)}, u32[]{:S(2)}) collective-permute-start(bf16[256,1024]{1,0:T(8,128)(2,1)S(1)} %slice_dynamic-update-slice_fusion.refs_0_), channel_id=1, source_target_pairs={{0,128},{128,0},{1,129},{129,1},{2,130},{130,2},{3,131},{131,3},{4... | collective-permute-start | bytes 1572872 | tf_op jit(solution)/shard_map/ppermute | solution.py:94
  71.2 8.7 %collective-permute-start.8 = (bf16[256,1024]{1,0:T(8,128)(2,1)S(1)}, bf16[256,1024]{1,0:T(8,128)(2,1)S(1)}, u32[]{:S(2)}, u32[]{:S(2)}) collective-permute-start(bf16[256,1024]{1,0:T(8,128)(2,1)S(1)} %constant_dynamic-update-slice_fusion.5.refs_2_), channel_id=1, source_target_pairs={{0,128},{128,0},{1,129},{129,1},{2,130},{130,2},{3,131},{131,3},{4... | collective-permute-start | bytes 1572872 | tf_op jit(solution)/shard_map/ppermute | solution.py:94
  73.8 1.7 %copy-start = (bf16[1280,1024]{1,0:T(8,128)(2,1)S(1)}, bf16[1280,1024]{1,0:T(8,128)(2,1)}, u32[]{:S(2)}) copy-start(bf16[1280,1024]{1,0:T(8,128)(2,1)} %w_ref.1) | copy-start | bytes 7864324
  110.2 5.0 %collective-permute-start.9 = (bf16[256,128]{1,0:T(8,128)(2,1)S(1)}, bf16[256,128]{1,0:T(8,128)(2,1)S(1)}, u32[]{:S(2)}, u32[]{:S(2)}) collective-permute-start(bf16[256,128]{1,0:T(8,128)(2,1)S(1)} %shard_map.84.g_ref), channel_id=1, source_target_pairs={{0,256},{256,0},{1,257},{257,1},{2,258},{258,2},{3,259},{259,3},{4... | collective-permute-start | bytes 196616 | tf_op jit(solution)/shard_map/ppermute | solution.py:94

commit v3 on v1

v3 whole, which is shorter than its diff:
```python
import jax
import jax.numpy as jnp
import numpy as np
from jax import lax
from jax.experimental import pallas as pl
from jax.experimental.pallas import tpu as pltpu
from jax.sharding import Mesh, PartitionSpec as P

BF = jnp.bfloat16
F32 = jnp.float32
AXES = ("ylo", "core", "zp", "par", "x", "yhi")
SIZES = (2, 2, 8, 2, 4, 2)
DP = ("zp", "par", "x", "yhi")
Z = ("zp", "par")
PLANE = ("x", "yhi", "ylo")
CHIP = ("ylo", "core")
PAD = 128
PARAMS = pltpu.CompilerParams(vmem_limit_bytes=24 * 2**20)


def column_order():
    was = np.arange(1024)
    goes = (was // 8 % 8) * 128 + (was // 64) * 8 + was % 8
    return jnp.asarray(goes[:, None] == was[None, :], BF)


def project_kernel(x_ref, w_ref, unit_ref, unit_b_ref, mag_ref, t_ref):
    projected = jnp.dot(x_ref[:, : w_ref.shape[0]], w_ref[...], preferred_element_type=F32)
    mag = jnp.sqrt(jnp.sum(projected * projected, axis=1, keepdims=True) + 1e-06)
    unit = projected / mag
    unit_ref[...] = unit
    unit_b_ref[...] = unit.astype(BF)
    mag_ref[...] = jnp.broadcast_to(mag, mag_ref.shape)
    t_ref[...] = x_ref[:, w_ref.shape[0] :]


def pair_kernel(scale_ref, place_ref, *refs):
    video, ids_ref, order_ref, audio_refs, out_ref = refs[:8], refs[8], refs[9], refs[10:14], refs[14]
    unit, unit_b, mag, x = (jnp.concatenate([a[...], b[...]], axis=0) for a, b in zip(video[:4], video[4:]))
    cold = scale_ref[0]
    offset = scale_ref[1]
    halves = x.astype(F32)
    targets = [halves[:, 2 * p : 2 * p + 1] * 128.0 + halves[:, 2 * p + 1 : 2 * p + 2] for p in range(5)]
    total = None
    at = 0
    for audio_ref in audio_refs:
        audio = audio_ref[...]
        n = audio.shape[0]
        ids = ids_ref[:1, at : at + n]
        at += n
        sims = lax.dot_general(unit_b, audio, (((1,), (1,)), ((), ())), preferred_element_type=F32)
        logits = cold * sims + offset
        hit = None
        for target in targets:
            same = target == ids
            hit = same if hit is None else hit | same
        weight = (jax.nn.sigmoid(logits) - jnp.where(hit, 1.0, 0.0)).astype(BF)
        term = jnp.dot(weight, audio, preferred_element_type=F32)
        total = term if total is None else total + term
    grad = cold * total
    inner = jnp.sum(unit * grad, axis=1, keepdims=True)
    gp = ((grad - unit * inner) / mag[:, :1]).astype(BF)
    gp = jnp.dot(gp, order_ref[...], preferred_element_type=F32).astype(BF)
    for h in range(2):
        half = place_ref[0] if h == 0 else 1 - place_ref[0]
        for t in range(8):
            out_ref[2 * t + half] = gp[256 * h : 256 * (h + 1), 128 * t : 128 * (t + 1)]


def weight_kernel(place_ref, g_ref, row_ref, far_ref, out_ref):
    total = g_ref[0].astype(F32)
    for s in range(1, g_ref.shape[0]):
        total = total + g_ref[s].astype(F32)
    gp = total.astype(BF)
    x = jnp.where(place_ref[1] == 1, row_ref[:, :1280], far_ref[:, :1280])
    part = lax.dot_general(gp, x, (((0,), (0,)), ((), ())), preferred_element_type=F32).astype(BF)
    for o in range(4):
        out_ref[o] = part[:, 320 * o : 320 * (o + 1)].reshape(16, 8, 320)


def add_kernel(in_ref, out_ref):
    total = in_ref[0].astype(F32)
    for s in range(1, in_ref.shape[0]):
        total = total + in_ref[s].astype(F32)
    out_ref[...] = total.astype(out_ref.dtype)


def fetch(a, far):
    return lax.ppermute(a, Z, [((z + far) % 16, z) for z in range(16)])


def swap(a, axis):
    return lax.ppermute(a, axis, [(0, 1), (1, 0)])


def local(frames, projector, sounds, matched, coldness, offset):
    ylo, core, zp, par, x, yhi = (lax.axis_index(a) for a in AXES)
    smem = pl.BlockSpec(memory_space=pltpu.SMEM)
    vmem = pl.BlockSpec(memory_space=pltpu.VMEM)

    same = lax.all_to_all(jnp.broadcast_to(sounds[None], (8, 32, 1024)), "zp", 0, 0, tiled=True).reshape(256, 1024)

    halves = jnp.stack([matched >> 7, matched & 127], axis=2).reshape(128, 10).astype(BF)
    wide = jnp.concatenate([frames, jnp.pad(halves, ((0, 0), (0, PAD - 10)))], axis=1)
    wide = lax.dynamic_slice_in_dim(wide, core * 64, 64, 0)
    row = lax.all_gather(wide, "x", axis=0, tiled=True)
    same, _ = lax.optimization_barrier((same, row))
    far = swap(row, "yhi")

    other = jnp.concatenate([fetch(same[:128], 1), fetch(same[128:], -1)], axis=0)
    far_same = swap(same, "core")
    far_other = swap(other, "core")
    place = jnp.stack([yhi, 1 - (yhi ^ ylo)]).astype(jnp.int32)
    pars = jnp.stack([par, par, 1 - par, 1 - par])
    cores = jnp.stack([core, 1 - core, core, 1 - core])
    firsts = ylo * 8192 + cores * 4096 + pars * 256 + (2 * x + yhi) * 32
    inside = np.arange(8)[:, None] * 512 + np.arange(32)[None, :]
    ids = (firsts[:, None] + jnp.asarray(inside.reshape(1, 256), jnp.int32)).astype(F32).reshape(1, 1024)

    project = pl.pallas_call(
        project_kernel,
        in_specs=[vmem, vmem],
        out_specs=[vmem] * 4,
        out_shape=[
            jax.ShapeDtypeStruct((256, 1024), F32),
            jax.ShapeDtypeStruct((256, 1024), BF),
            jax.ShapeDtypeStruct((256, 128), F32),
            jax.ShapeDtypeStruct((256, PAD), BF),
        ],
        compiler_params=PARAMS,
        cost_estimate=pl.CostEstimate(flops=2 * 256 * 1280 * 1024, bytes_accessed=5 * 2**20, transcendentals=0),
    )
    video = [*project(row, projector), *project(far, projector)]
    parts = pl.pallas_call(
        pair_kernel,
        in_specs=[smem, smem] + [vmem] * 14,
        out_specs=vmem,
        out_shape=jax.ShapeDtypeStruct((16, 256, 128), BF),
        compiler_params=PARAMS,
        cost_estimate=pl.CostEstimate(flops=5 * 512 * 1024 * 1024, bytes_accessed=8 * 2**20, transcendentals=2**20),
    )(
        jnp.concatenate([coldness, offset]),
        place,
        *video,
        ids,
        column_order(),
        same,
        far_same,
        other,
        far_other,
    )

    terms = lax.all_to_all(parts, PLANE, 0, 0, tiled=True)
    pieces = pl.pallas_call(
        weight_kernel,
        in_specs=[smem, vmem, vmem, vmem],
        out_specs=vmem,
        out_shape=jax.ShapeDtypeStruct((4, 16, 8, 320), BF),
        compiler_params=PARAMS,
    )(place, terms, row, far)
    mine = lax.all_to_all(pieces, CHIP, 0, 0, tiled=True)
    mine = pl.pallas_call(
        add_kernel, in_specs=[vmem], out_specs=vmem, out_shape=jax.ShapeDtypeStruct((16, 8, 320), BF), compiler_params=PARAMS
    )(mine)
    sums = lax.all_to_all(mine, Z, 0, 0, tiled=True)
    return jnp.sum(sums.astype(F32), axis=0).T


def solution(mesh):
    fine = Mesh(mesh.devices.reshape(SIZES), AXES)
    return jax.shard_map(
        local,
        mesh=fine,
        in_specs=(P(DP, None), P(), P(AXES, None), P(DP, None), P(), P()),
        out_specs=P(CHIP, DP),
        check_vma=False,
    )
```

time: 161 us -> 138 us (0.86)
  blocking collectives: 88.3 us -> 68.9 us
  local copies, waits for them, and re-layouts: 16.3 us -> 5.82 us
  starting transfers between devices: 28.5 us -> 34 us
    all_to_all x2 -> x3, blocking collectives: 75.9 us -> 56.4 us  [the longest x1 23 us: local(): sums = lax.all_to_all(mine, Z, 0, 0, tiled=True)]
    unnamed x8, local copies, waits for them, and re-layouts: 6.91 us -> 0.99 us
    ppermute x2 -> x5, starting transfers between devices: 12.8 us -> 18.4 us  [the longest x3 12.1 us: swap(): return lax.ppermute(a, axis, [(0, 1), (1, 0)])]
    reshape x1 -> x0, local copies, waits for them, and re-layouts: 4.53 us -> none  [by_owner(): return a.reshape(n, 16, 8, 8).transpose(0, 2, 1, 3).reshape(n, 1024)]
    transpose x2 -> x0, local copies, waits for them, and re-layouts: 3.47 us -> none  [by_owner(): return a.reshape(n, 16, 8, 8).transpose(0, 2, 1, 3).reshape(n, 1024)]
    all_to_all x1, waiting for transfers between devices: 13.6 us -> 11.6 us  [local(): lax.all_to_all(jnp.broadcast_to(sounds[None], (8, 32, 1024)), 'zp', 0, 0,...]
    slice x0 -> x1, local copies, waits for them, and re-layouts: none -> 1.86 us  [local(): same[128:]]
    pallas_call x3 -> x5, Pallas kernels: 10.3 us -> 10.7 us  [the longest x1 5.94 us: local(): pl.pallas_call(pair_kernel, in_specs=[smem, smem] + [vmem] * 14, out_spec...]
  transfers between devices with their start and end apart: 3 -> 6, of which waited for: 1 -> 2; matrix products, arithmetic and copies ran while one was open for 8% -> 3% of each run, Pallas kernels for 2% -> 2%
where the time goes in v3:
time: 138 us; the launch traced here: 136 us
  blocking collectives  68.9 us (50%)
  starting transfers between devices  34 us (25%)
  waiting for transfers between devices  12.9 us (9%)
  Pallas kernels  10.7 us (8%)
  local copies, waits for them, and re-layouts  5.82 us (4%)
  other arithmetic  2.56 us (2%)
  between operations  1.46 us (1%)
    all_to_all x1, blocking collectives, local(): sums = lax.all_to_all(mine, Z, 0, 0, tiled=True)  23 us
    all_to_all x1, blocking collectives, local(): terms = lax.all_to_all(parts, PLANE, 0, 0, tiled=True)  18.3 us
    all_to_all x1, starting transfers between devices, local(): lax.all_to_all(jnp.broadcast_to(sounds[None], (8, 32, 1024)), 'zp', 0, 0,...  15.6 us
    all_to_all x1, blocking collectives, local(): mine = lax.all_to_all(pieces, CHIP, 0, 0, tiled=True)  15.1 us
    all_gather x1, blocking collectives, local(): row = lax.all_gather(wide, 'x', axis=0, tiled=True)  12.5 us
    ppermute x3, starting transfers between devices, swap(): return lax.ppermute(a, axis, [(0, 1), (1, 0)])  12.1 us
    all_to_all x1, waiting for transfers between devices, local(): lax.all_to_all(jnp.broadcast_to(sounds[None], (8, 32, 1024)), 'zp', 0, 0,...  11.6 us
    ppermute x2, starting transfers between devices, fetch(): return lax.ppermute(a, Z, [((z + far) % 16, z) for z in range(16)])  6.35 us
  transfers between devices with their start and end apart: 6, of which 2 were waited for; matrix products, arithmetic and copies ran while one was open for 3% of the time, Pallas kernels for 2%

profile of v3, /device:TPU:1, one launch (start us, length us, event | category | flops | bytes accessed | tf_op | source)
XLA Modules:
  0.0 136.5 jit_solution(6361310098210221096)
XLA Ops:
  0.0 1.8 %broadcast_in_dim.2 = bf16[8,32,1024]{2,1,0:T(8,128)(2,1)} broadcast(bf16[32,1024]{1,0:T(8,128)(2,1)} %param.10), dimensions={1,2} | broadcast | bytes 589824 | tf_op jit(solution)/shard_map/broadcast_in_dim | solution.py:101
  1.8 15.6 %all-to-all-start = ((bf16[8,32,1024]{2,1,0:T(8,128)(2,1)}), bf16[8,32,1024]{2,1,0:T(8,128)(2,1)}, u32[]{:S(2)}, u32[]{:S(2)}) async-start(bf16[8,32,1024]{2,1,0:T(8,128)(2,1)} %broadcast_in_dim.2), calls=%async_computation | async-start | bytes 1048576 | tf_op jit(solution)/shard_map/all_to_all | solution.py:101
  17.5 0.7 fusion.2
  18.2 0.1 copy.11
  18.3 0.9 fusion.1
  19.3 12.5 %all_gather.3.x_ref.row_ref = bf16[256,1408]{1,0:T(8,128)(2,1)S(1)} all-gather(bf16[64,1408]{1,0:T(8,128)(2,1)S(1)} %fusion.1), channel_id=1, replica_groups=mesh['ylo'=2,'core'=2,'zp'=8,'par'=2,'x'=4,'yhi'=2] {'x'}, dimensions={0}, use_global_device_ids=true | all-gather | bytes 901120 | tf_op jit(solution)/shard_map/all_gather | solution.py:106
  31.8 11.6 %all-to-all-done = bf16[8,32,1024]{2,1,0:T(8,128)(2,1)} async-done(((bf16[8,32,1024]{2,1,0:T(8,128)(2,1)}), bf16[8,32,1024]{2,1,0:T(8,128)(2,1)}, u32[]{:S(2)}, u32[]{:S(2)}) %all-to-all-start) | async-done | bytes 524320 | tf_op jit(solution)/shard_map/all_to_all | solution.py:101
  43.4 1.9 %fusion.7 = (bf16[128,1024]{1,0:T(8,128)(2,1)}, bf16[128,1024]{1,0:T(8,128)(2,1)}) fusion(bf16[256,1024]{1,0:T(8,128)(2,1)} %bitcast.8.refs_10_), kind=kLoop, calls=%fused_computation.21 | loop fusion | bytes 1048576 | tf_op jit(solution)/shard_map/slice | solution.py:110
  45.3 4.4 %collective-permute-start.2 = (bf16[128,1024]{1,0:T(8,128)(2,1)}, bf16[128,1024]{1,0:T(8,128)(2,1)}, u32[]{:S(2)}, u32[]{:S(2)}) collective-permute-start(bf16[128,1024]{1,0:T(8,128)(2,1)} %get-tuple-element.24), channel_id=1, source_target_pairs={{8,0},{16,8},{24,16},{32,24},{40,32},{48,40},{56,48},{64,56},{72,6... | collective-permute-start | bytes 786440 | tf_op jit(solution)/shard_map/ppermute | solution.py:89
  49.7 1.9 %collective-permute-start.3 = (bf16[128,1024]{1,0:T(8,128)(2,1)}, bf16[128,1024]{1,0:T(8,128)(2,1)}, u32[]{:S(2)}, u32[]{:S(2)}) collective-permute-start(bf16[128,1024]{1,0:T(8,128)(2,1)} %get-tuple-element.23), channel_id=1, source_target_pairs={{120,0},{0,8},{8,16},{16,24},{24,32},{32,40},{40,48},{48,56},{56,6... | collective-permute-start | bytes 786440 | tf_op jit(solution)/shard_map/ppermute | solution.py:89
  51.7 4.8 %collective-permute-start = (bf16[256,1408]{1,0:T(8,128)(2,1)S(1)}, bf16[256,1408]{1,0:T(8,128)(2,1)}, u32[]{:S(2)}, u32[]{:S(2)}) collective-permute-start(bf16[256,1408]{1,0:T(8,128)(2,1)S(1)} %all_gather.3.x_ref.row_ref), channel_id=1, source_target_pairs={{0,1},{1,0},{2,3},{3,2},{4,5},{5,4},{6,7},{7,6},{8,9},{9,8},{10,11... | collective-permute-start | bytes 2162696 | tf_op jit(solution)/shard_map/ppermute | solution.py:93
  57.9 5.3 %collective-permute-start.1 = (bf16[256,1024]{1,0:T(8,128)(2,1)}, bf16[256,1024]{1,0:T(8,128)(2,1)S(1)}, u32[]{:S(2)}, u32[]{:S(2)}) collective-permute-start(bf16[256,1024]{1,0:T(8,128)(2,1)} %bitcast.8.refs_10_), channel_id=1, source_target_pairs={{0,128},{128,0},{1,129},{129,1},{2,130},{130,2},{3,131},{131,3},{4... | collective-permute-start | bytes 1572872 | tf_op jit(solution)/shard_map/ppermute | solution.py:93
  63.2 1.0 constant_dynamic-update-slice_fusion.1
  64.2 1.0 constant_dynamic-update-slice_fusion.refs_12_
  65.2 1.9 %collective-permute-start.4 = (bf16[256,1024]{1,0:T(8,128)(2,1)S(1)}, bf16[256,1024]{1,0:T(8,128)(2,1)S(1)}, u32[]{:S(2)}, u32[]{:S(2)}) collective-permute-start(bf16[256,1024]{1,0:T(8,128)(2,1)S(1)} %constant_dynamic-update-slice_fusion.refs_12_), channel_id=1, source_target_pairs={{0,128},{128,0},{1,129},{129,1},{2,130},{130,2},{3,131},{131,3},{4... | collective-permute-start | bytes 1572872 | tf_op jit(solution)/shard_map/ppermute | solution.py:93
  67.2 1.0 shard_map.82
  68.4 1.3 collective-permute-done.x_ref.far_ref
  69.6 2.1 %shard_map.83 = (f32[256,1024]{1,0:T(8,128)S(1)}, bf16[256,1024]{1,0:T(8,128)(2,1)S(1)}, f32[256,128]{1,0:T(8,128)S(1)}, bf16[256,128]{1,0:T(8,128)(2,1)S(1)}) custom-call(bf16[256,1408]{1,0:T(8,128)(2,1)} %collective-permute-done.x_ref.far_ref, bf16[1280,1024]{1,0:T(8,128)(2,1)S(1)} %copy-done), custom_call_target="tpu_custom_call" | custom-call | flops 671088640 | bytes 5242880 | tf_op jit(solution)/shard_map/pallas_call | solution.py:133
  71.8 5.9 %shard_map.84 = bf16[16,256,128]{2,1,0:T(8,128)(2,1)S(1)} custom-call(f32[2]{0:T(128)S(1)} %pad_maximum_fusion.1.scale_ref, s32[2]{0:T(128)S(1)} %pad_add_fusion.place_ref, f32[256,1024]{1,0:T(8,128)S(1)} %get-tuple-element.14.refs_0_, bf16[256,1024]{1,0:T(8,128)(2,1)S(1)} %get-tuple-element.15.refs_1_, f32[256,128]{1,0:T(8,128)S(1)} %get-tuple-element.16.refs_2_, ...), custom_call_target="tpu_custom_call" | custom-call | flops 2684354560 | bytes 8388608 | tf_op jit(solution)/shard_map/pallas_call | solution.py:134
  77.7 18.3 %all_to_all.20.g_ref = bf16[16,256,128]{2,1,0:T(8,128)(2,1)S(1)} all-to-all(bf16[16,256,128]{2,1,0:T(8,128)(2,1)S(1)} %shard_map.84), channel_id=1, replica_groups=mesh['ylo'=2,'core'=2,'zp'=8,'par'=2,'x'=4,'yhi'=2] {'x','yhi','ylo'}, dimensions={0} | all-to-all | bytes 2097152 | tf_op jit(solution)/shard_map/all_to_all | solution.py:153
  96.0 1.6 %shard_map.85 = bf16[4,16,8,320]{3,2,1,0:T(8,128)(2,1)S(1)} custom-call(s32[2]{0:T(128)S(1)} %pad_add_fusion.place_ref, bf16[16,256,128]{2,1,0:T(8,128)(2,1)S(1)} %all_to_all.20.g_ref, bf16[256,1408]{1,0:T(8,128)(2,1)S(1)} %all_gather.3.x_ref.row_ref, bf16[256,1408]{1,0:T(8,128)(2,1)} %collective-permute-done.x_ref.far_ref), custom_call_target="tpu_custom_call" | custom-call | tf_op jit(solution)/shard_map/pallas_call | solution.py:154
  97.6 15.1 %all_to_all.21.in_ref = bf16[4,16,8,320]{3,2,1,0:T(8,128)(2,1)S(1)} all-to-all(bf16[4,16,8,320]{3,2,1,0:T(8,128)(2,1)S(1)} %shard_map.85), channel_id=1, replica_groups=mesh['ylo'=2,'core'=2,'zp'=8,'par'=2,'x'=4,'yhi'=2] {'ylo','core'}, dimensions={0} | all-to-all | bytes 655360 | tf_op jit(solution)/shard_map/all_to_all | solution.py:161
  112.8 23.0 %all_to_all.22 = bf16[16,8,320]{2,1,0:T(8,128)(2,1)S(1)} all-to-all(bf16[16,8,320]{2,1,0:T(8,128)(2,1)S(1)} %shard_map.86), channel_id=1, replica_groups=mesh['ylo'=2,'core'=2,'zp'=8,'par'=2,'x'=4,'yhi'=2] {'zp','par'}, dimensions={0} | all-to-all | bytes 163840 | tf_op jit(solution)/shard_map/all_to_all | solution.py:165
  135.8 0.6 convert_reduce_fusion
  (19 shorter events, 0.4 us)
Async XLA Ops:
  0.0 67.1 %copy-start.2 = (s32[256]{0:T(256)S(1)}, s32[256]{0:T(256)}, u32[]{:S(2)}) copy-start(s32[256]{0:T(256)} %constant.54) | copy-start | bytes 3076
  0.0 67.2 %copy-start = (bf16[1280,1024]{1,0:T(8,128)(2,1)S(1)}, bf16[1280,1024]{1,0:T(8,128)(2,1)}, u32[]{:S(2)}) copy-start(bf16[1280,1024]{1,0:T(8,128)(2,1)} %w_ref.3) | copy-start | bytes 7864324
  1.8 41.6 %all-to-all-start = ((bf16[8,32,1024]{2,1,0:T(8,128)(2,1)}), bf16[8,32,1024]{2,1,0:T(8,128)(2,1)}, u32[]{:S(2)}, u32[]{:S(2)}) async-start(bf16[8,32,1024]{2,1,0:T(8,128)(2,1)} %broadcast_in_dim.2), calls=%async_computation | async-start | bytes 1048576 | tf_op jit(solution)/shard_map/all_to_all | solution.py:101
  45.3 17.9 %collective-permute-start.2 = (bf16[128,1024]{1,0:T(8,128)(2,1)}, bf16[128,1024]{1,0:T(8,128)(2,1)}, u32[]{:S(2)}, u32[]{:S(2)}) collective-permute-start(bf16[128,1024]{1,0:T(8,128)(2,1)} %get-tuple-element.24), channel_id=1, source_target_pairs={{8,0},{16,8},{24,16},{32,24},{40,32},{48,40},{56,48},{64,56},{72,6... | collective-permute-start | bytes 786440 | tf_op jit(solution)/shard_map/ppermute | solution.py:89
  49.7 14.5 %collective-permute-start.3 = (bf16[128,1024]{1,0:T(8,128)(2,1)}, bf16[128,1024]{1,0:T(8,128)(2,1)}, u32[]{:S(2)}, u32[]{:S(2)}) collective-permute-start(bf16[128,1024]{1,0:T(8,128)(2,1)} %get-tuple-element.23), channel_id=1, source_target_pairs={{120,0},{0,8},{8,16},{16,24},{24,32},{32,40},{40,48},{48,56},{56,6... | collective-permute-start | bytes 786440 | tf_op jit(solution)/shard_map/ppermute | solution.py:89
  51.7 18.0 %collective-permute-start = (bf16[256,1408]{1,0:T(8,128)(2,1)S(1)}, bf16[256,1408]{1,0:T(8,128)(2,1)}, u32[]{:S(2)}, u32[]{:S(2)}) collective-permute-start(bf16[256,1408]{1,0:T(8,128)(2,1)S(1)} %all_gather.3.x_ref.row_ref), channel_id=1, source_target_pairs={{0,1},{1,0},{2,3},{3,2},{4,5},{5,4},{6,7},{7,6},{8,9},{9,8},{10,11... | collective-permute-start | bytes 2162696 | tf_op jit(solution)/shard_map/ppermute | solution.py:93
  57.9 13.9 %collective-permute-start.1 = (bf16[256,1024]{1,0:T(8,128)(2,1)}, bf16[256,1024]{1,0:T(8,128)(2,1)S(1)}, u32[]{:S(2)}, u32[]{:S(2)}) collective-permute-start(bf16[256,1024]{1,0:T(8,128)(2,1)} %bitcast.8.refs_10_), channel_id=1, source_target_pairs={{0,128},{128,0},{1,129},{129,1},{2,130},{130,2},{3,131},{131,3},{4... | collective-permute-start | bytes 1572872 | tf_op jit(solution)/shard_map/ppermute | solution.py:93
  65.2 6.6 %collective-permute-start.4 = (bf16[256,1024]{1,0:T(8,128)(2,1)S(1)}, bf16[256,1024]{1,0:T(8,128)(2,1)S(1)}, u32[]{:S(2)}, u32[]{:S(2)}) collective-permute-start(bf16[256,1024]{1,0:T(8,128)(2,1)S(1)} %constant_dynamic-update-slice_fusion.refs_12_), channel_id=1, source_target_pairs={{0,128},{128,0},{1,129},{129,1},{2,130},{130,2},{3,131},{131,3},{4... | collective-permute-start | bytes 1572872 | tf_op jit(solution)/shard_map/ppermute | solution.py:93
  67.2 4.6 %copy-start.1 = (bf16[1024,1024]{1,0:T(8,128)(2,1)S(1)}, bf16[1024,1024]{1,0:T(8,128)(2,1)}, u32[]{:S(2)}) copy-start(bf16[1024,1024]{1,0:T(8,128)(2,1)} %constant.50.clone.refs_9_) | copy-start | bytes 6291460

commit v4 on v3

--- a/solution.py
+++ b/solution.py
@@ -67,26 +67,34 @@
             out_ref[2 * t + half] = gp[256 * h : 256 * (h + 1), 128 * t : 128 * (t + 1)]
 
 
-def weight_kernel(place_ref, g_ref, row_ref, far_ref, out_ref):
+def sum_kernel(g_ref, out_ref):
     total = g_ref[0].astype(F32)
     for s in range(1, g_ref.shape[0]):
         total = total + g_ref[s].astype(F32)
-    gp = total.astype(BF)
-    x = jnp.where(place_ref[1] == 1, row_ref[:, :1280], far_ref[:, :1280])
-    part = lax.dot_general(gp, x, (((0,), (0,)), ((), ())), preferred_element_type=F32).astype(BF)
-    for o in range(4):
-        out_ref[o] = part[:, 320 * o : 320 * (o + 1)].reshape(16, 8, 320)
+    out_ref[...] = total.astype(BF)
 
 
-def add_kernel(in_ref, out_ref):
-    total = in_ref[0].astype(F32)
-    for s in range(1, in_ref.shape[0]):
-        total = total + in_ref[s].astype(F32)
-    out_ref[...] = total.astype(out_ref.dtype)
+def weight_kernel(place_ref, mine_ref, other_ref, row_ref, far_ref, keep_ref, give_ref):
+    lanes = pl.ds(pl.multiple_of(place_ref[2] * 640, 128), 640)
+    mine, other = mine_ref[...], other_ref[...]
+    own = place_ref[1] == 1
+    part = None
+    for gp, rows in ((jnp.where(own, mine, other), row_ref[:, lanes]), (jnp.where(own, other, mine), far_ref[:, lanes])):
+        term = lax.dot_general(gp, rows, (((0,), (0,)), ((), ())), preferred_element_type=F32)
+        part = term if part is None else part + term
+    first, second = (part[:, 320 * c : 320 * (c + 1)].reshape(16, 8, 320) for c in range(2))
+    core = place_ref[3]
+    keep_ref[...] = jnp.where(core == 0, first, second)
+    give_ref[...] = jnp.where(core == 0, second, first).astype(BF)
 
 
-def fetch(a, far):
-    return lax.ppermute(a, Z, [((z + far) % 16, z) for z in range(16)])
+def add_kernel(a_ref, b_ref, out_ref):
+    out_ref[...] = (a_ref[...] + b_ref[...].astype(F32)).astype(BF)
+
+
+def fetch(a):
+    perm = [((z + 1) % 16, z) for z in range(16)] + [(16 + (z - 1) % 16, 16 + z) for z in range(16)]
+    return lax.ppermute(a, ("core", "zp", "par"), perm)
 
 
 def swap(a, axis):
@@ -103,14 +111,15 @@
     halves = jnp.stack([matched >> 7, matched & 127], axis=2).reshape(128, 10).astype(BF)
     wide = jnp.concatenate([frames, jnp.pad(halves, ((0, 0), (0, PAD - 10)))], axis=1)
     wide = lax.dynamic_slice_in_dim(wide, core * 64, 64, 0)
+    across = lax.ppermute(wide, ("ylo", "yhi"), [(0, 3), (3, 0), (1, 2), (2, 1)])
     row = lax.all_gather(wide, "x", axis=0, tiled=True)
-    same, _ = lax.optimization_barrier((same, row))
-    far = swap(row, "yhi")
+    far = lax.all_gather(across, "x", axis=0, tiled=True)
+    same, _, _ = lax.optimization_barrier((same, row, far))
 
-    other = jnp.concatenate([fetch(same[:128], 1), fetch(same[128:], -1)], axis=0)
+    other = fetch(same)
     far_same = swap(same, "core")
     far_other = swap(other, "core")
-    place = jnp.stack([yhi, 1 - (yhi ^ ylo)]).astype(jnp.int32)
+    place = jnp.stack([yhi, 1 - (yhi ^ ylo), ylo, core]).astype(jnp.int32)
     pars = jnp.stack([par, par, 1 - par, 1 - par])
     cores = jnp.stack([core, 1 - core, core, 1 - core])
     firsts = ylo * 8192 + cores * 4096 + pars * 256 + (2 * x + yhi) * 32
@@ -151,17 +160,23 @@
     )
 
     terms = lax.all_to_all(parts, PLANE, 0, 0, tiled=True)
-    pieces = pl.pallas_call(
+    mine = pl.pallas_call(
+        sum_kernel, in_specs=[vmem], out_specs=vmem, out_shape=jax.ShapeDtypeStruct((256, 128), BF), compiler_params=PARAMS
+    )(terms)
+    keep, give = pl.pallas_call(
         weight_kernel,
-        in_specs=[smem, vmem, vmem, vmem],
+        in_specs=[smem] + [vmem] * 4,
+        out_specs=[vmem, vmem],
+        out_shape=[jax.ShapeDtypeStruct((16, 8, 320), F32), jax.ShapeDtypeStruct((16, 8, 320), BF)],
+        compiler_params=PARAMS,
+    )(place, mine, swap(mine, "ylo"), row, far)
+    mine = pl.pallas_call(
+        add_kernel,
+        in_specs=[vmem, vmem],
         out_specs=vmem,
-        out_shape=jax.ShapeDtypeStruct((4, 16, 8, 320), BF),
+        out_shape=jax.ShapeDtypeStruct((16, 8, 320), BF),
         compiler_params=PARAMS,
-    )(place, terms, row, far)
-    mine = lax.all_to_all(pieces, CHIP, 0, 0, tiled=True)
-    mine = pl.pallas_call(
-        add_kernel, in_specs=[vmem], out_specs=vmem, out_shape=jax.ShapeDtypeStruct((16, 8, 320), BF), compiler_params=PARAMS
-    )(mine)
+    )(keep, swap(give, "core"))
     sums = lax.all_to_all(mine, Z, 0, 0, tiled=True)
     return jnp.sum(sums.astype(F32), axis=0).T
 

time: 138 us -> 132 us (0.957)
  starting transfers between devices: 34 us -> 46.4 us
  waiting for transfers between devices: 12.9 us -> 3.52 us
  local copies, waits for them, and re-layouts: 5.82 us -> 2.04 us
  blocking collectives: 68.9 us -> 65.8 us
  Pallas kernels: 10.7 us -> 9.22 us
    all_to_all x1 -> x0, blocking collectives: 15.1 us -> none  [local(): mine = lax.all_to_all(pieces, CHIP, 0, 0, tiled=True)]
    all_gather x0 -> x1, blocking collectives: none -> 11.7 us  [local(): far = lax.all_gather(across, 'x', axis=0, tiled=True)]
    all_to_all x1, waiting for transfers between devices: 11.6 us -> 0.01 us  [local(): lax.all_to_all(jnp.broadcast_to(sounds[None], (8, 32, 1024)), 'zp', 0, 0,...]
    ppermute x3 -> x4, starting transfers between devices: 12.1 us -> 23.5 us  [swap(): return lax.ppermute(a, axis, [(0, 1), (1, 0)])]
    ppermute x3 -> x4, waiting for transfers between devices: 1.29 us -> 3.52 us  [swap(): return lax.ppermute(a, axis, [(0, 1), (1, 0)])]
    slice x1 -> x0, local copies, waits for them, and re-layouts: 1.86 us -> none  [local(): same[128:]]
  transfers between devices with their start and end apart: 6 -> 7, of which waited for: 2 -> 2; matrix products, arithmetic and copies ran while one was open for 3% -> 2% of each run, Pallas kernels for 2% -> 2%
where the time goes in v4:
time: 132 us; the launch traced here: 131 us
  blocking collectives  65.8 us (50%)
  starting transfers between devices  46.4 us (35%)
  Pallas kernels  9.22 us (7%)
  waiting for transfers between devices  3.52 us (3%)
  other arithmetic  2.56 us (2%)
  local copies, waits for them, and re-layouts  2.04 us (2%)
  between operations  1.47 us (1%)
    ppermute x4, starting transfers between devices, swap(): return lax.ppermute(a, axis, [(0, 1), (1, 0)])  23.5 us
    all_to_all x1, blocking collectives, local(): sums = lax.all_to_all(mine, Z, 0, 0, tiled=True)  22.3 us
    all_to_all x1, blocking collectives, local(): terms = lax.all_to_all(parts, PLANE, 0, 0, tiled=True)  18.9 us
    all_to_all x1, starting transfers between devices, local(): lax.all_to_all(jnp.broadcast_to(sounds[None], (8, 32, 1024)), 'zp', 0, 0,...  15.6 us
    all_gather x1, blocking collectives, local(): row = lax.all_gather(wide, 'x', axis=0, tiled=True)  12.8 us
    all_gather x1, blocking collectives, local(): far = lax.all_gather(across, 'x', axis=0, tiled=True)  11.7 us
    pallas_call x1, Pallas kernels, local(): pl.pallas_call(pair_kernel, in_specs=[smem, smem] + [vmem] * 14, out_spec...  6.03 us
    ppermute x1, starting transfers between devices, local(): lax.ppermute(wide, ('ylo', 'yhi'), [(0, 3), (3, 0), (1, 2), (2, 1)])  4.64 us
  transfers between devices with their start and end apart: 7, of which 2 were waited for; matrix products, arithmetic and copies ran while one was open for 2% of the time, Pallas kernels for 2%

profile of v4, /device:TPU:1, one launch (start us, length us, event | category | flops | bytes accessed | tf_op | source)
XLA Modules:
  0.0 130.9 jit_solution(8959989515146925087)
XLA Ops:
  0.0 1.9 %broadcast_in_dim.2 = bf16[8,32,1024]{2,1,0:T(8,128)(2,1)} broadcast(bf16[32,1024]{1,0:T(8,128)(2,1)} %param.10), dimensions={1,2} | broadcast | bytes 589824 | tf_op jit(solution)/shard_map/broadcast_in_dim | solution.py:109
  1.9 15.6 %all-to-all-start = ((bf16[8,32,1024]{2,1,0:T(8,128)(2,1)}), bf16[8,32,1024]{2,1,0:T(8,128)(2,1)}, u32[]{:S(2)}, u32[]{:S(2)}) async-start(bf16[8,32,1024]{2,1,0:T(8,128)(2,1)} %broadcast_in_dim.2), calls=%async_computation | async-start | bytes 1048576 | tf_op jit(solution)/shard_map/all_to_all | solution.py:109
  17.5 0.7 fusion.2
  18.2 0.1 copy.11
  18.4 0.9 fusion.1
  19.3 4.6 %collective-permute-start = (bf16[64,1408]{1,0:T(8,128)(2,1)S(1)}, bf16[64,1408]{1,0:T(8,128)(2,1)S(1)}, u32[]{:S(2)}, u32[]{:S(2)}) collective-permute-start(bf16[64,1408]{1,0:T(8,128)(2,1)S(1)} %fusion.1), channel_id=1, source_target_pairs={{0,257},{257,0},{1,256},{256,1},{2,259},{259,2},{3,258},{258,3},{4... | collective-permute-start | bytes 540680 | tf_op jit(solution)/shard_map/ppermute | solution.py:114
  23.9 12.8 %all_gather.6.x_ref.row_ref = bf16[256,1408]{1,0:T(8,128)(2,1)S(1)} all-gather(bf16[64,1408]{1,0:T(8,128)(2,1)S(1)} %fusion.1), channel_id=1, replica_groups=mesh['ylo'=2,'core'=2,'zp'=8,'par'=2,'x'=4,'yhi'=2] {'x'}, dimensions={0}, use_global_device_ids=true | all-gather | bytes 901120 | tf_op jit(solution)/shard_map/all_gather | solution.py:115
  36.8 11.7 %all_gather.7.x_ref.far_ref = bf16[256,1408]{1,0:T(8,128)(2,1)} all-gather(bf16[64,1408]{1,0:T(8,128)(2,1)S(1)} %collective-permute-done), channel_id=1, replica_groups=mesh['ylo'=2,'core'=2,'zp'=8,'par'=2,'x'=4,'yhi'=2] {'x'}, dimensions={0}, use_global_device_ids=true | all-gather | bytes 901120 | tf_op jit(solution)/shard_map/all_gather | solution.py:116
  48.5 2.6 %collective-permute-start.2 = (bf16[256,1024]{1,0:T(8,128)(2,1)}, bf16[256,1024]{1,0:T(8,128)(2,1)}, u32[]{:S(2)}, u32[]{:S(2)}) collective-permute-start(bf16[256,1024]{1,0:T(8,128)(2,1)} %bitcast.9.refs_10_), channel_id=1, source_target_pairs={{8,0},{16,8},{24,16},{32,24},{40,32},{48,40},{56,48},{64,56},{72,6... | collective-permute-start | bytes 1572872 | tf_op jit(solution)/shard_map/ppermute | solution.py:97
  52.4 0.1 fusion.6
  52.5 10.3 %collective-permute-start.1 = (bf16[256,1024]{1,0:T(8,128)(2,1)}, bf16[256,1024]{1,0:T(8,128)(2,1)S(1)}, u32[]{:S(2)}, u32[]{:S(2)}) collective-permute-start(bf16[256,1024]{1,0:T(8,128)(2,1)} %bitcast.9.refs_10_), channel_id=1, source_target_pairs={{0,128},{128,0},{1,129},{129,1},{2,130},{130,2},{3,131},{131,3},{4... | collective-permute-start | bytes 1572872 | tf_op jit(solution)/shard_map/ppermute | solution.py:101
  62.8 5.4 %collective-permute-start.3 = (bf16[256,1024]{1,0:T(8,128)(2,1)}, bf16[256,1024]{1,0:T(8,128)(2,1)S(1)}, u32[]{:S(2)}, u32[]{:S(2)}) collective-permute-start(bf16[256,1024]{1,0:T(8,128)(2,1)} %collective-permute-done.2.refs_12_), channel_id=1, source_target_pairs={{0,128},{128,0},{1,129},{129,1},{2,130},{130,2},{3,131},{131,3},{4... | collective-permute-start | bytes 1572872 | tf_op jit(solution)/shard_map/ppermute | solution.py:101
  68.3 1.0 shard_map.82
  69.5 1.0 shard_map.83
  70.6 6.0 %shard_map.84 = bf16[16,256,128]{2,1,0:T(8,128)(2,1)S(1)} custom-call(f32[2]{0:T(128)S(1)} %pad_maximum_fusion.1.scale_ref, s32[4]{0:T(128)S(1)} %pad_add_fusion.place_ref, f32[256,1024]{1,0:T(8,128)S(1)} %get-tuple-element.16.refs_0_, bf16[256,1024]{1,0:T(8,128)(2,1)S(1)} %get-tuple-element.17.refs_1_, f32[256,128]{1,0:T(8,128)S(1)} %get-tuple-element.18.refs_2_, ...), custom_call_target="tpu_custom_call" | custom-call | flops 2684354560 | bytes 8388608 | tf_op jit(solution)/shard_map/pallas_call | solution.py:143
  76.6 18.9 %all_to_all.15.g_ref = bf16[16,256,128]{2,1,0:T(8,128)(2,1)S(1)} all-to-all(bf16[16,256,128]{2,1,0:T(8,128)(2,1)S(1)} %shard_map.84), channel_id=1, replica_groups=mesh['ylo'=2,'core'=2,'zp'=8,'par'=2,'x'=4,'yhi'=2] {'x','yhi','ylo'}, dimensions={0} | all-to-all | bytes 2097152 | tf_op jit(solution)/shard_map/all_to_all | solution.py:162
  95.5 0.1 shard_map.85.mine_ref
  95.7 2.4 %collective-permute-start.4 = (bf16[256,128]{1,0:T(8,128)(2,1)S(1)}, bf16[256,128]{1,0:T(8,128)(2,1)S(1)}, u32[]{:S(2)}, u32[]{:S(2)}) collective-permute-start(bf16[256,128]{1,0:T(8,128)(2,1)S(1)} %shard_map.85.mine_ref), channel_id=1, source_target_pairs={{0,256},{256,0},{1,257},{257,1},{2,258},{258,2},{3,259},{259,3},{4... | collective-permute-start | bytes 196616 | tf_op jit(solution)/shard_map/ppermute | solution.py:101
  98.1 2.6 %collective-permute-done.4.other_ref = bf16[256,128]{1,0:T(8,128)(2,1)S(1)} collective-permute-done((bf16[256,128]{1,0:T(8,128)(2,1)S(1)}, bf16[256,128]{1,0:T(8,128)(2,1)S(1)}, u32[]{:S(2)}, u32[]{:S(2)}) %collective-permute-start.4) | collective-permute-done | bytes 65568 | tf_op jit(solution)/shard_map/ppermute | solution.py:101
  100.7 1.0 shard_map.86
  101.7 5.4 %collective-permute-start.5 = (bf16[16,8,320]{2,1,0:T(8,128)(2,1)S(1)}, bf16[16,8,320]{2,1,0:T(8,128)(2,1)S(1)}, u32[]{:S(2)}, u32[]{:S(2)}) collective-permute-start(bf16[16,8,320]{2,1,0:T(8,128)(2,1)S(1)} %get-tuple-element.26), channel_id=1, source_target_pairs={{0,128},{128,0},{1,129},{129,1},{2,130},{130,2},{3,131},{131,3},{4... | collective-permute-start | bytes 245768 | tf_op jit(solution)/shard_map/ppermute | solution.py:101
  107.0 0.9 collective-permute-done.5.b_ref
  108.0 22.3 %all_to_all.16 = bf16[16,8,320]{2,1,0:T(8,128)(2,1)S(1)} all-to-all(bf16[16,8,320]{2,1,0:T(8,128)(2,1)S(1)} %shard_map.87), channel_id=1, replica_groups=mesh['ylo'=2,'core'=2,'zp'=8,'par'=2,'x'=4,'yhi'=2] {'zp','par'}, dimensions={0} | all-to-all | bytes 163840 | tf_op jit(solution)/shard_map/all_to_all | solution.py:180
  130.3 0.6 convert_reduce_fusion
  (21 shorter events, 0.3 us)
Async XLA Ops:
  0.0 68.2 %copy-start.3 = (s32[256]{0:T(256)S(1)}, s32[256]{0:T(256)}, u32[]{:S(2)}) copy-start(s32[256]{0:T(256)} %constant.54) | copy-start | bytes 3076
  0.0 68.3 %copy-start = (bf16[1280,1024]{1,0:T(8,128)(2,1)S(1)}, bf16[1280,1024]{1,0:T(8,128)(2,1)}, u32[]{:S(2)}) copy-start(bf16[1280,1024]{1,0:T(8,128)(2,1)} %w_ref.3) | copy-start | bytes 7864324
  1.9 46.6 %all-to-all-start = ((bf16[8,32,1024]{2,1,0:T(8,128)(2,1)}), bf16[8,32,1024]{2,1,0:T(8,128)(2,1)}, u32[]{:S(2)}, u32[]{:S(2)}) async-start(bf16[8,32,1024]{2,1,0:T(8,128)(2,1)} %broadcast_in_dim.2), calls=%async_computation | async-start | bytes 1048576 | tf_op jit(solution)/shard_map/all_to_all | solution.py:109
  19.3 17.5 %collective-permute-start = (bf16[64,1408]{1,0:T(8,128)(2,1)S(1)}, bf16[64,1408]{1,0:T(8,128)(2,1)S(1)}, u32[]{:S(2)}, u32[]{:S(2)}) collective-permute-start(bf16[64,1408]{1,0:T(8,128)(2,1)S(1)} %fusion.1), channel_id=1, source_target_pairs={{0,257},{257,0},{1,256},{256,1},{2,259},{259,2},{3,258},{258,3},{4... | collective-permute-start | bytes 540680 | tf_op jit(solution)/shard_map/ppermute | solution.py:114
  48.5 14.3 %collective-permute-start.2 = (bf16[256,1024]{1,0:T(8,128)(2,1)}, bf16[256,1024]{1,0:T(8,128)(2,1)}, u32[]{:S(2)}, u32[]{:S(2)}) collective-permute-start(bf16[256,1024]{1,0:T(8,128)(2,1)} %bitcast.9.refs_10_), channel_id=1, source_target_pairs={{8,0},{16,8},{24,16},{32,24},{40,32},{48,40},{56,48},{64,56},{72,6... | collective-permute-start | bytes 1572872 | tf_op jit(solution)/shard_map/ppermute | solution.py:97
  52.4 17.1 %copy-start.1 = (bf16[256,1408]{1,0:T(8,128)(2,1)S(1)}, bf16[256,1408]{1,0:T(8,128)(2,1)}, u32[]{:S(2)}) copy-start(bf16[256,1408]{1,0:T(8,128)(2,1)} %all_gather.7.x_ref.far_ref) | copy-start | bytes 2162692
  52.5 18.0 %collective-permute-start.1 = (bf16[256,1024]{1,0:T(8,128)(2,1)}, bf16[256,1024]{1,0:T(8,128)(2,1)S(1)}, u32[]{:S(2)}, u32[]{:S(2)}) collective-permute-start(bf16[256,1024]{1,0:T(8,128)(2,1)} %bitcast.9.refs_10_), channel_id=1, source_target_pairs={{0,128},{128,0},{1,129},{129,1},{2,130},{130,2},{3,131},{131,3},{4... | collective-permute-start | bytes 1572872 | tf_op jit(solution)/shard_map/ppermute | solution.py:101
  62.8 7.8 %collective-permute-start.3 = (bf16[256,1024]{1,0:T(8,128)(2,1)}, bf16[256,1024]{1,0:T(8,128)(2,1)S(1)}, u32[]{:S(2)}, u32[]{:S(2)}) collective-permute-start(bf16[256,1024]{1,0:T(8,128)(2,1)} %collective-permute-done.2.refs_12_), channel_id=1, source_target_pairs={{0,128},{128,0},{1,129},{129,1},{2,130},{130,2},{3,131},{131,3},{4... | collective-permute-start | bytes 1572872 | tf_op jit(solution)/shard_map/ppermute | solution.py:101
  68.3 2.2 %copy-start.2 = (bf16[1024,1024]{1,0:T(8,128)(2,1)S(1)}, bf16[1024,1024]{1,0:T(8,128)(2,1)}, u32[]{:S(2)}) copy-start(bf16[1024,1024]{1,0:T(8,128)(2,1)} %constant.50.clone.refs_9_) | copy-start | bytes 6291460
  95.7 5.0 %collective-permute-start.4 = (bf16[256,128]{1,0:T(8,128)(2,1)S(1)}, bf16[256,128]{1,0:T(8,128)(2,1)S(1)}, u32[]{:S(2)}, u32[]{:S(2)}) collective-permute-start(bf16[256,128]{1,0:T(8,128)(2,1)S(1)} %shard_map.85.mine_ref), channel_id=1, source_target_pairs={{0,256},{256,0},{1,257},{257,1},{2,258},{258,2},{3,259},{259,3},{4... | collective-permute-start | bytes 196616 | tf_op jit(solution)/shard_map/ppermute | solution.py:101
  101.7 6.3 %collective-permute-start.5 = (bf16[16,8,320]{2,1,0:T(8,128)(2,1)S(1)}, bf16[16,8,320]{2,1,0:T(8,128)(2,1)S(1)}, u32[]{:S(2)}, u32[]{:S(2)}) collective-permute-start(bf16[16,8,320]{2,1,0:T(8,128)(2,1)S(1)} %get-tuple-element.26), channel_id=1, source_target_pairs={{0,128},{128,0},{1,129},{129,1},{2,130},{130,2},{3,131},{131,3},{4... | collective-permute-start | bytes 245768 | tf_op jit(solution)/shard_map/ppermute | solution.py:101

commit v5 on v4

--- a/solution.py
+++ b/solution.py
@@ -15,7 +15,7 @@
 PLANE = ("x", "yhi", "ylo")
 CHIP = ("ylo", "core")
 PAD = 128
-PARAMS = pltpu.CompilerParams(vmem_limit_bytes=24 * 2**20)
+PARAMS = pltpu.CompilerParams(vmem_limit_bytes=18 * 2**20)
 
 
 def column_order():
@@ -24,22 +24,29 @@
     return jnp.asarray(goes[:, None] == was[None, :], BF)
 
 
-def project_kernel(x_ref, w_ref, unit_ref, unit_b_ref, mag_ref, t_ref):
-    projected = jnp.dot(x_ref[:, : w_ref.shape[0]], w_ref[...], preferred_element_type=F32)
+def project_kernel(place_ref, own_ref, next_ref, across_ref, last_ref, w_ref, x_ref, t_ref, unit_ref, unit_b_ref, mag_ref):
+    e = w_ref.shape[0]
+    x, yhi = place_ref[4], place_ref[0]
+    for k, ref in enumerate((own_ref, next_ref, across_ref, last_ref)):
+        for h in range(2):
+            half = yhi if h == 0 else 1 - yhi
+            at = pl.ds(pl.multiple_of(lax.rem(x + k, 4) * 128 + half * 64, 64), 64)
+            x_ref[at, :] = ref[64 * h : 64 * (h + 1), :e]
+            t_ref[at, :] = ref[64 * h : 64 * (h + 1), e:]
+    projected = jnp.dot(x_ref[...], w_ref[...], preferred_element_type=F32)
     mag = jnp.sqrt(jnp.sum(projected * projected, axis=1, keepdims=True) + 1e-06)
     unit = projected / mag
     unit_ref[...] = unit
     unit_b_ref[...] = unit.astype(BF)
     mag_ref[...] = jnp.broadcast_to(mag, mag_ref.shape)
-    t_ref[...] = x_ref[:, w_ref.shape[0] :]
-
-
-def pair_kernel(scale_ref, place_ref, *refs):
-    video, ids_ref, order_ref, audio_refs, out_ref = refs[:8], refs[8], refs[9], refs[10:14], refs[14]
-    unit, unit_b, mag, x = (jnp.concatenate([a[...], b[...]], axis=0) for a, b in zip(video[:4], video[4:]))
+
+
+def pair_kernel(scale_ref, t_ref, unit_ref, unit_b_ref, mag_ref, ids_ref, order_ref, *refs):
+    *audio_refs, out_ref = refs
     cold = scale_ref[0]
     offset = scale_ref[1]
-    halves = x.astype(F32)
+    unit_b = unit_b_ref[...]
+    halves = t_ref[...].astype(F32)
     targets = [halves[:, 2 * p : 2 * p + 1] * 128.0 + halves[:, 2 * p + 1 : 2 * p + 2] for p in range(5)]
     total = None
     at = 0
@@ -58,13 +65,13 @@
         term = jnp.dot(weight, audio, preferred_element_type=F32)
         total = term if total is None else total + term
     grad = cold * total
+    unit = unit_ref[...]
     inner = jnp.sum(unit * grad, axis=1, keepdims=True)
-    gp = ((grad - unit * inner) / mag[:, :1]).astype(BF)
+    gp = ((grad - unit * inner) / mag_ref[:, :1]).astype(BF)
     gp = jnp.dot(gp, order_ref[...], preferred_element_type=F32).astype(BF)
     for h in range(2):
-        half = place_ref[0] if h == 0 else 1 - place_ref[0]
         for t in range(8):
-            out_ref[2 * t + half] = gp[256 * h : 256 * (h + 1), 128 * t : 128 * (t + 1)]
+            out_ref[2 * t + h] = gp[256 * h : 256 * (h + 1), 128 * t : 128 * (t + 1)]
 
 
 def sum_kernel(g_ref, out_ref):
@@ -74,13 +81,13 @@
     out_ref[...] = total.astype(BF)
 
 
-def weight_kernel(place_ref, mine_ref, other_ref, row_ref, far_ref, keep_ref, give_ref):
-    lanes = pl.ds(pl.multiple_of(place_ref[2] * 640, 128), 640)
-    mine, other = mine_ref[...], other_ref[...]
-    own = place_ref[1] == 1
+def weight_kernel(place_ref, mine_ref, other_ref, x_ref, keep_ref, give_ref):
+    ylo = place_ref[2]
+    lanes = pl.ds(pl.multiple_of(ylo * 640, 128), 640)
     part = None
-    for gp, rows in ((jnp.where(own, mine, other), row_ref[:, lanes]), (jnp.where(own, other, mine), far_ref[:, lanes])):
-        term = lax.dot_general(gp, rows, (((0,), (0,)), ((), ())), preferred_element_type=F32)
+    for gp_ref, half in ((mine_ref, ylo), (other_ref, 1 - ylo)):
+        rows = x_ref[pl.ds(pl.multiple_of(half * 256, 256), 256), lanes]
+        term = lax.dot_general(gp_ref[...], rows, (((0,), (0,)), ((), ())), preferred_element_type=F32)
         part = term if part is None else part + term
     first, second = (part[:, 320 * c : 320 * (c + 1)].reshape(16, 8, 320) for c in range(2))
     core = place_ref[3]
@@ -97,6 +104,18 @@
     return lax.ppermute(a, ("core", "zp", "par"), perm)
 
 
+def after(a, *others):
+    anywhere = pl.BlockSpec(memory_space=pl.ANY)
+    return pl.pallas_call(
+        lambda *refs: None,
+        in_specs=[anywhere] * (1 + len(others)),
+        out_specs=anywhere,
+        out_shape=jax.ShapeDtypeStruct(a.shape, a.dtype),
+        input_output_aliases={0: 0},
+        compiler_params=pltpu.CompilerParams(vmem_limit_bytes=2**16),
+    )(a, *others)
+
+
 def swap(a, axis):
     return lax.ppermute(a, axis, [(0, 1), (1, 0)])
 
@@ -112,44 +131,43 @@
     wide = jnp.concatenate([frames, jnp.pad(halves, ((0, 0), (0, PAD - 10)))], axis=1)
     wide = lax.dynamic_slice_in_dim(wide, core * 64, 64, 0)
     across = lax.ppermute(wide, ("ylo", "yhi"), [(0, 3), (3, 0), (1, 2), (2, 1)])
-    row = lax.all_gather(wide, "x", axis=0, tiled=True)
-    far = lax.all_gather(across, "x", axis=0, tiled=True)
-    same, _, _ = lax.optimization_barrier((same, row, far))
+    wide = jnp.concatenate([wide, across], axis=0)
+    turned = [lax.ppermute(wide, "x", [((i + k) % 4, i) for i in range(4)]) for k in (1, 2, 3)]
+    same = after(same, *turned)
 
     other = fetch(same)
     far_same = swap(same, "core")
-    far_other = swap(other, "core")
-    place = jnp.stack([yhi, 1 - (yhi ^ ylo), ylo, core]).astype(jnp.int32)
+    place = jnp.stack([yhi, yhi, ylo, core, x]).astype(jnp.int32)
     pars = jnp.stack([par, par, 1 - par, 1 - par])
     cores = jnp.stack([core, 1 - core, core, 1 - core])
     firsts = ylo * 8192 + cores * 4096 + pars * 256 + (2 * x + yhi) * 32
     inside = np.arange(8)[:, None] * 512 + np.arange(32)[None, :]
     ids = (firsts[:, None] + jnp.asarray(inside.reshape(1, 256), jnp.int32)).astype(F32).reshape(1, 1024)
 
-    project = pl.pallas_call(
+    rows, *video = pl.pallas_call(
         project_kernel,
-        in_specs=[vmem, vmem],
-        out_specs=[vmem] * 4,
+        in_specs=[smem] + [vmem] * 5,
+        out_specs=[vmem] * 5,
         out_shape=[
-            jax.ShapeDtypeStruct((256, 1024), F32),
-            jax.ShapeDtypeStruct((256, 1024), BF),
-            jax.ShapeDtypeStruct((256, 128), F32),
-            jax.ShapeDtypeStruct((256, PAD), BF),
+            jax.ShapeDtypeStruct((512, 1280), BF),
+            jax.ShapeDtypeStruct((512, PAD), BF),
+            jax.ShapeDtypeStruct((512, 1024), F32),
+            jax.ShapeDtypeStruct((512, 1024), BF),
+            jax.ShapeDtypeStruct((512, 128), F32),
         ],
         compiler_params=PARAMS,
-        cost_estimate=pl.CostEstimate(flops=2 * 256 * 1280 * 1024, bytes_accessed=5 * 2**20, transcendentals=0),
-    )
-    video = [*project(row, projector), *project(far, projector)]
+        cost_estimate=pl.CostEstimate(flops=2 * 512 * 1280 * 1024, bytes_accessed=9 * 2**20, transcendentals=0),
+    )(place, wide, *turned, projector)
+    far_other = swap(other, "core")
     parts = pl.pallas_call(
         pair_kernel,
-        in_specs=[smem, smem] + [vmem] * 14,
+        in_specs=[smem] + [vmem] * 10,
         out_specs=vmem,
         out_shape=jax.ShapeDtypeStruct((16, 256, 128), BF),
         compiler_params=PARAMS,
         cost_estimate=pl.CostEstimate(flops=5 * 512 * 1024 * 1024, bytes_accessed=8 * 2**20, transcendentals=2**20),
     )(
         jnp.concatenate([coldness, offset]),
-        place,
         *video,
         ids,
         column_order(),
@@ -165,11 +183,11 @@
     )(terms)
     keep, give = pl.pallas_call(
         weight_kernel,
-        in_specs=[smem] + [vmem] * 4,
+        in_specs=[smem] + [vmem] * 3,
         out_specs=[vmem, vmem],
         out_shape=[jax.ShapeDtypeStruct((16, 8, 320), F32), jax.ShapeDtypeStruct((16, 8, 320), BF)],
         compiler_params=PARAMS,
-    )(place, mine, swap(mine, "ylo"), row, far)
+    )(place, mine, swap(mine, "ylo"), rows)
     mine = pl.pallas_call(
         add_kernel,
         in_specs=[vmem, vmem],

time: 132 us -> 135 us (1.023)
  waiting for transfers between devices: 3.52 us -> 27.4 us
  blocking collectives: 65.8 us -> 42.1 us
  local copies, waits for them, and re-layouts: 2.04 us -> 3.7 us
  starting transfers between devices: 46.4 us -> 47.9 us
    all_gather x2 -> x0, blocking collectives: 24.5 us -> none  [the longest x1 12.8 us: local(): row = lax.all_gather(wide, 'x', axis=0, tiled=True)]
    ppermute x0 -> x3, waiting for transfers between devices: none -> 16.5 us  [local(): lax.ppermute(wide, 'x', [((i + k) % 4, i) for i in range(4)])]
    ppermute x0 -> x3, starting transfers between devices: none -> 9.33 us  [local(): lax.ppermute(wide, 'x', [((i + k) % 4, i) for i in range(4)])]
    ppermute x4, starting transfers between devices: 23.5 us -> 15.5 us  [swap(): return lax.ppermute(a, axis, [(0, 1), (1, 0)])]
    ppermute x1, waiting for transfers between devices: 0.01 us -> 3.71 us  [fetch(): return lax.ppermute(a, ('core', 'zp', 'par'), perm)]
    ppermute x1, waiting for transfers between devices: 0.01 us -> 3.7 us  [local(): lax.ppermute(wide, ('ylo', 'yhi'), [(0, 3), (3, 0), (1, 2), (2, 1)])]
    unnamed x9 -> x7, local copies, waits for them, and re-layouts: 0.03 us -> 1.76 us
  transfers between devices with their start and end apart: 7 -> 10, of which waited for: 2 -> 7; matrix products, arithmetic and copies ran while one was open for 2% -> 2% of each run, Pallas kernels for 2% -> 2%
where the time goes in v5:
time: 135 us; the launch traced here: 134 us
  starting transfers between devices  47.9 us (35%)
  blocking collectives  42.1 us (31%)
  waiting for transfers between devices  27.4 us (20%)
  Pallas kernels  9 us (7%)
  local copies, waits for them, and re-layouts  3.7 us (3%)
  other arithmetic  2.51 us (2%)
  between operations  1.46 us (1%)
    all_to_all x1, blocking collectives, local(): sums = lax.all_to_all(mine, Z, 0, 0, tiled=True)  22.3 us
    all_to_all x1, blocking collectives, local(): terms = lax.all_to_all(parts, PLANE, 0, 0, tiled=True)  19.8 us
    ppermute x3, waiting for transfers between devices, local(): lax.ppermute(wide, 'x', [((i + k) % 4, i) for i in range(4)])  16.5 us
    all_to_all x1, starting transfers between devices, local(): lax.all_to_all(jnp.broadcast_to(sounds[None], (8, 32, 1024)), 'zp', 0, 0,...  15.8 us
    ppermute x4, starting transfers between devices, swap(): return lax.ppermute(a, axis, [(0, 1), (1, 0)])  15.5 us
    ppermute x3, starting transfers between devices, local(): lax.ppermute(wide, 'x', [((i + k) % 4, i) for i in range(4)])  9.33 us
    pallas_call x1, Pallas kernels, local(): pl.pallas_call(pair_kernel, in_specs=[smem] + [vmem] * 10, out_specs=vmem...  5.46 us
    ppermute x1, starting transfers between devices, local(): lax.ppermute(wide, ('ylo', 'yhi'), [(0, 3), (3, 0), (1, 2), (2, 1)])  4.64 us
  transfers between devices with their start and end apart: 10, of which 7 were waited for; matrix products, arithmetic and copies ran while one was open for 2% of the time, Pallas kernels for 2%

profile of v5, /device:TPU:1, one launch (start us, length us, event | category | flops | bytes accessed | tf_op | source)
XLA Modules:
  0.0 134.0 jit_solution(12277849562027153083)
XLA Ops:
  0.0 1.7 %broadcast_in_dim.2 = bf16[8,32,1024]{2,1,0:T(8,128)(2,1)} broadcast(bf16[32,1024]{1,0:T(8,128)(2,1)} %param.10), dimensions={1,2} | broadcast | bytes 589824 | tf_op jit(solution)/shard_map/broadcast_in_dim | solution.py:128
  1.7 15.8 %all-to-all-start = ((bf16[8,32,1024]{2,1,0:T(8,128)(2,1)}), bf16[8,32,1024]{2,1,0:T(8,128)(2,1)S(1)}, u32[]{:S(2)}, u32[]{:S(2)}) async-start(bf16[8,32,1024]{2,1,0:T(8,128)(2,1)} %broadcast_in_dim.2), calls=%async_computation | async-start | bytes 1048576 | tf_op jit(solution)/shard_map/all_to_all | solution.py:128
  18.3 0.9 fusion.1
  19.3 4.6 %collective-permute-start = (bf16[64,1408]{1,0:T(8,128)(2,1)S(1)}, bf16[64,1408]{1,0:T(8,128)(2,1)S(1)}, u32[]{:S(2)}, u32[]{:S(2)}) collective-permute-start(bf16[64,1408]{1,0:T(8,128)(2,1)S(1)} %fusion.1), channel_id=1, source_target_pairs={{0,257},{257,0},{1,256},{256,1},{2,259},{259,2},{3,258},{258,3},{4... | collective-permute-start | bytes 540680 | tf_op jit(solution)/shard_map/ppermute | solution.py:133
  23.9 3.7 %collective-permute-done = bf16[64,1408]{1,0:T(8,128)(2,1)S(1)} collective-permute-done((bf16[64,1408]{1,0:T(8,128)(2,1)S(1)}, bf16[64,1408]{1,0:T(8,128)(2,1)S(1)}, u32[]{:S(2)}, u32[]{:S(2)}) %collective-permute-start) | collective-permute-done | bytes 180256 | tf_op jit(solution)/shard_map/ppermute | solution.py:133
  27.6 4.4 %collective-permute-start.1 = (bf16[128,1408]{1,0:T(8,128)(2,1)S(1)}, bf16[128,1408]{1,0:T(8,128)(2,1)S(1)}, u32[]{:S(2)}, u32[]{:S(2)}) collective-permute-start(bf16[128,1408]{1,0:T(8,128)(2,1)S(1)} %pad_maximum_fusion.own_ref), channel_id=1, source_target_pairs={{2,0},{4,2},{6,4},{0,6},{3,1},{5,3},{7,5},{1,7},{10,8},{12,10},{14... | collective-permute-start | bytes 1081352 | tf_op jit(solution)/shard_map/ppermute | solution.py:135
  32.0 2.4 %collective-permute-start.2 = (bf16[128,1408]{1,0:T(8,128)(2,1)S(1)}, bf16[128,1408]{1,0:T(8,128)(2,1)S(1)}, u32[]{:S(2)}, u32[]{:S(2)}) collective-permute-start(bf16[128,1408]{1,0:T(8,128)(2,1)S(1)} %pad_maximum_fusion.own_ref), channel_id=1, source_target_pairs={{4,0},{6,2},{0,4},{2,6},{5,1},{7,3},{1,5},{3,7},{12,8},{14,10},{8,... | collective-permute-start | bytes 1081352 | tf_op jit(solution)/shard_map/ppermute | solution.py:135
  34.5 2.5 %collective-permute-start.3 = (bf16[128,1408]{1,0:T(8,128)(2,1)S(1)}, bf16[128,1408]{1,0:T(8,128)(2,1)S(1)}, u32[]{:S(2)}, u32[]{:S(2)}) collective-permute-start(bf16[128,1408]{1,0:T(8,128)(2,1)S(1)} %pad_maximum_fusion.own_ref), channel_id=1, source_target_pairs={{6,0},{0,2},{2,4},{4,6},{7,1},{1,3},{3,5},{5,7},{14,8},{8,10},{10,... | collective-permute-start | bytes 1081352 | tf_op jit(solution)/shard_map/ppermute | solution.py:135
  37.0 1.7 %collective-permute-done.1.next_ref.refs_1_ = bf16[128,1408]{1,0:T(8,128)(2,1)S(1)} collective-permute-done((bf16[128,1408]{1,0:T(8,128)(2,1)S(1)}, bf16[128,1408]{1,0:T(8,128)(2,1)S(1)}, u32[]{:S(2)}, u32[]{:S(2)}) %collective-permute-start.1) | collective-permute-done | bytes 360480 | tf_op jit(solution)/shard_map/ppermute | solution.py:135
  38.7 4.6 %collective-permute-done.2.across_ref.refs_2_ = bf16[128,1408]{1,0:T(8,128)(2,1)S(1)} collective-permute-done((bf16[128,1408]{1,0:T(8,128)(2,1)S(1)}, bf16[128,1408]{1,0:T(8,128)(2,1)S(1)}, u32[]{:S(2)}, u32[]{:S(2)}) %collective-permute-start.2) | collective-permute-done | bytes 360480 | tf_op jit(solution)/shard_map/ppermute | solution.py:135
  43.3 10.2 %collective-permute-done.3.last_ref.refs_3_ = bf16[128,1408]{1,0:T(8,128)(2,1)S(1)} collective-permute-done((bf16[128,1408]{1,0:T(8,128)(2,1)S(1)}, bf16[128,1408]{1,0:T(8,128)(2,1)S(1)}, u32[]{:S(2)}, u32[]{:S(2)}) %collective-permute-start.3) | collective-permute-done | bytes 360480 | tf_op jit(solution)/shard_map/ppermute | solution.py:135
  53.5 2.6 %collective-permute-start.5 = (bf16[256,1024]{1,0:T(8,128)(2,1)S(1)}, bf16[256,1024]{1,0:T(8,128)(2,1)S(1)}, u32[]{:S(2)}, u32[]{:S(2)}) collective-permute-start(bf16[256,1024]{1,0:T(8,128)(2,1)S(1)} %shard_map.83.refs_0_), channel_id=1, source_target_pairs={{8,0},{16,8},{24,16},{32,24},{40,32},{48,40},{56,48},{64,56},{72,6... | collective-permute-start | bytes 1572872 | tf_op jit(solution)/shard_map/ppermute | solution.py:104
  56.2 4.8 %collective-permute-start.4 = (bf16[256,1024]{1,0:T(8,128)(2,1)S(1)}, bf16[256,1024]{1,0:T(8,128)(2,1)S(1)}, u32[]{:S(2)}, u32[]{:S(2)}) collective-permute-start(bf16[256,1024]{1,0:T(8,128)(2,1)S(1)} %shard_map.83.refs_0_), channel_id=1, source_target_pairs={{0,128},{128,0},{1,129},{129,1},{2,130},{130,2},{3,131},{131,3},{4... | collective-permute-start | bytes 1572872 | tf_op jit(solution)/shard_map/ppermute | solution.py:120
  60.9 3.7 %collective-permute-done.5.refs_2_ = bf16[256,1024]{1,0:T(8,128)(2,1)S(1)} collective-permute-done((bf16[256,1024]{1,0:T(8,128)(2,1)S(1)}, bf16[256,1024]{1,0:T(8,128)(2,1)S(1)}, u32[]{:S(2)}, u32[]{:S(2)}) %collective-permute-start.5) | collective-permute-done | bytes 524320 | tf_op jit(solution)/shard_map/ppermute | solution.py:104
  64.7 2.9 %collective-permute-start.6 = (bf16[256,1024]{1,0:T(8,128)(2,1)S(1)}, bf16[256,1024]{1,0:T(8,128)(2,1)S(1)}, u32[]{:S(2)}, u32[]{:S(2)}) collective-permute-start(bf16[256,1024]{1,0:T(8,128)(2,1)S(1)} %collective-permute-done.5.refs_2_), channel_id=1, source_target_pairs={{0,128},{128,0},{1,129},{129,1},{2,130},{130,2},{3,131},{131,3},{4... | collective-permute-start | bytes 1572872 | tf_op jit(solution)/shard_map/ppermute | solution.py:120
  69.2 1.7 %copy-done = bf16[1280,1024]{1,0:T(8,128)(2,1)S(1)} copy-done((bf16[1280,1024]{1,0:T(8,128)(2,1)S(1)}, bf16[1280,1024]{1,0:T(8,128)(2,1)}, u32[]{:S(2)}) %copy-start) | copy-done | bytes 2621464
  71.0 2.4 %shard_map.82 = (bf16[512,1280]{1,0:T(8,128)(2,1)S(1)}, bf16[512,128]{1,0:T(8,128)(2,1)S(1)}, f32[512,1024]{1,0:T(8,128)S(1)}, bf16[512,1024]{1,0:T(8,128)(2,1)S(1)}, f32[512,128]{1,0:T(8,128)S(1)}) custom-call(s32[5]{0:T(128)S(1)} %stack.52.place_ref, bf16[128,1408]{1,0:T(8,128)(2,1)S(1)} %pad_maximum_fusion.own_ref, ...), custom_call_target="tpu_custom_call" | custom-call | flops 1342177280 | bytes 9437184 | tf_op jit(solution)/shard_map/pallas_call | solution.py:147
  73.4 5.5 %shard_map.84 = bf16[16,256,128]{2,1,0:T(8,128)(2,1)S(1)} custom-call(f32[2]{0:T(128)S(1)} %pad_maximum_fusion.2.scale_ref, bf16[512,128]{1,0:T(8,128)(2,1)S(1)} %get-tuple-element.12.t_ref, f32[512,1024]{1,0:T(8,128)S(1)} %get-tuple-element.13.unit_ref, bf16[512,1024]{1,0:T(8,128)(2,1)S(1)} %get-tuple-element.14.unit_b_ref, ...), custom_call_target="tpu_custom_call" | custom-call | flops 2684354560 | bytes 8388608 | tf_op jit(solution)/shard_map/pallas_call | solution.py:162
  78.9 19.8 %all_to_all.15.g_ref = bf16[16,256,128]{2,1,0:T(8,128)(2,1)S(1)} all-to-all(bf16[16,256,128]{2,1,0:T(8,128)(2,1)S(1)} %shard_map.84), channel_id=1, replica_groups=mesh['ylo'=2,'core'=2,'zp'=8,'par'=2,'x'=4,'yhi'=2] {'x','yhi','ylo'}, dimensions={0} | all-to-all | bytes 2097152 | tf_op jit(solution)/shard_map/all_to_all | solution.py:180
  98.8 2.4 %collective-permute-start.7 = (bf16[256,128]{1,0:T(8,128)(2,1)S(1)}, bf16[256,128]{1,0:T(8,128)(2,1)S(1)}, u32[]{:S(2)}, u32[]{:S(2)}) collective-permute-start(bf16[256,128]{1,0:T(8,128)(2,1)S(1)} %shard_map.85.mine_ref), channel_id=1, source_target_pairs={{0,256},{256,0},{1,257},{257,1},{2,258},{258,2},{3,259},{259,3},{4... | collective-permute-start | bytes 196616 | tf_op jit(solution)/shard_map/ppermute | solution.py:120
  101.2 2.6 %collective-permute-done.7.other_ref = bf16[256,128]{1,0:T(8,128)(2,1)S(1)} collective-permute-done((bf16[256,128]{1,0:T(8,128)(2,1)S(1)}, bf16[256,128]{1,0:T(8,128)(2,1)S(1)}, u32[]{:S(2)}, u32[]{:S(2)}) %collective-permute-start.7) | collective-permute-done | bytes 65568 | tf_op jit(solution)/shard_map/ppermute | solution.py:120
  103.8 1.0 shard_map.86
  104.8 5.4 %collective-permute-start.8 = (bf16[16,8,320]{2,1,0:T(8,128)(2,1)S(1)}, bf16[16,8,320]{2,1,0:T(8,128)(2,1)S(1)}, u32[]{:S(2)}, u32[]{:S(2)}) collective-permute-start(bf16[16,8,320]{2,1,0:T(8,128)(2,1)S(1)} %get-tuple-element.18), channel_id=1, source_target_pairs={{0,128},{128,0},{1,129},{129,1},{2,130},{130,2},{3,131},{131,3},{4... | collective-permute-start | bytes 245768 | tf_op jit(solution)/shard_map/ppermute | solution.py:120
  111.1 22.3 %all_to_all.16 = bf16[16,8,320]{2,1,0:T(8,128)(2,1)S(1)} all-to-all(bf16[16,8,320]{2,1,0:T(8,128)(2,1)S(1)} %shard_map.87), channel_id=1, replica_groups=mesh['ylo'=2,'core'=2,'zp'=8,'par'=2,'x'=4,'yhi'=2] {'zp','par'}, dimensions={0} | all-to-all | bytes 163840 | tf_op jit(solution)/shard_map/all_to_all | solution.py:198
  (24 shorter events, 2.9 us)
Async XLA Ops:
  1.7 66.0 %copy-start.2 = (s32[256]{0:T(256)S(1)}, s32[256]{0:T(256)}, u32[]{:S(2)}) copy-start(s32[256]{0:T(256)} %constant.54) | copy-start | bytes 3076
  1.7 51.8 %all-to-all-start = ((bf16[8,32,1024]{2,1,0:T(8,128)(2,1)}), bf16[8,32,1024]{2,1,0:T(8,128)(2,1)S(1)}, u32[]{:S(2)}, u32[]{:S(2)}) async-start(bf16[8,32,1024]{2,1,0:T(8,128)(2,1)} %broadcast_in_dim.2), calls=%async_computation | async-start | bytes 1048576 | tf_op jit(solution)/shard_map/all_to_all | solution.py:128
  19.3 8.4 %collective-permute-start = (bf16[64,1408]{1,0:T(8,128)(2,1)S(1)}, bf16[64,1408]{1,0:T(8,128)(2,1)S(1)}, u32[]{:S(2)}, u32[]{:S(2)}) collective-permute-start(bf16[64,1408]{1,0:T(8,128)(2,1)S(1)} %fusion.1), channel_id=1, source_target_pairs={{0,257},{257,0},{1,256},{256,1},{2,259},{259,2},{3,258},{258,3},{4... | collective-permute-start | bytes 540680 | tf_op jit(solution)/shard_map/ppermute | solution.py:133
  27.6 11.1 %collective-permute-start.1 = (bf16[128,1408]{1,0:T(8,128)(2,1)S(1)}, bf16[128,1408]{1,0:T(8,128)(2,1)S(1)}, u32[]{:S(2)}, u32[]{:S(2)}) collective-permute-start(bf16[128,1408]{1,0:T(8,128)(2,1)S(1)} %pad_maximum_fusion.own_ref), channel_id=1, source_target_pairs={{2,0},{4,2},{6,4},{0,6},{3,1},{5,3},{7,5},{1,7},{10,8},{12,10},{14... | collective-permute-start | bytes 1081352 | tf_op jit(solution)/shard_map/ppermute | solution.py:135
  32.0 11.3 %collective-permute-start.2 = (bf16[128,1408]{1,0:T(8,128)(2,1)S(1)}, bf16[128,1408]{1,0:T(8,128)(2,1)S(1)}, u32[]{:S(2)}, u32[]{:S(2)}) collective-permute-start(bf16[128,1408]{1,0:T(8,128)(2,1)S(1)} %pad_maximum_fusion.own_ref), channel_id=1, source_target_pairs={{4,0},{6,2},{0,4},{2,6},{5,1},{7,3},{1,5},{3,7},{12,8},{14,10},{8,... | collective-permute-start | bytes 1081352 | tf_op jit(solution)/shard_map/ppermute | solution.py:135
  34.5 19.0 %collective-permute-start.3 = (bf16[128,1408]{1,0:T(8,128)(2,1)S(1)}, bf16[128,1408]{1,0:T(8,128)(2,1)S(1)}, u32[]{:S(2)}, u32[]{:S(2)}) collective-permute-start(bf16[128,1408]{1,0:T(8,128)(2,1)S(1)} %pad_maximum_fusion.own_ref), channel_id=1, source_target_pairs={{6,0},{0,2},{2,4},{4,6},{7,1},{1,3},{3,5},{5,7},{14,8},{8,10},{10,... | collective-permute-start | bytes 1081352 | tf_op jit(solution)/shard_map/ppermute | solution.py:135
  53.5 11.2 %collective-permute-start.5 = (bf16[256,1024]{1,0:T(8,128)(2,1)S(1)}, bf16[256,1024]{1,0:T(8,128)(2,1)S(1)}, u32[]{:S(2)}, u32[]{:S(2)}) collective-permute-start(bf16[256,1024]{1,0:T(8,128)(2,1)S(1)} %shard_map.83.refs_0_), channel_id=1, source_target_pairs={{8,0},{16,8},{24,16},{32,24},{40,32},{48,40},{56,48},{64,56},{72,6... | collective-permute-start | bytes 1572872 | tf_op jit(solution)/shard_map/ppermute | solution.py:104
  56.2 17.2 %collective-permute-start.4 = (bf16[256,1024]{1,0:T(8,128)(2,1)S(1)}, bf16[256,1024]{1,0:T(8,128)(2,1)S(1)}, u32[]{:S(2)}, u32[]{:S(2)}) collective-permute-start(bf16[256,1024]{1,0:T(8,128)(2,1)S(1)} %shard_map.83.refs_0_), channel_id=1, source_target_pairs={{0,128},{128,0},{1,129},{129,1},{2,130},{130,2},{3,131},{131,3},{4... | collective-permute-start | bytes 1572872 | tf_op jit(solution)/shard_map/ppermute | solution.py:120
  64.7 8.7 %collective-permute-start.6 = (bf16[256,1024]{1,0:T(8,128)(2,1)S(1)}, bf16[256,1024]{1,0:T(8,128)(2,1)S(1)}, u32[]{:S(2)}, u32[]{:S(2)}) collective-permute-start(bf16[256,1024]{1,0:T(8,128)(2,1)S(1)} %collective-permute-done.5.refs_2_), channel_id=1, source_target_pairs={{0,128},{128,0},{1,129},{129,1},{2,130},{130,2},{3,131},{131,3},{4... | collective-permute-start | bytes 1572872 | tf_op jit(solution)/shard_map/ppermute | solution.py:120
  69.2 1.7 %copy-start = (bf16[1280,1024]{1,0:T(8,128)(2,1)S(1)}, bf16[1280,1024]{1,0:T(8,128)(2,1)}, u32[]{:S(2)}) copy-start(bf16[1280,1024]{1,0:T(8,128)(2,1)} %w_ref.1) | copy-start | bytes 7864324
  71.0 2.4 %copy-start.1 = (bf16[1024,1024]{1,0:T(8,128)(2,1)S(1)}, bf16[1024,1024]{1,0:T(8,128)(2,1)}, u32[]{:S(2)}) copy-start(bf16[1024,1024]{1,0:T(8,128)(2,1)} %constant.50.clone.order_ref) | copy-start | bytes 6291460
  98.8 5.0 %collective-permute-start.7 = (bf16[256,128]{1,0:T(8,128)(2,1)S(1)}, bf16[256,128]{1,0:T(8,128)(2,1)S(1)}, u32[]{:S(2)}, u32[]{:S(2)}) collective-permute-start(bf16[256,128]{1,0:T(8,128)(2,1)S(1)} %shard_map.85.mine_ref), channel_id=1, source_target_pairs={{0,256},{256,0},{1,257},{257,1},{2,258},{258,2},{3,259},{259,3},{4... | collective-permute-start | bytes 196616 | tf_op jit(solution)/shard_map/ppermute | solution.py:120
  104.8 6.3 %collective-permute-start.8 = (bf16[16,8,320]{2,1,0:T(8,128)(2,1)S(1)}, bf16[16,8,320]{2,1,0:T(8,128)(2,1)S(1)}, u32[]{:S(2)}, u32[]{:S(2)}) collective-permute-start(bf16[16,8,320]{2,1,0:T(8,128)(2,1)S(1)} %get-tuple-element.18), channel_id=1, source_target_pairs={{0,128},{128,0},{1,129},{129,1},{2,130},{130,2},{3,131},{131,3},{4... | collective-permute-start | bytes 245768 | tf_op jit(solution)/shard_map/ppermute | solution.py:120

commit v6 on v5

--- a/solution.py
+++ b/solution.py
@@ -1,3 +1,5 @@
+import functools
+
 import jax
 import jax.numpy as jnp
 import numpy as np
@@ -8,10 +10,9 @@
 
 BF = jnp.bfloat16
 F32 = jnp.float32
-AXES = ("ylo", "core", "zp", "par", "x", "yhi")
-SIZES = (2, 2, 8, 2, 4, 2)
-DP = ("zp", "par", "x", "yhi")
-Z = ("zp", "par")
+AXES = ("ylo", "core", "z", "x", "yhi")
+SIZES = (2, 2, 16, 4, 2)
+DP = ("z", "x", "yhi")
 PLANE = ("x", "yhi", "ylo")
 CHIP = ("ylo", "core")
 PAD = 128
@@ -26,7 +27,7 @@
 
 def project_kernel(place_ref, own_ref, next_ref, across_ref, last_ref, w_ref, x_ref, t_ref, unit_ref, unit_b_ref, mag_ref):
     e = w_ref.shape[0]
-    x, yhi = place_ref[4], place_ref[0]
+    x, yhi = place_ref[3], place_ref[0]
     for k, ref in enumerate((own_ref, next_ref, across_ref, last_ref)):
         for h in range(2):
             half = yhi if h == 0 else 1 - yhi
@@ -82,7 +83,7 @@
 
 
 def weight_kernel(place_ref, mine_ref, other_ref, x_ref, keep_ref, give_ref):
-    ylo = place_ref[2]
+    ylo = place_ref[1]
     lanes = pl.ds(pl.multiple_of(ylo * 640, 128), 640)
     part = None
     for gp_ref, half in ((mine_ref, ylo), (other_ref, 1 - ylo)):
@@ -90,7 +91,7 @@
         term = lax.dot_general(gp_ref[...], rows, (((0,), (0,)), ((), ())), preferred_element_type=F32)
         part = term if part is None else part + term
     first, second = (part[:, 320 * c : 320 * (c + 1)].reshape(16, 8, 320) for c in range(2))
-    core = place_ref[3]
+    core = place_ref[2]
     keep_ref[...] = jnp.where(core == 0, first, second)
     give_ref[...] = jnp.where(core == 0, second, first).astype(BF)
 
@@ -99,21 +100,31 @@
     out_ref[...] = (a_ref[...] + b_ref[...].astype(F32)).astype(BF)
 
 
-def fetch(a):
-    perm = [((z + 1) % 16, z) for z in range(16)] + [(16 + (z - 1) % 16, 16 + z) for z in range(16)]
-    return lax.ppermute(a, ("core", "zp", "par"), perm)
-
-
-def after(a, *others):
-    anywhere = pl.BlockSpec(memory_space=pl.ANY)
+def fetch(a, far, axis, n):
+    perm = [((i + far) % n, i) for i in range(n)] + [(n + (i - far) % n, n + i) for i in range(n)]
+    return lax.ppermute(a, ("core", axis), perm)
+
+
+def stack_kernel(*refs, takes):
+    for out_ref, take in zip(refs[-len(takes) :], takes):
+        at = 0
+        for i in take:
+            n = refs[i].shape[0]
+            out_ref[at : at + n] = refs[i][...]
+            at += n
+
+
+def stack(arrays, *takes):
+    vmem = pl.BlockSpec(memory_space=pltpu.VMEM)
     return pl.pallas_call(
-        lambda *refs: None,
-        in_specs=[anywhere] * (1 + len(others)),
-        out_specs=anywhere,
-        out_shape=jax.ShapeDtypeStruct(a.shape, a.dtype),
-        input_output_aliases={0: 0},
-        compiler_params=pltpu.CompilerParams(vmem_limit_bytes=2**16),
-    )(a, *others)
+        functools.partial(stack_kernel, takes=takes),
+        in_specs=[vmem] * len(arrays),
+        out_specs=[vmem] * len(takes),
+        out_shape=[
+            jax.ShapeDtypeStruct((sum(arrays[i].shape[0] for i in take), arrays[0].shape[1]), BF) for take in takes
+        ],
+        compiler_params=pltpu.CompilerParams(vmem_limit_bytes=4 * 2**20),
+    )(*arrays)
 
 
 def swap(a, axis):
@@ -121,28 +132,35 @@
 
 
 def local(frames, projector, sounds, matched, coldness, offset):
-    ylo, core, zp, par, x, yhi = (lax.axis_index(a) for a in AXES)
+    ylo, core, z, x, yhi = (lax.axis_index(a) for a in AXES)
     smem = pl.BlockSpec(memory_space=pltpu.SMEM)
     vmem = pl.BlockSpec(memory_space=pltpu.VMEM)
 
-    same = lax.all_to_all(jnp.broadcast_to(sounds[None], (8, 32, 1024)), "zp", 0, 0, tiled=True).reshape(256, 1024)
+    up6 = fetch(sounds, 6, "z", 16)
+    down6 = fetch(sounds, -6, "z", 16)
+    three, two = stack([sounds, up6, down6], (0, 1, 2), (0, 1))
+    up2 = fetch(three, 2, "z", 16)
+    down2 = fetch(two, -2, "z", 16)
+    (even,) = stack([three, up2, down2], (0, 1, 2))
+    odd = fetch(even, 1, "z", 16)
+    far_even = swap(even, "core")
+    far_odd = swap(odd, "core")
+    sign = 1 - 2 * core
+    evens = jnp.array([0, 6, -6, 2, 8, -4, -2, 4], jnp.int32)
+    steps = jnp.stack([sign * evens, -sign * evens, sign * (evens + 1), -sign * (evens + 1)])
+    cores = jnp.stack([core, 1 - core, core, 1 - core])
+    firsts = ylo * 8192 + cores[:, None] * 4096 + (z + steps) % 16 * 256 + (2 * x + yhi) * 32
+    ids = (firsts[:, :, None] + jnp.arange(32, dtype=jnp.int32)).astype(F32).reshape(1, 1024)
+    place = jnp.stack([yhi, ylo, core, x]).astype(jnp.int32)
 
     halves = jnp.stack([matched >> 7, matched & 127], axis=2).reshape(128, 10).astype(BF)
     wide = jnp.concatenate([frames, jnp.pad(halves, ((0, 0), (0, PAD - 10)))], axis=1)
     wide = lax.dynamic_slice_in_dim(wide, core * 64, 64, 0)
     across = lax.ppermute(wide, ("ylo", "yhi"), [(0, 3), (3, 0), (1, 2), (2, 1)])
     wide = jnp.concatenate([wide, across], axis=0)
-    turned = [lax.ppermute(wide, "x", [((i + k) % 4, i) for i in range(4)]) for k in (1, 2, 3)]
-    same = after(same, *turned)
-
-    other = fetch(same)
-    far_same = swap(same, "core")
-    place = jnp.stack([yhi, yhi, ylo, core, x]).astype(jnp.int32)
-    pars = jnp.stack([par, par, 1 - par, 1 - par])
-    cores = jnp.stack([core, 1 - core, core, 1 - core])
-    firsts = ylo * 8192 + cores * 4096 + pars * 256 + (2 * x + yhi) * 32
-    inside = np.arange(8)[:, None] * 512 + np.arange(32)[None, :]
-    ids = (firsts[:, None] + jnp.asarray(inside.reshape(1, 256), jnp.int32)).astype(F32).reshape(1, 1024)
+    after = lax.ppermute(wide, "x", [((i + 1) % 4, i) for i in range(4)])
+    before = lax.ppermute(wide, "x", [((i - 1) % 4, i) for i in range(4)])
+    opposite = fetch(jnp.where(core == 0, after, before), 1, "x", 4)
 
     rows, *video = pl.pallas_call(
         project_kernel,
@@ -157,8 +175,7 @@
         ],
         compiler_params=PARAMS,
         cost_estimate=pl.CostEstimate(flops=2 * 512 * 1280 * 1024, bytes_accessed=9 * 2**20, transcendentals=0),
-    )(place, wide, *turned, projector)
-    far_other = swap(other, "core")
+    )(place, wide, after, opposite, before, projector)
     parts = pl.pallas_call(
         pair_kernel,
         in_specs=[smem] + [vmem] * 10,
@@ -171,10 +188,10 @@
         *video,
         ids,
         column_order(),
-        same,
-        far_same,
-        other,
-        far_other,
+        even,
+        far_even,
+        odd,
+        far_odd,
     )
 
     terms = lax.all_to_all(parts, PLANE, 0, 0, tiled=True)
@@ -195,7 +212,7 @@
         out_shape=jax.ShapeDtypeStruct((16, 8, 320), BF),
         compiler_params=PARAMS,
     )(keep, swap(give, "core"))
-    sums = lax.all_to_all(mine, Z, 0, 0, tiled=True)
+    sums = lax.all_to_all(mine, "z", 0, 0, tiled=True)
     return jnp.sum(sums.astype(F32), axis=0).T
 
 

time: 135 us -> 131 us (0.970)
  starting transfers between devices: 47.9 us -> 61.4 us
  waiting for transfers between devices: 27.4 us -> 14.1 us
  blocking collectives: 42.1 us -> 35.1 us
  other arithmetic: 2.51 us -> 4.74 us
    ppermute x4 -> x8, starting transfers between devices: 12 us -> 36.2 us  [the longest x6 29.9 us: fetch(): return lax.ppermute(a, ('core', axis), perm)]
    all_to_all x1 -> x0, starting transfers between devices: 15.8 us -> none  [local(): lax.all_to_all(jnp.broadcast_to(sounds[None], (8, 32, 1024)), 'zp', 0, 0,...]
    ppermute x4 -> x8, waiting for transfers between devices: 20.2 us -> 10.4 us  [the longest x6 10.4 us: fetch(): return lax.ppermute(a, ('core', axis), perm)]
    all_to_all x1, blocking collectives: 22.3 us -> 16.9 us  [local(): sums = lax.all_to_all(mine, 'z', 0, 0, tiled=True)]
    ppermute x4, starting transfers between devices: 15.5 us -> 19.7 us  [swap(): return lax.ppermute(a, axis, [(0, 1), (1, 0)])]
    ppermute x1, waiting for transfers between devices: 3.7 us -> 0.01 us  [local(): lax.ppermute(wide, ('ylo', 'yhi'), [(0, 3), (3, 0), (1, 2), (2, 1)])]
    broadcast_in_dim x1 -> x0, local copies, waits for them, and re-layouts: 1.69 us -> none  [local(): jnp.broadcast_to(sounds[None], (8, 32, 1024))]
    all_to_all x1, blocking collectives: 19.8 us -> 18.2 us  [local(): terms = lax.all_to_all(parts, PLANE, 0, 0, tiled=True)]
  transfers between devices with their start and end apart: 10 -> 13, of which waited for: 7 -> 5; matrix products, arithmetic and copies ran while one was open for 2% -> 3% of each run, Pallas kernels for 2% -> 2%
where the time goes in v6:
time: 131 us; the launch traced here: 130 us
  starting transfers between devices  61.4 us (47%)
  blocking collectives  35.1 us (27%)
  waiting for transfers between devices  14.1 us (11%)
  Pallas kernels  9.05 us (7%)
  other arithmetic  4.74 us (4%)
  local copies, waits for them, and re-layouts  3.54 us (3%)
  between operations  1.52 us (1%)
    ppermute x6, starting transfers between devices, fetch(): return lax.ppermute(a, ('core', axis), perm)  29.9 us
    ppermute x4, starting transfers between devices, swap(): return lax.ppermute(a, axis, [(0, 1), (1, 0)])  19.7 us
    all_to_all x1, blocking collectives, local(): terms = lax.all_to_all(parts, PLANE, 0, 0, tiled=True)  18.2 us
    all_to_all x1, blocking collectives, local(): sums = lax.all_to_all(mine, 'z', 0, 0, tiled=True)  16.9 us
    ppermute x6, waiting for transfers between devices, fetch(): return lax.ppermute(a, ('core', axis), perm)  10.4 us
    ppermute x1, starting transfers between devices, local(): lax.ppermute(wide, ('ylo', 'yhi'), [(0, 3), (3, 0), (1, 2), (2, 1)])  5.47 us
    pallas_call x1, Pallas kernels, local(): pl.pallas_call(pair_kernel, in_specs=[smem] + [vmem] * 10, out_specs=vmem...  5.46 us
    ppermute x1, starting transfers between devices, local(): after = lax.ppermute(wide, 'x', [((i + 1) % 4, i) for i in range(4)])  4.39 us
  transfers between devices with their start and end apart: 13, of which 5 were waited for; matrix products, arithmetic and copies ran while one was open for 3% of the time, Pallas kernels for 2%

profile of v6, /device:TPU:1, one launch (start us, length us, event | category | flops | bytes accessed | tf_op | source)
XLA Modules:
  0.0 129.5 jit_solution(16195248026036370916)
XLA Ops:
  0.9 0.9 fusion.1
  1.8 5.5 %collective-permute-start = (bf16[64,1408]{1,0:T(8,128)(2,1)S(1)}, bf16[64,1408]{1,0:T(8,128)(2,1)S(1)}, u32[]{:S(2)}, u32[]{:S(2)}) collective-permute-start(bf16[64,1408]{1,0:T(8,128)(2,1)S(1)} %fusion.1), channel_id=1, source_target_pairs={{0,257},{257,0},{1,256},{256,1},{2,259},{259,2},{3,258},{258,3},{4... | collective-permute-start | bytes 540680 | tf_op jit(solution)/shard_map/ppermute | solution.py:159
  7.3 11.5 %collective-permute-start.4 = (bf16[32,1024]{1,0:T(8,128)(2,1)}, bf16[32,1024]{1,0:T(8,128)(2,1)S(1)}, u32[]{:S(2)}, u32[]{:S(2)}) collective-permute-start(bf16[32,1024]{1,0:T(8,128)(2,1)} %refs_0_.1), channel_id=1, source_target_pairs={{48,0},{56,8},{64,16},{72,24},{80,32},{88,40},{96,48},{104,56},{11... | collective-permute-start | bytes 196616 | tf_op jit(solution)/shard_map/ppermute | solution.py:105
  18.8 5.0 %collective-permute-start.5 = (bf16[32,1024]{1,0:T(8,128)(2,1)}, bf16[32,1024]{1,0:T(8,128)(2,1)S(1)}, u32[]{:S(2)}, u32[]{:S(2)}) collective-permute-start(bf16[32,1024]{1,0:T(8,128)(2,1)} %refs_0_.1), channel_id=1, source_target_pairs={{80,0},{88,8},{96,16},{104,24},{112,32},{120,40},{0,48},{8,56},{16... | collective-permute-start | bytes 196616 | tf_op jit(solution)/shard_map/ppermute | solution.py:105
  23.9 8.3 %collective-permute-done.5.refs_2_ = bf16[32,1024]{1,0:T(8,128)(2,1)S(1)} collective-permute-done((bf16[32,1024]{1,0:T(8,128)(2,1)}, bf16[32,1024]{1,0:T(8,128)(2,1)S(1)}, u32[]{:S(2)}, u32[]{:S(2)}) %collective-permute-start.5) | collective-permute-done | bytes 65568 | tf_op jit(solution)/shard_map/ppermute | solution.py:105
  33.1 7.3 %collective-permute-start.6 = (bf16[96,1024]{1,0:T(8,128)(2,1)S(1)}, bf16[96,1024]{1,0:T(8,128)(2,1)S(1)}, u32[]{:S(2)}, u32[]{:S(2)}) collective-permute-start(bf16[96,1024]{1,0:T(8,128)(2,1)S(1)} %get-tuple-element.18.refs_0_), channel_id=1, source_target_pairs={{16,0},{24,8},{32,16},{40,24},{48,32},{56,40},{64,48},{72,56},{80,... | collective-permute-start | bytes 589832 | tf_op jit(solution)/shard_map/ppermute | solution.py:105
  40.3 1.9 %collective-permute-start.7 = (bf16[64,1024]{1,0:T(8,128)(2,1)S(1)}, bf16[64,1024]{1,0:T(8,128)(2,1)S(1)}, u32[]{:S(2)}, u32[]{:S(2)}) collective-permute-start(bf16[64,1024]{1,0:T(8,128)(2,1)S(1)} %get-tuple-element.19), channel_id=1, source_target_pairs={{112,0},{120,8},{0,16},{8,24},{16,32},{24,40},{32,48},{40,56},{48,... | collective-permute-start | bytes 393224 | tf_op jit(solution)/shard_map/ppermute | solution.py:105
  42.3 4.4 %collective-permute-start.1 = (bf16[128,1408]{1,0:T(8,128)(2,1)S(1)}, bf16[128,1408]{1,0:T(8,128)(2,1)S(1)}, u32[]{:S(2)}, u32[]{:S(2)}) collective-permute-start(bf16[128,1408]{1,0:T(8,128)(2,1)S(1)} %pad_maximum_fusion.own_ref), channel_id=1, source_target_pairs={{2,0},{4,2},{6,4},{0,6},{3,1},{5,3},{7,5},{1,7},{10,8},{12,10},{14... | collective-permute-start | bytes 1081352 | tf_op jit(solution)/shard_map/ppermute | solution.py:161
  46.7 1.9 %collective-permute-start.2 = (bf16[128,1408]{1,0:T(8,128)(2,1)S(1)}, bf16[128,1408]{1,0:T(8,128)(2,1)S(1)}, u32[]{:S(2)}, u32[]{:S(2)}) collective-permute-start(bf16[128,1408]{1,0:T(8,128)(2,1)S(1)} %pad_maximum_fusion.own_ref), channel_id=1, source_target_pairs={{6,0},{0,2},{2,4},{4,6},{7,1},{1,3},{3,5},{5,7},{14,8},{8,10},{10,... | collective-permute-start | bytes 1081352 | tf_op jit(solution)/shard_map/ppermute | solution.py:162
  49.4 1.9 %collective-permute-done.7.refs_2_ = bf16[64,1024]{1,0:T(8,128)(2,1)S(1)} collective-permute-done((bf16[64,1024]{1,0:T(8,128)(2,1)S(1)}, bf16[64,1024]{1,0:T(8,128)(2,1)S(1)}, u32[]{:S(2)}, u32[]{:S(2)}) %collective-permute-start.7) | collective-permute-done | bytes 131104 | tf_op jit(solution)/shard_map/ppermute | solution.py:105
  51.4 1.9 %collective-permute-start.9 = (bf16[256,1024]{1,0:T(8,128)(2,1)S(1)}, bf16[256,1024]{1,0:T(8,128)(2,1)S(1)}, u32[]{:S(2)}, u32[]{:S(2)}) collective-permute-start(bf16[256,1024]{1,0:T(8,128)(2,1)S(1)} %shard_map.84.refs_0_), channel_id=1, source_target_pairs={{8,0},{16,8},{24,16},{32,24},{40,32},{48,40},{56,48},{64,56},{72,6... | collective-permute-start | bytes 1572872 | tf_op jit(solution)/shard_map/ppermute | solution.py:105
  53.4 6.3 %collective-permute-start.8 = (bf16[256,1024]{1,0:T(8,128)(2,1)S(1)}, bf16[256,1024]{1,0:T(8,128)(2,1)S(1)}, u32[]{:S(2)}, u32[]{:S(2)}) collective-permute-start(bf16[256,1024]{1,0:T(8,128)(2,1)S(1)} %shard_map.84.refs_0_), channel_id=1, source_target_pairs={{0,128},{128,0},{1,129},{129,1},{2,130},{130,2},{3,131},{131,3},{4... | collective-permute-start | bytes 1572872 | tf_op jit(solution)/shard_map/ppermute | solution.py:131
  60.5 2.4 %collective-permute-start.3 = (bf16[128,1408]{1,0:T(8,128)(2,1)}, bf16[128,1408]{1,0:T(8,128)(2,1)S(1)}, u32[]{:S(2)}, u32[]{:S(2)}) collective-permute-start(bf16[128,1408]{1,0:T(8,128)(2,1)} %broadcast_select_fusion), channel_id=1, source_target_pairs={{2,0},{4,2},{6,4},{0,6},{134,128},{128,130},{130,132},{132,134},{3... | collective-permute-start | bytes 1081352 | tf_op jit(solution)/shard_map/ppermute | solution.py:105
  62.9 4.7 %collective-permute-start.10 = (bf16[256,1024]{1,0:T(8,128)(2,1)S(1)}, bf16[256,1024]{1,0:T(8,128)(2,1)S(1)}, u32[]{:S(2)}, u32[]{:S(2)}) collective-permute-start(bf16[256,1024]{1,0:T(8,128)(2,1)S(1)} %collective-permute-done.9.refs_2_), channel_id=1, source_target_pairs={{0,128},{128,0},{1,129},{129,1},{2,130},{130,2},{3,131},{131,3},{4... | collective-permute-start | bytes 1572872 | tf_op jit(solution)/shard_map/ppermute | solution.py:131
  70.5 1.7 %copy-done.1 = bf16[1280,1024]{1,0:T(8,128)(2,1)S(1)} copy-done((bf16[1280,1024]{1,0:T(8,128)(2,1)S(1)}, bf16[1280,1024]{1,0:T(8,128)(2,1)}, u32[]{:S(2)}) %copy-start.1) | copy-done | bytes 2621464
  72.2 2.4 %shard_map.82 = (bf16[512,1280]{1,0:T(8,128)(2,1)S(1)}, bf16[512,128]{1,0:T(8,128)(2,1)S(1)}, f32[512,1024]{1,0:T(8,128)S(1)}, bf16[512,1024]{1,0:T(8,128)(2,1)S(1)}, f32[512,128]{1,0:T(8,128)S(1)}) custom-call(s32[4]{0:T(128)S(1)} %pad_add_fusion.place_ref, bf16[128,1408]{1,0:T(8,128)(2,1)S(1)} %pad_maximum_fusion.own_ref, ...), custom_call_target="tpu_custom_call" | custom-call | flops 1342177280 | bytes 9437184 | tf_op jit(solution)/shard_map/pallas_call | solution.py:165
  74.6 5.5 %shard_map.85 = bf16[16,256,128]{2,1,0:T(8,128)(2,1)S(1)} custom-call(f32[2]{0:T(128)S(1)} %pad_maximum_fusion.2.scale_ref, bf16[512,128]{1,0:T(8,128)(2,1)S(1)} %get-tuple-element.14.t_ref, f32[512,1024]{1,0:T(8,128)S(1)} %get-tuple-element.15.unit_ref, bf16[512,1024]{1,0:T(8,128)(2,1)S(1)} %get-tuple-element.16.unit_b_ref, ...), custom_call_target="tpu_custom_call" | custom-call | flops 2684354560 | bytes 8388608 | tf_op jit(solution)/shard_map/pallas_call | solution.py:179
  80.1 18.2 %all_to_all.10.g_ref = bf16[16,256,128]{2,1,0:T(8,128)(2,1)S(1)} all-to-all(bf16[16,256,128]{2,1,0:T(8,128)(2,1)S(1)} %shard_map.85), channel_id=1, replica_groups=mesh['ylo'=2,'core'=2,'z'=16,'x'=4,'yhi'=2] {'x','yhi','ylo'}, dimensions={0} | all-to-all | bytes 2097152 | tf_op jit(solution)/shard_map/all_to_all | solution.py:197
  98.4 2.2 %collective-permute-start.11 = (bf16[256,128]{1,0:T(8,128)(2,1)S(1)}, bf16[256,128]{1,0:T(8,128)(2,1)S(1)}, u32[]{:S(2)}, u32[]{:S(2)}) collective-permute-start(bf16[256,128]{1,0:T(8,128)(2,1)S(1)} %shard_map.86.mine_ref), channel_id=1, source_target_pairs={{0,256},{256,0},{1,257},{257,1},{2,258},{258,2},{3,259},{259,3},{4... | collective-permute-start | bytes 196616 | tf_op jit(solution)/shard_map/ppermute | solution.py:131
  100.6 2.8 %collective-permute-done.11.other_ref = bf16[256,128]{1,0:T(8,128)(2,1)S(1)} collective-permute-done((bf16[256,128]{1,0:T(8,128)(2,1)S(1)}, bf16[256,128]{1,0:T(8,128)(2,1)S(1)}, u32[]{:S(2)}, u32[]{:S(2)}) %collective-permute-start.11) | collective-permute-done | bytes 65568 | tf_op jit(solution)/shard_map/ppermute | solution.py:131
  103.5 1.0 shard_map.87
  104.4 6.5 %collective-permute-start.12 = (bf16[16,8,320]{2,1,0:T(8,128)(2,1)S(1)}, bf16[16,8,320]{2,1,0:T(8,128)(2,1)S(1)}, u32[]{:S(2)}, u32[]{:S(2)}) collective-permute-start(bf16[16,8,320]{2,1,0:T(8,128)(2,1)S(1)} %get-tuple-element.22), channel_id=1, source_target_pairs={{0,128},{128,0},{1,129},{129,1},{2,130},{130,2},{3,131},{131,3},{4... | collective-permute-start | bytes 245768 | tf_op jit(solution)/shard_map/ppermute | solution.py:131
  111.0 0.9 collective-permute-done.12.b_ref
  111.9 16.9 %all_to_all.11 = bf16[16,8,320]{2,1,0:T(8,128)(2,1)S(1)} all-to-all(bf16[16,8,320]{2,1,0:T(8,128)(2,1)S(1)} %shard_map.88), channel_id=1, replica_groups=mesh['ylo'=2,'core'=2,'z'=16,'x'=4,'yhi'=2] {'z'}, dimensions={0} | all-to-all | bytes 163840 | tf_op jit(solution)/shard_map/all_to_all | solution.py:215
  (33 shorter events, 6.0 us)
Async XLA Ops:
  1.8 40.5 %collective-permute-start = (bf16[64,1408]{1,0:T(8,128)(2,1)S(1)}, bf16[64,1408]{1,0:T(8,128)(2,1)S(1)}, u32[]{:S(2)}, u32[]{:S(2)}) collective-permute-start(bf16[64,1408]{1,0:T(8,128)(2,1)S(1)} %fusion.1), channel_id=1, source_target_pairs={{0,257},{257,0},{1,256},{256,1},{2,259},{259,2},{3,258},{258,3},{4... | collective-permute-start | bytes 540680 | tf_op jit(solution)/shard_map/ppermute | solution.py:159
  7.3 16.7 %collective-permute-start.4 = (bf16[32,1024]{1,0:T(8,128)(2,1)}, bf16[32,1024]{1,0:T(8,128)(2,1)S(1)}, u32[]{:S(2)}, u32[]{:S(2)}) collective-permute-start(bf16[32,1024]{1,0:T(8,128)(2,1)} %refs_0_.1), channel_id=1, source_target_pairs={{48,0},{56,8},{64,16},{72,24},{80,32},{88,40},{96,48},{104,56},{11... | collective-permute-start | bytes 196616 | tf_op jit(solution)/shard_map/ppermute | solution.py:105
  18.8 13.4 %collective-permute-start.5 = (bf16[32,1024]{1,0:T(8,128)(2,1)}, bf16[32,1024]{1,0:T(8,128)(2,1)S(1)}, u32[]{:S(2)}, u32[]{:S(2)}) collective-permute-start(bf16[32,1024]{1,0:T(8,128)(2,1)} %refs_0_.1), channel_id=1, source_target_pairs={{80,0},{88,8},{96,16},{104,24},{112,32},{120,40},{0,48},{8,56},{16... | collective-permute-start | bytes 196616 | tf_op jit(solution)/shard_map/ppermute | solution.py:105
  32.2 0.8 copy-start
  33.1 18.3 %collective-permute-start.6 = (bf16[96,1024]{1,0:T(8,128)(2,1)S(1)}, bf16[96,1024]{1,0:T(8,128)(2,1)S(1)}, u32[]{:S(2)}, u32[]{:S(2)}) collective-permute-start(bf16[96,1024]{1,0:T(8,128)(2,1)S(1)} %get-tuple-element.18.refs_0_), channel_id=1, source_target_pairs={{16,0},{24,8},{32,16},{40,24},{48,32},{56,40},{64,48},{72,56},{80,... | collective-permute-start | bytes 589832 | tf_op jit(solution)/shard_map/ppermute | solution.py:105
  40.3 11.0 %collective-permute-start.7 = (bf16[64,1024]{1,0:T(8,128)(2,1)S(1)}, bf16[64,1024]{1,0:T(8,128)(2,1)S(1)}, u32[]{:S(2)}, u32[]{:S(2)}) collective-permute-start(bf16[64,1024]{1,0:T(8,128)(2,1)S(1)} %get-tuple-element.19), channel_id=1, source_target_pairs={{112,0},{120,8},{0,16},{8,24},{16,32},{24,40},{32,48},{40,56},{48,... | collective-permute-start | bytes 393224 | tf_op jit(solution)/shard_map/ppermute | solution.py:105
  42.3 17.3 %collective-permute-start.1 = (bf16[128,1408]{1,0:T(8,128)(2,1)S(1)}, bf16[128,1408]{1,0:T(8,128)(2,1)S(1)}, u32[]{:S(2)}, u32[]{:S(2)}) collective-permute-start(bf16[128,1408]{1,0:T(8,128)(2,1)S(1)} %pad_maximum_fusion.own_ref), channel_id=1, source_target_pairs={{2,0},{4,2},{6,4},{0,6},{3,1},{5,3},{7,5},{1,7},{10,8},{12,10},{14... | collective-permute-start | bytes 1081352 | tf_op jit(solution)/shard_map/ppermute | solution.py:161
  46.7 13.0 %collective-permute-start.2 = (bf16[128,1408]{1,0:T(8,128)(2,1)S(1)}, bf16[128,1408]{1,0:T(8,128)(2,1)S(1)}, u32[]{:S(2)}, u32[]{:S(2)}) collective-permute-start(bf16[128,1408]{1,0:T(8,128)(2,1)S(1)} %pad_maximum_fusion.own_ref), channel_id=1, source_target_pairs={{6,0},{0,2},{2,4},{4,6},{7,1},{1,3},{3,5},{5,7},{14,8},{8,10},{10,... | collective-permute-start | bytes 1081352 | tf_op jit(solution)/shard_map/ppermute | solution.py:162
  51.4 11.5 %collective-permute-start.9 = (bf16[256,1024]{1,0:T(8,128)(2,1)S(1)}, bf16[256,1024]{1,0:T(8,128)(2,1)S(1)}, u32[]{:S(2)}, u32[]{:S(2)}) collective-permute-start(bf16[256,1024]{1,0:T(8,128)(2,1)S(1)} %shard_map.84.refs_0_), channel_id=1, source_target_pairs={{8,0},{16,8},{24,16},{32,24},{40,32},{48,40},{56,48},{64,56},{72,6... | collective-permute-start | bytes 1572872 | tf_op jit(solution)/shard_map/ppermute | solution.py:105
  53.4 21.2 %collective-permute-start.8 = (bf16[256,1024]{1,0:T(8,128)(2,1)S(1)}, bf16[256,1024]{1,0:T(8,128)(2,1)S(1)}, u32[]{:S(2)}, u32[]{:S(2)}) collective-permute-start(bf16[256,1024]{1,0:T(8,128)(2,1)S(1)} %shard_map.84.refs_0_), channel_id=1, source_target_pairs={{0,128},{128,0},{1,129},{129,1},{2,130},{130,2},{3,131},{131,3},{4... | collective-permute-start | bytes 1572872 | tf_op jit(solution)/shard_map/ppermute | solution.py:131
  60.5 10.0 %collective-permute-start.3 = (bf16[128,1408]{1,0:T(8,128)(2,1)}, bf16[128,1408]{1,0:T(8,128)(2,1)S(1)}, u32[]{:S(2)}, u32[]{:S(2)}) collective-permute-start(bf16[128,1408]{1,0:T(8,128)(2,1)} %broadcast_select_fusion), channel_id=1, source_target_pairs={{2,0},{4,2},{6,4},{0,6},{134,128},{128,130},{130,132},{132,134},{3... | collective-permute-start | bytes 1081352 | tf_op jit(solution)/shard_map/ppermute | solution.py:105
  62.9 11.8 %collective-permute-start.10 = (bf16[256,1024]{1,0:T(8,128)(2,1)S(1)}, bf16[256,1024]{1,0:T(8,128)(2,1)S(1)}, u32[]{:S(2)}, u32[]{:S(2)}) collective-permute-start(bf16[256,1024]{1,0:T(8,128)(2,1)S(1)} %collective-permute-done.9.refs_2_), channel_id=1, source_target_pairs={{0,128},{128,0},{1,129},{129,1},{2,130},{130,2},{3,131},{131,3},{4... | collective-permute-start | bytes 1572872 | tf_op jit(solution)/shard_map/ppermute | solution.py:131
  70.5 1.7 %copy-start.1 = (bf16[1280,1024]{1,0:T(8,128)(2,1)S(1)}, bf16[1280,1024]{1,0:T(8,128)(2,1)}, u32[]{:S(2)}) copy-start(bf16[1280,1024]{1,0:T(8,128)(2,1)} %w_ref.1) | copy-start | bytes 7864324
  72.2 2.4 %copy-start.2 = (bf16[1024,1024]{1,0:T(8,128)(2,1)S(1)}, bf16[1024,1024]{1,0:T(8,128)(2,1)}, u32[]{:S(2)}) copy-start(bf16[1024,1024]{1,0:T(8,128)(2,1)} %constant.67.clone.order_ref) | copy-start | bytes 6291460
  98.4 5.0 %collective-permute-start.11 = (bf16[256,128]{1,0:T(8,128)(2,1)S(1)}, bf16[256,128]{1,0:T(8,128)(2,1)S(1)}, u32[]{:S(2)}, u32[]{:S(2)}) collective-permute-start(bf16[256,128]{1,0:T(8,128)(2,1)S(1)} %shard_map.86.mine_ref), channel_id=1, source_target_pairs={{0,256},{256,0},{1,257},{257,1},{2,258},{258,2},{3,259},{259,3},{4... | collective-permute-start | bytes 196616 | tf_op jit(solution)/shard_map/ppermute | solution.py:131
  104.4 7.5 %collective-permute-start.12 = (bf16[16,8,320]{2,1,0:T(8,128)(2,1)S(1)}, bf16[16,8,320]{2,1,0:T(8,128)(2,1)S(1)}, u32[]{:S(2)}, u32[]{:S(2)}) collective-permute-start(bf16[16,8,320]{2,1,0:T(8,128)(2,1)S(1)} %get-tuple-element.22), channel_id=1, source_target_pairs={{0,128},{128,0},{1,129},{129,1},{2,130},{130,2},{3,131},{131,3},{4... | collective-permute-start | bytes 245768 | tf_op jit(solution)/shard_map/ppermute | solution.py:131

commit v7 on v5

--- a/solution.py
+++ b/solution.py
@@ -24,16 +24,27 @@
     return jnp.asarray(goes[:, None] == was[None, :], BF)
 
 
-def project_kernel(place_ref, own_ref, next_ref, across_ref, last_ref, w_ref, x_ref, t_ref, unit_ref, unit_b_ref, mag_ref):
+def project_kernel(place_ref, own_ref, next_ref, across_ref, last_ref, w_ref, x_ref, t_ref, unit_ref, unit_b_ref, mag_ref, held, sems):
     e = w_ref.shape[0]
-    x, yhi = place_ref[4], place_ref[0]
+    step = e // 4
+    copies = []
+    for c in range(4):
+        some = pl.ds(c * step, step)
+        copies.append(pltpu.make_async_copy(w_ref.at[some], held.at[some], sems.at[c]))
+        copies[-1].start()
+    x, yhi = place_ref[3], place_ref[0]
     for k, ref in enumerate((own_ref, next_ref, across_ref, last_ref)):
         for h in range(2):
             half = yhi if h == 0 else 1 - yhi
             at = pl.ds(pl.multiple_of(lax.rem(x + k, 4) * 128 + half * 64, 64), 64)
             x_ref[at, :] = ref[64 * h : 64 * (h + 1), :e]
             t_ref[at, :] = ref[64 * h : 64 * (h + 1), e:]
-    projected = jnp.dot(x_ref[...], w_ref[...], preferred_element_type=F32)
+    projected = None
+    for c, copy in enumerate(copies):
+        copy.wait()
+        some = slice(c * step, (c + 1) * step)
+        term = jnp.dot(x_ref[:, some], held[some], preferred_element_type=F32)
+        projected = term if projected is None else projected + term
     mag = jnp.sqrt(jnp.sum(projected * projected, axis=1, keepdims=True) + 1e-06)
     unit = projected / mag
     unit_ref[...] = unit
@@ -82,7 +93,7 @@
 
 
 def weight_kernel(place_ref, mine_ref, other_ref, x_ref, keep_ref, give_ref):
-    ylo = place_ref[2]
+    ylo = place_ref[1]
     lanes = pl.ds(pl.multiple_of(ylo * 640, 128), 640)
     part = None
     for gp_ref, half in ((mine_ref, ylo), (other_ref, 1 - ylo)):
@@ -90,7 +101,7 @@
         term = lax.dot_general(gp_ref[...], rows, (((0,), (0,)), ((), ())), preferred_element_type=F32)
         part = term if part is None else part + term
     first, second = (part[:, 320 * c : 320 * (c + 1)].reshape(16, 8, 320) for c in range(2))
-    core = place_ref[3]
+    core = place_ref[2]
     keep_ref[...] = jnp.where(core == 0, first, second)
     give_ref[...] = jnp.where(core == 0, second, first).astype(BF)
 
@@ -99,12 +110,12 @@
     out_ref[...] = (a_ref[...] + b_ref[...].astype(F32)).astype(BF)
 
 
-def fetch(a):
-    perm = [((z + 1) % 16, z) for z in range(16)] + [(16 + (z - 1) % 16, 16 + z) for z in range(16)]
-    return lax.ppermute(a, ("core", "zp", "par"), perm)
-
-
-def after(a, *others):
+def fetch(a, axes, n):
+    perm = [((i + 1) % n, i) for i in range(n)] + [(n + (i - 1) % n, n + i) for i in range(n)]
+    return lax.ppermute(a, ("core", *axes), perm)
+
+
+def behind(a, *others):
     anywhere = pl.BlockSpec(memory_space=pl.ANY)
     return pl.pallas_call(
         lambda *refs: None,
@@ -125,28 +136,31 @@
     smem = pl.BlockSpec(memory_space=pltpu.SMEM)
     vmem = pl.BlockSpec(memory_space=pltpu.VMEM)
 
-    same = lax.all_to_all(jnp.broadcast_to(sounds[None], (8, 32, 1024)), "zp", 0, 0, tiled=True).reshape(256, 1024)
+    even = lax.all_to_all(jnp.broadcast_to(sounds[None], (8, 32, 1024)), "zp", 0, 0, tiled=True).reshape(256, 1024)
+    pars = jnp.stack([par, par, 1 - par, 1 - par])
+    cores = jnp.stack([core, 1 - core, core, 1 - core])
+    firsts = ylo * 8192 + cores * 4096 + pars * 256 + (2 * x + yhi) * 32
+    inside = np.arange(8)[:, None] * 512 + np.arange(32)[None, :]
+    ids = (firsts[:, None] + jnp.asarray(inside.reshape(1, 256), jnp.int32)).astype(F32).reshape(1, 1024)
+    place = jnp.stack([yhi, ylo, core, x]).astype(jnp.int32)
 
     halves = jnp.stack([matched >> 7, matched & 127], axis=2).reshape(128, 10).astype(BF)
     wide = jnp.concatenate([frames, jnp.pad(halves, ((0, 0), (0, PAD - 10)))], axis=1)
     wide = lax.dynamic_slice_in_dim(wide, core * 64, 64, 0)
     across = lax.ppermute(wide, ("ylo", "yhi"), [(0, 3), (3, 0), (1, 2), (2, 1)])
     wide = jnp.concatenate([wide, across], axis=0)
-    turned = [lax.ppermute(wide, "x", [((i + k) % 4, i) for i in range(4)]) for k in (1, 2, 3)]
-    same = after(same, *turned)
-
-    other = fetch(same)
-    far_same = swap(same, "core")
-    place = jnp.stack([yhi, yhi, ylo, core, x]).astype(jnp.int32)
-    pars = jnp.stack([par, par, 1 - par, 1 - par])
-    cores = jnp.stack([core, 1 - core, core, 1 - core])
-    firsts = ylo * 8192 + cores * 4096 + pars * 256 + (2 * x + yhi) * 32
-    inside = np.arange(8)[:, None] * 512 + np.arange(32)[None, :]
-    ids = (firsts[:, None] + jnp.asarray(inside.reshape(1, 256), jnp.int32)).astype(F32).reshape(1, 1024)
+    after = lax.ppermute(wide, "x", [((i + 1) % 4, i) for i in range(4)])
+    before = lax.ppermute(wide, "x", [((i - 1) % 4, i) for i in range(4)])
+    opposite = fetch(jnp.where(core == 0, after, before), ("x",), 4)
+
+    even = behind(even, after, before)
+    odd = fetch(even, Z, 16)
+    far_even = swap(even, "core")
+    far_odd = swap(odd, "core")
 
     rows, *video = pl.pallas_call(
         project_kernel,
-        in_specs=[smem] + [vmem] * 5,
+        in_specs=[smem] + [vmem] * 4 + [pl.BlockSpec(memory_space=pltpu.HBM)],
         out_specs=[vmem] * 5,
         out_shape=[
             jax.ShapeDtypeStruct((512, 1280), BF),
@@ -155,10 +169,10 @@
             jax.ShapeDtypeStruct((512, 1024), BF),
             jax.ShapeDtypeStruct((512, 128), F32),
         ],
+        scratch_shapes=[pltpu.VMEM((1280, 1024), BF), pltpu.SemaphoreType.DMA((4,))],
         compiler_params=PARAMS,
         cost_estimate=pl.CostEstimate(flops=2 * 512 * 1280 * 1024, bytes_accessed=9 * 2**20, transcendentals=0),
-    )(place, wide, *turned, projector)
-    far_other = swap(other, "core")
+    )(place, wide, after, opposite, before, pltpu.with_memory_space_constraint(projector, pltpu.HBM))
     parts = pl.pallas_call(
         pair_kernel,
         in_specs=[smem] + [vmem] * 10,
@@ -171,10 +185,10 @@
         *video,
         ids,
         column_order(),
-        same,
-        far_same,
-        other,
-        far_other,
+        even,
+        far_even,
+        odd,
+        far_odd,
     )
 
     terms = lax.all_to_all(parts, PLANE, 0, 0, tiled=True)

time: 135 us -> 127 us (0.941)
  waiting for transfers between devices: 27.4 us -> 16.5 us
  starting transfers between devices: 47.9 us -> 50.4 us
  Pallas kernels: 9 us -> 11.2 us
  local copies, waits for them, and re-layouts: 3.7 us -> 1.87 us
    ppermute x4, waiting for transfers between devices: 20.2 us -> 9.01 us  [the longest x1 5.05 us: local(): before = lax.ppermute(wide, 'x', [((i - 1) % 4, i) for i in range(4)])]
    all_to_all x1, blocking collectives: 22.3 us -> 19.7 us  [local(): sums = lax.all_to_all(mine, Z, 0, 0, tiled=True)]
    all_to_all x1, blocking collectives: 19.8 us -> 22.3 us  [local(): terms = lax.all_to_all(parts, PLANE, 0, 0, tiled=True)]
    pallas_call x2, Pallas kernels: 2.39 us -> 4.73 us  [the longest x1 4.73 us: local(): pl.pallas_call(project_kernel, in_specs=[smem] + [vmem] * 4 + [pl.BlockSp...]
    unnamed x7 -> x5, local copies, waits for them, and re-layouts: 1.76 us -> 0.02 us
    ppermute x4, starting transfers between devices: 15.5 us -> 17.1 us  [swap(): return lax.ppermute(a, axis, [(0, 1), (1, 0)])]
  transfers between devices with their start and end apart: 10 -> 10, of which waited for: 7 -> 6; matrix products, arithmetic and copies ran while one was open for 2% -> 2% of each run, Pallas kernels for 2% -> 4%
where the time goes in v7:
time: 127 us; the launch traced here: 126 us
  starting transfers between devices  50.4 us (40%)
  blocking collectives  41.9 us (33%)
  waiting for transfers between devices  16.5 us (13%)
  Pallas kernels  11.2 us (9%)
  other arithmetic  2.63 us (2%)
  local copies, waits for them, and re-layouts  1.87 us (1%)
  between operations  1.47 us (1%)
    all_to_all x1, blocking collectives, local(): terms = lax.all_to_all(parts, PLANE, 0, 0, tiled=True)  22.3 us
    all_to_all x1, blocking collectives, local(): sums = lax.all_to_all(mine, Z, 0, 0, tiled=True)  19.7 us
    ppermute x4, starting transfers between devices, swap(): return lax.ppermute(a, axis, [(0, 1), (1, 0)])  17.1 us
    all_to_all x1, starting transfers between devices, local(): lax.all_to_all(jnp.broadcast_to(sounds[None], (8, 32, 1024)), 'zp', 0, 0,...  15.6 us
    ppermute x2, starting transfers between devices, fetch(): return lax.ppermute(a, ('core', *axes), perm)  6.7 us
    pallas_call x1, Pallas kernels, local(): pl.pallas_call(pair_kernel, in_specs=[smem] + [vmem] * 10, out_specs=vmem...  5.31 us
    ppermute x1, waiting for transfers between devices, local(): before = lax.ppermute(wide, 'x', [((i - 1) % 4, i) for i in range(4)])  5.05 us
    pallas_call x1, Pallas kernels, local(): pl.pallas_call(project_kernel, in_specs=[smem] + [vmem] * 4 + [pl.BlockSp...  4.73 us
  transfers between devices with their start and end apart: 10, of which 6 were waited for; matrix products, arithmetic and copies ran while one was open for 2% of the time, Pallas kernels for 4%

profile of v7, /device:TPU:1, one launch (start us, length us, event | category | flops | bytes accessed | tf_op | source)
XLA Modules:
  0.0 126.0 jit_solution(17954498913650950455)
XLA Ops:
  0.0 1.7 %broadcast_in_dim.2 = bf16[8,32,1024]{2,1,0:T(8,128)(2,1)} broadcast(bf16[32,1024]{1,0:T(8,128)(2,1)} %param.10), dimensions={1,2} | broadcast | bytes 589824 | tf_op jit(solution)/shard_map/broadcast_in_dim | solution.py:139
  1.7 15.6 %all-to-all-start = ((bf16[8,32,1024]{2,1,0:T(8,128)(2,1)}), bf16[8,32,1024]{2,1,0:T(8,128)(2,1)S(1)}, u32[]{:S(2)}, u32[]{:S(2)}) async-start(bf16[8,32,1024]{2,1,0:T(8,128)(2,1)} %broadcast_in_dim.2), calls=%async_computation | async-start | bytes 1048576 | tf_op jit(solution)/shard_map/all_to_all | solution.py:139
  17.3 0.7 fusion.2
  18.2 0.9 fusion.1
  19.1 4.6 %collective-permute-start = (bf16[64,1408]{1,0:T(8,128)(2,1)S(1)}, bf16[64,1408]{1,0:T(8,128)(2,1)S(1)}, u32[]{:S(2)}, u32[]{:S(2)}) collective-permute-start(bf16[64,1408]{1,0:T(8,128)(2,1)S(1)} %fusion.1), channel_id=1, source_target_pairs={{0,257},{257,0},{1,256},{256,1},{2,259},{259,2},{3,258},{258,3},{4... | collective-permute-start | bytes 540680 | tf_op jit(solution)/shard_map/ppermute | solution.py:150
  23.8 3.7 %collective-permute-done = bf16[64,1408]{1,0:T(8,128)(2,1)S(1)} collective-permute-done((bf16[64,1408]{1,0:T(8,128)(2,1)S(1)}, bf16[64,1408]{1,0:T(8,128)(2,1)S(1)}, u32[]{:S(2)}, u32[]{:S(2)}) %collective-permute-start) | collective-permute-done | bytes 180256 | tf_op jit(solution)/shard_map/ppermute | solution.py:150
  27.5 4.4 %collective-permute-start.1 = (bf16[128,1408]{1,0:T(8,128)(2,1)S(1)}, bf16[128,1408]{1,0:T(8,128)(2,1)S(1)}, u32[]{:S(2)}, u32[]{:S(2)}) collective-permute-start(bf16[128,1408]{1,0:T(8,128)(2,1)S(1)} %pad_maximum_fusion.own_ref), channel_id=1, source_target_pairs={{2,0},{4,2},{6,4},{0,6},{3,1},{5,3},{7,5},{1,7},{10,8},{12,10},{14... | collective-permute-start | bytes 1081352 | tf_op jit(solution)/shard_map/ppermute | solution.py:152
  31.9 1.9 %collective-permute-start.2 = (bf16[128,1408]{1,0:T(8,128)(2,1)S(1)}, bf16[128,1408]{1,0:T(8,128)(2,1)S(1)}, u32[]{:S(2)}, u32[]{:S(2)}) collective-permute-start(bf16[128,1408]{1,0:T(8,128)(2,1)S(1)} %pad_maximum_fusion.own_ref), channel_id=1, source_target_pairs={{6,0},{0,2},{2,4},{4,6},{7,1},{1,3},{3,5},{5,7},{14,8},{8,10},{10,... | collective-permute-start | bytes 1081352 | tf_op jit(solution)/shard_map/ppermute | solution.py:153
  33.9 4.0 %collective-permute-done.1.next_ref.refs_1_ = bf16[128,1408]{1,0:T(8,128)(2,1)S(1)} collective-permute-done((bf16[128,1408]{1,0:T(8,128)(2,1)S(1)}, bf16[128,1408]{1,0:T(8,128)(2,1)S(1)}, u32[]{:S(2)}, u32[]{:S(2)}) %collective-permute-start.1) | collective-permute-done | bytes 360480 | tf_op jit(solution)/shard_map/ppermute | solution.py:152
  37.8 5.0 %collective-permute-done.2.last_ref.refs_2_ = bf16[128,1408]{1,0:T(8,128)(2,1)S(1)} collective-permute-done((bf16[128,1408]{1,0:T(8,128)(2,1)S(1)}, bf16[128,1408]{1,0:T(8,128)(2,1)S(1)}, u32[]{:S(2)}, u32[]{:S(2)}) %collective-permute-start.2) | collective-permute-done | bytes 360480 | tf_op jit(solution)/shard_map/ppermute | solution.py:153
  43.2 3.6 %collective-permute-start.5 = (bf16[256,1024]{1,0:T(8,128)(2,1)S(1)}, bf16[256,1024]{1,0:T(8,128)(2,1)S(1)}, u32[]{:S(2)}, u32[]{:S(2)}) collective-permute-start(bf16[256,1024]{1,0:T(8,128)(2,1)S(1)} %shard_map.83.refs_0_), channel_id=1, source_target_pairs={{8,0},{16,8},{24,16},{32,24},{40,32},{48,40},{56,48},{64,56},{72,6... | collective-permute-start | bytes 1572872 | tf_op jit(solution)/shard_map/ppermute | solution.py:115
  46.9 3.1 %collective-permute-start.3 = (bf16[128,1408]{1,0:T(8,128)(2,1)S(1)}, bf16[128,1408]{1,0:T(8,128)(2,1)S(1)}, u32[]{:S(2)}, u32[]{:S(2)}) collective-permute-start(bf16[128,1408]{1,0:T(8,128)(2,1)S(1)} %broadcast_select_fusion), channel_id=1, source_target_pairs={{2,0},{4,2},{6,4},{0,6},{134,128},{128,130},{130,132},{132,134},{3... | collective-permute-start | bytes 1081352 | tf_op jit(solution)/shard_map/ppermute | solution.py:115
  50.0 7.4 %collective-permute-start.4 = (bf16[256,1024]{1,0:T(8,128)(2,1)S(1)}, bf16[256,1024]{1,0:T(8,128)(2,1)S(1)}, u32[]{:S(2)}, u32[]{:S(2)}) collective-permute-start(bf16[256,1024]{1,0:T(8,128)(2,1)S(1)} %shard_map.83.refs_0_), channel_id=1, source_target_pairs={{0,128},{128,0},{1,129},{129,1},{2,130},{130,2},{3,131},{131,3},{4... | collective-permute-start | bytes 1572872 | tf_op jit(solution)/shard_map/ppermute | solution.py:131
  57.5 2.0 %collective-permute-start.6 = (bf16[256,1024]{1,0:T(8,128)(2,1)S(1)}, bf16[256,1024]{1,0:T(8,128)(2,1)S(1)}, u32[]{:S(2)}, u32[]{:S(2)}) collective-permute-start(bf16[256,1024]{1,0:T(8,128)(2,1)S(1)} %collective-permute-done.5.refs_2_), channel_id=1, source_target_pairs={{0,128},{128,0},{1,129},{129,1},{2,130},{130,2},{3,131},{131,3},{4... | collective-permute-start | bytes 1572872 | tf_op jit(solution)/shard_map/ppermute | solution.py:131
  61.0 4.7 %shard_map.82 = (bf16[512,1280]{1,0:T(8,128)(2,1)S(1)}, bf16[512,128]{1,0:T(8,128)(2,1)S(1)}, f32[512,1024]{1,0:T(8,128)S(1)}, bf16[512,1024]{1,0:T(8,128)(2,1)S(1)}, f32[512,128]{1,0:T(8,128)S(1)}) custom-call(s32[4]{0:T(128)S(1)} %pad_add_fusion.place_ref, bf16[128,1408]{1,0:T(8,128)(2,1)S(1)} %pad_maximum_fusion.own_ref, ...), custom_call_target="tpu_custom_call" | custom-call | flops 1342177280 | bytes 9437184 | tf_op jit(solution)/shard_map/pallas_call | solution.py:161
  65.8 5.3 %shard_map.84 = bf16[16,256,128]{2,1,0:T(8,128)(2,1)S(1)} custom-call(f32[2]{0:T(128)S(1)} %pad_maximum_fusion.2.scale_ref, bf16[512,128]{1,0:T(8,128)(2,1)S(1)} %get-tuple-element.12.t_ref, f32[512,1024]{1,0:T(8,128)S(1)} %get-tuple-element.13.unit_ref, bf16[512,1024]{1,0:T(8,128)(2,1)S(1)} %get-tuple-element.14.unit_b_ref, ...), custom_call_target="tpu_custom_call" | custom-call | flops 2684354560 | bytes 8388608 | tf_op jit(solution)/shard_map/pallas_call | solution.py:176
  71.1 22.3 %all_to_all.15.g_ref = bf16[16,256,128]{2,1,0:T(8,128)(2,1)S(1)} all-to-all(bf16[16,256,128]{2,1,0:T(8,128)(2,1)S(1)} %shard_map.84), channel_id=1, replica_groups=mesh['ylo'=2,'core'=2,'zp'=8,'par'=2,'x'=4,'yhi'=2] {'x','yhi','ylo'}, dimensions={0} | all-to-all | bytes 2097152 | tf_op jit(solution)/shard_map/all_to_all | solution.py:194
  93.5 2.5 %collective-permute-start.7 = (bf16[256,128]{1,0:T(8,128)(2,1)S(1)}, bf16[256,128]{1,0:T(8,128)(2,1)S(1)}, u32[]{:S(2)}, u32[]{:S(2)}) collective-permute-start(bf16[256,128]{1,0:T(8,128)(2,1)S(1)} %shard_map.85.mine_ref), channel_id=1, source_target_pairs={{0,256},{256,0},{1,257},{257,1},{2,258},{258,2},{3,259},{259,3},{4... | collective-permute-start | bytes 196616 | tf_op jit(solution)/shard_map/ppermute | solution.py:131
  96.0 2.5 %collective-permute-done.7.other_ref = bf16[256,128]{1,0:T(8,128)(2,1)S(1)} collective-permute-done((bf16[256,128]{1,0:T(8,128)(2,1)S(1)}, bf16[256,128]{1,0:T(8,128)(2,1)S(1)}, u32[]{:S(2)}, u32[]{:S(2)}) %collective-permute-start.7) | collective-permute-done | bytes 65568 | tf_op jit(solution)/shard_map/ppermute | solution.py:131
  98.5 1.0 shard_map.86
  99.5 5.3 %collective-permute-start.8 = (bf16[16,8,320]{2,1,0:T(8,128)(2,1)S(1)}, bf16[16,8,320]{2,1,0:T(8,128)(2,1)S(1)}, u32[]{:S(2)}, u32[]{:S(2)}) collective-permute-start(bf16[16,8,320]{2,1,0:T(8,128)(2,1)S(1)} %get-tuple-element.18), channel_id=1, source_target_pairs={{0,128},{128,0},{1,129},{129,1},{2,130},{130,2},{3,131},{131,3},{4... | collective-permute-start | bytes 245768 | tf_op jit(solution)/shard_map/ppermute | solution.py:131
  104.8 0.9 collective-permute-done.8.b_ref
  105.7 19.7 %all_to_all.16 = bf16[16,8,320]{2,1,0:T(8,128)(2,1)S(1)} all-to-all(bf16[16,8,320]{2,1,0:T(8,128)(2,1)S(1)} %shard_map.87), channel_id=1, replica_groups=mesh['ylo'=2,'core'=2,'zp'=8,'par'=2,'x'=4,'yhi'=2] {'zp','par'}, dimensions={0} | all-to-all | bytes 163840 | tf_op jit(solution)/shard_map/all_to_all | solution.py:212
  125.4 0.6 convert_reduce_fusion
  (23 shorter events, 1.1 us)
Async XLA Ops:
  1.7 41.5 %all-to-all-start = ((bf16[8,32,1024]{2,1,0:T(8,128)(2,1)}), bf16[8,32,1024]{2,1,0:T(8,128)(2,1)S(1)}, u32[]{:S(2)}, u32[]{:S(2)}) async-start(bf16[8,32,1024]{2,1,0:T(8,128)(2,1)} %broadcast_in_dim.2), calls=%async_computation | async-start | bytes 1048576 | tf_op jit(solution)/shard_map/all_to_all | solution.py:139
  18.1 41.4 %copy-start.1 = (s32[256]{0:T(256)S(1)}, s32[256]{0:T(256)}, u32[]{:S(2)}) copy-start(s32[256]{0:T(256)} %constant.54) | copy-start | bytes 3076
  19.1 8.4 %collective-permute-start = (bf16[64,1408]{1,0:T(8,128)(2,1)S(1)}, bf16[64,1408]{1,0:T(8,128)(2,1)S(1)}, u32[]{:S(2)}, u32[]{:S(2)}) collective-permute-start(bf16[64,1408]{1,0:T(8,128)(2,1)S(1)} %fusion.1), channel_id=1, source_target_pairs={{0,257},{257,0},{1,256},{256,1},{2,259},{259,2},{3,258},{258,3},{4... | collective-permute-start | bytes 540680 | tf_op jit(solution)/shard_map/ppermute | solution.py:150
  27.5 10.3 %collective-permute-start.1 = (bf16[128,1408]{1,0:T(8,128)(2,1)S(1)}, bf16[128,1408]{1,0:T(8,128)(2,1)S(1)}, u32[]{:S(2)}, u32[]{:S(2)}) collective-permute-start(bf16[128,1408]{1,0:T(8,128)(2,1)S(1)} %pad_maximum_fusion.own_ref), channel_id=1, source_target_pairs={{2,0},{4,2},{6,4},{0,6},{3,1},{5,3},{7,5},{1,7},{10,8},{12,10},{14... | collective-permute-start | bytes 1081352 | tf_op jit(solution)/shard_map/ppermute | solution.py:152
  31.9 10.9 %collective-permute-start.2 = (bf16[128,1408]{1,0:T(8,128)(2,1)S(1)}, bf16[128,1408]{1,0:T(8,128)(2,1)S(1)}, u32[]{:S(2)}, u32[]{:S(2)}) collective-permute-start(bf16[128,1408]{1,0:T(8,128)(2,1)S(1)} %pad_maximum_fusion.own_ref), channel_id=1, source_target_pairs={{6,0},{0,2},{2,4},{4,6},{7,1},{1,3},{3,5},{5,7},{14,8},{8,10},{10,... | collective-permute-start | bytes 1081352 | tf_op jit(solution)/shard_map/ppermute | solution.py:153
  43.2 14.3 %collective-permute-start.5 = (bf16[256,1024]{1,0:T(8,128)(2,1)S(1)}, bf16[256,1024]{1,0:T(8,128)(2,1)S(1)}, u32[]{:S(2)}, u32[]{:S(2)}) collective-permute-start(bf16[256,1024]{1,0:T(8,128)(2,1)S(1)} %shard_map.83.refs_0_), channel_id=1, source_target_pairs={{8,0},{16,8},{24,16},{32,24},{40,32},{48,40},{56,48},{64,56},{72,6... | collective-permute-start | bytes 1572872 | tf_op jit(solution)/shard_map/ppermute | solution.py:115
  46.9 14.1 %collective-permute-start.3 = (bf16[128,1408]{1,0:T(8,128)(2,1)S(1)}, bf16[128,1408]{1,0:T(8,128)(2,1)S(1)}, u32[]{:S(2)}, u32[]{:S(2)}) collective-permute-start(bf16[128,1408]{1,0:T(8,128)(2,1)S(1)} %broadcast_select_fusion), channel_id=1, source_target_pairs={{2,0},{4,2},{6,4},{0,6},{134,128},{128,130},{130,132},{132,134},{3... | collective-permute-start | bytes 1081352 | tf_op jit(solution)/shard_map/ppermute | solution.py:115
  50.0 15.7 %collective-permute-start.4 = (bf16[256,1024]{1,0:T(8,128)(2,1)S(1)}, bf16[256,1024]{1,0:T(8,128)(2,1)S(1)}, u32[]{:S(2)}, u32[]{:S(2)}) collective-permute-start(bf16[256,1024]{1,0:T(8,128)(2,1)S(1)} %shard_map.83.refs_0_), channel_id=1, source_target_pairs={{0,128},{128,0},{1,129},{129,1},{2,130},{130,2},{3,131},{131,3},{4... | collective-permute-start | bytes 1572872 | tf_op jit(solution)/shard_map/ppermute | solution.py:131
  57.5 8.3 %collective-permute-start.6 = (bf16[256,1024]{1,0:T(8,128)(2,1)S(1)}, bf16[256,1024]{1,0:T(8,128)(2,1)S(1)}, u32[]{:S(2)}, u32[]{:S(2)}) collective-permute-start(bf16[256,1024]{1,0:T(8,128)(2,1)S(1)} %collective-permute-done.5.refs_2_), channel_id=1, source_target_pairs={{0,128},{128,0},{1,129},{129,1},{2,130},{130,2},{3,131},{131,3},{4... | collective-permute-start | bytes 1572872 | tf_op jit(solution)/shard_map/ppermute | solution.py:131
  61.0 4.8 %copy-start = (bf16[1024,1024]{1,0:T(8,128)(2,1)S(1)}, bf16[1024,1024]{1,0:T(8,128)(2,1)}, u32[]{:S(2)}) copy-start(bf16[1024,1024]{1,0:T(8,128)(2,1)} %constant.50.clone.order_ref) | copy-start | bytes 6291460
  93.5 5.0 %collective-permute-start.7 = (bf16[256,128]{1,0:T(8,128)(2,1)S(1)}, bf16[256,128]{1,0:T(8,128)(2,1)S(1)}, u32[]{:S(2)}, u32[]{:S(2)}) collective-permute-start(bf16[256,128]{1,0:T(8,128)(2,1)S(1)} %shard_map.85.mine_ref), channel_id=1, source_target_pairs={{0,256},{256,0},{1,257},{257,1},{2,258},{258,2},{3,259},{259,3},{4... | collective-permute-start | bytes 196616 | tf_op jit(solution)/shard_map/ppermute | solution.py:131
  99.5 6.2 %collective-permute-start.8 = (bf16[16,8,320]{2,1,0:T(8,128)(2,1)S(1)}, bf16[16,8,320]{2,1,0:T(8,128)(2,1)S(1)}, u32[]{:S(2)}, u32[]{:S(2)}) collective-permute-start(bf16[16,8,320]{2,1,0:T(8,128)(2,1)S(1)} %get-tuple-element.18), channel_id=1, source_target_pairs={{0,128},{128,0},{1,129},{129,1},{2,130},{130,2},{3,131},{131,3},{4... | collective-permute-start | bytes 245768 | tf_op jit(solution)/shard_map/ppermute | solution.py:131

commit v8 on v7

v8 whole, which is shorter than its diff:
```python
import jax
import jax.numpy as jnp
import numpy as np
from jax import lax
from jax.experimental import pallas as pl
from jax.experimental.pallas import tpu as pltpu
from jax.sharding import Mesh, PartitionSpec as P

BF = jnp.bfloat16
F32 = jnp.float32
AXES = ("ylo", "core", "zp", "par", "x", "yhi")
SIZES = (2, 2, 8, 2, 4, 2)
DP = ("zp", "par", "x", "yhi")
Z = ("zp", "par")
PLANE = ("x", "yhi", "ylo")
CHIP = ("ylo", "core")
PAD = 128
PARAMS = pltpu.CompilerParams(vmem_limit_bytes=18 * 2**20)
SMALL = pltpu.CompilerParams(vmem_limit_bytes=12 * 2**20)


def column_order():
    was = np.arange(1024)
    goes = (was // 8 % 8) * 128 + (was // 64) * 8 + was % 8
    return jnp.asarray(goes[:, None] == was[None, :], BF)


def copies_kernel(a_ref, out_ref, sems):
    copies = [pltpu.make_async_copy(a_ref, out_ref.at[i], sems.at[i]) for i in range(out_ref.shape[0])]
    for copy in copies:
        copy.start()
    for copy in copies:
        copy.wait()


def project_kernel(*refs):
    *x_refs, w_ref, unit_ref, unit_b_ref, mag_ref = refs
    x = jnp.concatenate([ref[:, : w_ref.shape[0]] for ref in x_refs], axis=0)
    projected = jnp.dot(x, w_ref[...], preferred_element_type=F32)
    mag = jnp.sqrt(jnp.sum(projected * projected, axis=1, keepdims=True) + 1e-06)
    unit = projected / mag
    unit_ref[...] = unit
    unit_b_ref[...] = unit.astype(BF)
    mag_ref[...] = jnp.broadcast_to(mag, mag_ref.shape)


def project(w, *blocks):
    vmem = pl.BlockSpec(memory_space=pltpu.VMEM)
    n = sum(block.shape[0] for block in blocks)
    return pl.pallas_call(
        project_kernel,
        in_specs=[vmem] * (len(blocks) + 1),
        out_specs=[vmem] * 3,
        out_shape=[
            jax.ShapeDtypeStruct((n, 1024), F32),
            jax.ShapeDtypeStruct((n, 1024), BF),
            jax.ShapeDtypeStruct((n, 128), F32),
        ],
        compiler_params=SMALL,
        cost_estimate=pl.CostEstimate(flops=2 * n * 1280 * 1024, bytes_accessed=4 * 2**20, transcendentals=0),
    )(*blocks, w)


def row_blocks(place_ref):
    x, yhi = place_ref[3], place_ref[0]
    for i, k in enumerate((0, 1, 3, 2)):
        for j in range(2):
            half = yhi if j == 0 else 1 - yhi
            yield 128 * i + 64 * j, lax.rem(x + k, 4) * 128 + half * 64


def pair_kernel(scale_ref, place_ref, *refs):
    x_refs, video, ids_ref, order_ref, audio_refs, out_ref = refs[:4], refs[4:13], refs[13], refs[14], refs[15:19], refs[19]
    unit, unit_b, mag = (jnp.concatenate([ref[...] for ref in video[i::3]], axis=0) for i in range(3))
    cold = scale_ref[0]
    offset = scale_ref[1]
    halves = jnp.concatenate([ref[:, 1280:] for ref in x_refs], axis=0).astype(F32)
    targets = [halves[:, 2 * p : 2 * p + 1] * 128.0 + halves[:, 2 * p + 1 : 2 * p + 2] for p in range(5)]
    total = None
    at = 0
    for audio_ref in audio_refs:
        audio = audio_ref[...]
        n = audio.shape[0]
        ids = ids_ref[:1, at : at + n]
        at += n
        sims = lax.dot_general(unit_b, audio, (((1,), (1,)), ((), ())), preferred_element_type=F32)
        logits = cold * sims + offset
        hit = None
        for target in targets:
            same = target == ids
            hit = same if hit is None else hit | same
        weight = (jax.nn.sigmoid(logits) - jnp.where(hit, 1.0, 0.0)).astype(BF)
        term = jnp.dot(weight, audio, preferred_element_type=F32)
        total = term if total is None else total + term
    grad = cold * total
    inner = jnp.sum(unit * grad, axis=1, keepdims=True)
    gp = ((grad - unit * inner) / mag[:, :1]).astype(BF)
    gp = jnp.dot(gp, order_ref[...], preferred_element_type=F32).astype(BF)
    for at, to in row_blocks(place_ref):
        rows = pl.ds(pl.multiple_of(lax.rem(to, 256), 64), 64)
        for t in range(8):
            out_ref[2 * t + to // 256, rows, :] = gp[at : at + 64, 128 * t : 128 * (t + 1)]


def sum_kernel(g_ref, out_ref):
    total = g_ref[0].astype(F32)
    for s in range(1, g_ref.shape[0]):
        total = total + g_ref[s].astype(F32)
    out_ref[...] = total.astype(BF)


def weight_kernel(place_ref, mine_ref, other_ref, *refs):
    *x_refs, keep_ref, give_ref, gp_ref = refs
    ylo = place_ref[1]
    lanes = pl.ds(pl.multiple_of(ylo * 640, 128), 640)
    for at, to in row_blocks(place_ref):
        rows = pl.ds(pl.multiple_of(lax.rem(to, 256), 64), 64)
        gp_ref[at : at + 64] = jnp.where(to // 256 == ylo, mine_ref[rows, :], other_ref[rows, :])
    part = None
    for i, x_ref in enumerate(x_refs):
        term = lax.dot_general(
            gp_ref[128 * i : 128 * (i + 1)], x_ref[:, lanes], (((0,), (0,)), ((), ())), preferred_element_type=F32
        )
        part = term if part is None else part + term
    first, second = (part[:, 320 * c : 320 * (c + 1)].reshape(16, 8, 320) for c in range(2))
    core = place_ref[2]
    keep_ref[...] = jnp.where(core == 0, first, second)
    give_ref[...] = jnp.where(core == 0, second, first).astype(BF)


def add_kernel(a_ref, b_ref, out_ref):
    out_ref[...] = (a_ref[...] + b_ref[...].astype(F32)).astype(BF)


def fetch(a, axes, n):
    perm = [((i + 1) % n, i) for i in range(n)] + [(n + (i - 1) % n, n + i) for i in range(n)]
    return lax.ppermute(a, ("core", *axes), perm)


def behind(a, *others):
    anywhere = pl.BlockSpec(memory_space=pl.ANY)
    return pl.pallas_call(
        lambda *refs: None,
        in_specs=[anywhere] * (1 + len(others)),
        out_specs=anywhere,
        out_shape=jax.ShapeDtypeStruct(a.shape, a.dtype),
        input_output_aliases={0: 0},
        compiler_params=pltpu.CompilerParams(vmem_limit_bytes=2**16),
    )(a, *others)


def swap(a, axis):
    return lax.ppermute(a, axis, [(0, 1), (1, 0)])


def local(frames, projector, sounds, matched, coldness, offset):
    ylo, core, zp, par, x, yhi = (lax.axis_index(a) for a in AXES)
    smem = pl.BlockSpec(memory_space=pltpu.SMEM)
    vmem = pl.BlockSpec(memory_space=pltpu.VMEM)

    eight = pl.pallas_call(
        copies_kernel,
        in_specs=[pl.BlockSpec(memory_space=pltpu.HBM)],
        out_specs=pl.BlockSpec(memory_space=pltpu.HBM),
        out_shape=jax.ShapeDtypeStruct((8, 32, 1024), BF),
        scratch_shapes=[pltpu.SemaphoreType.DMA((8,))],
        compiler_params=pltpu.CompilerParams(vmem_limit_bytes=2**20),
    )(pltpu.with_memory_space_constraint(sounds, pltpu.HBM))
    even = lax.all_to_all(eight, "zp", 0, 0, tiled=True).reshape(256, 1024)
    pars = jnp.stack([par, par, 1 - par, 1 - par])
    cores = jnp.stack([core, 1 - core, core, 1 - core])
    firsts = ylo * 8192 + cores * 4096 + pars * 256 + (2 * x + yhi) * 32
    inside = np.arange(8)[:, None] * 512 + np.arange(32)[None, :]
    ids = (firsts[:, None] + jnp.asarray(inside.reshape(1, 256), jnp.int32)).astype(F32).reshape(1, 1024)
    place = jnp.stack([yhi, ylo, core, x]).astype(jnp.int32)

    halves = jnp.stack([matched >> 7, matched & 127], axis=2).reshape(128, 10).astype(BF)
    wide = jnp.concatenate([frames, jnp.pad(halves, ((0, 0), (0, PAD - 10)))], axis=1)
    wide = lax.dynamic_slice_in_dim(wide, core * 64, 64, 0)
    across = lax.ppermute(wide, ("ylo", "yhi"), [(0, 3), (3, 0), (1, 2), (2, 1)])
    wide = jnp.concatenate([wide, across], axis=0)
    after = lax.ppermute(wide, "x", [((i + 1) % 4, i) for i in range(4)])
    before = lax.ppermute(wide, "x", [((i - 1) % 4, i) for i in range(4)])
    opposite = fetch(jnp.where(core == 0, after, before), ("x",), 4)

    early = project(projector, wide)
    even = behind(even, after, before, early[2])
    odd = fetch(even, Z, 16)
    far_even = swap(even, "core")
    far_odd = swap(odd, "core")

    video = (wide, after, before, opposite)
    units = [*early, *project(projector, after, before), *project(projector, opposite)]
    parts = pl.pallas_call(
        pair_kernel,
        in_specs=[smem, smem] + [vmem] * 19,
        out_specs=vmem,
        out_shape=jax.ShapeDtypeStruct((16, 256, 128), BF),
        compiler_params=PARAMS,
        cost_estimate=pl.CostEstimate(flops=5 * 512 * 1024 * 1024, bytes_accessed=8 * 2**20, transcendentals=2**20),
    )(
        jnp.concatenate([coldness, offset]),
        place,
        *video,
        *units,
        ids,
        column_order(),
        even,
        far_even,
        odd,
        far_odd,
    )

    terms = lax.all_to_all(parts, PLANE, 0, 0, tiled=True)
    mine = pl.pallas_call(
        sum_kernel, in_specs=[vmem], out_specs=vmem, out_shape=jax.ShapeDtypeStruct((256, 128), BF), compiler_params=SMALL
    )(terms)
    keep, give = pl.pallas_call(
        weight_kernel,
        in_specs=[smem] + [vmem] * 6,
        out_specs=[vmem, vmem],
        out_shape=[jax.ShapeDtypeStruct((16, 8, 320), F32), jax.ShapeDtypeStruct((16, 8, 320), BF)],
        scratch_shapes=[pltpu.VMEM((512, 128), BF)],
        compiler_params=SMALL,
    )(place, mine, swap(mine, "ylo"), *video)
    mine = pl.pallas_call(
        add_kernel,
        in_specs=[vmem, vmem],
        out_specs=vmem,
        out_shape=jax.ShapeDtypeStruct((16, 8, 320), BF),
        compiler_params=SMALL,
    )(keep, swap(give, "core"))
    sums = lax.all_to_all(mine, Z, 0, 0, tiled=True)
    return jnp.sum(sums.astype(F32), axis=0).T


def solution(mesh):
    fine = Mesh(mesh.devices.reshape(SIZES), AXES)
    return jax.shard_map(
        local,
        mesh=fine,
        in_specs=(P(DP, None), P(), P(AXES, None), P(DP, None), P(), P()),
        out_specs=P(CHIP, DP),
        check_vma=False,
    )
```

time: 127 us -> 142 us (1.12)
  Pallas kernels: 11.2 us -> 28.2 us
  waiting for transfers between devices: 16.5 us -> 12.6 us
    pallas_call x3 -> x6, Pallas kernels: 11 us -> 28 us  [the longest x1 17.1 us: local(): pl.pallas_call(copies_kernel, in_specs=[pl.BlockSpec(memory_space=pltpu.H...]
    ppermute x1, waiting for transfers between devices: 5.05 us -> 1.86 us  [local(): before = lax.ppermute(wide, 'x', [((i - 1) % 4, i) for i in range(4)])]
    ppermute x1, waiting for transfers between devices: 3.96 us -> 1.64 us  [local(): after = lax.ppermute(wide, 'x', [((i + 1) % 4, i) for i in range(4)])]
    broadcast_in_dim x1 -> x0, local copies, waits for them, and re-layouts: 1.69 us -> none  [local(): jnp.broadcast_to(sounds[None], (8, 32, 1024))]
    all_to_all x1, waiting for transfers between devices: 0.31 us -> 1.85 us  [local(): even = lax.all_to_all(eight, 'zp', 0, 0, tiled=True).reshape(256, 1024)]
    unnamed x5 -> x15, local copies, waits for them, and re-layouts: 0.02 us -> 1.53 us
  transfers between devices with their start and end apart: 10 -> 10, of which waited for: 6 -> 6; matrix products, arithmetic and copies ran while one was open for 2% -> 2% of each run, Pallas kernels for 4% -> 2%
where the time goes in v8:
time: 142 us; the launch traced here: 141 us
  starting transfers between devices  50.8 us (36%)
  blocking collectives  42.8 us (30%)
  Pallas kernels  28.2 us (20%)
  waiting for transfers between devices  12.6 us (9%)
  other arithmetic  3.38 us (2%)
  local copies, waits for them, and re-layouts  1.69 us (1%)
  between operations  1.54 us (1%)
    all_to_all x1, blocking collectives, local(): terms = lax.all_to_all(parts, PLANE, 0, 0, tiled=True)  22.3 us
    all_to_all x1, blocking collectives, local(): sums = lax.all_to_all(mine, Z, 0, 0, tiled=True)  20.5 us
    ppermute x4, starting transfers between devices, swap(): return lax.ppermute(a, axis, [(0, 1), (1, 0)])  17.4 us
    pallas_call x1, Pallas kernels, local(): pl.pallas_call(copies_kernel, in_specs=[pl.BlockSpec(memory_space=pltpu.H...  17.1 us
    all_to_all x1, starting transfers between devices, local(): even = lax.all_to_all(eight, 'zp', 0, 0, tiled=True).reshape(256, 1024)  15.7 us
    ppermute x2, starting transfers between devices, fetch(): return lax.ppermute(a, ('core', *axes), perm)  6.7 us
    pallas_call x1, Pallas kernels, local(): pl.pallas_call(pair_kernel, in_specs=[smem, smem] + [vmem] * 19, out_spec...  6.12 us
    ppermute x1, starting transfers between devices, local(): lax.ppermute(wide, ('ylo', 'yhi'), [(0, 3), (3, 0), (1, 2), (2, 1)])  4.64 us
  transfers between devices with their start and end apart: 10, of which 6 were waited for; matrix products, arithmetic and copies ran while one was open for 2% of the time, Pallas kernels for 2%

profile of v8, /device:TPU:1, one launch (start us, length us, event | category | flops | bytes accessed | tf_op | source)
XLA Modules:
  0.0 141.0 jit_solution(14269800996161734700)
XLA Ops:
  0.0 17.1 %shard_map.85 = bf16[8,32,1024]{2,1,0:T(8,128)(2,1)} custom-call(bf16[32,1024]{1,0:T(8,128)(2,1)} %a_ref.1), custom_call_target="tpu_custom_call" | custom-call | tf_op jit(solution)/shard_map/pallas_call | solution.py:161
  17.1 15.7 %all-to-all-start = ((bf16[8,32,1024]{2,1,0:T(8,128)(2,1)}), bf16[8,32,1024]{2,1,0:T(8,128)(2,1)}, u32[]{:S(2)}, u32[]{:S(2)}) async-start(bf16[8,32,1024]{2,1,0:T(8,128)(2,1)} %shard_map.85), calls=%async_computation | async-start | bytes 1048576 | tf_op jit(solution)/shard_map/all_to_all | solution.py:169
  33.6 0.9 fusion.1
  34.5 4.6 %collective-permute-start = (bf16[64,1408]{1,0:T(8,128)(2,1)S(1)}, bf16[64,1408]{1,0:T(8,128)(2,1)S(1)}, u32[]{:S(2)}, u32[]{:S(2)}) collective-permute-start(bf16[64,1408]{1,0:T(8,128)(2,1)S(1)} %fusion.1), channel_id=1, source_target_pairs={{0,257},{257,0},{1,256},{256,1},{2,259},{259,2},{3,258},{258,3},{4... | collective-permute-start | bytes 540680 | tf_op jit(solution)/shard_map/ppermute | solution.py:180
  39.2 3.7 %collective-permute-done = bf16[64,1408]{1,0:T(8,128)(2,1)S(1)} collective-permute-done((bf16[64,1408]{1,0:T(8,128)(2,1)S(1)}, bf16[64,1408]{1,0:T(8,128)(2,1)S(1)}, u32[]{:S(2)}, u32[]{:S(2)}) %collective-permute-start) | collective-permute-done | bytes 180256 | tf_op jit(solution)/shard_map/ppermute | solution.py:180
  43.6 3.1 %collective-permute-start.2 = (bf16[128,1408]{1,0:T(8,128)(2,1)}, bf16[128,1408]{1,0:T(8,128)(2,1)S(1)}, u32[]{:S(2)}, u32[]{:S(2)}) collective-permute-start(bf16[128,1408]{1,0:T(8,128)(2,1)} %pad_maximum_fusion.refs_0_), channel_id=1, source_target_pairs={{6,0},{0,2},{2,4},{4,6},{7,1},{1,3},{3,5},{5,7},{14,8},{8,10},{10,... | collective-permute-start | bytes 1081352 | tf_op jit(solution)/shard_map/ppermute | solution.py:183
  46.8 3.4 %collective-permute-start.1 = (bf16[128,1408]{1,0:T(8,128)(2,1)}, bf16[128,1408]{1,0:T(8,128)(2,1)S(1)}, u32[]{:S(2)}, u32[]{:S(2)}) collective-permute-start(bf16[128,1408]{1,0:T(8,128)(2,1)} %pad_maximum_fusion.refs_0_), channel_id=1, source_target_pairs={{2,0},{4,2},{6,4},{0,6},{3,1},{5,3},{7,5},{1,7},{10,8},{12,10},{14... | collective-permute-start | bytes 1081352 | tf_op jit(solution)/shard_map/ppermute | solution.py:182
  50.2 1.6 %shard_map.82 = (f32[128,1024]{1,0:T(8,128)S(1)}, bf16[128,1024]{1,0:T(8,128)(2,1)S(1)}, f32[128,128]{1,0:T(8,128)S(1)}) custom-call(bf16[128,1408]{1,0:T(8,128)(2,1)} %pad_maximum_fusion.refs_0_, bf16[1280,1024]{1,0:T(8,128)(2,1)S(1)} %copy-done), custom_call_target="tpu_custom_call" | custom-call | flops 335544320 | bytes 4194304 | tf_op jit(solution)/shard_map/pallas_call | solution.py:50
  53.3 1.9 %collective-permute-done.2.refs_1_.refs_2_ = bf16[128,1408]{1,0:T(8,128)(2,1)S(1)} collective-permute-done((bf16[128,1408]{1,0:T(8,128)(2,1)}, bf16[128,1408]{1,0:T(8,128)(2,1)S(1)}, u32[]{:S(2)}, u32[]{:S(2)}) %collective-permute-start.2) | collective-permute-done | bytes 360480 | tf_op jit(solution)/shard_map/ppermute | solution.py:183
  55.2 1.6 %collective-permute-done.1.refs_0_.refs_1_ = bf16[128,1408]{1,0:T(8,128)(2,1)S(1)} collective-permute-done((bf16[128,1408]{1,0:T(8,128)(2,1)}, bf16[128,1408]{1,0:T(8,128)(2,1)S(1)}, u32[]{:S(2)}, u32[]{:S(2)}) %collective-permute-start.1) | collective-permute-done | bytes 360480 | tf_op jit(solution)/shard_map/ppermute | solution.py:182
  56.8 1.8 %all-to-all-done = bf16[8,32,1024]{2,1,0:T(8,128)(2,1)} async-done(((bf16[8,32,1024]{2,1,0:T(8,128)(2,1)}), bf16[8,32,1024]{2,1,0:T(8,128)(2,1)}, u32[]{:S(2)}, u32[]{:S(2)}) %all-to-all-start) | async-done | bytes 524320 | tf_op jit(solution)/shard_map/all_to_all | solution.py:169
  58.7 3.6 %collective-permute-start.5 = (bf16[256,1024]{1,0:T(8,128)(2,1)}, bf16[256,1024]{1,0:T(8,128)(2,1)}, u32[]{:S(2)}, u32[]{:S(2)}) collective-permute-start(bf16[256,1024]{1,0:T(8,128)(2,1)} %shard_map.86.refs_15_), channel_id=1, source_target_pairs={{8,0},{16,8},{24,16},{32,24},{40,32},{48,40},{56,48},{64,56},{72,6... | collective-permute-start | bytes 1572872 | tf_op jit(solution)/shard_map/ppermute | solution.py:137
  62.4 3.1 %collective-permute-start.3 = (bf16[128,1408]{1,0:T(8,128)(2,1)S(1)}, bf16[128,1408]{1,0:T(8,128)(2,1)S(1)}, u32[]{:S(2)}, u32[]{:S(2)}) collective-permute-start(bf16[128,1408]{1,0:T(8,128)(2,1)S(1)} %broadcast_select_fusion), channel_id=1, source_target_pairs={{2,0},{4,2},{6,4},{0,6},{134,128},{128,130},{130,132},{132,134},{3... | collective-permute-start | bytes 1081352 | tf_op jit(solution)/shard_map/ppermute | solution.py:137
  65.5 7.4 %collective-permute-start.4 = (bf16[256,1024]{1,0:T(8,128)(2,1)}, bf16[256,1024]{1,0:T(8,128)(2,1)S(1)}, u32[]{:S(2)}, u32[]{:S(2)}) collective-permute-start(bf16[256,1024]{1,0:T(8,128)(2,1)} %shard_map.86.refs_15_), channel_id=1, source_target_pairs={{0,128},{128,0},{1,129},{129,1},{2,130},{130,2},{3,131},{131,3},{4... | collective-permute-start | bytes 1572872 | tf_op jit(solution)/shard_map/ppermute | solution.py:153
  73.0 2.2 %collective-permute-start.6 = (bf16[256,1024]{1,0:T(8,128)(2,1)}, bf16[256,1024]{1,0:T(8,128)(2,1)S(1)}, u32[]{:S(2)}, u32[]{:S(2)}) collective-permute-start(bf16[256,1024]{1,0:T(8,128)(2,1)} %collective-permute-done.5.refs_17_), channel_id=1, source_target_pairs={{0,128},{128,0},{1,129},{129,1},{2,130},{130,2},{3,131},{131,3},{4... | collective-permute-start | bytes 1572872 | tf_op jit(solution)/shard_map/ppermute | solution.py:153
  76.7 1.0 shard_map.83
  78.4 6.1 %shard_map.87 = bf16[16,256,128]{2,1,0:T(8,128)(2,1)S(1)} custom-call(f32[2]{0:T(128)S(1)} %pad_maximum_fusion.2.scale_ref, s32[4]{0:T(128)S(1)} %pad_add_fusion.place_ref, bf16[128,1408]{1,0:T(8,128)(2,1)} %pad_maximum_fusion.refs_0_, bf16[128,1408]{1,0:T(8,128)(2,1)S(1)} %collective-permute-done.1.refs_0_.refs_1_, ...), custom_call_target="tpu_custom_call" | custom-call | flops 2684354560 | bytes 8388608 | tf_op jit(solution)/shard_map/pallas_call | solution.py:194
  84.5 22.3 %all_to_all.15.g_ref = bf16[16,256,128]{2,1,0:T(8,128)(2,1)S(1)} all-to-all(bf16[16,256,128]{2,1,0:T(8,128)(2,1)S(1)} %shard_map.87), channel_id=1, replica_groups=mesh['ylo'=2,'core'=2,'zp'=8,'par'=2,'x'=4,'yhi'=2] {'x','yhi','ylo'}, dimensions={0} | all-to-all | bytes 2097152 | tf_op jit(solution)/shard_map/all_to_all | solution.py:214
  107.0 2.4 %collective-permute-start.7 = (bf16[256,128]{1,0:T(8,128)(2,1)S(1)}, bf16[256,128]{1,0:T(8,128)(2,1)S(1)}, u32[]{:S(2)}, u32[]{:S(2)}) collective-permute-start(bf16[256,128]{1,0:T(8,128)(2,1)S(1)} %shard_map.88.mine_ref), channel_id=1, source_target_pairs={{0,256},{256,0},{1,257},{257,1},{2,258},{258,2},{3,259},{259,3},{4... | collective-permute-start | bytes 196616 | tf_op jit(solution)/shard_map/ppermute | solution.py:153
  109.4 2.6 %collective-permute-done.7.other_ref = bf16[256,128]{1,0:T(8,128)(2,1)S(1)} collective-permute-done((bf16[256,128]{1,0:T(8,128)(2,1)S(1)}, bf16[256,128]{1,0:T(8,128)(2,1)S(1)}, u32[]{:S(2)}, u32[]{:S(2)}) %collective-permute-start.7) | collective-permute-done | bytes 65568 | tf_op jit(solution)/shard_map/ppermute | solution.py:153
  112.0 1.6 %shard_map.89 = (f32[16,8,320]{2,1,0:T(8,128)S(1)}, bf16[16,8,320]{2,1,0:T(8,128)(2,1)S(1)}) custom-call(s32[4]{0:T(128)S(1)} %pad_add_fusion.place_ref, bf16[256,128]{1,0:T(8,128)(2,1)S(1)} %shard_map.88.mine_ref, bf16[256,128]{1,0:T(8,128)(2,1)S(1)} %collective-permute-done.7.other_ref, bf16[128,1408]{1,0:T(8,128)(2,1)} %pad_maximum_fusion.refs_0_, ...), custom_call_target="tpu_custom_call" | custom-call | tf_op jit(solution)/shard_map/pallas_call | solution.py:218
  113.6 5.4 %collective-permute-start.8 = (bf16[16,8,320]{2,1,0:T(8,128)(2,1)S(1)}, bf16[16,8,320]{2,1,0:T(8,128)(2,1)S(1)}, u32[]{:S(2)}, u32[]{:S(2)}) collective-permute-start(bf16[16,8,320]{2,1,0:T(8,128)(2,1)S(1)} %get-tuple-element.26), channel_id=1, source_target_pairs={{0,128},{128,0},{1,129},{129,1},{2,130},{130,2},{3,131},{131,3},{4... | collective-permute-start | bytes 245768 | tf_op jit(solution)/shard_map/ppermute | solution.py:153
  118.9 0.9 collective-permute-done.8.b_ref
  119.9 20.5 %all_to_all.16 = bf16[16,8,320]{2,1,0:T(8,128)(2,1)S(1)} all-to-all(bf16[16,8,320]{2,1,0:T(8,128)(2,1)S(1)} %shard_map.90), channel_id=1, replica_groups=mesh['ylo'=2,'core'=2,'zp'=8,'par'=2,'x'=4,'yhi'=2] {'zp','par'}, dimensions={0} | all-to-all | bytes 163840 | tf_op jit(solution)/shard_map/all_to_all | solution.py:233
  (35 shorter events, 5.0 us)
Async XLA Ops:
  0.0 50.2 %copy-start = (bf16[1280,1024]{1,0:T(8,128)(2,1)S(1)}, bf16[1280,1024]{1,0:T(8,128)(2,1)}, u32[]{:S(2)}) copy-start(bf16[1280,1024]{1,0:T(8,128)(2,1)} %refs_1_.3) | copy-start | bytes 7864324
  17.1 41.6 %all-to-all-start = ((bf16[8,32,1024]{2,1,0:T(8,128)(2,1)}), bf16[8,32,1024]{2,1,0:T(8,128)(2,1)}, u32[]{:S(2)}, u32[]{:S(2)}) async-start(bf16[8,32,1024]{2,1,0:T(8,128)(2,1)} %shard_map.85), calls=%async_computation | async-start | bytes 1048576 | tf_op jit(solution)/shard_map/all_to_all | solution.py:169
  34.5 8.4 %collective-permute-start = (bf16[64,1408]{1,0:T(8,128)(2,1)S(1)}, bf16[64,1408]{1,0:T(8,128)(2,1)S(1)}, u32[]{:S(2)}, u32[]{:S(2)}) collective-permute-start(bf16[64,1408]{1,0:T(8,128)(2,1)S(1)} %fusion.1), channel_id=1, source_target_pairs={{0,257},{257,0},{1,256},{256,1},{2,259},{259,2},{3,258},{258,3},{4... | collective-permute-start | bytes 540680 | tf_op jit(solution)/shard_map/ppermute | solution.py:180
  43.6 11.5 %collective-permute-start.2 = (bf16[128,1408]{1,0:T(8,128)(2,1)}, bf16[128,1408]{1,0:T(8,128)(2,1)S(1)}, u32[]{:S(2)}, u32[]{:S(2)}) collective-permute-start(bf16[128,1408]{1,0:T(8,128)(2,1)} %pad_maximum_fusion.refs_0_), channel_id=1, source_target_pairs={{6,0},{0,2},{2,4},{4,6},{7,1},{1,3},{3,5},{5,7},{14,8},{8,10},{10,... | collective-permute-start | bytes 1081352 | tf_op jit(solution)/shard_map/ppermute | solution.py:183
  46.8 10.0 %collective-permute-start.1 = (bf16[128,1408]{1,0:T(8,128)(2,1)}, bf16[128,1408]{1,0:T(8,128)(2,1)S(1)}, u32[]{:S(2)}, u32[]{:S(2)}) collective-permute-start(bf16[128,1408]{1,0:T(8,128)(2,1)} %pad_maximum_fusion.refs_0_), channel_id=1, source_target_pairs={{2,0},{4,2},{6,4},{0,6},{3,1},{5,3},{7,5},{1,7},{10,8},{12,10},{14... | collective-permute-start | bytes 1081352 | tf_op jit(solution)/shard_map/ppermute | solution.py:182
  50.2 25.0 %copy-start.6 = (s32[256]{0:T(256)S(1)}, s32[256]{0:T(256)}, u32[]{:S(2)}) copy-start(s32[256]{0:T(256)} %constant.54) | copy-start | bytes 3076
  51.8 0.8 copy-start.2
  52.6 0.7 copy-start.4
  58.7 14.3 %collective-permute-start.5 = (bf16[256,1024]{1,0:T(8,128)(2,1)}, bf16[256,1024]{1,0:T(8,128)(2,1)}, u32[]{:S(2)}, u32[]{:S(2)}) collective-permute-start(bf16[256,1024]{1,0:T(8,128)(2,1)} %shard_map.86.refs_15_), channel_id=1, source_target_pairs={{8,0},{16,8},{24,16},{32,24},{40,32},{48,40},{56,48},{64,56},{72,6... | collective-permute-start | bytes 1572872 | tf_op jit(solution)/shard_map/ppermute | solution.py:137
  62.4 15.3 %collective-permute-start.3 = (bf16[128,1408]{1,0:T(8,128)(2,1)S(1)}, bf16[128,1408]{1,0:T(8,128)(2,1)S(1)}, u32[]{:S(2)}, u32[]{:S(2)}) collective-permute-start(bf16[128,1408]{1,0:T(8,128)(2,1)S(1)} %broadcast_select_fusion), channel_id=1, source_target_pairs={{2,0},{4,2},{6,4},{0,6},{134,128},{128,130},{130,132},{132,134},{3... | collective-permute-start | bytes 1081352 | tf_op jit(solution)/shard_map/ppermute | solution.py:137
  65.5 12.9 %collective-permute-start.4 = (bf16[256,1024]{1,0:T(8,128)(2,1)}, bf16[256,1024]{1,0:T(8,128)(2,1)S(1)}, u32[]{:S(2)}, u32[]{:S(2)}) collective-permute-start(bf16[256,1024]{1,0:T(8,128)(2,1)} %shard_map.86.refs_15_), channel_id=1, source_target_pairs={{0,128},{128,0},{1,129},{129,1},{2,130},{130,2},{3,131},{131,3},{4... | collective-permute-start | bytes 1572872 | tf_op jit(solution)/shard_map/ppermute | solution.py:153
  73.0 5.4 %collective-permute-start.6 = (bf16[256,1024]{1,0:T(8,128)(2,1)}, bf16[256,1024]{1,0:T(8,128)(2,1)S(1)}, u32[]{:S(2)}, u32[]{:S(2)}) collective-permute-start(bf16[256,1024]{1,0:T(8,128)(2,1)} %collective-permute-done.5.refs_17_), channel_id=1, source_target_pairs={{0,128},{128,0},{1,129},{129,1},{2,130},{130,2},{3,131},{131,3},{4... | collective-permute-start | bytes 1572872 | tf_op jit(solution)/shard_map/ppermute | solution.py:153
  76.7 1.7 %copy-start.1 = (bf16[1024,1024]{1,0:T(8,128)(2,1)S(1)}, bf16[1024,1024]{1,0:T(8,128)(2,1)}, u32[]{:S(2)}) copy-start(bf16[1024,1024]{1,0:T(8,128)(2,1)} %constant.50.clone.refs_14_) | copy-start | bytes 6291460
  76.7 1.7 %copy-start.3 = (f32[128,1024]{1,0:T(8,128)S(1)}, f32[128,1024]{1,0:T(8,128)}, u32[]{:S(2)}) copy-start(f32[128,1024]{1,0:T(8,128)} %copy-done.2) | copy-start | bytes 1572868
  76.7 1.7 %copy-start.5 = (bf16[128,1024]{1,0:T(8,128)(2,1)S(1)}, bf16[128,1024]{1,0:T(8,128)(2,1)}, u32[]{:S(2)}) copy-start(bf16[128,1024]{1,0:T(8,128)(2,1)} %copy-done.4) | copy-start | bytes 786436
  107.0 5.0 %collective-permute-start.7 = (bf16[256,128]{1,0:T(8,128)(2,1)S(1)}, bf16[256,128]{1,0:T(8,128)(2,1)S(1)}, u32[]{:S(2)}, u32[]{:S(2)}) collective-permute-start(bf16[256,128]{1,0:T(8,128)(2,1)S(1)} %shard_map.88.mine_ref), channel_id=1, source_target_pairs={{0,256},{256,0},{1,257},{257,1},{2,258},{258,2},{3,259},{259,3},{4... | collective-permute-start | bytes 196616 | tf_op jit(solution)/shard_map/ppermute | solution.py:153
  113.6 6.3 %collective-permute-start.8 = (bf16[16,8,320]{2,1,0:T(8,128)(2,1)S(1)}, bf16[16,8,320]{2,1,0:T(8,128)(2,1)S(1)}, u32[]{:S(2)}, u32[]{:S(2)}) collective-permute-start(bf16[16,8,320]{2,1,0:T(8,128)(2,1)S(1)} %get-tuple-element.26), channel_id=1, source_target_pairs={{0,128},{128,0},{1,129},{129,1},{2,130},{130,2},{3,131},{131,3},{4... | collective-permute-start | bytes 245768 | tf_op jit(solution)/shard_map/ppermute | solution.py:153

commit v9 on v8

--- a/solution.py
+++ b/solution.py
@@ -23,14 +23,6 @@
     was = np.arange(1024)
     goes = (was // 8 % 8) * 128 + (was // 64) * 8 + was % 8
     return jnp.asarray(goes[:, None] == was[None, :], BF)
-
-
-def copies_kernel(a_ref, out_ref, sems):
-    copies = [pltpu.make_async_copy(a_ref, out_ref.at[i], sems.at[i]) for i in range(out_ref.shape[0])]
-    for copy in copies:
-        copy.start()
-    for copy in copies:
-        copy.wait()
 
 
 def project_kernel(*refs):
@@ -116,12 +108,8 @@
     for at, to in row_blocks(place_ref):
         rows = pl.ds(pl.multiple_of(lax.rem(to, 256), 64), 64)
         gp_ref[at : at + 64] = jnp.where(to // 256 == ylo, mine_ref[rows, :], other_ref[rows, :])
-    part = None
-    for i, x_ref in enumerate(x_refs):
-        term = lax.dot_general(
-            gp_ref[128 * i : 128 * (i + 1)], x_ref[:, lanes], (((0,), (0,)), ((), ())), preferred_element_type=F32
-        )
-        part = term if part is None else part + term
+    x = jnp.concatenate([ref[:, lanes] for ref in x_refs], axis=0)
+    part = lax.dot_general(gp_ref[...], x, (((0,), (0,)), ((), ())), preferred_element_type=F32)
     first, second = (part[:, 320 * c : 320 * (c + 1)].reshape(16, 8, 320) for c in range(2))
     core = place_ref[2]
     keep_ref[...] = jnp.where(core == 0, first, second)
@@ -158,15 +146,7 @@
     smem = pl.BlockSpec(memory_space=pltpu.SMEM)
     vmem = pl.BlockSpec(memory_space=pltpu.VMEM)
 
-    eight = pl.pallas_call(
-        copies_kernel,
-        in_specs=[pl.BlockSpec(memory_space=pltpu.HBM)],
-        out_specs=pl.BlockSpec(memory_space=pltpu.HBM),
-        out_shape=jax.ShapeDtypeStruct((8, 32, 1024), BF),
-        scratch_shapes=[pltpu.SemaphoreType.DMA((8,))],
-        compiler_params=pltpu.CompilerParams(vmem_limit_bytes=2**20),
-    )(pltpu.with_memory_space_constraint(sounds, pltpu.HBM))
-    even = lax.all_to_all(eight, "zp", 0, 0, tiled=True).reshape(256, 1024)
+    even = lax.all_to_all(jnp.broadcast_to(sounds[None], (8, 32, 1024)), "zp", 0, 0, tiled=True).reshape(256, 1024)
     pars = jnp.stack([par, par, 1 - par, 1 - par])
     cores = jnp.stack([core, 1 - core, core, 1 - core])
     firsts = ylo * 8192 + cores * 4096 + pars * 256 + (2 * x + yhi) * 32
@@ -181,12 +161,15 @@
     wide = jnp.concatenate([wide, across], axis=0)
     after = lax.ppermute(wide, "x", [((i + 1) % 4, i) for i in range(4)])
     before = lax.ppermute(wide, "x", [((i - 1) % 4, i) for i in range(4)])
-    opposite = fetch(jnp.where(core == 0, after, before), ("x",), 4)
+    onward = jnp.where(core == 0, after, before)
+    opposite = fetch(onward, ("x",), 4)
 
     early = project(projector, wide)
-    even = behind(even, after, before, early[2])
+    scale = jnp.concatenate([coldness, offset])
+    even = behind(even, after, before, early[2], ids, place, scale)
     odd = fetch(even, Z, 16)
     far_even = swap(even, "core")
+    odd = behind(odd, opposite)
     far_odd = swap(odd, "core")
 
     video = (wide, after, before, opposite)
@@ -199,7 +182,7 @@
         compiler_params=PARAMS,
         cost_estimate=pl.CostEstimate(flops=5 * 512 * 1024 * 1024, bytes_accessed=8 * 2**20, transcendentals=2**20),
     )(
-        jnp.concatenate([coldness, offset]),
+        scale,
         place,
         *video,
         *units,

time: 142 us -> 127 us (0.89)
  Pallas kernels: 28.2 us -> 10.9 us
  starting transfers between devices: 50.8 us -> 53.8 us
  local copies, waits for them, and re-layouts: 1.69 us -> 3.54 us
  waiting for transfers between devices: 12.6 us -> 10.9 us
    pallas_call x1 -> x0, Pallas kernels: 17.1 us -> none  [local(): pl.pallas_call(copies_kernel, in_specs=[pl.BlockSpec(memory_space=pltpu.H...]
    ppermute x4, starting transfers between devices: 17.4 us -> 20.3 us  [swap(): return lax.ppermute(a, axis, [(0, 1), (1, 0)])]
    broadcast_in_dim x0 -> x1, local copies, waits for them, and re-layouts: none -> 1.84 us  [local(): jnp.broadcast_to(sounds[None], (8, 32, 1024))]
    all_to_all x1, blocking collectives: 20.5 us -> 18.9 us  [local(): sums = lax.all_to_all(mine, Z, 0, 0, tiled=True)]
    ppermute x1, waiting for transfers between devices: 1.86 us -> 0.32 us  [local(): before = lax.ppermute(wide, 'x', [((i - 1) % 4, i) for i in range(4)])]
  transfers between devices with their start and end apart: 10 -> 10, of which waited for: 6 -> 6; matrix products, arithmetic and copies ran while one was open for 2% -> 2% of each run, Pallas kernels for 2% -> 3%
where the time goes in v9:
time: 127 us; the launch traced here: 126 us
  starting transfers between devices  53.8 us (42%)
  blocking collectives  42 us (33%)
  waiting for transfers between devices  10.9 us (9%)
  Pallas kernels  10.9 us (9%)
  local copies, waits for them, and re-layouts  3.54 us (3%)
  other arithmetic  3.38 us (3%)
  between operations  1.56 us (1%)
    all_to_all x1, blocking collectives, local(): terms = lax.all_to_all(parts, PLANE, 0, 0, tiled=True)  23.1 us
    ppermute x4, starting transfers between devices, swap(): return lax.ppermute(a, axis, [(0, 1), (1, 0)])  20.3 us
    all_to_all x1, blocking collectives, local(): sums = lax.all_to_all(mine, Z, 0, 0, tiled=True)  18.9 us
    all_to_all x1, starting transfers between devices, local(): lax.all_to_all(jnp.broadcast_to(sounds[None], (8, 32, 1024)), 'zp', 0, 0,...  15.6 us
    ppermute x2, starting transfers between devices, fetch(): return lax.ppermute(a, ('core', *axes), perm)  6.7 us
    pallas_call x1, Pallas kernels, local(): pl.pallas_call(pair_kernel, in_specs=[smem, smem] + [vmem] * 19, out_spec...  5.97 us
    ppermute x1, starting transfers between devices, local(): lax.ppermute(wide, ('ylo', 'yhi'), [(0, 3), (3, 0), (1, 2), (2, 1)])  4.64 us
    ppermute x1, waiting for transfers between devices, local(): lax.ppermute(wide, ('ylo', 'yhi'), [(0, 3), (3, 0), (1, 2), (2, 1)])  3.6 us
  transfers between devices with their start and end apart: 10, of which 6 were waited for; matrix products, arithmetic and copies ran while one was open for 2% of the time, Pallas kernels for 3%

profile of v9, /device:TPU:1, one launch (start us, length us, event | category | flops | bytes accessed | tf_op | source)
XLA Modules:
  0.0 125.9 jit_solution(16399464726376436137)
XLA Ops:
  0.0 1.8 %broadcast_in_dim.2 = bf16[8,32,1024]{2,1,0:T(8,128)(2,1)} broadcast(bf16[32,1024]{1,0:T(8,128)(2,1)} %param.10), dimensions={1,2} | broadcast | bytes 589824 | tf_op jit(solution)/shard_map/broadcast_in_dim | solution.py:149
  1.8 15.6 %all-to-all-start = ((bf16[8,32,1024]{2,1,0:T(8,128)(2,1)}), bf16[8,32,1024]{2,1,0:T(8,128)(2,1)}, u32[]{:S(2)}, u32[]{:S(2)}) async-start(bf16[8,32,1024]{2,1,0:T(8,128)(2,1)} %broadcast_in_dim.2), calls=%async_computation | async-start | bytes 1048576 | tf_op jit(solution)/shard_map/all_to_all | solution.py:149
  18.4 0.9 fusion.1
  19.3 4.6 %collective-permute-start = (bf16[64,1408]{1,0:T(8,128)(2,1)S(1)}, bf16[64,1408]{1,0:T(8,128)(2,1)S(1)}, u32[]{:S(2)}, u32[]{:S(2)}) collective-permute-start(bf16[64,1408]{1,0:T(8,128)(2,1)S(1)} %fusion.1), channel_id=1, source_target_pairs={{0,257},{257,0},{1,256},{256,1},{2,259},{259,2},{3,258},{258,3},{4... | collective-permute-start | bytes 540680 | tf_op jit(solution)/shard_map/ppermute | solution.py:160
  24.0 3.6 %collective-permute-done = bf16[64,1408]{1,0:T(8,128)(2,1)S(1)} collective-permute-done((bf16[64,1408]{1,0:T(8,128)(2,1)S(1)}, bf16[64,1408]{1,0:T(8,128)(2,1)S(1)}, u32[]{:S(2)}, u32[]{:S(2)}) %collective-permute-start) | collective-permute-done | bytes 180256 | tf_op jit(solution)/shard_map/ppermute | solution.py:160
  28.4 3.1 %collective-permute-start.2 = (bf16[128,1408]{1,0:T(8,128)(2,1)}, bf16[128,1408]{1,0:T(8,128)(2,1)S(1)}, u32[]{:S(2)}, u32[]{:S(2)}) collective-permute-start(bf16[128,1408]{1,0:T(8,128)(2,1)} %pad_maximum_fusion.refs_0_), channel_id=1, source_target_pairs={{6,0},{0,2},{2,4},{4,6},{7,1},{1,3},{3,5},{5,7},{14,8},{8,10},{10,... | collective-permute-start | bytes 1081352 | tf_op jit(solution)/shard_map/ppermute | solution.py:163
  31.5 3.4 %collective-permute-start.1 = (bf16[128,1408]{1,0:T(8,128)(2,1)}, bf16[128,1408]{1,0:T(8,128)(2,1)S(1)}, u32[]{:S(2)}, u32[]{:S(2)}) collective-permute-start(bf16[128,1408]{1,0:T(8,128)(2,1)} %pad_maximum_fusion.refs_0_), channel_id=1, source_target_pairs={{2,0},{4,2},{6,4},{0,6},{3,1},{5,3},{7,5},{1,7},{10,8},{12,10},{14... | collective-permute-start | bytes 1081352 | tf_op jit(solution)/shard_map/ppermute | solution.py:162
  36.5 1.6 %shard_map.82 = (f32[128,1024]{1,0:T(8,128)S(1)}, bf16[128,1024]{1,0:T(8,128)(2,1)S(1)}, f32[128,128]{1,0:T(8,128)S(1)}) custom-call(bf16[128,1408]{1,0:T(8,128)(2,1)} %pad_maximum_fusion.refs_0_, bf16[1280,1024]{1,0:T(8,128)(2,1)S(1)} %copy-done), custom_call_target="tpu_custom_call" | custom-call | flops 335544320 | bytes 4194304 | tf_op jit(solution)/shard_map/pallas_call | solution.py:42
  38.1 0.8 copy-done.2
  39.9 1.6 %collective-permute-done.1.refs_0_.refs_1_ = bf16[128,1408]{1,0:T(8,128)(2,1)S(1)} collective-permute-done((bf16[128,1408]{1,0:T(8,128)(2,1)}, bf16[128,1408]{1,0:T(8,128)(2,1)S(1)}, u32[]{:S(2)}, u32[]{:S(2)}) %collective-permute-start.1) | collective-permute-done | bytes 360480 | tf_op jit(solution)/shard_map/ppermute | solution.py:162
  41.6 1.8 %all-to-all-done = bf16[8,32,1024]{2,1,0:T(8,128)(2,1)} async-done(((bf16[8,32,1024]{2,1,0:T(8,128)(2,1)}), bf16[8,32,1024]{2,1,0:T(8,128)(2,1)}, u32[]{:S(2)}, u32[]{:S(2)}) %all-to-all-start) | async-done | bytes 524320 | tf_op jit(solution)/shard_map/all_to_all | solution.py:149
  43.4 3.6 %collective-permute-start.5 = (bf16[256,1024]{1,0:T(8,128)(2,1)}, bf16[256,1024]{1,0:T(8,128)(2,1)S(1)}, u32[]{:S(2)}, u32[]{:S(2)}) collective-permute-start(bf16[256,1024]{1,0:T(8,128)(2,1)} %shard_map.85.refs_15_), channel_id=1, source_target_pairs={{8,0},{16,8},{24,16},{32,24},{40,32},{48,40},{56,48},{64,56},{72,6... | collective-permute-start | bytes 1572872 | tf_op jit(solution)/shard_map/ppermute | solution.py:125
  47.1 3.1 %collective-permute-start.3 = (bf16[128,1408]{1,0:T(8,128)(2,1)S(1)}, bf16[128,1408]{1,0:T(8,128)(2,1)S(1)}, u32[]{:S(2)}, u32[]{:S(2)}) collective-permute-start(bf16[128,1408]{1,0:T(8,128)(2,1)S(1)} %broadcast_select_fusion), channel_id=1, source_target_pairs={{2,0},{4,2},{6,4},{0,6},{134,128},{128,130},{130,132},{132,134},{3... | collective-permute-start | bytes 1081352 | tf_op jit(solution)/shard_map/ppermute | solution.py:125
  50.2 7.4 %collective-permute-start.4 = (bf16[256,1024]{1,0:T(8,128)(2,1)}, bf16[256,1024]{1,0:T(8,128)(2,1)S(1)}, u32[]{:S(2)}, u32[]{:S(2)}) collective-permute-start(bf16[256,1024]{1,0:T(8,128)(2,1)} %shard_map.85.refs_15_), channel_id=1, source_target_pairs={{0,128},{128,0},{1,129},{129,1},{2,130},{130,2},{3,131},{131,3},{4... | collective-permute-start | bytes 1572872 | tf_op jit(solution)/shard_map/ppermute | solution.py:141
  57.7 5.1 %collective-permute-start.6 = (bf16[256,1024]{1,0:T(8,128)(2,1)S(1)}, bf16[256,1024]{1,0:T(8,128)(2,1)S(1)}, u32[]{:S(2)}, u32[]{:S(2)}) collective-permute-start(bf16[256,1024]{1,0:T(8,128)(2,1)S(1)} %shard_map.86.refs_17_), channel_id=1, source_target_pairs={{0,128},{128,0},{1,129},{129,1},{2,130},{130,2},{3,131},{131,3},{4... | collective-permute-start | bytes 1572872 | tf_op jit(solution)/shard_map/ppermute | solution.py:141
  62.8 1.0 shard_map.83
  64.5 6.0 %shard_map.87 = bf16[16,256,128]{2,1,0:T(8,128)(2,1)S(1)} custom-call(f32[2]{0:T(128)S(1)} %pad_maximum_fusion.2.refs_6_.scale_ref, s32[4]{0:T(128)S(1)} %pad_add_fusion.refs_5_.place_ref, bf16[128,1408]{1,0:T(8,128)(2,1)} %pad_maximum_fusion.refs_0_, bf16[128,1408]{1,0:T(8,128)(2,1)S(1)} %collective-permute-done.1.refs_0_.refs_1_, ...), custom_call_target="tpu_custom_call" | custom-call | flops 2684354560 | bytes 8388608 | tf_op jit(solution)/shard_map/pallas_call | solution.py:177
  70.5 23.1 %all_to_all.15.g_ref = bf16[16,256,128]{2,1,0:T(8,128)(2,1)S(1)} all-to-all(bf16[16,256,128]{2,1,0:T(8,128)(2,1)S(1)} %shard_map.87), channel_id=1, replica_groups=mesh['ylo'=2,'core'=2,'zp'=8,'par'=2,'x'=4,'yhi'=2] {'x','yhi','ylo'}, dimensions={0} | all-to-all | bytes 2097152 | tf_op jit(solution)/shard_map/all_to_all | solution.py:197
  93.7 2.4 %collective-permute-start.7 = (bf16[256,128]{1,0:T(8,128)(2,1)S(1)}, bf16[256,128]{1,0:T(8,128)(2,1)S(1)}, u32[]{:S(2)}, u32[]{:S(2)}) collective-permute-start(bf16[256,128]{1,0:T(8,128)(2,1)S(1)} %shard_map.88.mine_ref), channel_id=1, source_target_pairs={{0,256},{256,0},{1,257},{257,1},{2,258},{258,2},{3,259},{259,3},{4... | collective-permute-start | bytes 196616 | tf_op jit(solution)/shard_map/ppermute | solution.py:141
  96.2 2.6 %collective-permute-done.7.other_ref = bf16[256,128]{1,0:T(8,128)(2,1)S(1)} collective-permute-done((bf16[256,128]{1,0:T(8,128)(2,1)S(1)}, bf16[256,128]{1,0:T(8,128)(2,1)S(1)}, u32[]{:S(2)}, u32[]{:S(2)}) %collective-permute-start.7) | collective-permute-done | bytes 65568 | tf_op jit(solution)/shard_map/ppermute | solution.py:141
  98.7 1.5 %shard_map.89 = (f32[16,8,320]{2,1,0:T(8,128)S(1)}, bf16[16,8,320]{2,1,0:T(8,128)(2,1)S(1)}) custom-call(s32[4]{0:T(128)S(1)} %pad_add_fusion.refs_5_.place_ref, bf16[256,128]{1,0:T(8,128)(2,1)S(1)} %shard_map.88.mine_ref, bf16[256,128]{1,0:T(8,128)(2,1)S(1)} %collective-permute-done.7.other_ref, bf16[128,1408]{1,0:T(8,128)(2,1)} %pad_maximum_fusion.refs_0_, ...), custom_call_target="tpu_custom_call" | custom-call | tf_op jit(solution)/shard_map/pallas_call | solution.py:201
  100.2 5.3 %collective-permute-start.8 = (bf16[16,8,320]{2,1,0:T(8,128)(2,1)S(1)}, bf16[16,8,320]{2,1,0:T(8,128)(2,1)S(1)}, u32[]{:S(2)}, u32[]{:S(2)}) collective-permute-start(bf16[16,8,320]{2,1,0:T(8,128)(2,1)S(1)} %get-tuple-element.26), channel_id=1, source_target_pairs={{0,128},{128,0},{1,129},{129,1},{2,130},{130,2},{3,131},{131,3},{4... | collective-permute-start | bytes 245768 | tf_op jit(solution)/shard_map/ppermute | solution.py:141
  105.5 0.9 collective-permute-done.8.b_ref
  106.4 18.9 %all_to_all.16 = bf16[16,8,320]{2,1,0:T(8,128)(2,1)S(1)} all-to-all(bf16[16,8,320]{2,1,0:T(8,128)(2,1)S(1)} %shard_map.90), channel_id=1, replica_groups=mesh['ylo'=2,'core'=2,'zp'=8,'par'=2,'x'=4,'yhi'=2] {'zp','par'}, dimensions={0} | all-to-all | bytes 163840 | tf_op jit(solution)/shard_map/all_to_all | solution.py:216
  (36 shorter events, 4.5 us)
Async XLA Ops:
  0.0 34.9 %copy-start.6 = (s32[256]{0:T(256)S(1)}, s32[256]{0:T(256)}, u32[]{:S(2)}) copy-start(s32[256]{0:T(256)} %constant.54) | copy-start | bytes 3076
  0.0 36.5 %copy-start = (bf16[1280,1024]{1,0:T(8,128)(2,1)S(1)}, bf16[1280,1024]{1,0:T(8,128)(2,1)}, u32[]{:S(2)}) copy-start(bf16[1280,1024]{1,0:T(8,128)(2,1)} %refs_1_.3) | copy-start | bytes 7864324
  1.8 41.6 %all-to-all-start = ((bf16[8,32,1024]{2,1,0:T(8,128)(2,1)}), bf16[8,32,1024]{2,1,0:T(8,128)(2,1)}, u32[]{:S(2)}, u32[]{:S(2)}) async-start(bf16[8,32,1024]{2,1,0:T(8,128)(2,1)} %broadcast_in_dim.2), calls=%async_computation | async-start | bytes 1048576 | tf_op jit(solution)/shard_map/all_to_all | solution.py:149
  19.3 8.4 %collective-permute-start = (bf16[64,1408]{1,0:T(8,128)(2,1)S(1)}, bf16[64,1408]{1,0:T(8,128)(2,1)S(1)}, u32[]{:S(2)}, u32[]{:S(2)}) collective-permute-start(bf16[64,1408]{1,0:T(8,128)(2,1)S(1)} %fusion.1), channel_id=1, source_target_pairs={{0,257},{257,0},{1,256},{256,1},{2,259},{259,2},{3,258},{258,3},{4... | collective-permute-start | bytes 540680 | tf_op jit(solution)/shard_map/ppermute | solution.py:160
  28.4 11.5 %collective-permute-start.2 = (bf16[128,1408]{1,0:T(8,128)(2,1)}, bf16[128,1408]{1,0:T(8,128)(2,1)S(1)}, u32[]{:S(2)}, u32[]{:S(2)}) collective-permute-start(bf16[128,1408]{1,0:T(8,128)(2,1)} %pad_maximum_fusion.refs_0_), channel_id=1, source_target_pairs={{6,0},{0,2},{2,4},{4,6},{7,1},{1,3},{3,5},{5,7},{14,8},{8,10},{10,... | collective-permute-start | bytes 1081352 | tf_op jit(solution)/shard_map/ppermute | solution.py:163
  31.5 10.0 %collective-permute-start.1 = (bf16[128,1408]{1,0:T(8,128)(2,1)}, bf16[128,1408]{1,0:T(8,128)(2,1)S(1)}, u32[]{:S(2)}, u32[]{:S(2)}) collective-permute-start(bf16[128,1408]{1,0:T(8,128)(2,1)} %pad_maximum_fusion.refs_0_), channel_id=1, source_target_pairs={{2,0},{4,2},{6,4},{0,6},{3,1},{5,3},{7,5},{1,7},{10,8},{12,10},{14... | collective-permute-start | bytes 1081352 | tf_op jit(solution)/shard_map/ppermute | solution.py:162
  38.1 0.8 copy-start.2
  38.9 0.7 copy-start.4
  43.4 14.2 %collective-permute-start.5 = (bf16[256,1024]{1,0:T(8,128)(2,1)}, bf16[256,1024]{1,0:T(8,128)(2,1)S(1)}, u32[]{:S(2)}, u32[]{:S(2)}) collective-permute-start(bf16[256,1024]{1,0:T(8,128)(2,1)} %shard_map.85.refs_15_), channel_id=1, source_target_pairs={{8,0},{16,8},{24,16},{32,24},{40,32},{48,40},{56,48},{64,56},{72,6... | collective-permute-start | bytes 1572872 | tf_op jit(solution)/shard_map/ppermute | solution.py:125
  47.1 10.6 %collective-permute-start.3 = (bf16[128,1408]{1,0:T(8,128)(2,1)S(1)}, bf16[128,1408]{1,0:T(8,128)(2,1)S(1)}, u32[]{:S(2)}, u32[]{:S(2)}) collective-permute-start(bf16[128,1408]{1,0:T(8,128)(2,1)S(1)} %broadcast_select_fusion), channel_id=1, source_target_pairs={{2,0},{4,2},{6,4},{0,6},{134,128},{128,130},{130,132},{132,134},{3... | collective-permute-start | bytes 1081352 | tf_op jit(solution)/shard_map/ppermute | solution.py:125
  50.2 14.3 %collective-permute-start.4 = (bf16[256,1024]{1,0:T(8,128)(2,1)}, bf16[256,1024]{1,0:T(8,128)(2,1)S(1)}, u32[]{:S(2)}, u32[]{:S(2)}) collective-permute-start(bf16[256,1024]{1,0:T(8,128)(2,1)} %shard_map.85.refs_15_), channel_id=1, source_target_pairs={{0,128},{128,0},{1,129},{129,1},{2,130},{130,2},{3,131},{131,3},{4... | collective-permute-start | bytes 1572872 | tf_op jit(solution)/shard_map/ppermute | solution.py:141
  57.7 6.8 %copy-start.1 = (bf16[1024,1024]{1,0:T(8,128)(2,1)S(1)}, bf16[1024,1024]{1,0:T(8,128)(2,1)}, u32[]{:S(2)}) copy-start(bf16[1024,1024]{1,0:T(8,128)(2,1)} %constant.50.clone.refs_14_) | copy-start | bytes 6291460
  57.7 6.8 %copy-start.3 = (f32[128,1024]{1,0:T(8,128)S(1)}, f32[128,1024]{1,0:T(8,128)}, u32[]{:S(2)}) copy-start(f32[128,1024]{1,0:T(8,128)} %copy-done.2) | copy-start | bytes 1572868
  57.7 6.8 %copy-start.5 = (bf16[128,1024]{1,0:T(8,128)(2,1)S(1)}, bf16[128,1024]{1,0:T(8,128)(2,1)}, u32[]{:S(2)}) copy-start(bf16[128,1024]{1,0:T(8,128)(2,1)} %copy-done.4) | copy-start | bytes 786436
  57.7 6.8 %collective-permute-start.6 = (bf16[256,1024]{1,0:T(8,128)(2,1)S(1)}, bf16[256,1024]{1,0:T(8,128)(2,1)S(1)}, u32[]{:S(2)}, u32[]{:S(2)}) collective-permute-start(bf16[256,1024]{1,0:T(8,128)(2,1)S(1)} %shard_map.86.refs_17_), channel_id=1, source_target_pairs={{0,128},{128,0},{1,129},{129,1},{2,130},{130,2},{3,131},{131,3},{4... | collective-permute-start | bytes 1572872 | tf_op jit(solution)/shard_map/ppermute | solution.py:141
  93.7 5.0 %collective-permute-start.7 = (bf16[256,128]{1,0:T(8,128)(2,1)S(1)}, bf16[256,128]{1,0:T(8,128)(2,1)S(1)}, u32[]{:S(2)}, u32[]{:S(2)}) collective-permute-start(bf16[256,128]{1,0:T(8,128)(2,1)S(1)} %shard_map.88.mine_ref), channel_id=1, source_target_pairs={{0,256},{256,0},{1,257},{257,1},{2,258},{258,2},{3,259},{259,3},{4... | collective-permute-start | bytes 196616 | tf_op jit(solution)/shard_map/ppermute | solution.py:141
  100.2 6.2 %collective-permute-start.8 = (bf16[16,8,320]{2,1,0:T(8,128)(2,1)S(1)}, bf16[16,8,320]{2,1,0:T(8,128)(2,1)S(1)}, u32[]{:S(2)}, u32[]{:S(2)}) collective-permute-start(bf16[16,8,320]{2,1,0:T(8,128)(2,1)S(1)} %get-tuple-element.26), channel_id=1, source_target_pairs={{0,128},{128,0},{1,129},{129,1},{2,130},{130,2},{3,131},{131,3},{4... | collective-permute-start | bytes 245768 | tf_op jit(solution)/shard_map/ppermute | solution.py:141

commit v10 on v9

--- a/solution.py
+++ b/solution.py
@@ -62,7 +62,7 @@
 
 
 def pair_kernel(scale_ref, place_ref, *refs):
-    x_refs, video, ids_ref, order_ref, audio_refs, out_ref = refs[:4], refs[4:13], refs[13], refs[14], refs[15:19], refs[19]
+    x_refs, video, ids_ref, order_ref, audio_refs, out_ref = refs[:4], refs[4:13], refs[13], refs[14], refs[15:17], refs[17]
     unit, unit_b, mag = (jnp.concatenate([ref[...] for ref in video[i::3]], axis=0) for i in range(3))
     cold = scale_ref[0]
     offset = scale_ref[1]
@@ -137,6 +137,24 @@
     )(a, *others)
 
 
+def stack_kernel(a_ref, b_ref, *refs):
+    out_ref = refs[-1]
+    n = a_ref.shape[0]
+    out_ref[:n] = a_ref[...]
+    out_ref[n:] = b_ref[...]
+
+
+def stack(a, b, *others):
+    vmem = pl.BlockSpec(memory_space=pltpu.VMEM)
+    return pl.pallas_call(
+        stack_kernel,
+        in_specs=[vmem, vmem] + [pl.BlockSpec(memory_space=pl.ANY)] * len(others),
+        out_specs=vmem,
+        out_shape=jax.ShapeDtypeStruct((a.shape[0] + b.shape[0], a.shape[1]), a.dtype),
+        compiler_params=pltpu.CompilerParams(vmem_limit_bytes=4 * 2**20),
+    )(a, b, *others)
+
+
 def swap(a, axis):
     return lax.ppermute(a, axis, [(0, 1), (1, 0)])
 
@@ -147,8 +165,8 @@
     vmem = pl.BlockSpec(memory_space=pltpu.VMEM)
 
     even = lax.all_to_all(jnp.broadcast_to(sounds[None], (8, 32, 1024)), "zp", 0, 0, tiled=True).reshape(256, 1024)
-    pars = jnp.stack([par, par, 1 - par, 1 - par])
-    cores = jnp.stack([core, 1 - core, core, 1 - core])
+    pars = jnp.stack([par, 1 - par, par, 1 - par])
+    cores = jnp.stack([core, core, 1 - core, 1 - core])
     firsts = ylo * 8192 + cores * 4096 + pars * 256 + (2 * x + yhi) * 32
     inside = np.arange(8)[:, None] * 512 + np.arange(32)[None, :]
     ids = (firsts[:, None] + jnp.asarray(inside.reshape(1, 256), jnp.int32)).astype(F32).reshape(1, 1024)
@@ -168,15 +186,15 @@
     scale = jnp.concatenate([coldness, offset])
     even = behind(even, after, before, early[2], ids, place, scale)
     odd = fetch(even, Z, 16)
-    far_even = swap(even, "core")
-    odd = behind(odd, opposite)
-    far_odd = swap(odd, "core")
+    late = project(projector, after, before)
+    audio = stack(even, odd, opposite, late[2])
+    far_audio = swap(audio, "core")
 
     video = (wide, after, before, opposite)
-    units = [*early, *project(projector, after, before), *project(projector, opposite)]
+    units = [*early, *late, *project(projector, opposite)]
     parts = pl.pallas_call(
         pair_kernel,
-        in_specs=[smem, smem] + [vmem] * 19,
+        in_specs=[smem, smem] + [vmem] * 17,
         out_specs=vmem,
         out_shape=jax.ShapeDtypeStruct((16, 256, 128), BF),
         compiler_params=PARAMS,
@@ -188,10 +206,8 @@
         *units,
         ids,
         column_order(),
-        even,
-        far_even,
-        odd,
-        far_odd,
+        audio,
+        far_audio,
     )
 
     terms = lax.all_to_all(parts, PLANE, 0, 0, tiled=True)

time: 127 us -> 128 us (level)
  waiting for transfers between devices: 10.9 us -> 17.9 us
  starting transfers between devices: 53.8 us -> 47.1 us
    ppermute x4 -> x3, starting transfers between devices: 20.3 us -> 13.6 us  [swap(): return lax.ppermute(a, axis, [(0, 1), (1, 0)])]
    ppermute x2, waiting for transfers between devices: 0.01 us -> 5.26 us  [fetch(): return lax.ppermute(a, ('core', *axes), perm)]
    ppermute x4 -> x3, waiting for transfers between devices: 3.48 us -> 5.21 us  [swap(): return lax.ppermute(a, axis, [(0, 1), (1, 0)])]
    pallas_call x1 -> x2, Pallas kernels: 5.97 us -> 6.61 us  [the longest x1 5.35 us: local(): pl.pallas_call(pair_kernel, in_specs=[smem, smem] + [vmem] * 17, out_spec...]
  transfers between devices with their start and end apart: 10 -> 9, of which waited for: 6 -> 8; matrix products, arithmetic and copies ran while one was open for 2% -> 2% of each run, Pallas kernels for 3% -> 3%
where the time goes in v10:
time: 128 us; the launch traced here: 127 us
  starting transfers between devices  47.1 us (37%)
  blocking collectives  42 us (33%)
  waiting for transfers between devices  17.9 us (14%)
  Pallas kernels  11.5 us (9%)
  local copies, waits for them, and re-layouts  3.54 us (3%)
  other arithmetic  3.37 us (3%)
  between operations  1.48 us (1%)
    all_to_all x1, blocking collectives, local(): terms = lax.all_to_all(parts, PLANE, 0, 0, tiled=True)  23.2 us
    all_to_all x1, blocking collectives, local(): sums = lax.all_to_all(mine, Z, 0, 0, tiled=True)  18.9 us
    all_to_all x1, starting transfers between devices, local(): lax.all_to_all(jnp.broadcast_to(sounds[None], (8, 32, 1024)), 'zp', 0, 0,...  15.6 us
    ppermute x3, starting transfers between devices, swap(): return lax.ppermute(a, axis, [(0, 1), (1, 0)])  13.6 us
    ppermute x2, starting transfers between devices, fetch(): return lax.ppermute(a, ('core', *axes), perm)  6.7 us
    pallas_call x1, Pallas kernels, local(): pl.pallas_call(pair_kernel, in_specs=[smem, smem] + [vmem] * 17, out_spec...  5.35 us
    ppermute x2, waiting for transfers between devices, fetch(): return lax.ppermute(a, ('core', *axes), perm)  5.26 us
    ppermute x3, waiting for transfers between devices, swap(): return lax.ppermute(a, axis, [(0, 1), (1, 0)])  5.21 us
  transfers between devices with their start and end apart: 9, of which 8 were waited for; matrix products, arithmetic and copies ran while one was open for 2% of the time, Pallas kernels for 3%

profile of v10, /device:TPU:1, one launch (start us, length us, event | category | flops | bytes accessed | tf_op | source)
XLA Modules:
  0.0 126.9 jit_solution(1435786632759217196)
XLA Ops:
  0.0 1.8 %broadcast_in_dim.2 = bf16[8,32,1024]{2,1,0:T(8,128)(2,1)} broadcast(bf16[32,1024]{1,0:T(8,128)(2,1)} %param.10), dimensions={1,2} | broadcast | bytes 589824 | tf_op jit(solution)/shard_map/broadcast_in_dim | solution.py:167
  1.8 15.6 %all-to-all-start = ((bf16[8,32,1024]{2,1,0:T(8,128)(2,1)}), bf16[8,32,1024]{2,1,0:T(8,128)(2,1)}, u32[]{:S(2)}, u32[]{:S(2)}) async-start(bf16[8,32,1024]{2,1,0:T(8,128)(2,1)} %broadcast_in_dim.2), calls=%async_computation | async-start | bytes 1048576 | tf_op jit(solution)/shard_map/all_to_all | solution.py:167
  18.4 0.9 fusion.1
  19.3 4.6 %collective-permute-start = (bf16[64,1408]{1,0:T(8,128)(2,1)S(1)}, bf16[64,1408]{1,0:T(8,128)(2,1)S(1)}, u32[]{:S(2)}, u32[]{:S(2)}) collective-permute-start(bf16[64,1408]{1,0:T(8,128)(2,1)S(1)} %fusion.1), channel_id=1, source_target_pairs={{0,257},{257,0},{1,256},{256,1},{2,259},{259,2},{3,258},{258,3},{4... | collective-permute-start | bytes 540680 | tf_op jit(solution)/shard_map/ppermute | solution.py:178
  24.0 3.6 %collective-permute-done = bf16[64,1408]{1,0:T(8,128)(2,1)S(1)} collective-permute-done((bf16[64,1408]{1,0:T(8,128)(2,1)S(1)}, bf16[64,1408]{1,0:T(8,128)(2,1)S(1)}, u32[]{:S(2)}, u32[]{:S(2)}) %collective-permute-start) | collective-permute-done | bytes 180256 | tf_op jit(solution)/shard_map/ppermute | solution.py:178
  28.4 3.1 %collective-permute-start.2 = (bf16[128,1408]{1,0:T(8,128)(2,1)}, bf16[128,1408]{1,0:T(8,128)(2,1)S(1)}, u32[]{:S(2)}, u32[]{:S(2)}) collective-permute-start(bf16[128,1408]{1,0:T(8,128)(2,1)} %pad_maximum_fusion.refs_0_), channel_id=1, source_target_pairs={{6,0},{0,2},{2,4},{4,6},{7,1},{1,3},{3,5},{5,7},{14,8},{8,10},{10,... | collective-permute-start | bytes 1081352 | tf_op jit(solution)/shard_map/ppermute | solution.py:181
  31.5 3.4 %collective-permute-start.1 = (bf16[128,1408]{1,0:T(8,128)(2,1)}, bf16[128,1408]{1,0:T(8,128)(2,1)S(1)}, u32[]{:S(2)}, u32[]{:S(2)}) collective-permute-start(bf16[128,1408]{1,0:T(8,128)(2,1)} %pad_maximum_fusion.refs_0_), channel_id=1, source_target_pairs={{2,0},{4,2},{6,4},{0,6},{3,1},{5,3},{7,5},{1,7},{10,8},{12,10},{14... | collective-permute-start | bytes 1081352 | tf_op jit(solution)/shard_map/ppermute | solution.py:180
  36.5 1.6 %shard_map.82 = (f32[128,1024]{1,0:T(8,128)S(1)}, bf16[128,1024]{1,0:T(8,128)(2,1)S(1)}, f32[128,128]{1,0:T(8,128)S(1)}) custom-call(bf16[128,1408]{1,0:T(8,128)(2,1)} %pad_maximum_fusion.refs_0_, bf16[1280,1024]{1,0:T(8,128)(2,1)S(1)} %copy-done), custom_call_target="tpu_custom_call" | custom-call | flops 335544320 | bytes 4194304 | tf_op jit(solution)/shard_map/pallas_call | solution.py:42
  39.9 1.6 %collective-permute-done.1.refs_0_.refs_1_ = bf16[128,1408]{1,0:T(8,128)(2,1)S(1)} collective-permute-done((bf16[128,1408]{1,0:T(8,128)(2,1)}, bf16[128,1408]{1,0:T(8,128)(2,1)S(1)}, u32[]{:S(2)}, u32[]{:S(2)}) %collective-permute-start.1) | collective-permute-done | bytes 360480 | tf_op jit(solution)/shard_map/ppermute | solution.py:180
  41.6 1.9 %all-to-all-done = bf16[8,32,1024]{2,1,0:T(8,128)(2,1)} async-done(((bf16[8,32,1024]{2,1,0:T(8,128)(2,1)}), bf16[8,32,1024]{2,1,0:T(8,128)(2,1)}, u32[]{:S(2)}, u32[]{:S(2)}) %all-to-all-start) | async-done | bytes 524320 | tf_op jit(solution)/shard_map/all_to_all | solution.py:167
  43.4 3.6 %collective-permute-start.4 = (bf16[256,1024]{1,0:T(8,128)(2,1)}, bf16[256,1024]{1,0:T(8,128)(2,1)S(1)}, u32[]{:S(2)}, u32[]{:S(2)}) collective-permute-start(bf16[256,1024]{1,0:T(8,128)(2,1)} %shard_map.85.a_ref), channel_id=1, source_target_pairs={{8,0},{16,8},{24,16},{32,24},{40,32},{48,40},{56,48},{64,56},{72,6... | collective-permute-start | bytes 1572872 | tf_op jit(solution)/shard_map/ppermute | solution.py:125
  47.1 3.1 %collective-permute-start.3 = (bf16[128,1408]{1,0:T(8,128)(2,1)S(1)}, bf16[128,1408]{1,0:T(8,128)(2,1)S(1)}, u32[]{:S(2)}, u32[]{:S(2)}) collective-permute-start(bf16[128,1408]{1,0:T(8,128)(2,1)S(1)} %broadcast_select_fusion), channel_id=1, source_target_pairs={{2,0},{4,2},{6,4},{0,6},{134,128},{128,130},{130,132},{132,134},{3... | collective-permute-start | bytes 1081352 | tf_op jit(solution)/shard_map/ppermute | solution.py:125
  50.2 1.0 shard_map.83
  51.2 5.3 %collective-permute-done.3.refs_0_.refs_3_ = bf16[128,1408]{1,0:T(8,128)(2,1)S(1)} collective-permute-done((bf16[128,1408]{1,0:T(8,128)(2,1)S(1)}, bf16[128,1408]{1,0:T(8,128)(2,1)S(1)}, u32[]{:S(2)}, u32[]{:S(2)}) %collective-permute-start.3) | collective-permute-done | bytes 360480 | tf_op jit(solution)/shard_map/ppermute | solution.py:125
  56.5 1.3 shard_map.86.refs_15_
  57.7 6.1 %collective-permute-start.5 = (bf16[512,1024]{1,0:T(8,128)(2,1)S(1)}, bf16[512,1024]{1,0:T(8,128)(2,1)S(1)}, u32[]{:S(2)}, u32[]{:S(2)}) collective-permute-start(bf16[512,1024]{1,0:T(8,128)(2,1)S(1)} %shard_map.86.refs_15_), channel_id=1, source_target_pairs={{0,128},{128,0},{1,129},{129,1},{2,130},{130,2},{3,131},{131,3},{4... | collective-permute-start | bytes 3145736 | tf_op jit(solution)/shard_map/ppermute | solution.py:159
  64.5 1.6 %collective-permute-done.5.refs_16_ = bf16[512,1024]{1,0:T(8,128)(2,1)S(1)} collective-permute-done((bf16[512,1024]{1,0:T(8,128)(2,1)S(1)}, bf16[512,1024]{1,0:T(8,128)(2,1)S(1)}, u32[]{:S(2)}, u32[]{:S(2)}) %collective-permute-start.5) | collective-permute-done | bytes 1048608 | tf_op jit(solution)/shard_map/ppermute | solution.py:159
  66.1 5.3 %shard_map.87 = bf16[16,256,128]{2,1,0:T(8,128)(2,1)S(1)} custom-call(f32[2]{0:T(128)S(1)} %pad_maximum_fusion.2.refs_6_.scale_ref, s32[4]{0:T(128)S(1)} %pad_add_fusion.refs_5_.place_ref, bf16[128,1408]{1,0:T(8,128)(2,1)} %pad_maximum_fusion.refs_0_, bf16[128,1408]{1,0:T(8,128)(2,1)S(1)} %collective-permute-done.1.refs_0_.refs_1_, ...), custom_call_target="tpu_custom_call" | custom-call | flops 2684354560 | bytes 8388608 | tf_op jit(solution)/shard_map/pallas_call | solution.py:195
  71.5 23.2 %all_to_all.15.g_ref = bf16[16,256,128]{2,1,0:T(8,128)(2,1)S(1)} all-to-all(bf16[16,256,128]{2,1,0:T(8,128)(2,1)S(1)} %shard_map.87), channel_id=1, replica_groups=mesh['ylo'=2,'core'=2,'zp'=8,'par'=2,'x'=4,'yhi'=2] {'x','yhi','ylo'}, dimensions={0} | all-to-all | bytes 2097152 | tf_op jit(solution)/shard_map/all_to_all | solution.py:213
  94.8 2.3 %collective-permute-start.6 = (bf16[256,128]{1,0:T(8,128)(2,1)S(1)}, bf16[256,128]{1,0:T(8,128)(2,1)S(1)}, u32[]{:S(2)}, u32[]{:S(2)}) collective-permute-start(bf16[256,128]{1,0:T(8,128)(2,1)S(1)} %shard_map.88.mine_ref), channel_id=1, source_target_pairs={{0,256},{256,0},{1,257},{257,1},{2,258},{258,2},{3,259},{259,3},{4... | collective-permute-start | bytes 196616 | tf_op jit(solution)/shard_map/ppermute | solution.py:159
  97.1 2.7 %collective-permute-done.6.other_ref = bf16[256,128]{1,0:T(8,128)(2,1)S(1)} collective-permute-done((bf16[256,128]{1,0:T(8,128)(2,1)S(1)}, bf16[256,128]{1,0:T(8,128)(2,1)S(1)}, u32[]{:S(2)}, u32[]{:S(2)}) %collective-permute-start.6) | collective-permute-done | bytes 65568 | tf_op jit(solution)/shard_map/ppermute | solution.py:159
  99.8 1.5 %shard_map.89 = (f32[16,8,320]{2,1,0:T(8,128)S(1)}, bf16[16,8,320]{2,1,0:T(8,128)(2,1)S(1)}) custom-call(s32[4]{0:T(128)S(1)} %pad_add_fusion.refs_5_.place_ref, bf16[256,128]{1,0:T(8,128)(2,1)S(1)} %shard_map.88.mine_ref, bf16[256,128]{1,0:T(8,128)(2,1)S(1)} %collective-permute-done.6.other_ref, bf16[128,1408]{1,0:T(8,128)(2,1)} %pad_maximum_fusion.refs_0_, ...), custom_call_target="tpu_custom_call" | custom-call | tf_op jit(solution)/shard_map/pallas_call | solution.py:217
  101.3 5.2 %collective-permute-start.7 = (bf16[16,8,320]{2,1,0:T(8,128)(2,1)S(1)}, bf16[16,8,320]{2,1,0:T(8,128)(2,1)S(1)}, u32[]{:S(2)}, u32[]{:S(2)}) collective-permute-start(bf16[16,8,320]{2,1,0:T(8,128)(2,1)S(1)} %get-tuple-element.26), channel_id=1, source_target_pairs={{0,128},{128,0},{1,129},{129,1},{2,130},{130,2},{3,131},{131,3},{4... | collective-permute-start | bytes 245768 | tf_op jit(solution)/shard_map/ppermute | solution.py:159
  107.4 18.9 %all_to_all.16 = bf16[16,8,320]{2,1,0:T(8,128)(2,1)S(1)} all-to-all(bf16[16,8,320]{2,1,0:T(8,128)(2,1)S(1)} %shard_map.90), channel_id=1, replica_groups=mesh['ylo'=2,'core'=2,'zp'=8,'par'=2,'x'=4,'yhi'=2] {'zp','par'}, dimensions={0} | all-to-all | bytes 163840 | tf_op jit(solution)/shard_map/all_to_all | solution.py:232
  (34 shorter events, 6.2 us)
Async XLA Ops:
  0.0 34.9 %copy-start.6 = (s32[256]{0:T(256)S(1)}, s32[256]{0:T(256)}, u32[]{:S(2)}) copy-start(s32[256]{0:T(256)} %constant.54) | copy-start | bytes 3076
  0.0 36.5 %copy-start = (bf16[1280,1024]{1,0:T(8,128)(2,1)S(1)}, bf16[1280,1024]{1,0:T(8,128)(2,1)}, u32[]{:S(2)}) copy-start(bf16[1280,1024]{1,0:T(8,128)(2,1)} %refs_1_.3) | copy-start | bytes 7864324
  1.8 41.6 %all-to-all-start = ((bf16[8,32,1024]{2,1,0:T(8,128)(2,1)}), bf16[8,32,1024]{2,1,0:T(8,128)(2,1)}, u32[]{:S(2)}, u32[]{:S(2)}) async-start(bf16[8,32,1024]{2,1,0:T(8,128)(2,1)} %broadcast_in_dim.2), calls=%async_computation | async-start | bytes 1048576 | tf_op jit(solution)/shard_map/all_to_all | solution.py:167
  19.3 8.4 %collective-permute-start = (bf16[64,1408]{1,0:T(8,128)(2,1)S(1)}, bf16[64,1408]{1,0:T(8,128)(2,1)S(1)}, u32[]{:S(2)}, u32[]{:S(2)}) collective-permute-start(bf16[64,1408]{1,0:T(8,128)(2,1)S(1)} %fusion.1), channel_id=1, source_target_pairs={{0,257},{257,0},{1,256},{256,1},{2,259},{259,2},{3,258},{258,3},{4... | collective-permute-start | bytes 540680 | tf_op jit(solution)/shard_map/ppermute | solution.py:178
  28.4 11.5 %collective-permute-start.2 = (bf16[128,1408]{1,0:T(8,128)(2,1)}, bf16[128,1408]{1,0:T(8,128)(2,1)S(1)}, u32[]{:S(2)}, u32[]{:S(2)}) collective-permute-start(bf16[128,1408]{1,0:T(8,128)(2,1)} %pad_maximum_fusion.refs_0_), channel_id=1, source_target_pairs={{6,0},{0,2},{2,4},{4,6},{7,1},{1,3},{3,5},{5,7},{14,8},{8,10},{10,... | collective-permute-start | bytes 1081352 | tf_op jit(solution)/shard_map/ppermute | solution.py:181
  31.5 10.0 %collective-permute-start.1 = (bf16[128,1408]{1,0:T(8,128)(2,1)}, bf16[128,1408]{1,0:T(8,128)(2,1)S(1)}, u32[]{:S(2)}, u32[]{:S(2)}) collective-permute-start(bf16[128,1408]{1,0:T(8,128)(2,1)} %pad_maximum_fusion.refs_0_), channel_id=1, source_target_pairs={{2,0},{4,2},{6,4},{0,6},{3,1},{5,3},{7,5},{1,7},{10,8},{12,10},{14... | collective-permute-start | bytes 1081352 | tf_op jit(solution)/shard_map/ppermute | solution.py:180
  38.1 0.8 copy-start.2
  38.9 0.7 copy-start.4
  43.4 13.0 %collective-permute-start.4 = (bf16[256,1024]{1,0:T(8,128)(2,1)}, bf16[256,1024]{1,0:T(8,128)(2,1)S(1)}, u32[]{:S(2)}, u32[]{:S(2)}) collective-permute-start(bf16[256,1024]{1,0:T(8,128)(2,1)} %shard_map.85.a_ref), channel_id=1, source_target_pairs={{8,0},{16,8},{24,16},{32,24},{40,32},{48,40},{56,48},{64,56},{72,6... | collective-permute-start | bytes 1572872 | tf_op jit(solution)/shard_map/ppermute | solution.py:125
  47.1 9.4 %collective-permute-start.3 = (bf16[128,1408]{1,0:T(8,128)(2,1)S(1)}, bf16[128,1408]{1,0:T(8,128)(2,1)S(1)}, u32[]{:S(2)}, u32[]{:S(2)}) collective-permute-start(bf16[128,1408]{1,0:T(8,128)(2,1)S(1)} %broadcast_select_fusion), channel_id=1, source_target_pairs={{2,0},{4,2},{6,4},{0,6},{134,128},{128,130},{130,132},{132,134},{3... | collective-permute-start | bytes 1081352 | tf_op jit(solution)/shard_map/ppermute | solution.py:125
  56.5 9.7 %copy-start.1 = (bf16[1024,1024]{1,0:T(8,128)(2,1)S(1)}, bf16[1024,1024]{1,0:T(8,128)(2,1)}, u32[]{:S(2)}) copy-start(bf16[1024,1024]{1,0:T(8,128)(2,1)} %constant.50.clone.refs_14_) | copy-start | bytes 6291460
  56.5 9.7 %copy-start.3 = (f32[128,1024]{1,0:T(8,128)S(1)}, f32[128,1024]{1,0:T(8,128)}, u32[]{:S(2)}) copy-start(f32[128,1024]{1,0:T(8,128)} %copy-done.2) | copy-start | bytes 1572868
  56.5 9.7 %copy-start.5 = (bf16[128,1024]{1,0:T(8,128)(2,1)S(1)}, bf16[128,1024]{1,0:T(8,128)(2,1)}, u32[]{:S(2)}) copy-start(bf16[128,1024]{1,0:T(8,128)(2,1)} %copy-done.4) | copy-start | bytes 786436
  57.7 8.4 %collective-permute-start.5 = (bf16[512,1024]{1,0:T(8,128)(2,1)S(1)}, bf16[512,1024]{1,0:T(8,128)(2,1)S(1)}, u32[]{:S(2)}, u32[]{:S(2)}) collective-permute-start(bf16[512,1024]{1,0:T(8,128)(2,1)S(1)} %shard_map.86.refs_15_), channel_id=1, source_target_pairs={{0,128},{128,0},{1,129},{129,1},{2,130},{130,2},{3,131},{131,3},{4... | collective-permute-start | bytes 3145736 | tf_op jit(solution)/shard_map/ppermute | solution.py:159
  94.8 5.0 %collective-permute-start.6 = (bf16[256,128]{1,0:T(8,128)(2,1)S(1)}, bf16[256,128]{1,0:T(8,128)(2,1)S(1)}, u32[]{:S(2)}, u32[]{:S(2)}) collective-permute-start(bf16[256,128]{1,0:T(8,128)(2,1)S(1)} %shard_map.88.mine_ref), channel_id=1, source_target_pairs={{0,256},{256,0},{1,257},{257,1},{2,258},{258,2},{3,259},{259,3},{4... | collective-permute-start | bytes 196616 | tf_op jit(solution)/shard_map/ppermute | solution.py:159
  101.3 6.1 %collective-permute-start.7 = (bf16[16,8,320]{2,1,0:T(8,128)(2,1)S(1)}, bf16[16,8,320]{2,1,0:T(8,128)(2,1)S(1)}, u32[]{:S(2)}, u32[]{:S(2)}) collective-permute-start(bf16[16,8,320]{2,1,0:T(8,128)(2,1)S(1)} %get-tuple-element.26), channel_id=1, source_target_pairs={{0,128},{128,0},{1,129},{129,1},{2,130},{130,2},{3,131},{131,3},{4... | collective-permute-start | bytes 245768 | tf_op jit(solution)/shard_map/ppermute | solution.py:159

commit v11 on v10

--- a/solution.py
+++ b/solution.py
@@ -61,30 +61,34 @@
             yield 128 * i + 64 * j, lax.rem(x + k, 4) * 128 + half * 64
 
 
-def pair_kernel(scale_ref, place_ref, *refs):
-    x_refs, video, ids_ref, order_ref, audio_refs, out_ref = refs[:4], refs[4:13], refs[13], refs[14], refs[15:17], refs[17]
-    unit, unit_b, mag = (jnp.concatenate([ref[...] for ref in video[i::3]], axis=0) for i in range(3))
+def pairs(scale_ref, x_refs, unit_b_refs, ids, audio_ref):
     cold = scale_ref[0]
     offset = scale_ref[1]
+    unit_b = jnp.concatenate([ref[...] for ref in unit_b_refs], axis=0)
     halves = jnp.concatenate([ref[:, 1280:] for ref in x_refs], axis=0).astype(F32)
-    targets = [halves[:, 2 * p : 2 * p + 1] * 128.0 + halves[:, 2 * p + 1 : 2 * p + 2] for p in range(5)]
-    total = None
-    at = 0
-    for audio_ref in audio_refs:
-        audio = audio_ref[...]
-        n = audio.shape[0]
-        ids = ids_ref[:1, at : at + n]
-        at += n
-        sims = lax.dot_general(unit_b, audio, (((1,), (1,)), ((), ())), preferred_element_type=F32)
-        logits = cold * sims + offset
-        hit = None
-        for target in targets:
-            same = target == ids
-            hit = same if hit is None else hit | same
-        weight = (jax.nn.sigmoid(logits) - jnp.where(hit, 1.0, 0.0)).astype(BF)
-        term = jnp.dot(weight, audio, preferred_element_type=F32)
-        total = term if total is None else total + term
-    grad = cold * total
+    audio = audio_ref[...]
+    sims = lax.dot_general(unit_b, audio, (((1,), (1,)), ((), ())), preferred_element_type=F32)
+    logits = cold * sims + offset
+    hit = None
+    for p in range(5):
+        target = halves[:, 2 * p : 2 * p + 1] * 128.0 + halves[:, 2 * p + 1 : 2 * p + 2]
+        same = target == ids
+        hit = same if hit is None else hit | same
+    weight = (jax.nn.sigmoid(logits) - jnp.where(hit, 1.0, 0.0)).astype(BF)
+    return jnp.dot(weight, audio, preferred_element_type=F32)
+
+
+def own_kernel(scale_ref, *refs):
+    refs[-1][...] = pairs(scale_ref, refs[:4], refs[4:7], refs[7][:, :512], refs[8])
+
+
+def pair_kernel(scale_ref, place_ref, *refs):
+    out_ref = refs[-1]
+    units, unit_bs, mags = (refs[4 + i : 13 : 3] for i in range(3))
+    ids_ref, audio_ref, own_ref, order_ref = refs[13:17]
+    total = own_ref[...] + pairs(scale_ref, refs[:4], unit_bs, ids_ref[:, 512:], audio_ref)
+    unit, mag = (jnp.concatenate([ref[...] for ref in part], axis=0) for part in (units, mags))
+    grad = scale_ref[0] * total
     inner = jnp.sum(unit * grad, axis=1, keepdims=True)
     gp = ((grad - unit * inner) / mag[:, :1]).astype(BF)
     gp = jnp.dot(gp, order_ref[...], preferred_element_type=F32).astype(BF)
@@ -192,23 +196,22 @@
 
     video = (wide, after, before, opposite)
     units = [*early, *late, *project(projector, opposite)]
+    own = pl.pallas_call(
+        own_kernel,
+        in_specs=[smem] + [vmem] * 9,
+        out_specs=vmem,
+        out_shape=jax.ShapeDtypeStruct((512, 1024), F32),
+        compiler_params=PARAMS,
+        cost_estimate=pl.CostEstimate(flops=2 * 512 * 1024 * 1024, bytes_accessed=4 * 2**20, transcendentals=2**19),
+    )(scale, *video, *units[1::3], ids, audio)
     parts = pl.pallas_call(
         pair_kernel,
         in_specs=[smem, smem] + [vmem] * 17,
         out_specs=vmem,
         out_shape=jax.ShapeDtypeStruct((16, 256, 128), BF),
         compiler_params=PARAMS,
-        cost_estimate=pl.CostEstimate(flops=5 * 512 * 1024 * 1024, bytes_accessed=8 * 2**20, transcendentals=2**20),
-    )(
-        scale,
-        place,
-        *video,
-        *units,
-        ids,
-        column_order(),
-        audio,
-        far_audio,
-    )
+        cost_estimate=pl.CostEstimate(flops=3 * 512 * 1024 * 1024, bytes_accessed=8 * 2**20, transcendentals=2**19),
+    )(scale, place, *video, *units, ids, far_audio, own, column_order())
 
     terms = lax.all_to_all(parts, PLANE, 0, 0, tiled=True)
     mine = pl.pallas_call(

time: 128 us -> 128 us (level)
  waiting for transfers between devices: 17.9 us -> 16.2 us
  Pallas kernels: 11.5 us -> 13.1 us
    pallas_call x0 -> x1, Pallas kernels: none -> 2.85 us  [local(): pl.pallas_call(own_kernel, in_specs=[smem] + [vmem] * 9, out_specs=vmem,...]
    ppermute x3, waiting for transfers between devices: 5.21 us -> 3.52 us  [swap(): return lax.ppermute(a, axis, [(0, 1), (1, 0)])]
  transfers between devices with their start and end apart: 9 -> 9, of which waited for: 8 -> 7; matrix products, arithmetic and copies ran while one was open for 2% -> 2% of each run, Pallas kernels for 3% -> 5%
where the time goes in v11:
time: 128 us; the launch traced here: 127 us
  starting transfers between devices  47.5 us (37%)
  blocking collectives  41.8 us (33%)
  waiting for transfers between devices  16.2 us (13%)
  Pallas kernels  13.1 us (10%)
  local copies, waits for them, and re-layouts  3.54 us (3%)
  other arithmetic  3.37 us (3%)
  between operations  1.53 us (1%)
    all_to_all x1, blocking collectives, local(): terms = lax.all_to_all(parts, PLANE, 0, 0, tiled=True)  23 us
    all_to_all x1, blocking collectives, local(): sums = lax.all_to_all(mine, Z, 0, 0, tiled=True)  18.9 us
    all_to_all x1, starting transfers between devices, local(): lax.all_to_all(jnp.broadcast_to(sounds[None], (8, 32, 1024)), 'zp', 0, 0,...  15.6 us
    ppermute x3, starting transfers between devices, swap(): return lax.ppermute(a, axis, [(0, 1), (1, 0)])  14 us
    ppermute x2, starting transfers between devices, fetch(): return lax.ppermute(a, ('core', *axes), perm)  6.7 us
    ppermute x2, waiting for transfers between devices, fetch(): return lax.ppermute(a, ('core', *axes), perm)  5.26 us
    ppermute x1, starting transfers between devices, local(): lax.ppermute(wide, ('ylo', 'yhi'), [(0, 3), (3, 0), (1, 2), (2, 1)])  4.64 us
    pallas_call x1, Pallas kernels, local(): pl.pallas_call(pair_kernel, in_specs=[smem, smem] + [vmem] * 17, out_spec...  4.23 us
  transfers between devices with their start and end apart: 9, of which 7 were waited for; matrix products, arithmetic and copies ran while one was open for 2% of the time, Pallas kernels for 5%

profile of v11, /device:TPU:1, one launch (start us, length us, event | category | flops | bytes accessed | tf_op | source)
XLA Modules:
  0.0 127.1 jit_solution(15237411971337009829)
XLA Ops:
  0.0 1.8 %broadcast_in_dim.2 = bf16[8,32,1024]{2,1,0:T(8,128)(2,1)} broadcast(bf16[32,1024]{1,0:T(8,128)(2,1)} %param.10), dimensions={1,2} | broadcast | bytes 589824 | tf_op jit(solution)/shard_map/broadcast_in_dim | solution.py:171
  1.8 15.6 %all-to-all-start = ((bf16[8,32,1024]{2,1,0:T(8,128)(2,1)}), bf16[8,32,1024]{2,1,0:T(8,128)(2,1)}, u32[]{:S(2)}, u32[]{:S(2)}) async-start(bf16[8,32,1024]{2,1,0:T(8,128)(2,1)} %broadcast_in_dim.2), calls=%async_computation | async-start | bytes 1048576 | tf_op jit(solution)/shard_map/all_to_all | solution.py:171
  18.4 0.9 fusion.1
  19.3 4.6 %collective-permute-start = (bf16[64,1408]{1,0:T(8,128)(2,1)S(1)}, bf16[64,1408]{1,0:T(8,128)(2,1)S(1)}, u32[]{:S(2)}, u32[]{:S(2)}) collective-permute-start(bf16[64,1408]{1,0:T(8,128)(2,1)S(1)} %fusion.1), channel_id=1, source_target_pairs={{0,257},{257,0},{1,256},{256,1},{2,259},{259,2},{3,258},{258,3},{4... | collective-permute-start | bytes 540680 | tf_op jit(solution)/shard_map/ppermute | solution.py:182
  24.0 3.6 %collective-permute-done = bf16[64,1408]{1,0:T(8,128)(2,1)S(1)} collective-permute-done((bf16[64,1408]{1,0:T(8,128)(2,1)S(1)}, bf16[64,1408]{1,0:T(8,128)(2,1)S(1)}, u32[]{:S(2)}, u32[]{:S(2)}) %collective-permute-start) | collective-permute-done | bytes 180256 | tf_op jit(solution)/shard_map/ppermute | solution.py:182
  28.4 3.1 %collective-permute-start.2 = (bf16[128,1408]{1,0:T(8,128)(2,1)}, bf16[128,1408]{1,0:T(8,128)(2,1)S(1)}, u32[]{:S(2)}, u32[]{:S(2)}) collective-permute-start(bf16[128,1408]{1,0:T(8,128)(2,1)} %pad_maximum_fusion.refs_0_), channel_id=1, source_target_pairs={{6,0},{0,2},{2,4},{4,6},{7,1},{1,3},{3,5},{5,7},{14,8},{8,10},{10,... | collective-permute-start | bytes 1081352 | tf_op jit(solution)/shard_map/ppermute | solution.py:185
  31.5 3.4 %collective-permute-start.1 = (bf16[128,1408]{1,0:T(8,128)(2,1)}, bf16[128,1408]{1,0:T(8,128)(2,1)S(1)}, u32[]{:S(2)}, u32[]{:S(2)}) collective-permute-start(bf16[128,1408]{1,0:T(8,128)(2,1)} %pad_maximum_fusion.refs_0_), channel_id=1, source_target_pairs={{2,0},{4,2},{6,4},{0,6},{3,1},{5,3},{7,5},{1,7},{10,8},{12,10},{14... | collective-permute-start | bytes 1081352 | tf_op jit(solution)/shard_map/ppermute | solution.py:184
  36.5 1.6 %shard_map.82 = (f32[128,1024]{1,0:T(8,128)S(1)}, bf16[128,1024]{1,0:T(8,128)(2,1)S(1)}, f32[128,128]{1,0:T(8,128)S(1)}) custom-call(bf16[128,1408]{1,0:T(8,128)(2,1)} %pad_maximum_fusion.refs_0_, bf16[1280,1024]{1,0:T(8,128)(2,1)S(1)} %copy-done), custom_call_target="tpu_custom_call" | custom-call | flops 335544320 | bytes 4194304 | tf_op jit(solution)/shard_map/pallas_call | solution.py:42
  39.9 1.6 %collective-permute-done.1.refs_0_.refs_1_ = bf16[128,1408]{1,0:T(8,128)(2,1)S(1)} collective-permute-done((bf16[128,1408]{1,0:T(8,128)(2,1)}, bf16[128,1408]{1,0:T(8,128)(2,1)S(1)}, u32[]{:S(2)}, u32[]{:S(2)}) %collective-permute-start.1) | collective-permute-done | bytes 360480 | tf_op jit(solution)/shard_map/ppermute | solution.py:184
  41.6 1.9 %all-to-all-done = bf16[8,32,1024]{2,1,0:T(8,128)(2,1)} async-done(((bf16[8,32,1024]{2,1,0:T(8,128)(2,1)}), bf16[8,32,1024]{2,1,0:T(8,128)(2,1)}, u32[]{:S(2)}, u32[]{:S(2)}) %all-to-all-start) | async-done | bytes 524320 | tf_op jit(solution)/shard_map/all_to_all | solution.py:171
  43.4 3.6 %collective-permute-start.4 = (bf16[256,1024]{1,0:T(8,128)(2,1)}, bf16[256,1024]{1,0:T(8,128)(2,1)S(1)}, u32[]{:S(2)}, u32[]{:S(2)}) collective-permute-start(bf16[256,1024]{1,0:T(8,128)(2,1)} %shard_map.85.a_ref), channel_id=1, source_target_pairs={{8,0},{16,8},{24,16},{32,24},{40,32},{48,40},{56,48},{64,56},{72,6... | collective-permute-start | bytes 1572872 | tf_op jit(solution)/shard_map/ppermute | solution.py:129
  47.1 3.1 %collective-permute-start.3 = (bf16[128,1408]{1,0:T(8,128)(2,1)S(1)}, bf16[128,1408]{1,0:T(8,128)(2,1)S(1)}, u32[]{:S(2)}, u32[]{:S(2)}) collective-permute-start(bf16[128,1408]{1,0:T(8,128)(2,1)S(1)} %broadcast_select_fusion), channel_id=1, source_target_pairs={{2,0},{4,2},{6,4},{0,6},{134,128},{128,130},{130,132},{132,134},{3... | collective-permute-start | bytes 1081352 | tf_op jit(solution)/shard_map/ppermute | solution.py:129
  50.2 1.0 shard_map.83
  51.2 5.3 %collective-permute-done.3.refs_0_.refs_3_ = bf16[128,1408]{1,0:T(8,128)(2,1)S(1)} collective-permute-done((bf16[128,1408]{1,0:T(8,128)(2,1)S(1)}, bf16[128,1408]{1,0:T(8,128)(2,1)S(1)}, u32[]{:S(2)}, u32[]{:S(2)}) %collective-permute-start.3) | collective-permute-done | bytes 360480 | tf_op jit(solution)/shard_map/ppermute | solution.py:129
  56.5 1.1 shard_map.86.refs_8_
  57.6 6.2 %collective-permute-start.5 = (bf16[512,1024]{1,0:T(8,128)(2,1)S(1)}, bf16[512,1024]{1,0:T(8,128)(2,1)S(1)}, u32[]{:S(2)}, u32[]{:S(2)}) collective-permute-start(bf16[512,1024]{1,0:T(8,128)(2,1)S(1)} %shard_map.86.refs_8_), channel_id=1, source_target_pairs={{0,128},{128,0},{1,129},{129,1},{2,130},{130,2},{3,131},{131,3},{4... | collective-permute-start | bytes 3145736 | tf_op jit(solution)/shard_map/ppermute | solution.py:163
  64.5 2.9 %shard_map.87.refs_15_ = f32[512,1024]{1,0:T(8,128)S(1)} custom-call(f32[2]{0:T(128)S(1)} %pad_maximum_fusion.2.refs_6_.scale_ref, bf16[128,1408]{1,0:T(8,128)(2,1)} %pad_maximum_fusion.refs_0_, bf16[128,1408]{1,0:T(8,128)(2,1)S(1)} %collective-permute-done.1.refs_0_.refs_1_, bf16[128,1408]{1,0:T(8,128)(2,1)S(1)} %collective-permute-done.2.refs_1_.refs_2_, ...), custom_call_target="tpu_custom_call" | custom-call | flops 1073741824 | bytes 4194304 | tf_op jit(solution)/shard_map/pallas_call | solution.py:199
  67.4 4.2 %shard_map.88 = bf16[16,256,128]{2,1,0:T(8,128)(2,1)S(1)} custom-call(f32[2]{0:T(128)S(1)} %pad_maximum_fusion.2.refs_6_.scale_ref, s32[4]{0:T(128)S(1)} %pad_add_fusion.refs_5_.place_ref, bf16[128,1408]{1,0:T(8,128)(2,1)} %pad_maximum_fusion.refs_0_, bf16[128,1408]{1,0:T(8,128)(2,1)S(1)} %collective-permute-done.1.refs_0_.refs_1_, ...), custom_call_target="tpu_custom_call" | custom-call | flops 1610612736 | bytes 8388608 | tf_op jit(solution)/shard_map/pallas_call | solution.py:207
  71.7 23.0 %all_to_all.15.g_ref = bf16[16,256,128]{2,1,0:T(8,128)(2,1)S(1)} all-to-all(bf16[16,256,128]{2,1,0:T(8,128)(2,1)S(1)} %shard_map.88), channel_id=1, replica_groups=mesh['ylo'=2,'core'=2,'zp'=8,'par'=2,'x'=4,'yhi'=2] {'x','yhi','ylo'}, dimensions={0} | all-to-all | bytes 2097152 | tf_op jit(solution)/shard_map/all_to_all | solution.py:216
  94.8 2.4 %collective-permute-start.6 = (bf16[256,128]{1,0:T(8,128)(2,1)S(1)}, bf16[256,128]{1,0:T(8,128)(2,1)S(1)}, u32[]{:S(2)}, u32[]{:S(2)}) collective-permute-start(bf16[256,128]{1,0:T(8,128)(2,1)S(1)} %shard_map.89.mine_ref), channel_id=1, source_target_pairs={{0,256},{256,0},{1,257},{257,1},{2,258},{258,2},{3,259},{259,3},{4... | collective-permute-start | bytes 196616 | tf_op jit(solution)/shard_map/ppermute | solution.py:163
  97.2 2.6 %collective-permute-done.6.other_ref = bf16[256,128]{1,0:T(8,128)(2,1)S(1)} collective-permute-done((bf16[256,128]{1,0:T(8,128)(2,1)S(1)}, bf16[256,128]{1,0:T(8,128)(2,1)S(1)}, u32[]{:S(2)}, u32[]{:S(2)}) %collective-permute-start.6) | collective-permute-done | bytes 65568 | tf_op jit(solution)/shard_map/ppermute | solution.py:163
  99.8 1.5 %shard_map.90 = (f32[16,8,320]{2,1,0:T(8,128)S(1)}, bf16[16,8,320]{2,1,0:T(8,128)(2,1)S(1)}) custom-call(s32[4]{0:T(128)S(1)} %pad_add_fusion.refs_5_.place_ref, bf16[256,128]{1,0:T(8,128)(2,1)S(1)} %shard_map.89.mine_ref, bf16[256,128]{1,0:T(8,128)(2,1)S(1)} %collective-permute-done.6.other_ref, bf16[128,1408]{1,0:T(8,128)(2,1)} %pad_maximum_fusion.refs_0_, ...), custom_call_target="tpu_custom_call" | custom-call | tf_op jit(solution)/shard_map/pallas_call | solution.py:220
  101.2 5.4 %collective-permute-start.7 = (bf16[16,8,320]{2,1,0:T(8,128)(2,1)S(1)}, bf16[16,8,320]{2,1,0:T(8,128)(2,1)S(1)}, u32[]{:S(2)}, u32[]{:S(2)}) collective-permute-start(bf16[16,8,320]{2,1,0:T(8,128)(2,1)S(1)} %get-tuple-element.26), channel_id=1, source_target_pairs={{0,128},{128,0},{1,129},{129,1},{2,130},{130,2},{3,131},{131,3},{4... | collective-permute-start | bytes 245768 | tf_op jit(solution)/shard_map/ppermute | solution.py:163
  107.6 18.9 %all_to_all.16 = bf16[16,8,320]{2,1,0:T(8,128)(2,1)S(1)} all-to-all(bf16[16,8,320]{2,1,0:T(8,128)(2,1)S(1)} %shard_map.91), channel_id=1, replica_groups=mesh['ylo'=2,'core'=2,'zp'=8,'par'=2,'x'=4,'yhi'=2] {'zp','par'}, dimensions={0} | all-to-all | bytes 163840 | tf_op jit(solution)/shard_map/all_to_all | solution.py:235
  (35 shorter events, 6.2 us)
Async XLA Ops:
  0.0 34.9 %copy-start.6 = (s32[256]{0:T(256)S(1)}, s32[256]{0:T(256)}, u32[]{:S(2)}) copy-start(s32[256]{0:T(256)} %constant.54) | copy-start | bytes 3076
  0.0 36.5 %copy-start = (bf16[1280,1024]{1,0:T(8,128)(2,1)S(1)}, bf16[1280,1024]{1,0:T(8,128)(2,1)}, u32[]{:S(2)}) copy-start(bf16[1280,1024]{1,0:T(8,128)(2,1)} %refs_1_.3) | copy-start | bytes 7864324
  1.8 41.6 %all-to-all-start = ((bf16[8,32,1024]{2,1,0:T(8,128)(2,1)}), bf16[8,32,1024]{2,1,0:T(8,128)(2,1)}, u32[]{:S(2)}, u32[]{:S(2)}) async-start(bf16[8,32,1024]{2,1,0:T(8,128)(2,1)} %broadcast_in_dim.2), calls=%async_computation | async-start | bytes 1048576 | tf_op jit(solution)/shard_map/all_to_all | solution.py:171
  19.3 8.4 %collective-permute-start = (bf16[64,1408]{1,0:T(8,128)(2,1)S(1)}, bf16[64,1408]{1,0:T(8,128)(2,1)S(1)}, u32[]{:S(2)}, u32[]{:S(2)}) collective-permute-start(bf16[64,1408]{1,0:T(8,128)(2,1)S(1)} %fusion.1), channel_id=1, source_target_pairs={{0,257},{257,0},{1,256},{256,1},{2,259},{259,2},{3,258},{258,3},{4... | collective-permute-start | bytes 540680 | tf_op jit(solution)/shard_map/ppermute | solution.py:182
  28.4 11.5 %collective-permute-start.2 = (bf16[128,1408]{1,0:T(8,128)(2,1)}, bf16[128,1408]{1,0:T(8,128)(2,1)S(1)}, u32[]{:S(2)}, u32[]{:S(2)}) collective-permute-start(bf16[128,1408]{1,0:T(8,128)(2,1)} %pad_maximum_fusion.refs_0_), channel_id=1, source_target_pairs={{6,0},{0,2},{2,4},{4,6},{7,1},{1,3},{3,5},{5,7},{14,8},{8,10},{10,... | collective-permute-start | bytes 1081352 | tf_op jit(solution)/shard_map/ppermute | solution.py:185
  31.5 10.0 %collective-permute-start.1 = (bf16[128,1408]{1,0:T(8,128)(2,1)}, bf16[128,1408]{1,0:T(8,128)(2,1)S(1)}, u32[]{:S(2)}, u32[]{:S(2)}) collective-permute-start(bf16[128,1408]{1,0:T(8,128)(2,1)} %pad_maximum_fusion.refs_0_), channel_id=1, source_target_pairs={{2,0},{4,2},{6,4},{0,6},{3,1},{5,3},{7,5},{1,7},{10,8},{12,10},{14... | collective-permute-start | bytes 1081352 | tf_op jit(solution)/shard_map/ppermute | solution.py:184
  38.1 0.7 copy-start.2
  38.8 0.8 copy-start.4
  43.4 13.0 %collective-permute-start.4 = (bf16[256,1024]{1,0:T(8,128)(2,1)}, bf16[256,1024]{1,0:T(8,128)(2,1)S(1)}, u32[]{:S(2)}, u32[]{:S(2)}) collective-permute-start(bf16[256,1024]{1,0:T(8,128)(2,1)} %shard_map.85.a_ref), channel_id=1, source_target_pairs={{8,0},{16,8},{24,16},{32,24},{40,32},{48,40},{56,48},{64,56},{72,6... | collective-permute-start | bytes 1572872 | tf_op jit(solution)/shard_map/ppermute | solution.py:129
  47.1 9.4 %collective-permute-start.3 = (bf16[128,1408]{1,0:T(8,128)(2,1)S(1)}, bf16[128,1408]{1,0:T(8,128)(2,1)S(1)}, u32[]{:S(2)}, u32[]{:S(2)}) collective-permute-start(bf16[128,1408]{1,0:T(8,128)(2,1)S(1)} %broadcast_select_fusion), channel_id=1, source_target_pairs={{2,0},{4,2},{6,4},{0,6},{134,128},{128,130},{130,132},{132,134},{3... | collective-permute-start | bytes 1081352 | tf_op jit(solution)/shard_map/ppermute | solution.py:129
  57.6 7.0 %copy-start.3 = (bf16[128,1024]{1,0:T(8,128)(2,1)S(1)}, bf16[128,1024]{1,0:T(8,128)(2,1)}, u32[]{:S(2)}) copy-start(bf16[128,1024]{1,0:T(8,128)(2,1)} %copy-done.2) | copy-start | bytes 786436
  57.6 9.8 %collective-permute-start.5 = (bf16[512,1024]{1,0:T(8,128)(2,1)S(1)}, bf16[512,1024]{1,0:T(8,128)(2,1)S(1)}, u32[]{:S(2)}, u32[]{:S(2)}) collective-permute-start(bf16[512,1024]{1,0:T(8,128)(2,1)S(1)} %shard_map.86.refs_8_), channel_id=1, source_target_pairs={{0,128},{128,0},{1,129},{129,1},{2,130},{130,2},{3,131},{131,3},{4... | collective-permute-start | bytes 3145736 | tf_op jit(solution)/shard_map/ppermute | solution.py:163
  64.5 2.9 %copy-start.1 = (bf16[1024,1024]{1,0:T(8,128)(2,1)S(1)}, bf16[1024,1024]{1,0:T(8,128)(2,1)}, u32[]{:S(2)}) copy-start(bf16[1024,1024]{1,0:T(8,128)(2,1)} %constant.50.clone.refs_16_) | copy-start | bytes 6291460
  64.5 2.9 %copy-start.5 = (f32[128,1024]{1,0:T(8,128)S(1)}, f32[128,1024]{1,0:T(8,128)}, u32[]{:S(2)}) copy-start(f32[128,1024]{1,0:T(8,128)} %copy-done.4) | copy-start | bytes 1572868
  94.8 5.0 %collective-permute-start.6 = (bf16[256,128]{1,0:T(8,128)(2,1)S(1)}, bf16[256,128]{1,0:T(8,128)(2,1)S(1)}, u32[]{:S(2)}, u32[]{:S(2)}) collective-permute-start(bf16[256,128]{1,0:T(8,128)(2,1)S(1)} %shard_map.89.mine_ref), channel_id=1, source_target_pairs={{0,256},{256,0},{1,257},{257,1},{2,258},{258,2},{3,259},{259,3},{4... | collective-permute-start | bytes 196616 | tf_op jit(solution)/shard_map/ppermute | solution.py:163
  101.2 6.3 %collective-permute-start.7 = (bf16[16,8,320]{2,1,0:T(8,128)(2,1)S(1)}, bf16[16,8,320]{2,1,0:T(8,128)(2,1)S(1)}, u32[]{:S(2)}, u32[]{:S(2)}) collective-permute-start(bf16[16,8,320]{2,1,0:T(8,128)(2,1)S(1)} %get-tuple-element.26), channel_id=1, source_target_pairs={{0,128},{128,0},{1,129},{129,1},{2,130},{130,2},{3,131},{131,3},{4... | collective-permute-start | bytes 245768 | tf_op jit(solution)/shard_map/ppermute | solution.py:163

commit v12 on v7

--- a/solution.py
+++ b/solution.py
@@ -24,27 +24,8 @@
     return jnp.asarray(goes[:, None] == was[None, :], BF)
 
 
-def project_kernel(place_ref, own_ref, next_ref, across_ref, last_ref, w_ref, x_ref, t_ref, unit_ref, unit_b_ref, mag_ref, held, sems):
-    e = w_ref.shape[0]
-    step = e // 4
-    copies = []
-    for c in range(4):
-        some = pl.ds(c * step, step)
-        copies.append(pltpu.make_async_copy(w_ref.at[some], held.at[some], sems.at[c]))
-        copies[-1].start()
-    x, yhi = place_ref[3], place_ref[0]
-    for k, ref in enumerate((own_ref, next_ref, across_ref, last_ref)):
-        for h in range(2):
-            half = yhi if h == 0 else 1 - yhi
-            at = pl.ds(pl.multiple_of(lax.rem(x + k, 4) * 128 + half * 64, 64), 64)
-            x_ref[at, :] = ref[64 * h : 64 * (h + 1), :e]
-            t_ref[at, :] = ref[64 * h : 64 * (h + 1), e:]
-    projected = None
-    for c, copy in enumerate(copies):
-        copy.wait()
-        some = slice(c * step, (c + 1) * step)
-        term = jnp.dot(x_ref[:, some], held[some], preferred_element_type=F32)
-        projected = term if projected is None else projected + term
+def project_kernel(x_ref, w_ref, unit_ref, unit_b_ref, mag_ref):
+    projected = jnp.dot(x_ref[:, : w_ref.shape[0]], w_ref[...], preferred_element_type=F32)
     mag = jnp.sqrt(jnp.sum(projected * projected, axis=1, keepdims=True) + 1e-06)
     unit = projected / mag
     unit_ref[...] = unit
@@ -52,12 +33,12 @@
     mag_ref[...] = jnp.broadcast_to(mag, mag_ref.shape)
 
 
-def pair_kernel(scale_ref, t_ref, unit_ref, unit_b_ref, mag_ref, ids_ref, order_ref, *refs):
+def pair_kernel(scale_ref, x_ref, unit_ref, unit_b_ref, mag_ref, ids_ref, order_ref, *refs):
     *audio_refs, out_ref = refs
     cold = scale_ref[0]
     offset = scale_ref[1]
     unit_b = unit_b_ref[...]
-    halves = t_ref[...].astype(F32)
+    halves = x_ref[:, 1280:].astype(F32)
     targets = [halves[:, 2 * p : 2 * p + 1] * 128.0 + halves[:, 2 * p + 1 : 2 * p + 2] for p in range(5)]
     total = None
     at = 0
@@ -110,9 +91,9 @@
     out_ref[...] = (a_ref[...] + b_ref[...].astype(F32)).astype(BF)
 
 
-def fetch(a, axes, n):
-    perm = [((i + 1) % n, i) for i in range(n)] + [(n + (i - 1) % n, n + i) for i in range(n)]
-    return lax.ppermute(a, ("core", *axes), perm)
+def fetch(a):
+    perm = [((i + 1) % 16, i) for i in range(16)] + [(16 + (i - 1) % 16, 16 + i) for i in range(16)]
+    return lax.ppermute(a, ("core", *Z), perm)
 
 
 def behind(a, *others):
@@ -136,43 +117,39 @@
     smem = pl.BlockSpec(memory_space=pltpu.SMEM)
     vmem = pl.BlockSpec(memory_space=pltpu.VMEM)
 
-    even = lax.all_to_all(jnp.broadcast_to(sounds[None], (8, 32, 1024)), "zp", 0, 0, tiled=True).reshape(256, 1024)
     pars = jnp.stack([par, par, 1 - par, 1 - par])
     cores = jnp.stack([core, 1 - core, core, 1 - core])
     firsts = ylo * 8192 + cores * 4096 + pars * 256 + (2 * x + yhi) * 32
     inside = np.arange(8)[:, None] * 512 + np.arange(32)[None, :]
     ids = (firsts[:, None] + jnp.asarray(inside.reshape(1, 256), jnp.int32)).astype(F32).reshape(1, 1024)
     place = jnp.stack([yhi, ylo, core, x]).astype(jnp.int32)
+    scale = jnp.concatenate([coldness, offset])
 
     halves = jnp.stack([matched >> 7, matched & 127], axis=2).reshape(128, 10).astype(BF)
     wide = jnp.concatenate([frames, jnp.pad(halves, ((0, 0), (0, PAD - 10)))], axis=1)
     wide = lax.dynamic_slice_in_dim(wide, core * 64, 64, 0)
-    across = lax.ppermute(wide, ("ylo", "yhi"), [(0, 3), (3, 0), (1, 2), (2, 1)])
-    wide = jnp.concatenate([wide, across], axis=0)
-    after = lax.ppermute(wide, "x", [((i + 1) % 4, i) for i in range(4)])
-    before = lax.ppermute(wide, "x", [((i - 1) % 4, i) for i in range(4)])
-    opposite = fetch(jnp.where(core == 0, after, before), ("x",), 4)
-
-    even = behind(even, after, before)
-    odd = fetch(even, Z, 16)
+    rows = lax.all_to_all(jnp.broadcast_to(wide[None], (8, 64, 1280 + PAD)), ("x", "yhi"), 0, 0, tiled=True)
+    rows = rows.reshape(512, 1280 + PAD)
+
+    even = lax.all_gather(sounds, "zp", axis=0, tiled=True)
+    even = behind(even, ids, place, scale)
+    odd = fetch(even)
     far_even = swap(even, "core")
-    far_odd = swap(odd, "core")
-
-    rows, *video = pl.pallas_call(
+    units = pl.pallas_call(
         project_kernel,
-        in_specs=[smem] + [vmem] * 4 + [pl.BlockSpec(memory_space=pltpu.HBM)],
-        out_specs=[vmem] * 5,
+        in_specs=[vmem] * 2,
+        out_specs=[vmem] * 3,
         out_shape=[
-            jax.ShapeDtypeStruct((512, 1280), BF),
-            jax.ShapeDtypeStruct((512, PAD), BF),
             jax.ShapeDtypeStruct((512, 1024), F32),
             jax.ShapeDtypeStruct((512, 1024), BF),
             jax.ShapeDtypeStruct((512, 128), F32),
         ],
-        scratch_shapes=[pltpu.VMEM((1280, 1024), BF), pltpu.SemaphoreType.DMA((4,))],
         compiler_params=PARAMS,
         cost_estimate=pl.CostEstimate(flops=2 * 512 * 1280 * 1024, bytes_accessed=9 * 2**20, transcendentals=0),
-    )(place, wide, after, opposite, before, pltpu.with_memory_space_constraint(projector, pltpu.HBM))
+    )(rows, projector)
+    odd = behind(odd, units[2])
+    far_odd = swap(odd, "core")
+
     parts = pl.pallas_call(
         pair_kernel,
         in_specs=[smem] + [vmem] * 10,
@@ -181,8 +158,9 @@
         compiler_params=PARAMS,
         cost_estimate=pl.CostEstimate(flops=5 * 512 * 1024 * 1024, bytes_accessed=8 * 2**20, transcendentals=2**20),
     )(
-        jnp.concatenate([coldness, offset]),
-        *video,
+        scale,
+        rows,
+        *units,
         ids,
         column_order(),
         even,

time: 127 us -> 126 us (level)
  blocking collectives: 41.9 us -> 75.4 us
  starting transfers between devices: 50.4 us -> 29.1 us
  waiting for transfers between devices: 16.5 us -> 5.12 us
  Pallas kernels: 11.2 us -> 8.34 us
  local copies, waits for them, and re-layouts: 1.87 us -> 3.16 us
    all_gather x0 -> x1, blocking collectives: none -> 33.4 us  [local(): even = lax.all_gather(sounds, 'zp', axis=0, tiled=True)]
    ppermute x5 -> x1, starting transfers between devices: 17.6 us -> 2.5 us  [fetch(): return lax.ppermute(a, ('core', *Z), perm)]
    ppermute x5 -> x1, waiting for transfers between devices: 12.7 us -> 0.01 us  [fetch(): return lax.ppermute(a, ('core', *Z), perm)]
    all_to_all x1, starting transfers between devices: 15.6 us -> 7.48 us  [local(): lax.all_to_all(jnp.broadcast_to(wide[None], (8, 64, 1280 + PAD)), ('x', '...]
    pallas_call x1, Pallas kernels: 4.73 us -> 1.75 us  [local(): pl.pallas_call(project_kernel, in_specs=[vmem] * 2, out_specs=[vmem] * 3,...]
    ppermute x4, starting transfers between devices: 17.1 us -> 19.1 us  [swap(): return lax.ppermute(a, axis, [(0, 1), (1, 0)])]
    unnamed x5 -> x10, local copies, waits for them, and re-layouts: 0.02 us -> 1.9 us
    ppermute x4, waiting for transfers between devices: 3.47 us -> 5.11 us  [swap(): return lax.ppermute(a, axis, [(0, 1), (1, 0)])]
  transfers between devices with their start and end apart: 10 -> 6, of which waited for: 6 -> 3; matrix products, arithmetic and copies ran while one was open for 2% -> 0% of each run, Pallas kernels for 4% -> 1%
where the time goes in v12:
time: 126 us; the launch traced here: 125 us
  blocking collectives  75.4 us (60%)
  starting transfers between devices  29.1 us (23%)
  Pallas kernels  8.34 us (7%)
  waiting for transfers between devices  5.12 us (4%)
  local copies, waits for them, and re-layouts  3.16 us (3%)
  other arithmetic  2.56 us (2%)
  between operations  1.44 us (1%)
    all_gather x1, blocking collectives, local(): even = lax.all_gather(sounds, 'zp', axis=0, tiled=True)  33.4 us
    all_to_all x1, blocking collectives, local(): terms = lax.all_to_all(parts, PLANE, 0, 0, tiled=True)  23 us
    ppermute x4, starting transfers between devices, swap(): return lax.ppermute(a, axis, [(0, 1), (1, 0)])  19.1 us
    all_to_all x1, blocking collectives, local(): sums = lax.all_to_all(mine, Z, 0, 0, tiled=True)  19.1 us
    all_to_all x1, starting transfers between devices, local(): lax.all_to_all(jnp.broadcast_to(wide[None], (8, 64, 1280 + PAD)), ('x', '...  7.48 us
    pallas_call x1, Pallas kernels, local(): pl.pallas_call(pair_kernel, in_specs=[smem] + [vmem] * 10, out_specs=vmem...  5.45 us
    ppermute x4, waiting for transfers between devices, swap(): return lax.ppermute(a, axis, [(0, 1), (1, 0)])  5.11 us
  transfers between devices with their start and end apart: 6, of which 3 were waited for; matrix products, arithmetic and copies ran while one was open for 0% of the time, Pallas kernels for 1%

profile of v12, /device:TPU:1, one launch (start us, length us, event | category | flops | bytes accessed | tf_op | source)
XLA Modules:
  0.0 125.1 jit_solution(4266324762266089600)
XLA Ops:
  0.0 0.7 fusion.2
  0.7 0.1 copy.13
  0.9 0.9 fusion.1
  1.8 1.2 broadcast_in_dim.2
  3.1 7.5 %all-to-all-start = ((bf16[8,64,1408]{2,1,0:T(8,128)(2,1)}), bf16[8,64,1408]{2,1,0:T(8,128)(2,1)S(1)}, u32[]{:S(2)}, u32[]{:S(2)}) async-start(bf16[8,64,1408]{2,1,0:T(8,128)(2,1)} %broadcast_in_dim.2), calls=%async_computation | async-start | bytes 2883584 | tf_op jit(solution)/shard_map/all_to_all | solution.py:131
  11.8 0.1 fusion.6
  12.1 0.1 pad_add_fusion.refs_2_.place_ref
  12.2 33.4 %all_gather.3.refs_0_ = bf16[256,1024]{1,0:T(8,128)(2,1)S(1)} all-gather(bf16[32,1024]{1,0:T(8,128)(2,1)S(1)} %copy-done.2), channel_id=1, replica_groups=mesh['ylo'=2,'core'=2,'zp'=8,'par'=2,'x'=4,'yhi'=2] {'zp'}, dimensions={0}, use_global_device_ids=true | all-gather | bytes 589824 | tf_op jit(solution)/shard_map/all_gather | solution.py:134
  45.5 2.5 %collective-permute-start.1 = (bf16[256,1024]{1,0:T(8,128)(2,1)S(1)}, bf16[256,1024]{1,0:T(8,128)(2,1)S(1)}, u32[]{:S(2)}, u32[]{:S(2)}) collective-permute-start(bf16[256,1024]{1,0:T(8,128)(2,1)S(1)} %shard_map.83.refs_0_), channel_id=1, source_target_pairs={{8,0},{16,8},{24,16},{32,24},{40,32},{48,40},{56,48},{64,56},{72,6... | collective-permute-start | bytes 1572872 | tf_op jit(solution)/shard_map/ppermute | solution.py:96
  48.0 8.4 %collective-permute-start = (bf16[256,1024]{1,0:T(8,128)(2,1)S(1)}, bf16[256,1024]{1,0:T(8,128)(2,1)S(1)}, u32[]{:S(2)}, u32[]{:S(2)}) collective-permute-start(bf16[256,1024]{1,0:T(8,128)(2,1)S(1)} %shard_map.83.refs_0_), channel_id=1, source_target_pairs={{0,128},{128,0},{1,129},{129,1},{2,130},{130,2},{3,131},{131,3},{4... | collective-permute-start | bytes 1572872 | tf_op jit(solution)/shard_map/ppermute | solution.py:112
  56.4 1.7 %copy-done.1 = bf16[1280,1024]{1,0:T(8,128)(2,1)S(1)} copy-done((bf16[1280,1024]{1,0:T(8,128)(2,1)S(1)}, bf16[1280,1024]{1,0:T(8,128)(2,1)}, u32[]{:S(2)}) %copy-start.1) | copy-done | bytes 2621464
  58.2 1.8 %shard_map.82 = (f32[512,1024]{1,0:T(8,128)S(1)}, bf16[512,1024]{1,0:T(8,128)(2,1)S(1)}, f32[512,128]{1,0:T(8,128)S(1)}) custom-call(bf16[512,1408]{1,0:T(8,128)(2,1)S(1)} %bitcast.19, bf16[1280,1024]{1,0:T(8,128)(2,1)S(1)} %copy-done.1), custom_call_target="tpu_custom_call" | custom-call | flops 1342177280 | bytes 9437184 | tf_op jit(solution)/shard_map/pallas_call | solution.py:138
  59.9 3.3 %collective-permute-start.2 = (bf16[256,1024]{1,0:T(8,128)(2,1)S(1)}, bf16[256,1024]{1,0:T(8,128)(2,1)S(1)}, u32[]{:S(2)}, u32[]{:S(2)}) collective-permute-start(bf16[256,1024]{1,0:T(8,128)(2,1)S(1)} %shard_map.84.refs_2_), channel_id=1, source_target_pairs={{0,128},{128,0},{1,129},{129,1},{2,130},{130,2},{3,131},{131,3},{4... | collective-permute-start | bytes 1572872 | tf_op jit(solution)/shard_map/ppermute | solution.py:112
  63.2 1.5 %collective-permute-done.2.refs_3_ = bf16[256,1024]{1,0:T(8,128)(2,1)S(1)} collective-permute-done((bf16[256,1024]{1,0:T(8,128)(2,1)S(1)}, bf16[256,1024]{1,0:T(8,128)(2,1)S(1)}, u32[]{:S(2)}, u32[]{:S(2)}) %collective-permute-start.2) | collective-permute-done | bytes 524320 | tf_op jit(solution)/shard_map/ppermute | solution.py:112
  64.7 5.4 %shard_map.85 = bf16[16,256,128]{2,1,0:T(8,128)(2,1)S(1)} custom-call(f32[2]{0:T(128)S(1)} %pad_maximum_fusion.1.refs_3_.scale_ref, bf16[512,1408]{1,0:T(8,128)(2,1)S(1)} %bitcast.20, f32[512,1024]{1,0:T(8,128)S(1)} %get-tuple-element.10.unit_ref, bf16[512,1024]{1,0:T(8,128)(2,1)S(1)} %get-tuple-element.11.unit_b_ref, ...), custom_call_target="tpu_custom_call" | custom-call | flops 2684354560 | bytes 8388608 | tf_op jit(solution)/shard_map/pallas_call | solution.py:153
  70.2 23.0 %all_to_all.15.g_ref = bf16[16,256,128]{2,1,0:T(8,128)(2,1)S(1)} all-to-all(bf16[16,256,128]{2,1,0:T(8,128)(2,1)S(1)} %shard_map.85), channel_id=1, replica_groups=mesh['ylo'=2,'core'=2,'zp'=8,'par'=2,'x'=4,'yhi'=2] {'x','yhi','ylo'}, dimensions={0} | all-to-all | bytes 2097152 | tf_op jit(solution)/shard_map/all_to_all | solution.py:172
  93.2 0.1 shard_map.86.mine_ref
  93.3 2.3 %collective-permute-start.3 = (bf16[256,128]{1,0:T(8,128)(2,1)S(1)}, bf16[256,128]{1,0:T(8,128)(2,1)S(1)}, u32[]{:S(2)}, u32[]{:S(2)}) collective-permute-start(bf16[256,128]{1,0:T(8,128)(2,1)S(1)} %shard_map.86.mine_ref), channel_id=1, source_target_pairs={{0,256},{256,0},{1,257},{257,1},{2,258},{258,2},{3,259},{259,3},{4... | collective-permute-start | bytes 196616 | tf_op jit(solution)/shard_map/ppermute | solution.py:112
  95.7 2.7 %collective-permute-done.3.other_ref = bf16[256,128]{1,0:T(8,128)(2,1)S(1)} collective-permute-done((bf16[256,128]{1,0:T(8,128)(2,1)S(1)}, bf16[256,128]{1,0:T(8,128)(2,1)S(1)}, u32[]{:S(2)}, u32[]{:S(2)}) %collective-permute-start.3) | collective-permute-done | bytes 65568 | tf_op jit(solution)/shard_map/ppermute | solution.py:112
  98.4 1.0 shard_map.87
  99.3 5.1 %collective-permute-start.4 = (bf16[16,8,320]{2,1,0:T(8,128)(2,1)S(1)}, bf16[16,8,320]{2,1,0:T(8,128)(2,1)S(1)}, u32[]{:S(2)}, u32[]{:S(2)}) collective-permute-start(bf16[16,8,320]{2,1,0:T(8,128)(2,1)S(1)} %get-tuple-element.14), channel_id=1, source_target_pairs={{0,128},{128,0},{1,129},{129,1},{2,130},{130,2},{3,131},{131,3},{4... | collective-permute-start | bytes 245768 | tf_op jit(solution)/shard_map/ppermute | solution.py:112
  104.5 0.9 collective-permute-done.4.b_ref
  105.4 19.1 %all_to_all.16 = bf16[16,8,320]{2,1,0:T(8,128)(2,1)S(1)} all-to-all(bf16[16,8,320]{2,1,0:T(8,128)(2,1)S(1)} %shard_map.88), channel_id=1, replica_groups=mesh['ylo'=2,'core'=2,'zp'=8,'par'=2,'x'=4,'yhi'=2] {'zp','par'}, dimensions={0} | all-to-all | bytes 163840 | tf_op jit(solution)/shard_map/all_to_all | solution.py:190
  124.5 0.6 convert_reduce_fusion
  (19 shorter events, 0.3 us)
Async XLA Ops:
  1.8 10.1 %copy-start.3 = (s32[256]{0:T(256)S(1)}, s32[256]{0:T(256)}, u32[]{:S(2)}) copy-start(s32[256]{0:T(256)} %constant.54) | copy-start | bytes 3076
  1.8 10.4 %copy-start.2 = (bf16[32,1024]{1,0:T(8,128)(2,1)S(1)}, bf16[32,1024]{1,0:T(8,128)(2,1)}, u32[]{:S(2)}) copy-start(bf16[32,1024]{1,0:T(8,128)(2,1)} %param.10) | copy-start | bytes 196612
  3.1 53.3 %all-to-all-start = ((bf16[8,64,1408]{2,1,0:T(8,128)(2,1)}), bf16[8,64,1408]{2,1,0:T(8,128)(2,1)S(1)}, u32[]{:S(2)}, u32[]{:S(2)}) async-start(bf16[8,64,1408]{2,1,0:T(8,128)(2,1)} %broadcast_in_dim.2), calls=%async_computation | async-start | bytes 2883584 | tf_op jit(solution)/shard_map/all_to_all | solution.py:131
  45.5 14.4 %collective-permute-start.1 = (bf16[256,1024]{1,0:T(8,128)(2,1)S(1)}, bf16[256,1024]{1,0:T(8,128)(2,1)S(1)}, u32[]{:S(2)}, u32[]{:S(2)}) collective-permute-start(bf16[256,1024]{1,0:T(8,128)(2,1)S(1)} %shard_map.83.refs_0_), channel_id=1, source_target_pairs={{8,0},{16,8},{24,16},{32,24},{40,32},{48,40},{56,48},{64,56},{72,6... | collective-permute-start | bytes 1572872 | tf_op jit(solution)/shard_map/ppermute | solution.py:96
  48.0 15.2 %collective-permute-start = (bf16[256,1024]{1,0:T(8,128)(2,1)S(1)}, bf16[256,1024]{1,0:T(8,128)(2,1)S(1)}, u32[]{:S(2)}, u32[]{:S(2)}) collective-permute-start(bf16[256,1024]{1,0:T(8,128)(2,1)S(1)} %shard_map.83.refs_0_), channel_id=1, source_target_pairs={{0,128},{128,0},{1,129},{129,1},{2,130},{130,2},{3,131},{131,3},{4... | collective-permute-start | bytes 1572872 | tf_op jit(solution)/shard_map/ppermute | solution.py:112
  56.4 1.7 %copy-start.1 = (bf16[1280,1024]{1,0:T(8,128)(2,1)S(1)}, bf16[1280,1024]{1,0:T(8,128)(2,1)}, u32[]{:S(2)}) copy-start(bf16[1280,1024]{1,0:T(8,128)(2,1)} %w_ref.1) | copy-start | bytes 7864324
  58.2 6.6 %copy-start = (bf16[1024,1024]{1,0:T(8,128)(2,1)S(1)}, bf16[1024,1024]{1,0:T(8,128)(2,1)}, u32[]{:S(2)}) copy-start(bf16[1024,1024]{1,0:T(8,128)(2,1)} %constant.50.clone.order_ref) | copy-start | bytes 6291460
  59.9 4.8 %collective-permute-start.2 = (bf16[256,1024]{1,0:T(8,128)(2,1)S(1)}, bf16[256,1024]{1,0:T(8,128)(2,1)S(1)}, u32[]{:S(2)}, u32[]{:S(2)}) collective-permute-start(bf16[256,1024]{1,0:T(8,128)(2,1)S(1)} %shard_map.84.refs_2_), channel_id=1, source_target_pairs={{0,128},{128,0},{1,129},{129,1},{2,130},{130,2},{3,131},{131,3},{4... | collective-permute-start | bytes 1572872 | tf_op jit(solution)/shard_map/ppermute | solution.py:112
  93.3 5.0 %collective-permute-start.3 = (bf16[256,128]{1,0:T(8,128)(2,1)S(1)}, bf16[256,128]{1,0:T(8,128)(2,1)S(1)}, u32[]{:S(2)}, u32[]{:S(2)}) collective-permute-start(bf16[256,128]{1,0:T(8,128)(2,1)S(1)} %shard_map.86.mine_ref), channel_id=1, source_target_pairs={{0,256},{256,0},{1,257},{257,1},{2,258},{258,2},{3,259},{259,3},{4... | collective-permute-start | bytes 196616 | tf_op jit(solution)/shard_map/ppermute | solution.py:112
  99.3 6.1 %collective-permute-start.4 = (bf16[16,8,320]{2,1,0:T(8,128)(2,1)S(1)}, bf16[16,8,320]{2,1,0:T(8,128)(2,1)S(1)}, u32[]{:S(2)}, u32[]{:S(2)}) collective-permute-start(bf16[16,8,320]{2,1,0:T(8,128)(2,1)S(1)} %get-tuple-element.14), channel_id=1, source_target_pairs={{0,128},{128,0},{1,129},{129,1},{2,130},{130,2},{3,131},{131,3},{4... | collective-permute-start | bytes 245768 | tf_op jit(solution)/shard_map/ppermute | solution.py:112

commit v13 on v12

--- a/solution.py
+++ b/solution.py
@@ -125,16 +125,18 @@
     place = jnp.stack([yhi, ylo, core, x]).astype(jnp.int32)
     scale = jnp.concatenate([coldness, offset])
 
+    even = lax.all_gather(sounds, "zp", axis=0, tiled=True)
+
     halves = jnp.stack([matched >> 7, matched & 127], axis=2).reshape(128, 10).astype(BF)
     wide = jnp.concatenate([frames, jnp.pad(halves, ((0, 0), (0, PAD - 10)))], axis=1)
     wide = lax.dynamic_slice_in_dim(wide, core * 64, 64, 0)
+    wide = behind(wide, even)
     rows = lax.all_to_all(jnp.broadcast_to(wide[None], (8, 64, 1280 + PAD)), ("x", "yhi"), 0, 0, tiled=True)
     rows = rows.reshape(512, 1280 + PAD)
 
-    even = lax.all_gather(sounds, "zp", axis=0, tiled=True)
-    even = behind(even, ids, place, scale)
     odd = fetch(even)
     far_even = swap(even, "core")
+    odd = behind(odd, ids, place, scale)
     units = pl.pallas_call(
         project_kernel,
         in_specs=[vmem] * 2,
@@ -147,7 +149,6 @@
         compiler_params=PARAMS,
         cost_estimate=pl.CostEstimate(flops=2 * 512 * 1280 * 1024, bytes_accessed=9 * 2**20, transcendentals=0),
     )(rows, projector)
-    odd = behind(odd, units[2])
     far_odd = swap(odd, "core")
 
     parts = pl.pallas_call(

time: 126 us -> 127 us (level)
  starting transfers between devices: 29.1 us -> 31.5 us
  waiting for transfers between devices: 5.12 us -> 3.53 us
    ppermute x4, starting transfers between devices: 19.1 us -> 22.7 us  [swap(): return lax.ppermute(a, axis, [(0, 1), (1, 0)])]
    ppermute x4, waiting for transfers between devices: 5.11 us -> 3.52 us  [swap(): return lax.ppermute(a, axis, [(0, 1), (1, 0)])]
  transfers between devices with their start and end apart: 6 -> 6, of which waited for: 3 -> 2; matrix products, arithmetic and copies ran while one was open for 0% -> 0% of each run, Pallas kernels for 1% -> 1%
where the time goes in v13:
time: 127 us; the launch traced here: 126 us
  blocking collectives  75.3 us (59%)
  starting transfers between devices  31.5 us (25%)
  Pallas kernels  8.34 us (7%)
  waiting for transfers between devices  3.53 us (3%)
  local copies, waits for them, and re-layouts  3.16 us (2%)
  other arithmetic  2.55 us (2%)
  between operations  1.45 us (1%)
    all_gather x1, blocking collectives, local(): even = lax.all_gather(sounds, 'zp', axis=0, tiled=True)  33.3 us
    ppermute x4, starting transfers between devices, swap(): return lax.ppermute(a, axis, [(0, 1), (1, 0)])  22.7 us
    all_to_all x1, blocking collectives, local(): terms = lax.all_to_all(parts, PLANE, 0, 0, tiled=True)  22.7 us
    all_to_all x1, blocking collectives, local(): sums = lax.all_to_all(mine, Z, 0, 0, tiled=True)  19.3 us
    all_to_all x1, starting transfers between devices, local(): lax.all_to_all(jnp.broadcast_to(wide[None], (8, 64, 1280 + PAD)), ('x', '...  6.65 us
    pallas_call x1, Pallas kernels, local(): pl.pallas_call(pair_kernel, in_specs=[smem] + [vmem] * 10, out_specs=vmem...  5.44 us
    ppermute x4, waiting for transfers between devices, swap(): return lax.ppermute(a, axis, [(0, 1), (1, 0)])  3.52 us
  transfers between devices with their start and end apart: 6, of which 2 were waited for; matrix products, arithmetic and copies ran while one was open for 0% of the time, Pallas kernels for 1%

profile of v13, /device:TPU:1, one launch (start us, length us, event | category | flops | bytes accessed | tf_op | source)
XLA Modules:
  0.0 125.8 jit_solution(1760092221808187463)
XLA Ops:
  0.0 0.7 fusion.2
  0.7 0.1 copy.13
  0.9 33.3 %all_gather.3.refs_1_.refs_0_ = bf16[256,1024]{1,0:T(8,128)(2,1)S(1)} all-gather(bf16[32,1024]{1,0:T(8,128)(2,1)} %param.10), channel_id=1, replica_groups=mesh['ylo'=2,'core'=2,'zp'=8,'par'=2,'x'=4,'yhi'=2] {'zp'}, dimensions={0}, use_global_device_ids=true | all-gather | bytes 589824 | tf_op jit(solution)/shard_map/all_gather | solution.py:128
  34.2 0.9 fusion.1.refs_0_
  35.1 1.2 broadcast_in_dim.2
  36.4 6.7 %all-to-all-start = ((bf16[8,64,1408]{2,1,0:T(8,128)(2,1)}), bf16[8,64,1408]{2,1,0:T(8,128)(2,1)S(1)}, u32[]{:S(2)}, u32[]{:S(2)}) async-start(bf16[8,64,1408]{2,1,0:T(8,128)(2,1)} %broadcast_in_dim.2), calls=%async_computation | async-start | bytes 2883584 | tf_op jit(solution)/shard_map/all_to_all | solution.py:134
  43.0 2.1 %collective-permute-start.1 = (bf16[256,1024]{1,0:T(8,128)(2,1)S(1)}, bf16[256,1024]{1,0:T(8,128)(2,1)S(1)}, u32[]{:S(2)}, u32[]{:S(2)}) collective-permute-start(bf16[256,1024]{1,0:T(8,128)(2,1)S(1)} %all_gather.3.refs_1_.refs_0_), channel_id=1, source_target_pairs={{8,0},{16,8},{24,16},{32,24},{40,32},{48,40},{56,48},{64,56},{72,6... | collective-permute-start | bytes 1572872 | tf_op jit(solution)/shard_map/ppermute | solution.py:96
  45.1 9.7 %collective-permute-start = (bf16[256,1024]{1,0:T(8,128)(2,1)S(1)}, bf16[256,1024]{1,0:T(8,128)(2,1)S(1)}, u32[]{:S(2)}, u32[]{:S(2)}) collective-permute-start(bf16[256,1024]{1,0:T(8,128)(2,1)S(1)} %all_gather.3.refs_1_.refs_0_), channel_id=1, source_target_pairs={{0,128},{128,0},{1,129},{129,1},{2,130},{130,2},{3,131},{131,3},{4... | collective-permute-start | bytes 1572872 | tf_op jit(solution)/shard_map/ppermute | solution.py:112
  56.1 0.1 fusion.6
  56.3 0.1 pad_maximum_fusion.1.refs_3_.scale_ref
  56.4 0.1 pad_add_fusion.refs_2_.place_ref
  56.5 5.4 %collective-permute-start.2 = (bf16[256,1024]{1,0:T(8,128)(2,1)S(1)}, bf16[256,1024]{1,0:T(8,128)(2,1)S(1)}, u32[]{:S(2)}, u32[]{:S(2)}) collective-permute-start(bf16[256,1024]{1,0:T(8,128)(2,1)S(1)} %shard_map.84.refs_2_), channel_id=1, source_target_pairs={{0,128},{128,0},{1,129},{129,1},{2,130},{130,2},{3,131},{131,3},{4... | collective-permute-start | bytes 1572872 | tf_op jit(solution)/shard_map/ppermute | solution.py:112
  61.9 1.7 %copy-done.1 = bf16[1280,1024]{1,0:T(8,128)(2,1)S(1)} copy-done((bf16[1280,1024]{1,0:T(8,128)(2,1)S(1)}, bf16[1280,1024]{1,0:T(8,128)(2,1)}, u32[]{:S(2)}) %copy-start.1) | copy-done | bytes 2621464
  63.6 1.8 %shard_map.83 = (f32[512,1024]{1,0:T(8,128)S(1)}, bf16[512,1024]{1,0:T(8,128)(2,1)S(1)}, f32[512,128]{1,0:T(8,128)S(1)}) custom-call(bf16[512,1408]{1,0:T(8,128)(2,1)S(1)} %bitcast.19, bf16[1280,1024]{1,0:T(8,128)(2,1)S(1)} %copy-done.1), custom_call_target="tpu_custom_call" | custom-call | flops 1342177280 | bytes 9437184 | tf_op jit(solution)/shard_map/pallas_call | solution.py:140
  65.4 5.4 %shard_map.85 = bf16[16,256,128]{2,1,0:T(8,128)(2,1)S(1)} custom-call(f32[2]{0:T(128)S(1)} %pad_maximum_fusion.1.refs_3_.scale_ref, bf16[512,1408]{1,0:T(8,128)(2,1)S(1)} %bitcast.20, f32[512,1024]{1,0:T(8,128)S(1)} %get-tuple-element.10.unit_ref, bf16[512,1024]{1,0:T(8,128)(2,1)S(1)} %get-tuple-element.11.unit_b_ref, ...), custom_call_target="tpu_custom_call" | custom-call | flops 2684354560 | bytes 8388608 | tf_op jit(solution)/shard_map/pallas_call | solution.py:154
  70.9 22.7 %all_to_all.15.g_ref = bf16[16,256,128]{2,1,0:T(8,128)(2,1)S(1)} all-to-all(bf16[16,256,128]{2,1,0:T(8,128)(2,1)S(1)} %shard_map.85), channel_id=1, replica_groups=mesh['ylo'=2,'core'=2,'zp'=8,'par'=2,'x'=4,'yhi'=2] {'x','yhi','ylo'}, dimensions={0} | all-to-all | bytes 2097152 | tf_op jit(solution)/shard_map/all_to_all | solution.py:173
  93.6 0.1 shard_map.86.mine_ref
  93.7 2.4 %collective-permute-start.3 = (bf16[256,128]{1,0:T(8,128)(2,1)S(1)}, bf16[256,128]{1,0:T(8,128)(2,1)S(1)}, u32[]{:S(2)}, u32[]{:S(2)}) collective-permute-start(bf16[256,128]{1,0:T(8,128)(2,1)S(1)} %shard_map.86.mine_ref), channel_id=1, source_target_pairs={{0,256},{256,0},{1,257},{257,1},{2,258},{258,2},{3,259},{259,3},{4... | collective-permute-start | bytes 196616 | tf_op jit(solution)/shard_map/ppermute | solution.py:112
  96.1 2.6 %collective-permute-done.3.other_ref = bf16[256,128]{1,0:T(8,128)(2,1)S(1)} collective-permute-done((bf16[256,128]{1,0:T(8,128)(2,1)S(1)}, bf16[256,128]{1,0:T(8,128)(2,1)S(1)}, u32[]{:S(2)}, u32[]{:S(2)}) %collective-permute-start.3) | collective-permute-done | bytes 65568 | tf_op jit(solution)/shard_map/ppermute | solution.py:112
  98.7 1.0 shard_map.87
  99.7 5.2 %collective-permute-start.4 = (bf16[16,8,320]{2,1,0:T(8,128)(2,1)S(1)}, bf16[16,8,320]{2,1,0:T(8,128)(2,1)S(1)}, u32[]{:S(2)}, u32[]{:S(2)}) collective-permute-start(bf16[16,8,320]{2,1,0:T(8,128)(2,1)S(1)} %get-tuple-element.14), channel_id=1, source_target_pairs={{0,128},{128,0},{1,129},{129,1},{2,130},{130,2},{3,131},{131,3},{4... | collective-permute-start | bytes 245768 | tf_op jit(solution)/shard_map/ppermute | solution.py:112
  104.9 0.9 collective-permute-done.4.b_ref
  105.9 19.3 %all_to_all.16 = bf16[16,8,320]{2,1,0:T(8,128)(2,1)S(1)} all-to-all(bf16[16,8,320]{2,1,0:T(8,128)(2,1)S(1)} %shard_map.88), channel_id=1, replica_groups=mesh['ylo'=2,'core'=2,'zp'=8,'par'=2,'x'=4,'yhi'=2] {'zp','par'}, dimensions={0} | all-to-all | bytes 163840 | tf_op jit(solution)/shard_map/all_to_all | solution.py:191
  125.2 0.6 convert_reduce_fusion
  (17 shorter events, 0.2 us)
Async XLA Ops:
  35.1 21.1 %copy-start.2 = (s32[256]{0:T(256)S(1)}, s32[256]{0:T(256)}, u32[]{:S(2)}) copy-start(s32[256]{0:T(256)} %constant.54) | copy-start | bytes 3076
  36.4 25.5 %all-to-all-start = ((bf16[8,64,1408]{2,1,0:T(8,128)(2,1)}), bf16[8,64,1408]{2,1,0:T(8,128)(2,1)S(1)}, u32[]{:S(2)}, u32[]{:S(2)}) async-start(bf16[8,64,1408]{2,1,0:T(8,128)(2,1)} %broadcast_in_dim.2), calls=%async_computation | async-start | bytes 2883584 | tf_op jit(solution)/shard_map/all_to_all | solution.py:134
  43.0 13.4 %collective-permute-start.1 = (bf16[256,1024]{1,0:T(8,128)(2,1)S(1)}, bf16[256,1024]{1,0:T(8,128)(2,1)S(1)}, u32[]{:S(2)}, u32[]{:S(2)}) collective-permute-start(bf16[256,1024]{1,0:T(8,128)(2,1)S(1)} %all_gather.3.refs_1_.refs_0_), channel_id=1, source_target_pairs={{8,0},{16,8},{24,16},{32,24},{40,32},{48,40},{56,48},{64,56},{72,6... | collective-permute-start | bytes 1572872 | tf_op jit(solution)/shard_map/ppermute | solution.py:96
  45.1 20.3 %collective-permute-start = (bf16[256,1024]{1,0:T(8,128)(2,1)S(1)}, bf16[256,1024]{1,0:T(8,128)(2,1)S(1)}, u32[]{:S(2)}, u32[]{:S(2)}) collective-permute-start(bf16[256,1024]{1,0:T(8,128)(2,1)S(1)} %all_gather.3.refs_1_.refs_0_), channel_id=1, source_target_pairs={{0,128},{128,0},{1,129},{129,1},{2,130},{130,2},{3,131},{131,3},{4... | collective-permute-start | bytes 1572872 | tf_op jit(solution)/shard_map/ppermute | solution.py:112
  56.5 8.9 %collective-permute-start.2 = (bf16[256,1024]{1,0:T(8,128)(2,1)S(1)}, bf16[256,1024]{1,0:T(8,128)(2,1)S(1)}, u32[]{:S(2)}, u32[]{:S(2)}) collective-permute-start(bf16[256,1024]{1,0:T(8,128)(2,1)S(1)} %shard_map.84.refs_2_), channel_id=1, source_target_pairs={{0,128},{128,0},{1,129},{129,1},{2,130},{130,2},{3,131},{131,3},{4... | collective-permute-start | bytes 1572872 | tf_op jit(solution)/shard_map/ppermute | solution.py:112
  61.9 1.7 %copy-start.1 = (bf16[1280,1024]{1,0:T(8,128)(2,1)S(1)}, bf16[1280,1024]{1,0:T(8,128)(2,1)}, u32[]{:S(2)}) copy-start(bf16[1280,1024]{1,0:T(8,128)(2,1)} %w_ref.1) | copy-start | bytes 7864324
  63.6 1.8 %copy-start = (bf16[1024,1024]{1,0:T(8,128)(2,1)S(1)}, bf16[1024,1024]{1,0:T(8,128)(2,1)}, u32[]{:S(2)}) copy-start(bf16[1024,1024]{1,0:T(8,128)(2,1)} %constant.50.clone.order_ref) | copy-start | bytes 6291460
  93.7 5.0 %collective-permute-start.3 = (bf16[256,128]{1,0:T(8,128)(2,1)S(1)}, bf16[256,128]{1,0:T(8,128)(2,1)S(1)}, u32[]{:S(2)}, u32[]{:S(2)}) collective-permute-start(bf16[256,128]{1,0:T(8,128)(2,1)S(1)} %shard_map.86.mine_ref), channel_id=1, source_target_pairs={{0,256},{256,0},{1,257},{257,1},{2,258},{258,2},{3,259},{259,3},{4... | collective-permute-start | bytes 196616 | tf_op jit(solution)/shard_map/ppermute | solution.py:112
  99.7 6.2 %collective-permute-start.4 = (bf16[16,8,320]{2,1,0:T(8,128)(2,1)S(1)}, bf16[16,8,320]{2,1,0:T(8,128)(2,1)S(1)}, u32[]{:S(2)}, u32[]{:S(2)}) collective-permute-start(bf16[16,8,320]{2,1,0:T(8,128)(2,1)S(1)} %get-tuple-element.14), channel_id=1, source_target_pairs={{0,128},{128,0},{1,129},{129,1},{2,130},{130,2},{3,131},{131,3},{4... | collective-permute-start | bytes 245768 | tf_op jit(solution)/shard_map/ppermute | solution.py:112

commit v14 on v12

--- a/solution.py
+++ b/solution.py
@@ -22,6 +22,26 @@
     was = np.arange(1024)
     goes = (was // 8 % 8) * 128 + (was // 64) * 8 + was % 8
     return jnp.asarray(goes[:, None] == was[None, :], BF)
+
+
+def spread_kernel(core_ref, frames_ref, matched_ref, out_ref, held, sems):
+    rows = pl.ds(pl.multiple_of(core_ref[0] * 64, 64), 64)
+    load = pltpu.make_async_copy(frames_ref.at[rows], held.at[:, pl.ds(0, 1280)], sems.at[8])
+    load.start()
+    targets = matched_ref[rows, :]
+    lane = lax.broadcasted_iota(jnp.int32, (64, PAD), 1)
+    halves = jnp.zeros((64, PAD), jnp.int32)
+    for p in range(5):
+        target = targets[:, p : p + 1]
+        halves = jnp.where(lane == 2 * p, target >> 7, halves)
+        halves = jnp.where(lane == 2 * p + 1, target & 127, halves)
+    held[:, 1280:] = halves.astype(F32).astype(BF)
+    load.wait()
+    copies = [pltpu.make_async_copy(held, out_ref.at[i], sems.at[i]) for i in range(8)]
+    for copy in copies:
+        copy.start()
+    for copy in copies:
+        copy.wait()
 
 
 def project_kernel(x_ref, w_ref, unit_ref, unit_b_ref, mag_ref):
@@ -125,14 +145,18 @@
     place = jnp.stack([yhi, ylo, core, x]).astype(jnp.int32)
     scale = jnp.concatenate([coldness, offset])
 
-    halves = jnp.stack([matched >> 7, matched & 127], axis=2).reshape(128, 10).astype(BF)
-    wide = jnp.concatenate([frames, jnp.pad(halves, ((0, 0), (0, PAD - 10)))], axis=1)
-    wide = lax.dynamic_slice_in_dim(wide, core * 64, 64, 0)
-    rows = lax.all_to_all(jnp.broadcast_to(wide[None], (8, 64, 1280 + PAD)), ("x", "yhi"), 0, 0, tiled=True)
+    wide = pl.pallas_call(
+        spread_kernel,
+        in_specs=[smem, pl.BlockSpec(memory_space=pltpu.HBM), vmem],
+        out_specs=pl.BlockSpec(memory_space=pltpu.HBM),
+        out_shape=jax.ShapeDtypeStruct((8, 64, 1280 + PAD), BF),
+        scratch_shapes=[pltpu.VMEM((64, 1280 + PAD), BF), pltpu.SemaphoreType.DMA((9,))],
+        compiler_params=pltpu.CompilerParams(vmem_limit_bytes=4 * 2**20),
+    )(core.reshape(1).astype(jnp.int32), pltpu.with_memory_space_constraint(frames, pltpu.HBM), matched)
+    rows = lax.all_to_all(wide, ("x", "yhi"), 0, 0, tiled=True)
     rows = rows.reshape(512, 1280 + PAD)
 
     even = lax.all_gather(sounds, "zp", axis=0, tiled=True)
-    even = behind(even, ids, place, scale)
     odd = fetch(even)
     far_even = swap(even, "core")
     units = pl.pallas_call(
@@ -147,7 +171,7 @@
         compiler_params=PARAMS,
         cost_estimate=pl.CostEstimate(flops=2 * 512 * 1280 * 1024, bytes_accessed=9 * 2**20, transcendentals=0),
     )(rows, projector)
-    odd = behind(odd, units[2])
+    odd = behind(odd, units[2], ids, place, scale)
     far_odd = swap(odd, "core")
 
     parts = pl.pallas_call(

time: 126 us -> 124 us (0.984)
  Pallas kernels: 8.34 us -> 10.5 us
  other arithmetic: 2.56 us -> 0.92 us
    pallas_call x0 -> x1, Pallas kernels: none -> 2.16 us  [local(): pl.pallas_call(spread_kernel, in_specs=[smem, pl.BlockSpec(memory_space=p...]
where the time goes in v14:
time: 124 us; the launch traced here: 123 us
  blocking collectives  74.3 us (60%)
  starting transfers between devices  28.3 us (23%)
  Pallas kernels  10.5 us (8%)
  waiting for transfers between devices  5.4 us (4%)
  local copies, waits for them, and re-layouts  2.56 us (2%)
  between operations  1.44 us (1%)
    all_gather x1, blocking collectives, local(): even = lax.all_gather(sounds, 'zp', axis=0, tiled=True)  33.1 us
    all_to_all x1, blocking collectives, local(): terms = lax.all_to_all(parts, PLANE, 0, 0, tiled=True)  22.4 us
    all_to_all x1, blocking collectives, local(): sums = lax.all_to_all(mine, Z, 0, 0, tiled=True)  18.9 us
    ppermute x4, starting transfers between devices, swap(): return lax.ppermute(a, axis, [(0, 1), (1, 0)])  18.3 us
    all_to_all x1, starting transfers between devices, local(): rows = lax.all_to_all(wide, ('x', 'yhi'), 0, 0, tiled=True)  7.49 us
    pallas_call x1, Pallas kernels, local(): pl.pallas_call(pair_kernel, in_specs=[smem] + [vmem] * 10, out_specs=vmem...  5.45 us
    ppermute x4, waiting for transfers between devices, swap(): return lax.ppermute(a, axis, [(0, 1), (1, 0)])  5.39 us
    unnamed x10, local copies, waits for them, and re-layouts  2.56 us
  transfers between devices with their start and end apart: 6, of which 3 were waited for; matrix products, arithmetic and copies ran while one was open for 0% of the time, Pallas kernels for 1%

profile of v14, /device:TPU:1, one launch (start us, length us, event | category | flops | bytes accessed | tf_op | source)
XLA Modules:
  0.0 123.5 jit_solution(6154062633136017483)
XLA Ops:
  0.0 0.8 copy.10.matched_ref
  0.8 2.2 %shard_map.82 = bf16[8,64,1408]{2,1,0:T(8,128)(2,1)} custom-call(s32[1]{0:T(128)} %bitcast.2.core_ref, bf16[128,1280]{1,0:T(8,128)(2,1)} %frames_ref.1, s32[128,5]{1,0:T(8,128)S(1)} %copy.10.matched_ref), custom_call_target="tpu_custom_call" | custom-call | tf_op jit(solution)/shard_map/pallas_call | solution.py:148
  3.0 7.5 %all-to-all-start = ((bf16[8,64,1408]{2,1,0:T(8,128)(2,1)}), bf16[8,64,1408]{2,1,0:T(8,128)(2,1)S(1)}, u32[]{:S(2)}, u32[]{:S(2)}) async-start(bf16[8,64,1408]{2,1,0:T(8,128)(2,1)} %shard_map.82), calls=%async_computation | async-start | bytes 2883584 | tf_op jit(solution)/shard_map/all_to_all | solution.py:156
  10.5 33.1 %all_gather.3.refs_0_ = bf16[256,1024]{1,0:T(8,128)(2,1)S(1)} all-gather(bf16[32,1024]{1,0:T(8,128)(2,1)S(1)} %copy-done.2), channel_id=1, replica_groups=mesh['ylo'=2,'core'=2,'zp'=8,'par'=2,'x'=4,'yhi'=2] {'zp'}, dimensions={0}, use_global_device_ids=true | all-gather | bytes 589824 | tf_op jit(solution)/shard_map/all_gather | solution.py:159
  43.6 2.5 %collective-permute-start.1 = (bf16[256,1024]{1,0:T(8,128)(2,1)S(1)}, bf16[256,1024]{1,0:T(8,128)(2,1)S(1)}, u32[]{:S(2)}, u32[]{:S(2)}) collective-permute-start(bf16[256,1024]{1,0:T(8,128)(2,1)S(1)} %all_gather.3.refs_0_), channel_id=1, source_target_pairs={{8,0},{16,8},{24,16},{32,24},{40,32},{48,40},{56,48},{64,56},{72,6... | collective-permute-start | bytes 1572872 | tf_op jit(solution)/shard_map/ppermute | solution.py:116
  46.1 8.7 %collective-permute-start = (bf16[256,1024]{1,0:T(8,128)(2,1)S(1)}, bf16[256,1024]{1,0:T(8,128)(2,1)S(1)}, u32[]{:S(2)}, u32[]{:S(2)}) collective-permute-start(bf16[256,1024]{1,0:T(8,128)(2,1)S(1)} %all_gather.3.refs_0_), channel_id=1, source_target_pairs={{0,128},{128,0},{1,129},{129,1},{2,130},{130,2},{3,131},{131,3},{4... | collective-permute-start | bytes 1572872 | tf_op jit(solution)/shard_map/ppermute | solution.py:132
  56.1 0.1 fusion.2
  56.2 0.1 convert_bitcast_fusion
  56.3 0.1 pad_maximum_fusion.refs_4_.scale_ref
  56.4 0.1 pad_add_fusion.refs_3_.place_ref
  56.5 1.7 %copy-done.1 = bf16[1280,1024]{1,0:T(8,128)(2,1)S(1)} copy-done((bf16[1280,1024]{1,0:T(8,128)(2,1)S(1)}, bf16[1280,1024]{1,0:T(8,128)(2,1)}, u32[]{:S(2)}) %copy-start.1) | copy-done | bytes 2621464
  58.2 1.8 %shard_map.83 = (f32[512,1024]{1,0:T(8,128)S(1)}, bf16[512,1024]{1,0:T(8,128)(2,1)S(1)}, f32[512,128]{1,0:T(8,128)S(1)}) custom-call(bf16[512,1408]{1,0:T(8,128)(2,1)S(1)} %bitcast.13, bf16[1280,1024]{1,0:T(8,128)(2,1)S(1)} %copy-done.1), custom_call_target="tpu_custom_call" | custom-call | flops 1342177280 | bytes 9437184 | tf_op jit(solution)/shard_map/pallas_call | solution.py:162
  60.0 1.9 %collective-permute-start.2 = (bf16[256,1024]{1,0:T(8,128)(2,1)S(1)}, bf16[256,1024]{1,0:T(8,128)(2,1)S(1)}, u32[]{:S(2)}, u32[]{:S(2)}) collective-permute-start(bf16[256,1024]{1,0:T(8,128)(2,1)S(1)} %shard_map.84.refs_2_), channel_id=1, source_target_pairs={{0,128},{128,0},{1,129},{129,1},{2,130},{130,2},{3,131},{131,3},{4... | collective-permute-start | bytes 1572872 | tf_op jit(solution)/shard_map/ppermute | solution.py:132
  61.9 1.9 %collective-permute-done.2.refs_3_ = bf16[256,1024]{1,0:T(8,128)(2,1)S(1)} collective-permute-done((bf16[256,1024]{1,0:T(8,128)(2,1)S(1)}, bf16[256,1024]{1,0:T(8,128)(2,1)S(1)}, u32[]{:S(2)}, u32[]{:S(2)}) %collective-permute-start.2) | collective-permute-done | bytes 524320 | tf_op jit(solution)/shard_map/ppermute | solution.py:132
  63.8 5.5 %shard_map.85 = bf16[16,256,128]{2,1,0:T(8,128)(2,1)S(1)} custom-call(f32[2]{0:T(128)S(1)} %pad_maximum_fusion.refs_4_.scale_ref, bf16[512,1408]{1,0:T(8,128)(2,1)S(1)} %bitcast.14, f32[512,1024]{1,0:T(8,128)S(1)} %get-tuple-element.10.unit_ref, bf16[512,1024]{1,0:T(8,128)(2,1)S(1)} %get-tuple-element.11.unit_b_ref, ...), custom_call_target="tpu_custom_call" | custom-call | flops 2684354560 | bytes 8388608 | tf_op jit(solution)/shard_map/pallas_call | solution.py:177
  69.3 22.4 %all_to_all.15.g_ref = bf16[16,256,128]{2,1,0:T(8,128)(2,1)S(1)} all-to-all(bf16[16,256,128]{2,1,0:T(8,128)(2,1)S(1)} %shard_map.85), channel_id=1, replica_groups=mesh['ylo'=2,'core'=2,'zp'=8,'par'=2,'x'=4,'yhi'=2] {'x','yhi','ylo'}, dimensions={0} | all-to-all | bytes 2097152 | tf_op jit(solution)/shard_map/all_to_all | solution.py:196
  91.6 0.1 shard_map.86.mine_ref
  91.8 2.4 %collective-permute-start.3 = (bf16[256,128]{1,0:T(8,128)(2,1)S(1)}, bf16[256,128]{1,0:T(8,128)(2,1)S(1)}, u32[]{:S(2)}, u32[]{:S(2)}) collective-permute-start(bf16[256,128]{1,0:T(8,128)(2,1)S(1)} %shard_map.86.mine_ref), channel_id=1, source_target_pairs={{0,256},{256,0},{1,257},{257,1},{2,258},{258,2},{3,259},{259,3},{4... | collective-permute-start | bytes 196616 | tf_op jit(solution)/shard_map/ppermute | solution.py:132
  94.2 2.6 %collective-permute-done.3.other_ref = bf16[256,128]{1,0:T(8,128)(2,1)S(1)} collective-permute-done((bf16[256,128]{1,0:T(8,128)(2,1)S(1)}, bf16[256,128]{1,0:T(8,128)(2,1)S(1)}, u32[]{:S(2)}, u32[]{:S(2)}) %collective-permute-start.3) | collective-permute-done | bytes 65568 | tf_op jit(solution)/shard_map/ppermute | solution.py:132
  96.8 1.0 shard_map.87
  97.8 5.2 %collective-permute-start.4 = (bf16[16,8,320]{2,1,0:T(8,128)(2,1)S(1)}, bf16[16,8,320]{2,1,0:T(8,128)(2,1)S(1)}, u32[]{:S(2)}, u32[]{:S(2)}) collective-permute-start(bf16[16,8,320]{2,1,0:T(8,128)(2,1)S(1)} %get-tuple-element.14), channel_id=1, source_target_pairs={{0,128},{128,0},{1,129},{129,1},{2,130},{130,2},{3,131},{131,3},{4... | collective-permute-start | bytes 245768 | tf_op jit(solution)/shard_map/ppermute | solution.py:132
  103.0 0.9 collective-permute-done.4.b_ref
  104.0 18.9 %all_to_all.16 = bf16[16,8,320]{2,1,0:T(8,128)(2,1)S(1)} all-to-all(bf16[16,8,320]{2,1,0:T(8,128)(2,1)S(1)} %shard_map.88), channel_id=1, replica_groups=mesh['ylo'=2,'core'=2,'zp'=8,'par'=2,'x'=4,'yhi'=2] {'zp','par'}, dimensions={0} | all-to-all | bytes 163840 | tf_op jit(solution)/shard_map/all_to_all | solution.py:214
  122.9 0.6 convert_reduce_fusion
  (13 shorter events, 0.1 us)
Async XLA Ops:
  0.8 9.7 %copy-start.2 = (bf16[32,1024]{1,0:T(8,128)(2,1)S(1)}, bf16[32,1024]{1,0:T(8,128)(2,1)}, u32[]{:S(2)}) copy-start(bf16[32,1024]{1,0:T(8,128)(2,1)} %param.10) | copy-start | bytes 196612
  3.0 53.3 %copy-start.3 = (s32[256]{0:T(256)S(1)}, s32[256]{0:T(256)}, u32[]{:S(2)}) copy-start(s32[256]{0:T(256)} %constant.40) | copy-start | bytes 3076
  3.0 53.5 %all-to-all-start = ((bf16[8,64,1408]{2,1,0:T(8,128)(2,1)}), bf16[8,64,1408]{2,1,0:T(8,128)(2,1)S(1)}, u32[]{:S(2)}, u32[]{:S(2)}) async-start(bf16[8,64,1408]{2,1,0:T(8,128)(2,1)} %shard_map.82), calls=%async_computation | async-start | bytes 2883584 | tf_op jit(solution)/shard_map/all_to_all | solution.py:156
  43.6 16.4 %collective-permute-start.1 = (bf16[256,1024]{1,0:T(8,128)(2,1)S(1)}, bf16[256,1024]{1,0:T(8,128)(2,1)S(1)}, u32[]{:S(2)}, u32[]{:S(2)}) collective-permute-start(bf16[256,1024]{1,0:T(8,128)(2,1)S(1)} %all_gather.3.refs_0_), channel_id=1, source_target_pairs={{8,0},{16,8},{24,16},{32,24},{40,32},{48,40},{56,48},{64,56},{72,6... | collective-permute-start | bytes 1572872 | tf_op jit(solution)/shard_map/ppermute | solution.py:116
  46.1 15.8 %collective-permute-start = (bf16[256,1024]{1,0:T(8,128)(2,1)S(1)}, bf16[256,1024]{1,0:T(8,128)(2,1)S(1)}, u32[]{:S(2)}, u32[]{:S(2)}) collective-permute-start(bf16[256,1024]{1,0:T(8,128)(2,1)S(1)} %all_gather.3.refs_0_), channel_id=1, source_target_pairs={{0,128},{128,0},{1,129},{129,1},{2,130},{130,2},{3,131},{131,3},{4... | collective-permute-start | bytes 1572872 | tf_op jit(solution)/shard_map/ppermute | solution.py:132
  56.5 1.7 %copy-start.1 = (bf16[1280,1024]{1,0:T(8,128)(2,1)S(1)}, bf16[1280,1024]{1,0:T(8,128)(2,1)}, u32[]{:S(2)}) copy-start(bf16[1280,1024]{1,0:T(8,128)(2,1)} %w_ref.1) | copy-start | bytes 7864324
  58.2 5.6 %copy-start = (bf16[1024,1024]{1,0:T(8,128)(2,1)S(1)}, bf16[1024,1024]{1,0:T(8,128)(2,1)}, u32[]{:S(2)}) copy-start(bf16[1024,1024]{1,0:T(8,128)(2,1)} %constant.38.clone.order_ref) | copy-start | bytes 6291460
  60.0 3.8 %collective-permute-start.2 = (bf16[256,1024]{1,0:T(8,128)(2,1)S(1)}, bf16[256,1024]{1,0:T(8,128)(2,1)S(1)}, u32[]{:S(2)}, u32[]{:S(2)}) collective-permute-start(bf16[256,1024]{1,0:T(8,128)(2,1)S(1)} %shard_map.84.refs_2_), channel_id=1, source_target_pairs={{0,128},{128,0},{1,129},{129,1},{2,130},{130,2},{3,131},{131,3},{4... | collective-permute-start | bytes 1572872 | tf_op jit(solution)/shard_map/ppermute | solution.py:132
  91.8 5.0 %collective-permute-start.3 = (bf16[256,128]{1,0:T(8,128)(2,1)S(1)}, bf16[256,128]{1,0:T(8,128)(2,1)S(1)}, u32[]{:S(2)}, u32[]{:S(2)}) collective-permute-start(bf16[256,128]{1,0:T(8,128)(2,1)S(1)} %shard_map.86.mine_ref), channel_id=1, source_target_pairs={{0,256},{256,0},{1,257},{257,1},{2,258},{258,2},{3,259},{259,3},{4... | collective-permute-start | bytes 196616 | tf_op jit(solution)/shard_map/ppermute | solution.py:132
  97.8 6.2 %collective-permute-start.4 = (bf16[16,8,320]{2,1,0:T(8,128)(2,1)S(1)}, bf16[16,8,320]{2,1,0:T(8,128)(2,1)S(1)}, u32[]{:S(2)}, u32[]{:S(2)}) collective-permute-start(bf16[16,8,320]{2,1,0:T(8,128)(2,1)S(1)} %get-tuple-element.14), channel_id=1, source_target_pairs={{0,128},{128,0},{1,129},{129,1},{2,130},{130,2},{3,131},{131,3},{4... | collective-permute-start | bytes 245768 | tf_op jit(solution)/shard_map/ppermute | solution.py:132

commit v15 on v14

--- a/solution.py
+++ b/solution.py
@@ -53,20 +53,22 @@
     mag_ref[...] = jnp.broadcast_to(mag, mag_ref.shape)
 
 
-def pair_kernel(scale_ref, x_ref, unit_ref, unit_b_ref, mag_ref, ids_ref, order_ref, *refs):
+def pair_kernel(cold_ref, offset_ref, place_ref, x_ref, unit_ref, unit_b_ref, mag_ref, order_ref, *refs):
     *audio_refs, out_ref = refs
-    cold = scale_ref[0]
-    offset = scale_ref[1]
+    cold = cold_ref[0]
+    offset = offset_ref[0]
+    yhi, ylo, core, x, par = (place_ref[i] for i in range(5))
     unit_b = unit_b_ref[...]
     halves = x_ref[:, 1280:].astype(F32)
     targets = [halves[:, 2 * p : 2 * p + 1] * 128.0 + halves[:, 2 * p + 1 : 2 * p + 2] for p in range(5)]
     total = None
-    at = 0
-    for audio_ref in audio_refs:
+    lane = lax.broadcasted_iota(jnp.int32, (1, 256), 1)
+    inside = (lane >> 5) * 512 + (lane & 31)
+    for side, audio_ref in enumerate(audio_refs):
         audio = audio_ref[...]
-        n = audio.shape[0]
-        ids = ids_ref[:1, at : at + n]
-        at += n
+        on = core if side % 2 == 0 else 1 - core
+        odd = par if side < 2 else 1 - par
+        ids = (inside + (ylo * 8192 + on * 4096 + odd * 256 + (2 * x + yhi) * 32)).astype(F32)
         sims = lax.dot_general(unit_b, audio, (((1,), (1,)), ((), ())), preferred_element_type=F32)
         logits = cold * sims + offset
         hit = None
@@ -137,13 +139,7 @@
     smem = pl.BlockSpec(memory_space=pltpu.SMEM)
     vmem = pl.BlockSpec(memory_space=pltpu.VMEM)
 
-    pars = jnp.stack([par, par, 1 - par, 1 - par])
-    cores = jnp.stack([core, 1 - core, core, 1 - core])
-    firsts = ylo * 8192 + cores * 4096 + pars * 256 + (2 * x + yhi) * 32
-    inside = np.arange(8)[:, None] * 512 + np.arange(32)[None, :]
-    ids = (firsts[:, None] + jnp.asarray(inside.reshape(1, 256), jnp.int32)).astype(F32).reshape(1, 1024)
-    place = jnp.stack([yhi, ylo, core, x]).astype(jnp.int32)
-    scale = jnp.concatenate([coldness, offset])
+    place = jnp.stack([yhi, ylo, core, x, par]).astype(jnp.int32)
 
     wide = pl.pallas_call(
         spread_kernel,
@@ -171,21 +167,22 @@
         compiler_params=PARAMS,
         cost_estimate=pl.CostEstimate(flops=2 * 512 * 1280 * 1024, bytes_accessed=9 * 2**20, transcendentals=0),
     )(rows, projector)
-    odd = behind(odd, units[2], ids, place, scale)
+    odd = behind(odd, units[2], place)
     far_odd = swap(odd, "core")
 
     parts = pl.pallas_call(
         pair_kernel,
-        in_specs=[smem] + [vmem] * 10,
+        in_specs=[smem] * 3 + [vmem] * 9,
         out_specs=vmem,
         out_shape=jax.ShapeDtypeStruct((16, 256, 128), BF),
         compiler_params=PARAMS,
         cost_estimate=pl.CostEstimate(flops=5 * 512 * 1024 * 1024, bytes_accessed=8 * 2**20, transcendentals=2**20),
     )(
-        scale,
+        coldness,
+        offset,
+        place,
         rows,
         *units,
-        ids,
         column_order(),
         even,
         far_even,

time: 124 us -> 124 us (level)
  waiting for transfers between devices: 5.4 us -> 3.82 us
    ppermute x4, waiting for transfers between devices: 5.39 us -> 3.82 us  [swap(): return lax.ppermute(a, axis, [(0, 1), (1, 0)])]
    unnamed x10 -> x7, local copies, waits for them, and re-layouts: 2.56 us -> 2.54 us
where the time goes in v15:
time: 124 us; the launch traced here: 123 us
  blocking collectives  75.1 us (61%)
  starting transfers between devices  29.4 us (24%)
  Pallas kernels  10.5 us (8%)
  waiting for transfers between devices  3.82 us (3%)
  local copies, waits for them, and re-layouts  2.63 us (2%)
  between operations  1.41 us (1%)
    all_gather x1, blocking collectives, local(): even = lax.all_gather(sounds, 'zp', axis=0, tiled=True)  33.1 us
    all_to_all x1, blocking collectives, local(): terms = lax.all_to_all(parts, PLANE, 0, 0, tiled=True)  23 us
    ppermute x4, starting transfers between devices, swap(): return lax.ppermute(a, axis, [(0, 1), (1, 0)])  19.3 us
    all_to_all x1, blocking collectives, local(): sums = lax.all_to_all(mine, Z, 0, 0, tiled=True)  19 us
    all_to_all x1, starting transfers between devices, local(): rows = lax.all_to_all(wide, ('x', 'yhi'), 0, 0, tiled=True)  7.49 us
    pallas_call x1, Pallas kernels, local(): pl.pallas_call(pair_kernel, in_specs=[smem] * 3 + [vmem] * 9, out_specs=v...  5.43 us
    ppermute x4, waiting for transfers between devices, swap(): return lax.ppermute(a, axis, [(0, 1), (1, 0)])  3.82 us
    unnamed x7, local copies, waits for them, and re-layouts  2.54 us
  transfers between devices with their start and end apart: 6, of which 3 were waited for; matrix products, arithmetic and copies ran while one was open for 0% of the time, Pallas kernels for 1%

profile of v15, /device:TPU:1, one launch (start us, length us, event | category | flops | bytes accessed | tf_op | source)
XLA Modules:
  0.0 123.4 jit_solution(4158474301846115320)
XLA Ops:
  0.0 0.8 copy.9.matched_ref
  0.8 2.1 %shard_map.73 = bf16[8,64,1408]{2,1,0:T(8,128)(2,1)} custom-call(s32[1]{0:T(128)} %bitcast.2.core_ref, bf16[128,1280]{1,0:T(8,128)(2,1)} %frames_ref.1, s32[128,5]{1,0:T(8,128)S(1)} %copy.9.matched_ref), custom_call_target="tpu_custom_call" | custom-call | tf_op jit(solution)/shard_map/pallas_call | solution.py:144
  3.0 7.5 %all-to-all-start = ((bf16[8,64,1408]{2,1,0:T(8,128)(2,1)}), bf16[8,64,1408]{2,1,0:T(8,128)(2,1)S(1)}, u32[]{:S(2)}, u32[]{:S(2)}) async-start(bf16[8,64,1408]{2,1,0:T(8,128)(2,1)} %shard_map.73), calls=%async_computation | async-start | bytes 2883584 | tf_op jit(solution)/shard_map/all_to_all | solution.py:152
  10.5 33.1 %all_gather.3.refs_0_ = bf16[256,1024]{1,0:T(8,128)(2,1)S(1)} all-gather(bf16[32,1024]{1,0:T(8,128)(2,1)S(1)} %copy-done.2), channel_id=1, replica_groups=mesh['ylo'=2,'core'=2,'zp'=8,'par'=2,'x'=4,'yhi'=2] {'zp'}, dimensions={0}, use_global_device_ids=true | all-gather | bytes 589824 | tf_op jit(solution)/shard_map/all_gather | solution.py:155
  43.5 2.5 %collective-permute-start.1 = (bf16[256,1024]{1,0:T(8,128)(2,1)S(1)}, bf16[256,1024]{1,0:T(8,128)(2,1)S(1)}, u32[]{:S(2)}, u32[]{:S(2)}) collective-permute-start(bf16[256,1024]{1,0:T(8,128)(2,1)S(1)} %all_gather.3.refs_0_), channel_id=1, source_target_pairs={{8,0},{16,8},{24,16},{32,24},{40,32},{48,40},{56,48},{64,56},{72,6... | collective-permute-start | bytes 1572872 | tf_op jit(solution)/shard_map/ppermute | solution.py:118
  46.1 8.7 %collective-permute-start = (bf16[256,1024]{1,0:T(8,128)(2,1)S(1)}, bf16[256,1024]{1,0:T(8,128)(2,1)S(1)}, u32[]{:S(2)}, u32[]{:S(2)}) collective-permute-start(bf16[256,1024]{1,0:T(8,128)(2,1)S(1)} %all_gather.3.refs_0_), channel_id=1, source_target_pairs={{0,128},{128,0},{1,129},{129,1},{2,130},{130,2},{3,131},{131,3},{4... | collective-permute-start | bytes 1572872 | tf_op jit(solution)/shard_map/ppermute | solution.py:134
  54.8 0.1 stack.23.refs_2_.place_ref
  54.9 0.0 all-to-all-done
  54.9 1.7 %copy-done.1 = bf16[1280,1024]{1,0:T(8,128)(2,1)S(1)} copy-done((bf16[1280,1024]{1,0:T(8,128)(2,1)S(1)}, bf16[1280,1024]{1,0:T(8,128)(2,1)}, u32[]{:S(2)}) %copy-start.1) | copy-done | bytes 2621464
  56.6 1.8 %shard_map.74 = (f32[512,1024]{1,0:T(8,128)S(1)}, bf16[512,1024]{1,0:T(8,128)(2,1)S(1)}, f32[512,128]{1,0:T(8,128)S(1)}) custom-call(bf16[512,1408]{1,0:T(8,128)(2,1)S(1)} %bitcast.7, bf16[1280,1024]{1,0:T(8,128)(2,1)S(1)} %copy-done.1), custom_call_target="tpu_custom_call" | custom-call | flops 1342177280 | bytes 9437184 | tf_op jit(solution)/shard_map/pallas_call | solution.py:158
  58.4 0.0 collective-permute-done.1.refs_0_
  58.4 3.1 %collective-permute-start.2 = (bf16[256,1024]{1,0:T(8,128)(2,1)S(1)}, bf16[256,1024]{1,0:T(8,128)(2,1)S(1)}, u32[]{:S(2)}, u32[]{:S(2)}) collective-permute-start(bf16[256,1024]{1,0:T(8,128)(2,1)S(1)} %shard_map.75.refs_2_), channel_id=1, source_target_pairs={{0,128},{128,0},{1,129},{129,1},{2,130},{130,2},{3,131},{131,3},{4... | collective-permute-start | bytes 1572872 | tf_op jit(solution)/shard_map/ppermute | solution.py:134
  62.9 0.0 collective-permute-done.refs_1_
  62.9 0.2 collective-permute-done.2.refs_3_
  63.1 5.4 %shard_map.76 = bf16[16,256,128]{2,1,0:T(8,128)(2,1)S(1)} custom-call(f32[1]{0:T(128)S(6)} %copy.11.cold_ref, f32[1]{0:T(128)S(6)} %copy.12.offset_ref, s32[5]{0:T(128)S(1)} %stack.23.refs_2_.place_ref, bf16[512,1408]{1,0:T(8,128)(2,1)S(1)} %bitcast.8, f32[512,1024]{1,0:T(8,128)S(1)} %get-tuple-element.10.unit_ref, ...), custom_call_target="tpu_custom_call" | custom-call | flops 2684354560 | bytes 8388608 | tf_op jit(solution)/shard_map/pallas_call | solution.py:173
  68.5 23.0 %all_to_all.15.g_ref = bf16[16,256,128]{2,1,0:T(8,128)(2,1)S(1)} all-to-all(bf16[16,256,128]{2,1,0:T(8,128)(2,1)S(1)} %shard_map.76), channel_id=1, replica_groups=mesh['ylo'=2,'core'=2,'zp'=8,'par'=2,'x'=4,'yhi'=2] {'x','yhi','ylo'}, dimensions={0} | all-to-all | bytes 2097152 | tf_op jit(solution)/shard_map/all_to_all | solution.py:193
  91.5 0.1 shard_map.77.mine_ref
  91.7 2.3 %collective-permute-start.3 = (bf16[256,128]{1,0:T(8,128)(2,1)S(1)}, bf16[256,128]{1,0:T(8,128)(2,1)S(1)}, u32[]{:S(2)}, u32[]{:S(2)}) collective-permute-start(bf16[256,128]{1,0:T(8,128)(2,1)S(1)} %shard_map.77.mine_ref), channel_id=1, source_target_pairs={{0,256},{256,0},{1,257},{257,1},{2,258},{258,2},{3,259},{259,3},{4... | collective-permute-start | bytes 196616 | tf_op jit(solution)/shard_map/ppermute | solution.py:134
  94.0 2.7 %collective-permute-done.3.other_ref = bf16[256,128]{1,0:T(8,128)(2,1)S(1)} collective-permute-done((bf16[256,128]{1,0:T(8,128)(2,1)S(1)}, bf16[256,128]{1,0:T(8,128)(2,1)S(1)}, u32[]{:S(2)}, u32[]{:S(2)}) %collective-permute-start.3) | collective-permute-done | bytes 65568 | tf_op jit(solution)/shard_map/ppermute | solution.py:134
  96.7 1.0 shard_map.78
  97.7 5.1 %collective-permute-start.4 = (bf16[16,8,320]{2,1,0:T(8,128)(2,1)S(1)}, bf16[16,8,320]{2,1,0:T(8,128)(2,1)S(1)}, u32[]{:S(2)}, u32[]{:S(2)}) collective-permute-start(bf16[16,8,320]{2,1,0:T(8,128)(2,1)S(1)} %get-tuple-element.14), channel_id=1, source_target_pairs={{0,128},{128,0},{1,129},{129,1},{2,130},{130,2},{3,131},{131,3},{4... | collective-permute-start | bytes 245768 | tf_op jit(solution)/shard_map/ppermute | solution.py:134
  102.8 0.9 collective-permute-done.4.b_ref
  103.8 19.0 %all_to_all.16 = bf16[16,8,320]{2,1,0:T(8,128)(2,1)S(1)} all-to-all(bf16[16,8,320]{2,1,0:T(8,128)(2,1)S(1)} %shard_map.79), channel_id=1, replica_groups=mesh['ylo'=2,'core'=2,'zp'=8,'par'=2,'x'=4,'yhi'=2] {'zp','par'}, dimensions={0} | all-to-all | bytes 163840 | tf_op jit(solution)/shard_map/all_to_all | solution.py:211
  122.8 0.6 convert_reduce_fusion
  (7 shorter events, 0.0 us)
Async XLA Ops:
  0.8 9.7 %copy-start.2 = (bf16[32,1024]{1,0:T(8,128)(2,1)S(1)}, bf16[32,1024]{1,0:T(8,128)(2,1)}, u32[]{:S(2)}) copy-start(bf16[32,1024]{1,0:T(8,128)(2,1)} %param.9) | copy-start | bytes 196612
  3.0 51.9 %all-to-all-start = ((bf16[8,64,1408]{2,1,0:T(8,128)(2,1)}), bf16[8,64,1408]{2,1,0:T(8,128)(2,1)S(1)}, u32[]{:S(2)}, u32[]{:S(2)}) async-start(bf16[8,64,1408]{2,1,0:T(8,128)(2,1)} %shard_map.73), calls=%async_computation | async-start | bytes 2883584 | tf_op jit(solution)/shard_map/all_to_all | solution.py:152
  43.5 14.9 %collective-permute-start.1 = (bf16[256,1024]{1,0:T(8,128)(2,1)S(1)}, bf16[256,1024]{1,0:T(8,128)(2,1)S(1)}, u32[]{:S(2)}, u32[]{:S(2)}) collective-permute-start(bf16[256,1024]{1,0:T(8,128)(2,1)S(1)} %all_gather.3.refs_0_), channel_id=1, source_target_pairs={{8,0},{16,8},{24,16},{32,24},{40,32},{48,40},{56,48},{64,56},{72,6... | collective-permute-start | bytes 1572872 | tf_op jit(solution)/shard_map/ppermute | solution.py:118
  46.1 16.8 %collective-permute-start = (bf16[256,1024]{1,0:T(8,128)(2,1)S(1)}, bf16[256,1024]{1,0:T(8,128)(2,1)S(1)}, u32[]{:S(2)}, u32[]{:S(2)}) collective-permute-start(bf16[256,1024]{1,0:T(8,128)(2,1)S(1)} %all_gather.3.refs_0_), channel_id=1, source_target_pairs={{0,128},{128,0},{1,129},{129,1},{2,130},{130,2},{3,131},{131,3},{4... | collective-permute-start | bytes 1572872 | tf_op jit(solution)/shard_map/ppermute | solution.py:134
  54.9 1.7 %copy-start.1 = (bf16[1280,1024]{1,0:T(8,128)(2,1)S(1)}, bf16[1280,1024]{1,0:T(8,128)(2,1)}, u32[]{:S(2)}) copy-start(bf16[1280,1024]{1,0:T(8,128)(2,1)} %w_ref.1) | copy-start | bytes 7864324
  56.6 6.5 %copy-start = (bf16[1024,1024]{1,0:T(8,128)(2,1)S(1)}, bf16[1024,1024]{1,0:T(8,128)(2,1)}, u32[]{:S(2)}) copy-start(bf16[1024,1024]{1,0:T(8,128)(2,1)} %constant.23.clone.order_ref) | copy-start | bytes 6291460
  58.4 4.7 %collective-permute-start.2 = (bf16[256,1024]{1,0:T(8,128)(2,1)S(1)}, bf16[256,1024]{1,0:T(8,128)(2,1)S(1)}, u32[]{:S(2)}, u32[]{:S(2)}) collective-permute-start(bf16[256,1024]{1,0:T(8,128)(2,1)S(1)} %shard_map.75.refs_2_), channel_id=1, source_target_pairs={{0,128},{128,0},{1,129},{129,1},{2,130},{130,2},{3,131},{131,3},{4... | collective-permute-start | bytes 1572872 | tf_op jit(solution)/shard_map/ppermute | solution.py:134
  91.7 5.0 %collective-permute-start.3 = (bf16[256,128]{1,0:T(8,128)(2,1)S(1)}, bf16[256,128]{1,0:T(8,128)(2,1)S(1)}, u32[]{:S(2)}, u32[]{:S(2)}) collective-permute-start(bf16[256,128]{1,0:T(8,128)(2,1)S(1)} %shard_map.77.mine_ref), channel_id=1, source_target_pairs={{0,256},{256,0},{1,257},{257,1},{2,258},{258,2},{3,259},{259,3},{4... | collective-permute-start | bytes 196616 | tf_op jit(solution)/shard_map/ppermute | solution.py:134
  97.7 6.1 %collective-permute-start.4 = (bf16[16,8,320]{2,1,0:T(8,128)(2,1)S(1)}, bf16[16,8,320]{2,1,0:T(8,128)(2,1)S(1)}, u32[]{:S(2)}, u32[]{:S(2)}) collective-permute-start(bf16[16,8,320]{2,1,0:T(8,128)(2,1)S(1)} %get-tuple-element.14), channel_id=1, source_target_pairs={{0,128},{128,0},{1,129},{129,1},{2,130},{130,2},{3,131},{131,3},{4... | collective-permute-start | bytes 245768 | tf_op jit(solution)/shard_map/ppermute | solution.py:134

commit v16 on v15

--- a/solution.py
+++ b/solution.py
@@ -24,18 +24,24 @@
     return jnp.asarray(goes[:, None] == was[None, :], BF)
 
 
-def spread_kernel(core_ref, frames_ref, matched_ref, out_ref, held, sems):
+def spread_kernel(core_ref, frames_ref, matched_ref, out_ref, held, listed, sems):
     rows = pl.ds(pl.multiple_of(core_ref[0] * 64, 64), 64)
     load = pltpu.make_async_copy(frames_ref.at[rows], held.at[:, pl.ds(0, 1280)], sems.at[8])
     load.start()
-    targets = matched_ref[rows, :]
-    lane = lax.broadcasted_iota(jnp.int32, (64, PAD), 1)
-    halves = jnp.zeros((64, PAD), jnp.int32)
-    for p in range(5):
-        target = targets[:, p : p + 1]
-        halves = jnp.where(lane == 2 * p, target >> 7, halves)
-        halves = jnp.where(lane == 2 * p + 1, target & 127, halves)
-    held[:, 1280:] = halves.astype(F32).astype(BF)
+    fetch_targets = pltpu.make_async_copy(matched_ref, listed, sems.at[9])
+    fetch_targets.start()
+    fetch_targets.wait()
+    targets = listed[...]
+    lane = lax.broadcasted_iota(jnp.int32, (5, PAD), 1)
+    twice = lax.broadcasted_iota(jnp.int32, (5, PAD), 0) * 2
+    halves = None
+    for i, part in enumerate((targets >> 7, targets & 127)):
+        column = jnp.where(lane == twice + i, 1.0, 0.0).astype(BF)
+        term = lax.dot_general(
+            part.astype(F32).astype(BF), column, (((0,), (0,)), ((), ())), preferred_element_type=F32
+        )
+        halves = term if halves is None else halves + term
+    held[:, 1280:] = jnp.where(core_ref[0] == 0, halves[:64], halves[64:]).astype(BF)
     load.wait()
     copies = [pltpu.make_async_copy(held, out_ref.at[i], sems.at[i]) for i in range(8)]
     for copy in copies:
@@ -143,12 +149,12 @@
 
     wide = pl.pallas_call(
         spread_kernel,
-        in_specs=[smem, pl.BlockSpec(memory_space=pltpu.HBM), vmem],
+        in_specs=[smem, pl.BlockSpec(memory_space=pltpu.HBM), pl.BlockSpec(memory_space=pltpu.HBM)],
         out_specs=pl.BlockSpec(memory_space=pltpu.HBM),
         out_shape=jax.ShapeDtypeStruct((8, 64, 1280 + PAD), BF),
-        scratch_shapes=[pltpu.VMEM((64, 1280 + PAD), BF), pltpu.SemaphoreType.DMA((9,))],
+        scratch_shapes=[pltpu.VMEM((64, 1280 + PAD), BF), pltpu.VMEM((5, 128), jnp.int32), pltpu.SemaphoreType.DMA((10,))],
         compiler_params=pltpu.CompilerParams(vmem_limit_bytes=4 * 2**20),
-    )(core.reshape(1).astype(jnp.int32), pltpu.with_memory_space_constraint(frames, pltpu.HBM), matched)
+    )(core.reshape(1).astype(jnp.int32), pltpu.with_memory_space_constraint(frames, pltpu.HBM), pltpu.with_memory_space_constraint(matched.T, pltpu.HBM))
     rows = lax.all_to_all(wide, ("x", "yhi"), 0, 0, tiled=True)
     rows = rows.reshape(512, 1280 + PAD)
 

time: 124 us -> 124 us (level)
    unnamed x7 -> x6, local copies, waits for them, and re-layouts: 2.54 us -> 1.75 us
where the time goes in v16:
time: 124 us; the launch traced here: 123 us
  blocking collectives  75.1 us (61%)
  starting transfers between devices  29.4 us (24%)
  Pallas kernels  10.5 us (8%)
  waiting for transfers between devices  3.82 us (3%)
  local copies, waits for them, and re-layouts  1.83 us (1%)
  between operations  1.41 us (1%)
    all_gather x1, blocking collectives, local(): even = lax.all_gather(sounds, 'zp', axis=0, tiled=True)  33.1 us
    all_to_all x1, blocking collectives, local(): terms = lax.all_to_all(parts, PLANE, 0, 0, tiled=True)  22.9 us
    ppermute x4, starting transfers between devices, swap(): return lax.ppermute(a, axis, [(0, 1), (1, 0)])  19.3 us
    all_to_all x1, blocking collectives, local(): sums = lax.all_to_all(mine, Z, 0, 0, tiled=True)  19.2 us
    all_to_all x1, starting transfers between devices, local(): rows = lax.all_to_all(wide, ('x', 'yhi'), 0, 0, tiled=True)  7.49 us
    pallas_call x1, Pallas kernels, local(): pl.pallas_call(pair_kernel, in_specs=[smem] * 3 + [vmem] * 9, out_specs=v...  5.42 us
    ppermute x4, waiting for transfers between devices, swap(): return lax.ppermute(a, axis, [(0, 1), (1, 0)])  3.82 us
    ppermute x1, starting transfers between devices, fetch(): return lax.ppermute(a, ('core', *Z), perm)  2.53 us
  transfers between devices with their start and end apart: 6, of which 3 were waited for; matrix products, arithmetic and copies ran while one was open for 0% of the time, Pallas kernels for 1%

profile of v16, /device:TPU:1, one launch (start us, length us, event | category | flops | bytes accessed | tf_op | source)
XLA Modules:
  0.0 122.7 jit_solution(9342375339611689026)
XLA Ops:
  0.0 2.2 %shard_map.73 = bf16[8,64,1408]{2,1,0:T(8,128)(2,1)} custom-call(s32[1]{0:T(128)} %bitcast.2.core_ref, bf16[128,1280]{1,0:T(8,128)(2,1)} %frames_ref.1, s32[5,128]{1,0:T(8,128)} %bitcast.11), custom_call_target="tpu_custom_call" | custom-call | tf_op jit(solution)/shard_map/pallas_call | solution.py:150
  2.2 7.5 %all-to-all-start = ((bf16[8,64,1408]{2,1,0:T(8,128)(2,1)}), bf16[8,64,1408]{2,1,0:T(8,128)(2,1)S(1)}, u32[]{:S(2)}, u32[]{:S(2)}) async-start(bf16[8,64,1408]{2,1,0:T(8,128)(2,1)} %shard_map.73), calls=%async_computation | async-start | bytes 2883584 | tf_op jit(solution)/shard_map/all_to_all | solution.py:158
  9.7 0.0 copy-done.2
  9.7 33.1 %all_gather.3.refs_0_ = bf16[256,1024]{1,0:T(8,128)(2,1)S(1)} all-gather(bf16[32,1024]{1,0:T(8,128)(2,1)S(1)} %copy-done.2), channel_id=1, replica_groups=mesh['ylo'=2,'core'=2,'zp'=8,'par'=2,'x'=4,'yhi'=2] {'zp'}, dimensions={0}, use_global_device_ids=true | all-gather | bytes 589824 | tf_op jit(solution)/shard_map/all_gather | solution.py:161
  42.8 2.5 %collective-permute-start.1 = (bf16[256,1024]{1,0:T(8,128)(2,1)S(1)}, bf16[256,1024]{1,0:T(8,128)(2,1)S(1)}, u32[]{:S(2)}, u32[]{:S(2)}) collective-permute-start(bf16[256,1024]{1,0:T(8,128)(2,1)S(1)} %all_gather.3.refs_0_), channel_id=1, source_target_pairs={{8,0},{16,8},{24,16},{32,24},{40,32},{48,40},{56,48},{64,56},{72,6... | collective-permute-start | bytes 1572872 | tf_op jit(solution)/shard_map/ppermute | solution.py:124
  45.3 8.7 %collective-permute-start = (bf16[256,1024]{1,0:T(8,128)(2,1)S(1)}, bf16[256,1024]{1,0:T(8,128)(2,1)S(1)}, u32[]{:S(2)}, u32[]{:S(2)}) collective-permute-start(bf16[256,1024]{1,0:T(8,128)(2,1)S(1)} %all_gather.3.refs_0_), channel_id=1, source_target_pairs={{0,128},{128,0},{1,129},{129,1},{2,130},{130,2},{3,131},{131,3},{4... | collective-permute-start | bytes 1572872 | tf_op jit(solution)/shard_map/ppermute | solution.py:140
  54.1 0.1 stack.23.refs_2_.place_ref
  54.2 0.0 all-to-all-done
  54.2 1.7 %copy-done.1 = bf16[1280,1024]{1,0:T(8,128)(2,1)S(1)} copy-done((bf16[1280,1024]{1,0:T(8,128)(2,1)S(1)}, bf16[1280,1024]{1,0:T(8,128)(2,1)}, u32[]{:S(2)}) %copy-start.1) | copy-done | bytes 2621464
  55.9 1.8 %shard_map.74 = (f32[512,1024]{1,0:T(8,128)S(1)}, bf16[512,1024]{1,0:T(8,128)(2,1)S(1)}, f32[512,128]{1,0:T(8,128)S(1)}) custom-call(bf16[512,1408]{1,0:T(8,128)(2,1)S(1)} %bitcast.8, bf16[1280,1024]{1,0:T(8,128)(2,1)S(1)} %copy-done.1), custom_call_target="tpu_custom_call" | custom-call | flops 1342177280 | bytes 9437184 | tf_op jit(solution)/shard_map/pallas_call | solution.py:164
  57.7 0.0 collective-permute-done.1.refs_0_
  57.7 3.1 %collective-permute-start.2 = (bf16[256,1024]{1,0:T(8,128)(2,1)S(1)}, bf16[256,1024]{1,0:T(8,128)(2,1)S(1)}, u32[]{:S(2)}, u32[]{:S(2)}) collective-permute-start(bf16[256,1024]{1,0:T(8,128)(2,1)S(1)} %shard_map.75.refs_2_), channel_id=1, source_target_pairs={{0,128},{128,0},{1,129},{129,1},{2,130},{130,2},{3,131},{131,3},{4... | collective-permute-start | bytes 1572872 | tf_op jit(solution)/shard_map/ppermute | solution.py:140
  62.1 0.0 collective-permute-done.refs_1_
  62.1 0.2 collective-permute-done.2.refs_3_
  62.4 5.4 %shard_map.76 = bf16[16,256,128]{2,1,0:T(8,128)(2,1)S(1)} custom-call(f32[1]{0:T(128)S(6)} %copy.10.cold_ref, f32[1]{0:T(128)S(6)} %copy.11.offset_ref, s32[5]{0:T(128)S(1)} %stack.23.refs_2_.place_ref, bf16[512,1408]{1,0:T(8,128)(2,1)S(1)} %bitcast.9, f32[512,1024]{1,0:T(8,128)S(1)} %get-tuple-element.10.unit_ref, ...), custom_call_target="tpu_custom_call" | custom-call | flops 2684354560 | bytes 8388608 | tf_op jit(solution)/shard_map/pallas_call | solution.py:179
  67.8 22.9 %all_to_all.15.g_ref = bf16[16,256,128]{2,1,0:T(8,128)(2,1)S(1)} all-to-all(bf16[16,256,128]{2,1,0:T(8,128)(2,1)S(1)} %shard_map.76), channel_id=1, replica_groups=mesh['ylo'=2,'core'=2,'zp'=8,'par'=2,'x'=4,'yhi'=2] {'x','yhi','ylo'}, dimensions={0} | all-to-all | bytes 2097152 | tf_op jit(solution)/shard_map/all_to_all | solution.py:199
  90.7 0.1 shard_map.77.mine_ref
  90.8 2.3 %collective-permute-start.3 = (bf16[256,128]{1,0:T(8,128)(2,1)S(1)}, bf16[256,128]{1,0:T(8,128)(2,1)S(1)}, u32[]{:S(2)}, u32[]{:S(2)}) collective-permute-start(bf16[256,128]{1,0:T(8,128)(2,1)S(1)} %shard_map.77.mine_ref), channel_id=1, source_target_pairs={{0,256},{256,0},{1,257},{257,1},{2,258},{258,2},{3,259},{259,3},{4... | collective-permute-start | bytes 196616 | tf_op jit(solution)/shard_map/ppermute | solution.py:140
  93.2 2.7 %collective-permute-done.3.other_ref = bf16[256,128]{1,0:T(8,128)(2,1)S(1)} collective-permute-done((bf16[256,128]{1,0:T(8,128)(2,1)S(1)}, bf16[256,128]{1,0:T(8,128)(2,1)S(1)}, u32[]{:S(2)}, u32[]{:S(2)}) %collective-permute-start.3) | collective-permute-done | bytes 65568 | tf_op jit(solution)/shard_map/ppermute | solution.py:140
  95.9 1.0 shard_map.78
  96.8 5.1 %collective-permute-start.4 = (bf16[16,8,320]{2,1,0:T(8,128)(2,1)S(1)}, bf16[16,8,320]{2,1,0:T(8,128)(2,1)S(1)}, u32[]{:S(2)}, u32[]{:S(2)}) collective-permute-start(bf16[16,8,320]{2,1,0:T(8,128)(2,1)S(1)} %get-tuple-element.14), channel_id=1, source_target_pairs={{0,128},{128,0},{1,129},{129,1},{2,130},{130,2},{3,131},{131,3},{4... | collective-permute-start | bytes 245768 | tf_op jit(solution)/shard_map/ppermute | solution.py:140
  102.0 0.9 collective-permute-done.4.b_ref
  102.9 19.2 %all_to_all.16 = bf16[16,8,320]{2,1,0:T(8,128)(2,1)S(1)} all-to-all(bf16[16,8,320]{2,1,0:T(8,128)(2,1)S(1)} %shard_map.79), channel_id=1, replica_groups=mesh['ylo'=2,'core'=2,'zp'=8,'par'=2,'x'=4,'yhi'=2] {'zp','par'}, dimensions={0} | all-to-all | bytes 163840 | tf_op jit(solution)/shard_map/all_to_all | solution.py:217
  122.1 0.6 convert_reduce_fusion
  (6 shorter events, 0.0 us)
Async XLA Ops:
  0.0 9.7 %copy-start.2 = (bf16[32,1024]{1,0:T(8,128)(2,1)S(1)}, bf16[32,1024]{1,0:T(8,128)(2,1)}, u32[]{:S(2)}) copy-start(bf16[32,1024]{1,0:T(8,128)(2,1)} %param.9) | copy-start | bytes 196612
  2.2 51.9 %all-to-all-start = ((bf16[8,64,1408]{2,1,0:T(8,128)(2,1)}), bf16[8,64,1408]{2,1,0:T(8,128)(2,1)S(1)}, u32[]{:S(2)}, u32[]{:S(2)}) async-start(bf16[8,64,1408]{2,1,0:T(8,128)(2,1)} %shard_map.73), calls=%async_computation | async-start | bytes 2883584 | tf_op jit(solution)/shard_map/all_to_all | solution.py:158
  42.8 14.9 %collective-permute-start.1 = (bf16[256,1024]{1,0:T(8,128)(2,1)S(1)}, bf16[256,1024]{1,0:T(8,128)(2,1)S(1)}, u32[]{:S(2)}, u32[]{:S(2)}) collective-permute-start(bf16[256,1024]{1,0:T(8,128)(2,1)S(1)} %all_gather.3.refs_0_), channel_id=1, source_target_pairs={{8,0},{16,8},{24,16},{32,24},{40,32},{48,40},{56,48},{64,56},{72,6... | collective-permute-start | bytes 1572872 | tf_op jit(solution)/shard_map/ppermute | solution.py:124
  45.3 16.8 %collective-permute-start = (bf16[256,1024]{1,0:T(8,128)(2,1)S(1)}, bf16[256,1024]{1,0:T(8,128)(2,1)S(1)}, u32[]{:S(2)}, u32[]{:S(2)}) collective-permute-start(bf16[256,1024]{1,0:T(8,128)(2,1)S(1)} %all_gather.3.refs_0_), channel_id=1, source_target_pairs={{0,128},{128,0},{1,129},{129,1},{2,130},{130,2},{3,131},{131,3},{4... | collective-permute-start | bytes 1572872 | tf_op jit(solution)/shard_map/ppermute | solution.py:140
  54.2 1.7 %copy-start.1 = (bf16[1280,1024]{1,0:T(8,128)(2,1)S(1)}, bf16[1280,1024]{1,0:T(8,128)(2,1)}, u32[]{:S(2)}) copy-start(bf16[1280,1024]{1,0:T(8,128)(2,1)} %w_ref.1) | copy-start | bytes 7864324
  55.9 6.4 %copy-start = (bf16[1024,1024]{1,0:T(8,128)(2,1)S(1)}, bf16[1024,1024]{1,0:T(8,128)(2,1)}, u32[]{:S(2)}) copy-start(bf16[1024,1024]{1,0:T(8,128)(2,1)} %constant.23.clone.order_ref) | copy-start | bytes 6291460
  57.7 4.7 %collective-permute-start.2 = (bf16[256,1024]{1,0:T(8,128)(2,1)S(1)}, bf16[256,1024]{1,0:T(8,128)(2,1)S(1)}, u32[]{:S(2)}, u32[]{:S(2)}) collective-permute-start(bf16[256,1024]{1,0:T(8,128)(2,1)S(1)} %shard_map.75.refs_2_), channel_id=1, source_target_pairs={{0,128},{128,0},{1,129},{129,1},{2,130},{130,2},{3,131},{131,3},{4... | collective-permute-start | bytes 1572872 | tf_op jit(solution)/shard_map/ppermute | solution.py:140
  90.8 5.0 %collective-permute-start.3 = (bf16[256,128]{1,0:T(8,128)(2,1)S(1)}, bf16[256,128]{1,0:T(8,128)(2,1)S(1)}, u32[]{:S(2)}, u32[]{:S(2)}) collective-permute-start(bf16[256,128]{1,0:T(8,128)(2,1)S(1)} %shard_map.77.mine_ref), channel_id=1, source_target_pairs={{0,256},{256,0},{1,257},{257,1},{2,258},{258,2},{3,259},{259,3},{4... | collective-permute-start | bytes 196616 | tf_op jit(solution)/shard_map/ppermute | solution.py:140
  96.8 6.1 %collective-permute-start.4 = (bf16[16,8,320]{2,1,0:T(8,128)(2,1)S(1)}, bf16[16,8,320]{2,1,0:T(8,128)(2,1)S(1)}, u32[]{:S(2)}, u32[]{:S(2)}) collective-permute-start(bf16[16,8,320]{2,1,0:T(8,128)(2,1)S(1)} %get-tuple-element.14), channel_id=1, source_target_pairs={{0,128},{128,0},{1,129},{129,1},{2,130},{130,2},{3,131},{131,3},{4... | collective-permute-start | bytes 245768 | tf_op jit(solution)/shard_map/ppermute | solution.py:140
